TPU v7x, 512 devices: a whole 4x8x8 slice. The times are simulated.
512 devices in a mesh: tm: 64 (over z, y_hi, core), freq: 8 (over x, y_lo).
Axes of the slice: x: 4, y: 8 (y_hi: 4, y_lo: 2; y = y_hi * 2 + y_lo), z: 8, core: 2. Of those that a mesh axis runs over, the one named last changes fastest.
Arguments:
- tokens: bfloat16 [2, 64, 512, 768], P(None, 'freq', 'tm'), may hold values from -6 to 6
- cotangent: bfloat16 [2, 64, 512, 768], P(None, 'freq', 'tm'), may hold values from -6 to 6
- qkv_plain: bfloat16 [768, 1152], P(None, 'freq'), may hold values from -0.21875 to 0.21875
- qkv_shift: bfloat16 [768, 1152], P(None, 'freq'), may hold values from -0.21875 to 0.21875
- proj_plain: bfloat16 [384, 768], P('freq'), may hold values from -0.3125 to 0.3125
- proj_shift: bfloat16 [384, 768], P('freq'), may hold values from -0.3125 to 0.3125
- table_plain: float32 [12, 225], replicated, may hold values from -5 to 305
- table_shift: float32 [12, 225], replicated, may hold values from -5 to 305
Outputs:
- grad_tokens: bfloat16 [2, 64, 512, 768], P(None, 'freq', 'tm')
- grad_proj_plain: float32 [384, 768], P('freq')
- grad_proj_shift: float32 [384, 768], P('freq')
All inputs are finite; a program needn't handle non-finite values.
Results may differ from a plain program's by a relative error of at most 0.022.
Values may be sent and summed in bfloat16 or wider, within the bound.
No kernel may reach another device: no remote copies, remote signals or barrier semaphores. Data moves between devices by JAX's collectives and lax.ppermute only.
A program may use at most 64 MiB of HBM per device.

v0:
```python
import math

import jax
import jax.numpy as jnp
from jax import lax
from jax.sharding import PartitionSpec as P

D = 768
HEADS = 12
HEAD_DIM = 32
WIN = 8
REL = 225


NEG = -1e30
EPS = 1e-05


def from_behind(value, axis, steps):
    count = lax.axis_size(axis)
    pairs = [(source, (source + steps) % count) for source in range(count)]
    return lax.ppermute(value, axis, pairs)


def normalize(values):
    center = values - jnp.mean(values, axis=-1, keepdims=True)
    rstd = lax.rsqrt(jnp.mean(center * center, axis=-1, keepdims=True) + EPS)
    return (center * rstd, rstd)


def offset_bias(table):
    spots = jnp.arange(WIN * WIN)
    rows = spots // WIN
    cols = spots % WIN
    index = (
        (rows[:, None] - rows[None, :] + WIN - 1) * (2 * WIN - 1)
        + cols[:, None]
        - cols[None, :]
        + WIN
        - 1
    )
    onehot = (index.reshape(-1, 1) == jnp.arange(REL)[None, :]).astype(jnp.float32)
    bias = lax.dot_general(table, onehot, (((1,), (1,)), ((), ())), precision=lax.Precision.HIGHEST)
    return bias.reshape(HEADS, WIN * WIN, WIN * WIN)


def shift_mask(tile):
    spots = jnp.arange(tile * tile)
    rows = spots // tile
    cols = spots % tile
    last_freq = lax.axis_index("freq") == lax.axis_size("freq") - 1
    last_time = lax.axis_index("tm") == lax.axis_size("tm") - 1
    region_f = jnp.where(last_freq, 1 + (rows >= tile // 2).astype(jnp.int32), 0)
    region_t = jnp.where(last_time, 1 + (cols >= tile // 2).astype(jnp.int32), 0)
    label = region_f * 3 + region_t
    return label[:, None] == label[None, :]


def attend(window_tokens, w_qkv, bias, allow):
    samples = window_tokens.shape[0]
    spots = window_tokens.shape[1]
    normed, rstd = normalize(window_tokens.reshape(-1, D).astype(jnp.float32))
    packed = jnp.dot(normed.astype(jnp.bfloat16), w_qkv, preferred_element_type=jnp.float32).astype(
        jnp.bfloat16
    )
    packed = packed.reshape(samples, spots, 3, HEADS, HEAD_DIM)
    query = packed[:, :, 0]
    key = packed[:, :, 1]
    value = packed[:, :, 2]
    scale = HEAD_DIM ** (-0.5)
    scores = (
        jnp.einsum("sqhd,skhd->shqk", query, key, preferred_element_type=jnp.float32) * scale
        + bias[None]
    )
    if allow is not None:
        scores = jnp.where(allow[None, None], scores, NEG)
    top = jnp.max(scores, axis=-1, keepdims=True)
    expo = jnp.exp(scores - top)
    probs = expo / jnp.sum(expo, axis=-1, keepdims=True)
    weights = probs.astype(jnp.bfloat16)
    mixed = jnp.einsum(
        "shqk,skhd->sqhd", weights, value, preferred_element_type=jnp.float32
    ).astype(jnp.bfloat16)
    mixed = mixed.reshape(samples * spots, HEADS * HEAD_DIM)
    return (normed, rstd, query, key, value, probs, weights, mixed)


def attend_back(saved, grad_out, w_qkv, w_proj, grad_scale):
    normed, rstd, query, key, value, probs, weights, mixed = saved
    samples = query.shape[0]
    spots = query.shape[1]
    scale = HEAD_DIM ** (-0.5)
    local = (
        jnp.einsum("ti,td->id", mixed, grad_out, preferred_element_type=jnp.float32) * grad_scale
    )
    d_mixed = jnp.einsum("td,id->ti", grad_out, w_proj, preferred_element_type=jnp.float32).astype(
        jnp.bfloat16
    )
    d_mixed = d_mixed.reshape(samples, spots, HEADS, HEAD_DIM)
    d_probs = jnp.einsum("sqhd,skhd->shqk", d_mixed, value, preferred_element_type=jnp.float32)
    d_value = jnp.einsum(
        "shqk,sqhd->skhd", weights, d_mixed, preferred_element_type=jnp.float32
    ).astype(jnp.bfloat16)
    d_scores = (probs * (d_probs - jnp.sum(probs * d_probs, axis=-1, keepdims=True))).astype(
        jnp.bfloat16
    )
    d_query = (
        jnp.einsum("shqk,skhd->sqhd", d_scores, key, preferred_element_type=jnp.float32) * scale
    ).astype(jnp.bfloat16)
    d_key = (
        jnp.einsum("shqk,sqhd->skhd", d_scores, query, preferred_element_type=jnp.float32) * scale
    ).astype(jnp.bfloat16)
    d_packed = jnp.stack([d_query, d_key, d_value], axis=2).reshape(
        samples * spots, 3 * HEADS * HEAD_DIM
    )
    d_normed = jnp.einsum("tc,dc->td", d_packed, w_qkv, preferred_element_type=jnp.float32)
    d_input = rstd * (
        d_normed
        - jnp.mean(d_normed, axis=-1, keepdims=True)
        - normed * jnp.mean(d_normed * normed, axis=-1, keepdims=True)
    )
    return (grad_out.astype(jnp.float32) + d_input, local)


def to_shifted(tile_data):
    half = tile_data.shape[1] // 2
    below = from_behind(tile_data[:, :half], "freq", -1)
    rows_moved = jnp.concatenate([tile_data[:, half:], below], axis=1)
    right = from_behind(rows_moved[:, :, :half], "tm", -1)
    return jnp.concatenate([rows_moved[:, :, half:], right], axis=2)


def from_shifted(tile_data):
    half = tile_data.shape[1] // 2
    left = from_behind(tile_data[:, :, half:], "tm", 1)
    cols_moved = jnp.concatenate([left, tile_data[:, :, :half]], axis=2)
    above = from_behind(cols_moved[:, half:], "freq", 1)
    return jnp.concatenate([above, cols_moved[:, :half]], axis=1)


def reduce_grad(local):
    share = lax.psum_scatter(
        local.astype(jnp.bfloat16), "freq", scatter_dimension=0, tiled=True
    ).astype(jnp.float32)
    return lax.psum(share, "tm")


def shards(
    tokens, cotangent, qkv_plain, qkv_shift, proj_plain, proj_shift, table_plain, table_shift
):
    gathered = (
        lax.all_gather(qkv_plain, "freq", axis=1, tiled=True),
        lax.all_gather(qkv_shift, "freq", axis=1, tiled=True),
        lax.all_gather(proj_plain, "freq", axis=0, tiled=True),
        lax.all_gather(proj_shift, "freq", axis=0, tiled=True),
    )
    w_qkv_plain, w_qkv_shift, w_proj_plain, w_proj_shift = gathered
    samples = tokens.shape[0]
    tile = tokens.shape[1]
    spots = tile * tile
    grad_scale = 1.0 / math.sqrt(samples * spots * lax.axis_size("tm") * lax.axis_size("freq"))
    saved_plain = attend(
        tokens.reshape(samples, spots, D), w_qkv_plain, offset_bias(table_plain), None
    )
    block_out = tokens.reshape(-1, D).astype(jnp.float32) + jnp.dot(
        saved_plain[-1], w_proj_plain, preferred_element_type=jnp.float32
    )
    block_out = block_out.astype(jnp.bfloat16).reshape(tokens.shape)
    shifted_in = to_shifted(block_out)
    shifted_cot = to_shifted(cotangent)
    saved_shift = attend(
        shifted_in.reshape(samples, spots, D),
        w_qkv_shift,
        offset_bias(table_shift),
        shift_mask(tile),
    )
    back_shift, local_shift = attend_back(
        saved_shift, shifted_cot.reshape(-1, D), w_qkv_shift, w_proj_shift, grad_scale
    )
    d_block = from_shifted(back_shift.astype(jnp.bfloat16).reshape(tokens.shape))
    back_plain, local_plain = attend_back(
        saved_plain, d_block.reshape(-1, D), w_qkv_plain, w_proj_plain, grad_scale
    )
    grad_shift = reduce_grad(local_shift)
    grad_plain = reduce_grad(local_plain)
    return (back_plain.astype(jnp.bfloat16).reshape(tokens.shape), grad_plain, grad_shift)


def solution(mesh):
    placed = (
        P(None, "freq", "tm", None),
        P(None, "freq", "tm", None),
        P(None, "freq"),
        P(None, "freq"),
        P("freq", None),
        P("freq", None),
        P(),
        P(),
    )
    return jax.shard_map(
        shards,
        mesh=mesh,
        in_specs=placed,
        out_specs=(P(None, "freq", "tm", None), P("freq", None), P("freq", None)),
        check_vma=False,
    )
```

profile of v0, /device:TPU:1, one launch (start us, length us, event | category | flops | bytes accessed | tf_op | source)
XLA Modules:
  0.0 537.7 jit_solution(4686875333041067942)
XLA Ops:
  8.9 6.2 %collective-permute-start = (bf16[2,4,8,768]{3,2,1,0:T(8,128)(2,1)S(1)}, bf16[2,4,8,768]{3,2,1,0:T(8,128)(2,1)S(1)}, u32[]{:S(2)}, u32[]{:S(2)}) collective-permute-start(bf16[2,4,8,768]{3,2,1,0:T(8,128)(2,1)S(1)} %get-tuple-element.24), channel_id=1, source_target_pairs={{0,7},{1,0},{2,1},{3,2},{4,3},{5,4},{6,5},{7,6},{8,15},{9,8},{10,9... | collective-permute-start | bytes 294920 | tf_op jit(solution)/shard_map/ppermute | solution.py:22
  15.3 1.0 convert_reduce_fusion
  16.4 1.1 multiply_reduce_fusion.5
  17.8 2.6 convolution_bitcast_fusion
  20.4 2.6 convolution_bitcast_fusion.1
  23.0 28.0 %all_gather.13 = bf16[384,768]{1,0:T(8,128)(2,1)S(1)} all-gather(bf16[48,768]{1,0:T(8,128)(2,1)S(1)} %copy-done.19), channel_id=1, replica_groups=mesh['tm'=64,'freq'=8] {'freq'}, dimensions={0}, use_global_device_ids=true | all-gather | bytes 663552 | tf_op jit(solution)/shard_map/all_gather | solution.py:154
  50.9 29.6 %all_gather.15 = bf16[384,768]{1,0:T(8,128)(2,1)S(1)} all-gather(bf16[48,768]{1,0:T(8,128)(2,1)S(1)} %copy-done.20), channel_id=1, replica_groups=mesh['tm'=64,'freq'=8] {'freq'}, dimensions={0}, use_global_device_ids=true | all-gather | bytes 663552 | tf_op jit(solution)/shard_map/all_gather | solution.py:155
  82.9 12.9 %collective-permute-start.1 = (bf16[2,8,4,768]{3,2,1,0:T(4,128)(2,1)S(1)}, bf16[2,8,4,768]{3,2,1,0:T(4,128)(2,1)S(1)}, u32[]{:S(2)}, u32[]{:S(2)}) collective-permute-start(bf16[2,8,4,768]{3,2,1,0:T(4,128)(2,1)S(1)} %get-tuple-element.22), channel_id=1, source_target_pairs={{0,504},{8,0},{16,8},{24,16},{32,24},{40,32},{48,40},{56,48},{64,5... | collective-permute-start | bytes 294920 | tf_op jit(solution)/shard_map/ppermute | solution.py:22
  95.8 2.2 convolution_convert_fusion.1
  99.1 2.5 fusion.57
  101.6 1.4 fusion.22
  103.7 4.3 collective-permute-start.2
  108.2 3.9 collective-permute-done.2
  112.2 4.3 collective-permute-start.3
  117.7 1.5 collective-permute-done.3
  120.3 22.1 %all-gather.5.cloned.1.call-done = bf16[768,1152]{0,1:T(8,128)(2,1)} async-done(((bf16[768,144]{0,1:T(8,128)(2,1)}), bf16[768,1152]{0,1:T(8,128)(2,1)}) %all-gather.5.cloned.1.call-update) | async-done | bytes 1769488 | tf_op jit(solution)/shard_map/all_gather | solution.py:153
  142.4 2.2 convolution_convert_fusion
  146.0 1.3 fusion.58
  147.2 2.0 fusion.23
  150.7 1.4 copy.49
  152.1 2.1 reshape.279
  154.2 1.6 fusion.51
  156.2 4.9 collective-permute-start.4
  161.1 1.2 fusion.25
  163.8 2.1 collective-permute-start.5
  165.8 1.1 fusion.7
  167.2 4.2 collective-permute-done.5
  174.2 1.1 fusion.6
  177.5 1.5 fusion.50
  179.9 28.0 %reduce-scatter.5.cloned.1.call-done = bf16[48,768]{1,0:T(8,128)(2,1)} async-done(((bf16[384,768]{1,0:T(8,128)(2,1)}), bf16[48,768]{1,0:T(8,128)(2,1)}) %reduce-scatter.5.cloned.1.call-update) | async-done | bytes 73744 | tf_op jit(solution)/shard_map/reduce_scatter | solution.py:142
  207.9 44.7 %reduce-scatter.3.cloned.1.call-done = bf16[48,768]{1,0:T(8,128)(2,1)} async-done(((bf16[384,768]{1,0:T(8,128)(2,1)}), bf16[48,768]{1,0:T(8,128)(2,1)}) %reduce-scatter.3.cloned.1.call-update) | async-done | bytes 73744 | tf_op jit(solution)/shard_map/reduce_scatter | solution.py:142
  252.6 278.6 %all-reduce.2 = (f32[48,768]{1,0:T(8,128)}, f32[48,768]{1,0:T(8,128)}) all-reduce(bf16[48,768]{1,0:T(8,128)(2,1)} %reduce-scatter.3.cloned.1.call-done, bf16[48,768]{1,0:T(8,128)(2,1)} %reduce-scatter.5.cloned.1.call-done), channel_id=1, replica_groups=mesh['tm'=64,'freq'=8] {'tm'}, use_global_device_ids=true, to_apply=%region_15.16 | all-reduce | flops 73728 | bytes 442368 | tf_op jit(solution)/shard_map/psum | solution.py:145
  (146 shorter events, 19.0 us)
Async XLA Ops:
  7.2 10.7 %copy-start = (f32[12,225]{1,0:T(8,128)S(1)}, f32[12,225]{1,0:T(8,128)}, u32[]{:S(2)}) copy-start(f32[12,225]{1,0:T(8,128)} %param.15) | copy-start | bytes 32404
  7.2 13.2 %copy-start.33 = (f32[12,225]{1,0:T(8,128)S(1)}, f32[12,225]{1,0:T(8,128)}, u32[]{:S(2)}) copy-start(f32[12,225]{1,0:T(8,128)} %param.14) | copy-start | bytes 32404
  7.2 15.8 %copy-start.19 = (bf16[48,768]{1,0:T(8,128)(2,1)S(1)}, bf16[48,768]{1,0:T(8,128)(2,1)}, u32[]{:S(2)}) copy-start(bf16[48,768]{1,0:T(8,128)(2,1)} %param.12) | copy-start | bytes 221188
  7.2 88.6 %all-gather.3.cloned.1.call-start = ((), (), s32[]{:S(2)}) async-start(), calls=%async_computation.2 | async-start | bytes 1990656 | tf_op jit(solution)/shard_map/all_gather | solution.py:152
  7.9 134.5 %all-gather.5.cloned.1.call-start = ((), (), s32[]{:S(2)}) async-start(), calls=%async_computation.3 | async-start | bytes 1990656 | tf_op jit(solution)/shard_map/all_gather | solution.py:153
  8.9 73.9 %collective-permute-start = (bf16[2,4,8,768]{3,2,1,0:T(8,128)(2,1)S(1)}, bf16[2,4,8,768]{3,2,1,0:T(8,128)(2,1)S(1)}, u32[]{:S(2)}, u32[]{:S(2)}) collective-permute-start(bf16[2,4,8,768]{3,2,1,0:T(8,128)(2,1)S(1)} %get-tuple-element.24), channel_id=1, source_target_pairs={{0,7},{1,0},{2,1},{3,2},{4,3},{5,4},{6,5},{7,6},{8,15},{9,8},{10,9... | collective-permute-start | bytes 294920 | tf_op jit(solution)/shard_map/ppermute | solution.py:22
  15.2 35.7 %copy-start.20 = (bf16[48,768]{1,0:T(8,128)(2,1)S(1)}, bf16[48,768]{1,0:T(8,128)(2,1)}, u32[]{:S(2)}) copy-start(bf16[48,768]{1,0:T(8,128)(2,1)} %param.13) | copy-start | bytes 221188
  15.2 192.7 %reduce-scatter.5.cloned.1.call-start = ((), (), s32[]{:S(2)}) async-start(), calls=%async_computation.5 | async-start | bytes 663552 | tf_op jit(solution)/shard_map/reduce_scatter | solution.py:142
  16.4 64.2 %copy-start.25 = (f32[128]{0:T(128)}, f32[128]{0:T(128)S(1)}, u32[]{:S(2)}) copy-start(f32[128]{0:T(128)S(1)} %div.61) | copy-start | bytes 1540
  17.7 62.9 %copy-start.27 = (f32[128]{0:T(128)}, f32[128]{0:T(128)S(1)}, u32[]{:S(2)}) copy-start(f32[128]{0:T(128)S(1)} %rsqrt.23) | copy-start | bytes 1540
  17.8 62.8 %copy-start.3 = (bf16[2,8,8,768]{3,2,1,0:T(8,128)(2,1)S(1)}, bf16[2,8,8,768]{3,2,1,0:T(8,128)(2,1)}, u32[]{:S(2)}) copy-start(bf16[2,8,8,768]{3,2,1,0:T(8,128)(2,1)} %param.8) | copy-start | bytes 589828
  82.9 25.1 %collective-permute-start.1 = (bf16[2,8,4,768]{3,2,1,0:T(4,128)(2,1)S(1)}, bf16[2,8,4,768]{3,2,1,0:T(4,128)(2,1)S(1)}, u32[]{:S(2)}, u32[]{:S(2)}) collective-permute-start(bf16[2,8,4,768]{3,2,1,0:T(4,128)(2,1)S(1)} %get-tuple-element.22), channel_id=1, source_target_pairs={{0,504},{8,0},{16,8},{24,16},{32,24},{40,32},{48,40},{56,48},{64,5... | collective-permute-start | bytes 294920 | tf_op jit(solution)/shard_map/ppermute | solution.py:22
  99.1 2.6 copy-start.14
  99.1 3.9 copy-start.9
  99.1 3.9 copy-start.11
  103.4 8.7 %copy-start.7 = (bf16[128,384]{0,1:T(8,128)(2,1)}, bf16[128,384]{0,1:T(8,128)(2,1)S(1)}, u32[]{:S(2)}) copy-start(bf16[128,384]{0,1:T(8,128)(2,1)S(1)} %reshape.275) | copy-start | bytes 294916
  103.7 8.4 %collective-permute-start.2 = (bf16[2,4,8,768]{3,2,1,0:T(8,128)(2,1)S(1)}, bf16[2,4,8,768]{3,2,1,0:T(8,128)(2,1)S(1)}, u32[]{:S(2)}, u32[]{:S(2)}) collective-permute-start(bf16[2,4,8,768]{3,2,1,0:T(8,128)(2,1)S(1)} %get-tuple-element.20), channel_id=1, source_target_pairs={{0,7},{1,0},{2,1},{3,2},{4,3},{5,4},{6,5},{7,6},{8,15},{9,8},{10,9... | collective-permute-start | bytes 294920 | tf_op jit(solution)/shard_map/ppermute | solution.py:22
  108.2 8.3 %copy-start.4 = (bf16[2,8,8,768]{3,2,1,0:T(8,128)(2,1)}, bf16[2,8,8,768]{3,2,1,0:T(8,128)(2,1)S(1)}, u32[]{:S(2)}) copy-start(bf16[2,8,8,768]{3,2,1,0:T(8,128)(2,1)S(1)} %pad_maximum_fusion.3) | copy-start | bytes 589828
  112.2 7.0 %collective-permute-start.3 = (bf16[2,8,4,768]{3,2,1,0:T(4,128)(2,1)S(1)}, bf16[2,8,4,768]{3,2,1,0:T(4,128)(2,1)S(1)}, u32[]{:S(2)}, u32[]{:S(2)}) collective-permute-start(bf16[2,8,4,768]{3,2,1,0:T(4,128)(2,1)S(1)} %get-tuple-element.18), channel_id=1, source_target_pairs={{0,504},{8,0},{16,8},{24,16},{32,24},{40,32},{48,40},{56,48},{64,5... | collective-permute-start | bytes 294920 | tf_op jit(solution)/shard_map/ppermute | solution.py:22
  145.6 3.6 copy-start.16
  147.2 2.4 copy-start.21
  147.2 2.0 copy-start.18
  150.5 3.7 copy-start.2
  156.1 9.7 %copy-start.6 = (bf16[2,8,8,768]{3,2,1,0:T(8,128)(2,1)S(1)}, bf16[2,8,8,768]{3,2,1,0:T(8,128)(2,1)}, u32[]{:S(2)}) copy-start(bf16[2,8,8,768]{3,2,1,0:T(8,128)(2,1)} %copy-done.4) | copy-start | bytes 589828
  156.2 7.5 %collective-permute-start.4 = (bf16[2,8,4,768]{3,2,1,0:T(4,128)(2,1)S(1)}, bf16[2,8,4,768]{3,2,1,0:T(4,128)(2,1)S(1)}, u32[]{:S(2)}, u32[]{:S(2)}) collective-permute-start(bf16[2,8,4,768]{3,2,1,0:T(4,128)(2,1)S(1)} %get-tuple-element.15), channel_id=1, source_target_pairs={{0,8},{8,16},{16,24},{24,32},{32,40},{40,48},{48,56},{56,64},{64,7... | collective-permute-start | bytes 294920 | tf_op jit(solution)/shard_map/ppermute | solution.py:22
  163.7 8.3 %copy-start.13 = (f32[2,12,64,64]{2,3,1,0:T(8,128)S(1)}, f32[2,12,64,64]{2,3,1,0:T(8,128)}, u32[]{:S(2)}) copy-start(f32[2,12,64,64]{2,3,1,0:T(8,128)} %get-tuple-element.26) | copy-start | bytes 1179652
  163.7 8.3 %copy-start.15 = (bf16[2,64,1,12,32]{1,0,4,3,2:T(2,128)(2,1)S(1)}, bf16[2,64,1,12,32]{1,0,4,3,2:T(2,128)(2,1)}, u32[]{:S(2)}) copy-start(bf16[2,64,1,12,32]{1,0,4,3,2:T(2,128)(2,1)} %copy-done.14) | copy-start | bytes 294916
  163.7 8.3 %copy-start.24 = (f32[2,12,64]{2,1,0:T(8,128)S(1)}, f32[2,12,64]{2,1,0:T(8,128)}, u32[]{:S(2)}) copy-start(f32[2,12,64]{2,1,0:T(8,128)} %copy-done.23) | copy-start | bytes 18436
  163.8 7.6 %collective-permute-start.5 = (bf16[2,4,8,768]{3,2,1,0:T(8,128)(2,1)S(1)}, bf16[2,4,8,768]{3,2,1,0:T(8,128)(2,1)S(1)}, u32[]{:S(2)}, u32[]{:S(2)}) collective-permute-start(bf16[2,4,8,768]{3,2,1,0:T(8,128)(2,1)S(1)} %fusion.41), channel_id=1, source_target_pairs={{0,1},{1,2},{2,3},{3,4},{4,5},{5,6},{6,7},{7,0},{8,9},{9,10},{10,1... | collective-permute-start | bytes 294920 | tf_op jit(solution)/shard_map/ppermute | solution.py:22
  167.0 85.6 %reduce-scatter.3.cloned.1.call-start = ((), (), s32[]{:S(2)}) async-start(), calls=%async_computation.4 | async-start | bytes 663552 | tf_op jit(solution)/shard_map/reduce_scatter | solution.py:142
  173.5 1.8 copy-start.10
  175.7 1.8 copy-start.1
  (12 other events, 15.0 us)
Sparse Core Ops, SparseCore 0:
  10.1 74.8 all-gather.2
  87.1 55.2 all-gather.4
  167.1 40.7 reduce-scatter.4
  210.5 42.0 reduce-scatter.2
where the time goes:
time: 542 us; the launch traced here: 538 us
  blocking collectives  336 us (62%)
  waiting for transfers between devices  106 us (20%)
  starting transfers between devices  35 us (6%)
  matrix products  25.3 us (5%)
  between operations  14.5 us (3%)
  local copies, waits for them, and re-layouts  13.6 us (3%)
  other arithmetic  6.97 us (1%)
    psum x1, blocking collectives, reduce_grad(): return lax.psum(share, 'tm')  279 us
    reduce_scatter x2, waiting for transfers between devices, reduce_grad(): lax.psum_scatter(local.astype(jnp.bfloat16), 'freq', scatter_dimension=0,...  72.7 us
    ppermute x6, starting transfers between devices, from_behind(): return lax.ppermute(value, axis, pairs)  34.7 us
    all_gather x1, blocking collectives, shards(): lax.all_gather(proj_shift, 'freq', axis=0, tiled=True)  29.6 us
    all_gather x1, blocking collectives, shards(): lax.all_gather(proj_plain, 'freq', axis=0, tiled=True)  28 us
    all_gather x1, waiting for transfers between devices, shards(): lax.all_gather(qkv_shift, 'freq', axis=1, tiled=True)  22.1 us
  transfers between devices with their start and end apart: 10, of which 7 were waited for; matrix products, arithmetic and copies ran while one was open for 6% of the time, Pallas kernels for 0%

commit v1 on v0

--- a/solution.py
+++ b/solution.py
@@ -138,23 +138,66 @@
     return jnp.concatenate([above, cols_moved[:, :half]], axis=1)
 
 
-def reduce_grad(local):
-    share = lax.psum_scatter(
-        local.astype(jnp.bfloat16), "freq", scatter_dimension=0, tiled=True
-    ).astype(jnp.float32)
-    return lax.psum(share, "tm")
+def tm_groups(bits):
+    size = lax.axis_size("tm")
+    step = {"core": 1, "y_hi": 2, "z": 8}[bits]
+    count = {"core": 2, "y_hi": 4, "z": 8}[bits]
+    groups = []
+    for first in range(size):
+        if (first // step) % count == 0:
+            groups.append([first + step * i for i in range(count)])
+    return groups
+
+
+def swap(value, axis, groups=None):
+    return lax.all_to_all(value, axis, 0, 0, axis_index_groups=groups)
+
+
+def total(blocks):
+    return jnp.sum(blocks.astype(jnp.float32), axis=0).astype(jnp.bfloat16)
+
+
+def copies(value, count):
+    return jnp.broadcast_to(value[None], (count,) + value.shape)
+
+
+def gather_weights(qkv_plain, qkv_shift, proj_plain, proj_shift):
+    core = lax.axis_index("tm") % 2
+    mine = jnp.concatenate([qkv_plain.T, proj_plain, qkv_shift.T, proj_shift], axis=0)
+    half = lax.dynamic_slice_in_dim(mine, core * (D // 2), D // 2, axis=1)
+    own = swap(copies(half, 8), "freq")
+    count = lax.axis_size("tm")
+    other = lax.ppermute(own, "tm", [(i, i ^ 1) for i in range(count)])
+    low = jnp.where(core == 0, own, other)
+    high = jnp.where(core == 0, other, own)
+    full = jnp.concatenate([low, high], axis=2)
+    return (
+        full[:, :144].reshape(1152, D).T,
+        full[:, 192:336].reshape(1152, D).T,
+        full[:, 144:192].reshape(384, D),
+        full[:, 336:].reshape(384, D),
+    )
+
+
+def reduce_grads(plain, shift):
+    both = jnp.stack([plain, shift]).astype(jnp.bfloat16)
+    rows = both.reshape(2, 8, 2, 24, D).transpose(2, 1, 0, 3, 4)
+    part = total(swap(rows, "tm", tm_groups("core")))
+    part = total(swap(part, "freq"))
+    part = total(swap(part.reshape(8, 6, D), "tm", tm_groups("z")))
+    part = total(swap(copies(part, 4), "tm", tm_groups("y_hi")))
+    part = swap(copies(part, 8), "tm", tm_groups("z")).reshape(2, 24, D)
+    part = lax.all_gather(part, "tm", axis_index_groups=tm_groups("core"))
+    part = part.transpose(1, 0, 2, 3).reshape(2, 48, D).astype(jnp.float32)
+    return (part[0], part[1])
 
 
 def shards(
     tokens, cotangent, qkv_plain, qkv_shift, proj_plain, proj_shift, table_plain, table_shift
 ):
-    gathered = (
-        lax.all_gather(qkv_plain, "freq", axis=1, tiled=True),
-        lax.all_gather(qkv_shift, "freq", axis=1, tiled=True),
-        lax.all_gather(proj_plain, "freq", axis=0, tiled=True),
-        lax.all_gather(proj_shift, "freq", axis=0, tiled=True),
-    )
-    w_qkv_plain, w_qkv_shift, w_proj_plain, w_proj_shift = gathered
+    w_qkv_plain, w_qkv_shift, w_proj_plain, w_proj_shift = gather_weights(
+        qkv_plain, qkv_shift, proj_plain, proj_shift
+    )
     samples = tokens.shape[0]
     tile = tokens.shape[1]
     spots = tile * tile
@@ -181,8 +224,7 @@
     back_plain, local_plain = attend_back(
         saved_plain, d_block.reshape(-1, D), w_qkv_plain, w_proj_plain, grad_scale
     )
-    grad_shift = reduce_grad(local_shift)
-    grad_plain = reduce_grad(local_plain)
+    grad_plain, grad_shift = reduce_grads(local_plain, local_shift)
     return (back_plain.astype(jnp.bfloat16).reshape(tokens.shape), grad_plain, grad_shift)
 
 

time: 542 us -> 216 us (0.40)
  blocking collectives: 336 us -> 50.6 us
  waiting for transfers between devices: 106 us -> 29.4 us
  local copies, waits for them, and re-layouts: 13.6 us -> 37.9 us
  starting transfers between devices: 35 us -> 48.1 us
  between operations: 14.5 us -> 1.41 us
  other arithmetic: 6.97 us -> 19 us
    psum x1 -> x0, blocking collectives: 279 us -> none  [reduce_grad(): return lax.psum(share, 'tm')]
    reduce_scatter x2 -> x0, waiting for transfers between devices: 72.7 us -> none  [reduce_grad(): lax.psum_scatter(local.astype(jnp.bfloat16), 'freq', scatter_dimension=0,...]
    all_gather x2 -> x1, blocking collectives: 57.6 us -> 6.65 us  [reduce_grads(): part = lax.all_gather(part, 'tm', axis_index_groups=tm_groups('core'))]
    all_to_all x0 -> x2, blocking collectives: none -> 44 us  [swap(): return lax.all_to_all(value, axis, 0, 0, axis_index_groups=groups)]
    all_to_all x0 -> x4, waiting for transfers between devices: none -> 23.8 us  [swap(): return lax.all_to_all(value, axis, 0, 0, axis_index_groups=groups)]
    all_gather x2 -> x0, waiting for transfers between devices: 22.2 us -> none  [the longest x1 22.1 us: shards(): lax.all_gather(qkv_shift, 'freq', axis=1, tiled=True)]
    all_to_all x0 -> x4, starting transfers between devices: none -> 13.5 us  [swap(): return lax.all_to_all(value, axis, 0, 0, axis_index_groups=groups)]
    ppermute x6, starting transfers between devices: 34.7 us -> 27.9 us  [from_behind(): return lax.ppermute(value, axis, pairs)]
  transfers between devices with their start and end apart: 10 -> 11, of which waited for: 7 -> 6; matrix products, arithmetic and copies ran while one was open for 6% -> 22% of each run, Pallas kernels for 0% -> 0%
where the time goes in v1:
time: 216 us; the launch traced here: 215 us
  blocking collectives  50.6 us (23%)
  starting transfers between devices  48.1 us (22%)
  local copies, waits for them, and re-layouts  37.9 us (18%)
  waiting for transfers between devices  29.4 us (14%)
  matrix products  28.3 us (13%)
  other arithmetic  19 us (9%)
    all_to_all x2, blocking collectives, swap(): return lax.all_to_all(value, axis, 0, 0, axis_index_groups=groups)  44 us
    ppermute x6, starting transfers between devices, from_behind(): return lax.ppermute(value, axis, pairs)  27.9 us
    all_to_all x4, waiting for transfers between devices, swap(): return lax.all_to_all(value, axis, 0, 0, axis_index_groups=groups)  23.8 us
    all_to_all x4, starting transfers between devices, swap(): return lax.all_to_all(value, axis, 0, 0, axis_index_groups=groups)  13.5 us
    ppermute x1, starting transfers between devices, gather_weights(): other = lax.ppermute(own, 'tm', [(i, i ^ 1) for i in range(count)])  6.65 us
    all_gather x1, blocking collectives, reduce_grads(): part = lax.all_gather(part, 'tm', axis_index_groups=tm_groups('core'))  6.65 us
    ppermute x6, waiting for transfers between devices, from_behind(): return lax.ppermute(value, axis, pairs)  5.58 us
    dot_general x2, matrix products, offset_bias(): lax.dot_general(table, onehot, (((1,), (1,)), ((), ())), precision=lax.Pr...  5.16 us
  transfers between devices with their start and end apart: 11, of which 6 were waited for; matrix products, arithmetic and copies ran while one was open for 22% of the time, Pallas kernels for 0%

profile of v1, /device:TPU:1, one launch (start us, length us, event | category | flops | bytes accessed | tf_op | source)
XLA Modules:
  0.0 214.8 jit_solution(1560053013419677995)
XLA Ops:
  1.9 32.1 %all_to_all.30 = bf16[8,384,384]{2,1,0:T(8,128)(2,1)S(1)} all-to-all(bf16[8,384,384]{2,1,0:T(8,128)(2,1)S(1)} %broadcast_in_dim.16), channel_id=1, replica_groups=mesh['tm'=64,'freq'=8] {'freq'}, dimensions={0} | all-to-all | bytes 4718592 | tf_op jit(solution)/shard_map/all_to_all | solution.py:153
  34.0 6.7 %collective-permute-start.2 = (bf16[8,384,384]{2,1,0:T(8,128)(2,1)S(1)}, bf16[8,384,384]{2,1,0:T(8,128)(2,1)}, u32[]{:S(2)}, u32[]{:S(2)}) collective-permute-start(bf16[8,384,384]{2,1,0:T(8,128)(2,1)S(1)} %all_to_all.30), channel_id=1, source_target_pairs={{0,8},{8,0},{16,24},{24,16},{32,40},{40,32},{48,56},{56,48},{64,72... | collective-permute-start | bytes 7077896 | tf_op jit(solution)/shard_map/ppermute | solution.py:170
  41.4 3.0 %collective-permute-start = (bf16[2,4,8,768]{3,2,1,0:T(8,128)(2,1)}, bf16[2,4,8,768]{3,2,1,0:T(8,128)(2,1)S(1)}, u32[]{:S(2)}, u32[]{:S(2)}) collective-permute-start(bf16[2,4,8,768]{3,2,1,0:T(8,128)(2,1)} %get-tuple-element.30), channel_id=1, source_target_pairs={{0,7},{1,0},{2,1},{3,2},{4,3},{5,4},{6,5},{7,6},{8,15},{9,8},{10,9... | collective-permute-start | bytes 294920 | tf_op jit(solution)/shard_map/ppermute | solution.py:22
  44.9 2.6 %convolution_bitcast_fusion.1 = f32[12,4096]{1,0:T(8,128)S(1)} fusion(f32[12,225]{1,0:T(8,128)S(1)} %copy-done, s32[4096]{0:T(1024)S(1)} %reshape.390), kind=kOutput, calls=%fused_computation.9 | convolution fusion | flops 133632000 | bytes 223792 | tf_op jit(solution)/shard_map/dot_general | solution.py:43
  47.4 2.6 %convolution_bitcast_fusion = f32[12,4096]{1,0:T(8,128)S(1)} fusion(f32[12,225]{1,0:T(8,128)S(1)} %copy-done.27, s32[4096]{0:T(1024)S(1)} %reshape.390), kind=kOutput, calls=%fused_computation.8 | convolution fusion | flops 133632000 | bytes 223792 | tf_op jit(solution)/shard_map/dot_general | solution.py:43
  55.8 2.2 %collective-permute-start.1 = (bf16[2,8,4,768]{3,2,1,0:T(4,128)(2,1)}, bf16[2,8,4,768]{3,2,1,0:T(4,128)(2,1)}, u32[]{:S(2)}, u32[]{:S(2)}) collective-permute-start(bf16[2,8,4,768]{3,2,1,0:T(4,128)(2,1)} %get-tuple-element.28), channel_id=1, source_target_pairs={{0,504},{8,0},{16,8},{24,16},{32,24},{40,32},{48,40},{56,48},{64,5... | collective-permute-start | bytes 294920 | tf_op jit(solution)/shard_map/ppermute | solution.py:22
  58.0 2.1 broadcast_select_fusion.1
  63.5 1.8 copy.154
  65.4 2.1 reshape.370
  67.4 2.4 %fusion.57 = (bf16[2,64,1,12,32]{1,0,4,3,2:T(2,128)(2,1)}, bf16[2,64,1,12,32]{1,0,4,3,2:T(2,128)(2,1)}, bf16[2,64,1,12,32]{1,0,4,3,2:T(2,128)(2,1)}) fusion(bf16[2,64,3,12,32]{1,0,4,3,2:T(2,128)(2,1)} %reshape.370), kind=kLoop, calls=%fused_computation.149 | loop fusion | bytes 589824 | tf_op jit(solution)/shard_map/slice | solution.py:68
  69.8 3.1 %fusion.62 = (f32[2,12,64]{2,1,0:T(8,128)}, f32[2,12,64,64]{2,3,1,0:T(8,128)}) fusion(f32[12,64,64]{1,2,0:T(8,128)} %copy.158, bf16[2,64,1,12,32]{1,0,4,3,2:T(2,128)(2,1)} %get-tuple-element.17, bf16[2,64,1,12,32]{1,0,4,3,2:T(2,128)(2,1)} %get-tuple-element.16), kind=kOutput, calls=%fused_computation.154 | convolution fusion | flops 6684735 | bytes 792576 | tf_op jit(solution)/shard_map/sub | solution.py:78
  78.4 2.5 %collective-permute-start.3 = (bf16[2,4,8,768]{3,2,1,0:T(8,128)(2,1)S(1)}, bf16[2,4,8,768]{3,2,1,0:T(8,128)(2,1)S(1)}, u32[]{:S(2)}, u32[]{:S(2)}) collective-permute-start(bf16[2,4,8,768]{3,2,1,0:T(8,128)(2,1)S(1)} %get-tuple-element.26), channel_id=1, source_target_pairs={{0,7},{1,0},{2,1},{3,2},{4,3},{5,4},{6,5},{7,6},{8,15},{9,8},{10,9... | collective-permute-start | bytes 294920 | tf_op jit(solution)/shard_map/ppermute | solution.py:22
  82.0 1.8 collective-permute-done.3
  84.5 14.7 %collective-permute-start.4 = (bf16[2,8,4,768]{3,2,1,0:T(4,128)(2,1)}, bf16[2,8,4,768]{3,2,1,0:T(4,128)(2,1)}, u32[]{:S(2)}, u32[]{:S(2)}) collective-permute-start(bf16[2,8,4,768]{3,2,1,0:T(4,128)(2,1)} %get-tuple-element.24), channel_id=1, source_target_pairs={{0,504},{8,0},{16,8},{24,16},{32,24},{40,32},{48,40},{56,48},{64,5... | collective-permute-start | bytes 294920 | tf_op jit(solution)/shard_map/ppermute | solution.py:22
  108.3 1.9 copy.161
  110.2 2.1 reshape.375
  119.1 2.5 %fusion.25 = bf16[2,64,1,12,32]{1,4,3,0,2:T(8,128)(2,1)} fusion(bf16[2,64,12,32]{1,0,3,2:T(2,128)(2,1)} %reshape.377, f32[2,12,64]{2,1,0:T(8,128)} %copy-done.21, f32[2,12,64,64]{2,3,1,0:T(8,128)} %copy-done.5), kind=kOutput, calls=%fused_computation.53 | convolution fusion | flops 6637119 | bytes 595968 | tf_op jit(solution)/shard_map/shqk,sqhd->skhd/dot_general | solution.py:101
  127.0 2.1 reshape.378
  132.1 2.2 %collective-permute-start.5 = (bf16[2,8,4,768]{3,2,1,0:T(4,128)(2,1)S(1)}, bf16[2,8,4,768]{3,2,1,0:T(4,128)(2,1)S(1)}, u32[]{:S(2)}, u32[]{:S(2)}) collective-permute-start(bf16[2,8,4,768]{3,2,1,0:T(4,128)(2,1)S(1)} %get-tuple-element.21), channel_id=1, source_target_pairs={{0,8},{8,16},{16,24},{24,32},{32,40},{40,48},{48,56},{56,64},{64,7... | collective-permute-start | bytes 294920 | tf_op jit(solution)/shard_map/ppermute | solution.py:22
  136.5 3.4 %collective-permute-start.6 = (bf16[2,4,8,768]{3,2,1,0:T(8,128)(2,1)S(1)}, bf16[2,4,8,768]{3,2,1,0:T(8,128)(2,1)S(1)}, u32[]{:S(2)}, u32[]{:S(2)}) collective-permute-start(bf16[2,4,8,768]{3,2,1,0:T(8,128)(2,1)S(1)} %fusion.45), channel_id=1, source_target_pairs={{0,1},{1,2},{2,3},{3,4},{4,5},{5,6},{6,7},{7,0},{8,9},{9,10},{10,1... | collective-permute-start | bytes 294920 | tf_op jit(solution)/shard_map/ppermute | solution.py:22
  140.2 3.8 %collective-permute-done.6 = bf16[2,4,8,768]{3,2,1,0:T(8,128)(2,1)S(1)} collective-permute-done((bf16[2,4,8,768]{3,2,1,0:T(8,128)(2,1)S(1)}, bf16[2,4,8,768]{3,2,1,0:T(8,128)(2,1)S(1)}, u32[]{:S(2)}, u32[]{:S(2)}) %collective-permute-start.6) | collective-permute-done | bytes 98336 | tf_op jit(solution)/shard_map/ppermute | solution.py:22
  144.8 11.8 %all_to_all.31 = bf16[2,8,2,24,768]{4,3,1,2,0:T(8,128)(2,1)S(1)} all-to-all(bf16[2,8,2,24,768]{4,3,1,2,0:T(8,128)(2,1)S(1)} %copy_bitcast_fusion), channel_id=1, replica_groups={{0,8},{16,24},{32,40},{48,56},{64,72},{80,88},{96,104},{112,120},{128,1..., dimensions={0} | all-to-all | bytes 2359296 | tf_op jit(solution)/shard_map/all_to_all | solution.py:153
  157.8 2.0 copy.185
  159.8 3.5 %all-to-all-start.2 = ((bf16[8,2,24,768]{3,2,1,0:T(8,128)(2,1)}), bf16[8,2,24,768]{3,2,1,0:T(8,128)(2,1)S(1)}, u32[]{:S(2)}, u32[]{:S(2)}) async-start(bf16[8,2,24,768]{3,2,1,0:T(8,128)(2,1)} %copy.185), calls=%async_computation.2 | async-start | bytes 1179648 | tf_op jit(solution)/shard_map/all_to_all | solution.py:153
  170.5 3.0 %all-to-all-done.2 = bf16[8,2,24,768]{3,2,1,0:T(8,128)(2,1)S(1)} async-done(((bf16[8,2,24,768]{3,2,1,0:T(8,128)(2,1)}), bf16[8,2,24,768]{3,2,1,0:T(8,128)(2,1)S(1)}, u32[]{:S(2)}, u32[]{:S(2)}) %all-to-all-start.2) | async-done | bytes 589856 | tf_op jit(solution)/shard_map/all_to_all | solution.py:153
  174.2 3.4 %all-to-all-start.3 = ((bf16[8,6,768]{2,1,0:T(8,128)(2,1)}), bf16[8,6,768]{2,1,0:T(8,128)(2,1)S(1)}, u32[]{:S(2)}, u32[]{:S(2)}) async-start(bf16[8,6,768]{2,1,0:T(8,128)(2,1)} %reshape.385), calls=%async_computation.3 | async-start | bytes 196608 | tf_op jit(solution)/shard_map/all_to_all | solution.py:153
  177.6 7.5 %all-to-all-done.3 = bf16[8,6,768]{2,1,0:T(8,128)(2,1)S(1)} async-done(((bf16[8,6,768]{2,1,0:T(8,128)(2,1)}), bf16[8,6,768]{2,1,0:T(8,128)(2,1)S(1)}, u32[]{:S(2)}, u32[]{:S(2)}) %all-to-all-start.3) | async-done | bytes 73760 | tf_op jit(solution)/shard_map/all_to_all | solution.py:153
  185.7 3.3 %all-to-all-start.4 = ((bf16[4,6,768]{2,1,0:T(8,128)(2,1)}), bf16[4,6,768]{2,1,0:T(8,128)(2,1)S(1)}, u32[]{:S(2)}, u32[]{:S(2)}) async-start(bf16[4,6,768]{2,1,0:T(8,128)(2,1)} %broadcast_in_dim.20), calls=%async_computation.4 | async-start | bytes 98304 | tf_op jit(solution)/shard_map/all_to_all | solution.py:153
  189.0 6.8 %all-to-all-done.4 = bf16[4,6,768]{2,1,0:T(8,128)(2,1)S(1)} async-done(((bf16[4,6,768]{2,1,0:T(8,128)(2,1)}), bf16[4,6,768]{2,1,0:T(8,128)(2,1)S(1)}, u32[]{:S(2)}, u32[]{:S(2)}) %all-to-all-start.4) | async-done | bytes 36896 | tf_op jit(solution)/shard_map/all_to_all | solution.py:153
  196.5 3.4 %all-to-all-start.5 = ((bf16[8,6,768]{2,1,0:T(8,128)(2,1)}), bf16[8,6,768]{2,1,0:T(8,128)(2,1)S(1)}, u32[]{:S(2)}, u32[]{:S(2)}) async-start(bf16[8,6,768]{2,1,0:T(8,128)(2,1)} %broadcast_in_dim.21), calls=%async_computation.5 | async-start | bytes 196608 | tf_op jit(solution)/shard_map/all_to_all | solution.py:153
  200.7 6.6 %all-to-all-done.5 = bf16[8,6,768]{2,1,0:T(8,128)(2,1)S(1)} async-done(((bf16[8,6,768]{2,1,0:T(8,128)(2,1)}), bf16[8,6,768]{2,1,0:T(8,128)(2,1)S(1)}, u32[]{:S(2)}, u32[]{:S(2)}) %all-to-all-start.5) | async-done | bytes 73760 | tf_op jit(solution)/shard_map/all_to_all | solution.py:153
  207.3 6.7 %all_gather.3 = bf16[2,2,24,768]{3,2,1,0:T(8,128)(2,1)S(1)} all-gather(bf16[1,2,24,768]{3,2,1,0:T(8,128)(2,1)S(1)} %all_gather_reshape.3), channel_id=1, replica_groups={{0,8},{16,24},{32,40},{48,56},{64,72},{80,88},{96,104},{112,120},{128,1..., dimensions={0}, use_global_device_ids=true | all-gather | bytes 221184 | tf_op jit(solution)/shard_map/all_gather | solution.py:190
  (149 shorter events, 58.1 us)
Async XLA Ops:
  0.6 44.2 %copy-start = (f32[12,225]{1,0:T(8,128)S(1)}, f32[12,225]{1,0:T(8,128)}, u32[]{:S(2)}) copy-start(f32[12,225]{1,0:T(8,128)} %param.14) | copy-start | bytes 32404
  1.9 38.8 %copy-start.17 = (bf16[2,8,8,768]{3,2,1,0:T(8,128)(2,1)S(1)}, bf16[2,8,8,768]{3,2,1,0:T(8,128)(2,1)}, u32[]{:S(2)}) copy-start(bf16[2,8,8,768]{3,2,1,0:T(8,128)(2,1)} %param.9) | copy-start | bytes 589828
  1.9 42.6 %copy-start.1 = (bf16[2,8,8,768]{3,2,1,0:T(8,128)(2,1)S(1)}, bf16[2,8,8,768]{3,2,1,0:T(8,128)(2,1)}, u32[]{:S(2)}) copy-start(bf16[2,8,8,768]{3,2,1,0:T(8,128)(2,1)} %param.8) | copy-start | bytes 589828
  34.0 13.4 %copy-start.27 = (f32[12,225]{1,0:T(8,128)S(1)}, f32[12,225]{1,0:T(8,128)}, u32[]{:S(2)}) copy-start(f32[12,225]{1,0:T(8,128)} %param.15) | copy-start | bytes 32404
  34.0 23.9 %collective-permute-start.2 = (bf16[8,384,384]{2,1,0:T(8,128)(2,1)S(1)}, bf16[8,384,384]{2,1,0:T(8,128)(2,1)}, u32[]{:S(2)}, u32[]{:S(2)}) collective-permute-start(bf16[8,384,384]{2,1,0:T(8,128)(2,1)S(1)} %all_to_all.30), channel_id=1, source_target_pairs={{0,8},{8,0},{16,24},{24,16},{32,40},{40,32},{48,56},{56,48},{64,72... | collective-permute-start | bytes 7077896 | tf_op jit(solution)/shard_map/ppermute | solution.py:170
  41.4 13.7 %collective-permute-start = (bf16[2,4,8,768]{3,2,1,0:T(8,128)(2,1)}, bf16[2,4,8,768]{3,2,1,0:T(8,128)(2,1)S(1)}, u32[]{:S(2)}, u32[]{:S(2)}) collective-permute-start(bf16[2,4,8,768]{3,2,1,0:T(8,128)(2,1)} %get-tuple-element.30), channel_id=1, source_target_pairs={{0,7},{1,0},{2,1},{3,2},{4,3},{5,4},{6,5},{7,6},{8,15},{9,8},{10,9... | collective-permute-start | bytes 294920 | tf_op jit(solution)/shard_map/ppermute | solution.py:22
  55.8 25.2 %collective-permute-start.1 = (bf16[2,8,4,768]{3,2,1,0:T(4,128)(2,1)}, bf16[2,8,4,768]{3,2,1,0:T(4,128)(2,1)}, u32[]{:S(2)}, u32[]{:S(2)}) collective-permute-start(bf16[2,8,4,768]{3,2,1,0:T(4,128)(2,1)} %get-tuple-element.28), channel_id=1, source_target_pairs={{0,504},{8,0},{16,8},{24,16},{32,24},{40,32},{48,40},{56,48},{64,5... | collective-permute-start | bytes 294920 | tf_op jit(solution)/shard_map/ppermute | solution.py:22
  76.9 22.3 %copy-start.9 = (bf16[8,48,768]{2,1,0:T(8,128)(2,1)S(1)}, bf16[8,48,768]{2,1,0:T(8,128)(2,1)}, u32[]{:S(2)}) copy-start(bf16[8,48,768]{2,1,0:T(8,128)(2,1)} %get-tuple-element.10) | copy-start | bytes 1769476
  78.4 5.4 %collective-permute-start.3 = (bf16[2,4,8,768]{3,2,1,0:T(8,128)(2,1)S(1)}, bf16[2,4,8,768]{3,2,1,0:T(8,128)(2,1)S(1)}, u32[]{:S(2)}, u32[]{:S(2)}) collective-permute-start(bf16[2,4,8,768]{3,2,1,0:T(8,128)(2,1)S(1)} %get-tuple-element.26), channel_id=1, source_target_pairs={{0,7},{1,0},{2,1},{3,2},{4,3},{5,4},{6,5},{7,6},{8,15},{9,8},{10,9... | collective-permute-start | bytes 294920 | tf_op jit(solution)/shard_map/ppermute | solution.py:22
  82.0 17.2 %copy-start.6 = (bf16[2,8,8,768]{3,2,1,0:T(8,128)(2,1)}, bf16[2,8,8,768]{3,2,1,0:T(8,128)(2,1)S(1)}, u32[]{:S(2)}) copy-start(bf16[2,8,8,768]{3,2,1,0:T(8,128)(2,1)S(1)} %pad_maximum_fusion.5) | copy-start | bytes 589828
  84.5 19.0 %collective-permute-start.4 = (bf16[2,8,4,768]{3,2,1,0:T(4,128)(2,1)}, bf16[2,8,4,768]{3,2,1,0:T(4,128)(2,1)}, u32[]{:S(2)}, u32[]{:S(2)}) collective-permute-start(bf16[2,8,4,768]{3,2,1,0:T(4,128)(2,1)} %get-tuple-element.24), channel_id=1, source_target_pairs={{0,504},{8,0},{16,8},{24,16},{32,24},{40,32},{48,40},{56,48},{64,5... | collective-permute-start | bytes 294920 | tf_op jit(solution)/shard_map/ppermute | solution.py:22
  113.9 3.1 %copy-start.16 = (bf16[2,64,1,12,32]{1,0,4,3,2:T(2,128)(2,1)}, bf16[2,64,1,12,32]{1,0,4,3,2:T(2,128)(2,1)S(1)}, u32[]{:S(2)}) copy-start(bf16[2,64,1,12,32]{1,0,4,3,2:T(2,128)(2,1)S(1)} %get-tuple-element.13) | copy-start | bytes 294916
  113.9 2.7 %copy-start.18 = (bf16[2,64,12,32]{1,0,3,2:T(2,128)(2,1)S(1)}, bf16[2,64,12,32]{1,0,3,2:T(2,128)(2,1)}, u32[]{:S(2)}) copy-start(bf16[2,64,12,32]{1,0,3,2:T(2,128)(2,1)} %reshape.377) | copy-start | bytes 294916
  115.4 1.6 copy-start.5
  129.1 1.7 copy-start.4
  129.1 1.7 copy-start.7
  129.1 1.7 copy-start.25
  129.1 1.7 copy-start.26
  132.1 7.8 %copy-start.8 = (bf16[2,8,8,768]{3,2,1,0:T(8,128)(2,1)S(1)}, bf16[2,8,8,768]{3,2,1,0:T(8,128)(2,1)}, u32[]{:S(2)}) copy-start(bf16[2,8,8,768]{3,2,1,0:T(8,128)(2,1)} %copy-done.6) | copy-start | bytes 589828
  132.1 4.4 %collective-permute-start.5 = (bf16[2,8,4,768]{3,2,1,0:T(4,128)(2,1)S(1)}, bf16[2,8,4,768]{3,2,1,0:T(4,128)(2,1)S(1)}, u32[]{:S(2)}, u32[]{:S(2)}) collective-permute-start(bf16[2,8,4,768]{3,2,1,0:T(4,128)(2,1)S(1)} %get-tuple-element.21), channel_id=1, source_target_pairs={{0,8},{8,16},{16,24},{24,32},{32,40},{40,48},{48,56},{56,64},{64,7... | collective-permute-start | bytes 294920 | tf_op jit(solution)/shard_map/ppermute | solution.py:22
  136.1 8.0 %copy-start.10 = (bf16[128,384]{0,1:T(8,128)(2,1)S(1)}, bf16[128,384]{0,1:T(8,128)(2,1)}, u32[]{:S(2)}) copy-start(bf16[128,384]{0,1:T(8,128)(2,1)} %reshape.371) | copy-start | bytes 294916
  136.1 8.3 %copy-start.3 = (bf16[8,48,768]{2,1,0:T(8,128)(2,1)S(1)}, bf16[8,48,768]{2,1,0:T(8,128)(2,1)}, u32[]{:S(2)}) copy-start(bf16[8,48,768]{2,1,0:T(8,128)(2,1)} %get-tuple-element.9) | copy-start | bytes 1769476
  136.5 7.5 %collective-permute-start.6 = (bf16[2,4,8,768]{3,2,1,0:T(8,128)(2,1)S(1)}, bf16[2,4,8,768]{3,2,1,0:T(8,128)(2,1)S(1)}, u32[]{:S(2)}, u32[]{:S(2)}) collective-permute-start(bf16[2,4,8,768]{3,2,1,0:T(8,128)(2,1)S(1)} %fusion.45), channel_id=1, source_target_pairs={{0,1},{1,2},{2,3},{3,4},{4,5},{5,6},{6,7},{7,0},{8,9},{9,10},{10,1... | collective-permute-start | bytes 294920 | tf_op jit(solution)/shard_map/ppermute | solution.py:22
  157.8 5.8 %copy-start.15 = (bf16[2,64,1,12,32]{1,0,4,3,2:T(2,128)(2,1)S(1)}, bf16[2,64,1,12,32]{1,0,4,3,2:T(2,128)(2,1)}, u32[]{:S(2)}) copy-start(bf16[2,64,1,12,32]{1,0,4,3,2:T(2,128)(2,1)} %get-tuple-element.18) | copy-start | bytes 294916
  157.8 5.8 %copy-start.22 = (f32[2,12,64]{2,1,0:T(8,128)S(1)}, f32[2,12,64]{2,1,0:T(8,128)}, u32[]{:S(2)}) copy-start(f32[2,12,64]{2,1,0:T(8,128)} %get-tuple-element.31) | copy-start | bytes 18436
  159.8 13.7 %all-to-all-start.2 = ((bf16[8,2,24,768]{3,2,1,0:T(8,128)(2,1)}), bf16[8,2,24,768]{3,2,1,0:T(8,128)(2,1)S(1)}, u32[]{:S(2)}, u32[]{:S(2)}) async-start(bf16[8,2,24,768]{3,2,1,0:T(8,128)(2,1)} %copy.185), calls=%async_computation.2 | async-start | bytes 1179648 | tf_op jit(solution)/shard_map/all_to_all | solution.py:153
  166.9 3.0 %copy-start.2 = (bf16[2,8,8,768]{3,2,1,0:T(8,128)(2,1)S(1)}, bf16[2,8,8,768]{3,2,1,0:T(8,128)(2,1)}, u32[]{:S(2)}) copy-start(bf16[2,8,8,768]{3,2,1,0:T(8,128)(2,1)} %param.8) | copy-start | bytes 589828
  166.9 3.0 %copy-start.23 = (f32[128]{0:T(128)S(1)}, f32[128]{0:T(128)}, u32[]{:S(2)}) copy-start(f32[128]{0:T(128)} %rsqrt.27) | copy-start | bytes 1540
  167.0 3.0 %copy-start.24 = (f32[128]{0:T(128)S(1)}, f32[128]{0:T(128)}, u32[]{:S(2)}) copy-start(f32[128]{0:T(128)} %div.74) | copy-start | bytes 1540
  174.2 10.9 %all-to-all-start.3 = ((bf16[8,6,768]{2,1,0:T(8,128)(2,1)}), bf16[8,6,768]{2,1,0:T(8,128)(2,1)S(1)}, u32[]{:S(2)}, u32[]{:S(2)}) async-start(bf16[8,6,768]{2,1,0:T(8,128)(2,1)} %reshape.385), calls=%async_computation.3 | async-start | bytes 196608 | tf_op jit(solution)/shard_map/all_to_all | solution.py:153
  185.7 10.0 %all-to-all-start.4 = ((bf16[4,6,768]{2,1,0:T(8,128)(2,1)}), bf16[4,6,768]{2,1,0:T(8,128)(2,1)S(1)}, u32[]{:S(2)}, u32[]{:S(2)}) async-start(bf16[4,6,768]{2,1,0:T(8,128)(2,1)} %broadcast_in_dim.20), calls=%async_computation.4 | async-start | bytes 98304 | tf_op jit(solution)/shard_map/all_to_all | solution.py:153
  196.5 10.9 %all-to-all-start.5 = ((bf16[8,6,768]{2,1,0:T(8,128)(2,1)}), bf16[8,6,768]{2,1,0:T(8,128)(2,1)S(1)}, u32[]{:S(2)}, u32[]{:S(2)}) async-start(bf16[8,6,768]{2,1,0:T(8,128)(2,1)} %broadcast_in_dim.21), calls=%async_computation.5 | async-start | bytes 196608 | tf_op jit(solution)/shard_map/all_to_all | solution.py:153
  (7 other events, 7.5 us)

commit v2 on v1

v2 whole, which is shorter than its diff:
```python
import math

import jax
import jax.numpy as jnp
import numpy as np
from jax import lax
from jax.experimental import pallas as pl
from jax.experimental.pallas import tpu as pltpu
from jax.sharding import PartitionSpec as P

D = 768
HEADS = 12
HEAD_DIM = 32
WIN = 8
SPOTS = 64
REL = 225
WIDE = HEADS * HEAD_DIM
LANES = HEADS * SPOTS
HALF = D // 2
SHARE = 144
ROWS = 48

NEG = -1e30
EPS = 1e-05
SCALE = HEAD_DIM ** (-0.5)

NN = (((1,), (0,)), ((), ()))
NT = (((1,), (1,)), ((), ()))
TN = (((0,), (0,)), ((), ()))

F32 = jnp.float32
BF16 = jnp.bfloat16


def shifted_pick():
    pick = np.zeros((2 * SPOTS, 4 * 2 * SPOTS), np.float32)
    for s in range(2):
        for a in range(WIN):
            for b in range(WIN):
                window = 2 * (a >= 4) + (b >= 4)
                source = window * 128 + s * SPOTS + (a ^ 4) * WIN + (b ^ 4)
                pick[s * SPOTS + a * WIN + b, source] = 1.0
    return pick


def quadrant_pick():
    pick = np.zeros((2 * SPOTS, 2 * SPOTS), np.float32)
    for quad in range(4):
        for s in range(2):
            for a in range(4):
                for b in range(4):
                    row = quad * 32 + s * 16 + a * 4 + b
                    spot = (a + 4 * (quad // 2)) * WIN + b + 4 * (quad % 2)
                    pick[row, s * SPOTS + spot] = 1.0
    return pick


def offset_pick():
    pick = np.zeros((256, WIN * 128), np.float32)
    for d in range(WIN):
        for row in range(15):
            for b in range(WIN):
                pick[row * 15 + b - d + 7, d * 128 + row * WIN + b] = 1.0
    return pick


def dot(left, right, dims=NN):
    return lax.dot_general(left, right, dims, preferred_element_type=F32)


def normalize(values):
    center = values - jnp.mean(values, axis=-1, keepdims=True)
    rstd = lax.rsqrt(jnp.mean(center * center, axis=-1, keepdims=True) + EPS)
    return (center * rstd, rstd)


def lane(shape):
    return lax.broadcasted_iota(jnp.int32, shape, len(shape) - 1)


def head_mask():
    row = lax.broadcasted_iota(jnp.int32, (LANES, WIDE), 0)
    return jnp.where(row // SPOTS == lane((LANES, WIDE)) // HEAD_DIM, 1.0, 0.0).astype(BF16)


def expand(value, mask_ref):
    return jnp.concatenate([value] * HEADS, axis=0) * mask_ref[...]


def fold(full):
    head = lane((SPOTS, WIDE)) // HEAD_DIM
    out = jnp.zeros((SPOTS, WIDE), F32)
    for h in range(HEADS):
        out = out + jnp.where(head == h, full[h * SPOTS : (h + 1) * SPOTS], 0.0)
    return out


def softmax_down(scores):
    expo = jnp.exp(scores - jnp.max(scores, axis=0, keepdims=True))
    return expo / jnp.sum(expo, axis=0, keepdims=True)


def attention_back(query, key, value, d_mixed, probs, query_wide, mask_ref):
    weights = probs.astype(BF16)
    d_wide = expand(d_mixed, mask_ref)
    d_probs = dot(value, d_wide, NT)
    d_value = dot(weights, d_wide).astype(BF16)
    d_scores = (probs * (d_probs - jnp.sum(probs * d_probs, axis=0, keepdims=True))).astype(BF16)
    d_key = (dot(d_scores, query_wide) * SCALE).astype(BF16)
    d_query = (fold(dot(d_scores, key, TN)) * SCALE).astype(BF16)
    return (d_query, d_key, d_value)


def prepare(core_ref, tok, cot, qkv_p, qkv_s, proj_p, proj_s, quad, out_w, out_r, out_b, out_d):
    out_r[0:128] = tok[...]
    out_b[0:128] = tok[...]
    out_d[0:128] = tok[...]
    quads = dot(quad[...], cot[...]).astype(BF16)
    out_r[128:160] = quads[64:96]
    out_b[128:160] = quads[32:64]
    out_d[128:160] = quads[0:32]
    start = pl.multiple_of(core_ref[0] * HALF, 128)
    first = qkv_p[pl.ds(start, HALF), :].astype(F32).T.astype(BF16)
    third = qkv_s[pl.ds(start, HALF), :].astype(F32).T.astype(BF16)
    second = proj_p[:, pl.ds(start, HALF)]
    fourth = proj_s[:, pl.ds(start, HALF)]
    for i in range(8):
        out_w[i, 0:144] = first
        out_w[i, 144:192] = second
        out_w[i, 192:336] = third
        out_w[i, 336:384] = fourth


def biases(edge_ref, tables, pick, out_p, out_q, out_s, wide):
    values = tables[...]
    high = values.astype(BF16)
    rest = values - high.astype(F32)
    middle = rest.astype(BF16)
    low = (rest - middle.astype(F32)).astype(BF16)
    ones = pick[...]
    spread = (dot(high, ones) + dot(middle, ones)) + dot(low, ones)
    for row in range(2 * HEADS):
        for d in range(WIN):
            wide[row * WIN + d : row * WIN + d + 1] = spread[row : row + 1, d * 128 : (d + 1) * 128]
    left = lane((WIN, 128)) < SPOTS
    for c in range(WIN):
        move = (7 - c) * WIN
        for pair in range(HEADS // 2):
            for t, out in ((0, out_p), (1, out_s)):
                even = (t * HEADS + 2 * pair) * WIN
                first = pltpu.roll(wide[even : even + WIN], (128 - move) % 128, 1)
                second = pltpu.roll(wide[even + WIN : even + 2 * WIN], (SPOTS - move) % 128, 1)
                out[c * WIN : (c + 1) * WIN, pair * 128 : (pair + 1) * 128] = jnp.where(left, first, second)
    at = lane((SPOTS, LANES))
    plain = out_p[...]
    turned = jnp.where((at & 4) != 0, pltpu.roll(plain, 4, 1), pltpu.roll(plain, LANES - 4, 1))
    turned = jnp.where((at & 32) != 0, pltpu.roll(turned, 32, 1), pltpu.roll(turned, LANES - 32, 1))
    out_q[...] = turned
    key_at = lax.broadcasted_iota(jnp.int32, (SPOTS, LANES), 0)
    cross = at ^ key_at
    barred = (cross & 32) * edge_ref[0] + (cross & 4) * edge_ref[1]
    out_s[...] = jnp.where(barred != 0, NEG, out_s[...])


def project(rows_ref, w_mine, w_other, mine, other):
    return dot(rows_ref[:, pl.ds(mine, HALF)], w_mine, NT) + dot(
        rows_ref[:, pl.ds(other, HALF)], w_other, NT
    )


def sides(core_ref):
    mine = pl.multiple_of(core_ref[0] * HALF, 128)
    return (mine, pl.multiple_of(HALF - mine, 128))


def qkv_of(block):
    return block[:, 0:SHARE].reshape(3 * WIDE, HALF)


def proj_of(block):
    return block[:, SHARE : SHARE + ROWS].reshape(WIDE, HALF)


def input_grad(grad, normed, rstd, d_packed, w_mine, w_other, mine, other, sums):
    sums[:, pl.ds(mine, HALF)] = dot(d_packed, w_mine)
    sums[:, pl.ds(other, HALF)] = dot(d_packed, w_other)
    d_normed = sums[...]
    d_input = rstd * (
        d_normed
        - jnp.mean(d_normed, axis=-1, keepdims=True)
        - normed * jnp.mean(d_normed * normed, axis=-1, keepdims=True)
    )
    return (grad + d_input).astype(BF16)


def main_kernel(
    grad_scale,
    core_ref,
    tok,
    cot,
    right,
    below,
    diag,
    wp_mine,
    wp_other,
    ws_mine,
    ws_other,
    bias_q,
    bias_s,
    pick,
    pick_quad,
    quad,
    out_grad,
    out_local,
    rows,
    rows_small,
    grads,
    sums,
    mask,
):
    mine, other = sides(core_ref)
    mask[...] = head_mask()
    sources = (tok, right, below, diag)
    for w, source in enumerate(sources):
        for s in range(2):
            normed, _ = normalize(source[s * SPOTS : (s + 1) * SPOTS].astype(F32))
            rows[s * 256 + w * SPOTS : s * 256 + (w + 1) * SPOTS] = normed.astype(BF16)
    shifted = dot(pick[:, 0:128], tok[...])
    cot_in = dot(pick[:, 0:128], cot[...])
    for w in range(1, 4):
        shifted = shifted + dot(pick[:, w * 128 : (w + 1) * 128], sources[w][0:128])
        cot_in = cot_in + dot(pick_quad[:, (w - 1) * 32 : w * 32], sources[w][128:160])
    grads[...] = cot_in.astype(BF16)
    normed, _ = normalize(shifted)
    rows_small[...] = normed.astype(BF16)
    w_mine, w_other = qkv_of(wp_mine[...]), qkv_of(wp_other[...])
    query = project(rows_small, w_mine[:WIDE], w_other[:WIDE], mine, other).astype(BF16)
    key_value = project(rows, w_mine[WIDE:], w_other[WIDE:], mine, other).astype(BF16)
    at = lane((SPOTS, LANES))
    lower = (at & 32) != 0
    later = (at & 4) != 0
    mixed = []
    for s in range(2):
        key = key_value[s * 256 : (s + 1) * 256, :WIDE]
        value = key_value[s * 256 : (s + 1) * 256, WIDE:]
        full = dot(key, expand(query[s * SPOTS : (s + 1) * SPOTS], mask), NT)
        scores = jnp.where(
            lower,
            jnp.where(later, full[192:256], full[128:192]),
            jnp.where(later, full[64:128], full[0:64]),
        )
        probs = softmax_down(scores * SCALE + bias_q[...])
        quarters = [
            jnp.where(lower | later, 0.0, probs),
            jnp.where(lower, 0.0, jnp.where(later, probs, 0.0)),
            jnp.where(lower, jnp.where(later, 0.0, probs), 0.0),
            jnp.where(lower & later, probs, 0.0),
        ]
        wide = jnp.concatenate([q.astype(BF16) for q in quarters], axis=0)
        mixed.append(fold(dot(wide, value, TN)).astype(BF16))
    mixed_plain = jnp.concatenate(mixed, axis=0)
    sums[:, pl.ds(mine, HALF)] = dot(mixed_plain, proj_of(wp_mine[...]))
    sums[:, pl.ds(other, HALF)] = dot(mixed_plain, proj_of(wp_other[...]))
    block_out = (shifted + sums[...]).astype(BF16).astype(F32)
    normed, rstd = normalize(block_out)
    rows_small[...] = normed.astype(BF16)
    w_mine, w_other = qkv_of(ws_mine[...]), qkv_of(ws_other[...])
    packed = project(rows_small, w_mine, w_other, mine, other).astype(BF16)
    d_mixed = project(grads, proj_of(ws_mine[...]), proj_of(ws_other[...]), mine, other).astype(BF16)
    mixed, d_packed = [], []
    for s in range(2):
        part = packed[s * SPOTS : (s + 1) * SPOTS]
        query, key, value = part[:, :WIDE], part[:, WIDE : 2 * WIDE], part[:, 2 * WIDE :]
        query_wide = expand(query, mask)
        probs = softmax_down(dot(key, query_wide, NT) * SCALE + bias_s[...])
        mixed.append(fold(dot(probs.astype(BF16), value, TN)).astype(BF16))
        back = attention_back(
            query, key, value, d_mixed[s * SPOTS : (s + 1) * SPOTS], probs, query_wide, mask
        )
        d_packed.append(jnp.concatenate(back, axis=1))
    mixed_shift = jnp.concatenate(mixed, axis=0)
    d_packed = jnp.concatenate(d_packed, axis=0)
    grad = input_grad(
        grads[...].astype(F32), normed, rstd, d_packed, w_mine, w_other, mine, other, sums
    )
    out_grad[...] = dot(quad[...], grad).astype(BF16)
    local_plain = (dot(mixed_plain, grad, TN) * grad_scale).astype(BF16)
    local_shift = (dot(mixed_shift, grads[...], TN) * grad_scale).astype(BF16)
    for side in range(2):
        for i in range(8):
            at_rows = slice(i * ROWS, (i + 1) * ROWS)
            at_lanes = slice(side * HALF, (side + 1) * HALF)
            out_local[side, i, 0] = local_plain[at_rows, at_lanes]
            out_local[side, i, 1] = local_shift[at_rows, at_lanes]


def plain_back(
    core_ref, tok, g_own, g_left, g_above, g_diag, wp_mine, wp_other, bias_p, pick, out, rows, grads, sums, mask
):
    mine, other = sides(core_ref)
    mask[...] = head_mask()
    normed, rstd = normalize(tok[...].astype(F32))
    rows[...] = normed.astype(BF16)
    w_mine, w_other = qkv_of(wp_mine[...]), qkv_of(wp_other[...])
    packed = project(rows, w_mine, w_other, mine, other).astype(BF16)
    gathered = (
        dot(pick[:, 0:32], g_diag[...])
        + dot(pick[:, 32:64], g_above[...])
        + dot(pick[:, 64:96], g_left[...])
        + dot(pick[:, 96:128], g_own[...])
    )
    grads[...] = gathered.astype(BF16)
    d_mixed = project(grads, proj_of(wp_mine[...]), proj_of(wp_other[...]), mine, other).astype(BF16)
    d_packed = []
    for s in range(2):
        part = packed[s * SPOTS : (s + 1) * SPOTS]
        query, key, value = part[:, :WIDE], part[:, WIDE : 2 * WIDE], part[:, 2 * WIDE :]
        query_wide = expand(query, mask)
        probs = softmax_down(dot(key, query_wide, NT) * SCALE + bias_p[...])
        back = attention_back(
            query, key, value, d_mixed[s * SPOTS : (s + 1) * SPOTS], probs, query_wide, mask
        )
        d_packed.append(jnp.concatenate(back, axis=1))
    d_packed = jnp.concatenate(d_packed, axis=0)
    out[...] = input_grad(gathered, normed, rstd, d_packed, w_mine, w_other, mine, other, sums)


VMEM = pl.BlockSpec(memory_space=pltpu.VMEM)
SMEM = pl.BlockSpec(memory_space=pltpu.SMEM)


def params():
    return pltpu.CompilerParams(vmem_limit_bytes=50 * 1024 * 1024)


def cost(flops, size):
    return pl.CostEstimate(flops=flops, bytes_accessed=size, transcendentals=0)


def tm_groups(bits):
    size = lax.axis_size("tm")
    step = {"core": 1, "y_hi": 2, "z": 8}[bits]
    count = {"core": 2, "y_hi": 4, "z": 8}[bits]
    groups = []
    for first in range(size):
        if (first // step) % count == 0:
            groups.append([first + step * i for i in range(count)])
    return groups


def swap(value, axis, groups=None):
    return lax.all_to_all(value, axis, 0, 0, axis_index_groups=groups)


def total(blocks):
    return jnp.sum(blocks.astype(F32), axis=0).astype(BF16)


def copies(value, count):
    return jnp.broadcast_to(value[None], (count,) + value.shape)


def from_offset(value, along_tm, along_freq):
    n_tm, n_freq = lax.axis_size("tm"), lax.axis_size("freq")
    pairs = []
    for t in range(n_tm):
        for f in range(n_freq):
            source = ((t + along_tm) % n_tm) * n_freq + (f + along_freq) % n_freq
            pairs.append((source, t * n_freq + f))
    return lax.ppermute(value, ("tm", "freq"), pairs)


def reduce_grads(local):
    part = total(swap(local, "tm", tm_groups("core")))
    part = total(swap(part, "freq"))
    part = total(swap(part.reshape(8, 12, HALF), "tm", tm_groups("z")))
    part = total(swap(copies(part, 4), "tm", tm_groups("y_hi")))
    part = swap(copies(part, 8), "tm", tm_groups("z")).reshape(2, ROWS, HALF)
    part = lax.all_gather(part, "tm", axis_index_groups=tm_groups("core"))
    part = jnp.concatenate([part[0], part[1]], axis=-1).astype(F32)
    return (part[0], part[1])


def shards(
    tokens, cotangent, qkv_plain, qkv_shift, proj_plain, proj_shift, table_plain, table_shift
):
    core = (lax.axis_index("tm") % 2).astype(jnp.int32).reshape(1)
    last_freq = lax.axis_index("freq") == lax.axis_size("freq") - 1
    last_time = lax.axis_index("tm") == lax.axis_size("tm") - 1
    edge = jnp.stack([last_freq, last_time]).astype(jnp.int32)
    grad_scale = 1.0 / math.sqrt(128 * lax.axis_size("tm") * lax.axis_size("freq"))
    pick = jnp.asarray(shifted_pick(), BF16)
    quad = jnp.asarray(quadrant_pick(), BF16)
    pick_quad = jnp.asarray(quadrant_pick()[32:].T, BF16)
    pick_back = jnp.asarray(quadrant_pick().T, BF16)
    tok = tokens.reshape(128, D)
    cot = cotangent.reshape(128, D)

    message = jax.ShapeDtypeStruct((160, D), BF16)
    weights, to_left, to_above, to_diag = pl.pallas_call(
        prepare,
        out_shape=(jax.ShapeDtypeStruct((8, 384, HALF), BF16), message, message, message),
        in_specs=[SMEM] + [VMEM] * 7,
        out_specs=[VMEM] * 4,
        compiler_params=params(),
        name="prepare",
    )(core, tok, cot, qkv_plain, qkv_shift, proj_plain, proj_shift, quad)

    right = from_offset(to_left, 1, 0)
    below = from_offset(to_above, 0, 1)
    diag = from_offset(to_diag, 1, 1)
    w_mine = swap(weights, "freq")
    n_tm = lax.axis_size("tm")
    w_other = lax.ppermute(w_mine, "tm", [(i, i ^ 1) for i in range(n_tm)])

    tables = jnp.concatenate([table_plain, table_shift], axis=0)
    tables = jnp.pad(tables, ((0, 8), (0, 256 - REL)))
    table = jax.ShapeDtypeStruct((SPOTS, LANES), F32)
    bias_p, bias_q, bias_s = pl.pallas_call(
        biases,
        out_shape=(table, table, table),
        in_specs=[SMEM, VMEM, VMEM],
        out_specs=[VMEM] * 3,
        scratch_shapes=[pltpu.VMEM((2 * HEADS * WIN, 128), F32)],
        compiler_params=params(),
        name="biases",
    )(edge, tables, jnp.asarray(offset_pick(), BF16))

    plain_block = pl.BlockSpec((8, 192, HALF), lambda i: (0, 0, 0))
    shift_block = pl.BlockSpec((8, 192, HALF), lambda i: (0, 1, 0))
    quads, local = pl.pallas_call(
        lambda *refs: main_kernel(grad_scale, *refs),
        grid=(1,),
        out_shape=(
            jax.ShapeDtypeStruct((128, D), BF16),
            jax.ShapeDtypeStruct((2, 8, 2, ROWS, HALF), BF16),
        ),
        in_specs=[SMEM]
        + [VMEM] * 5
        + [plain_block, plain_block, shift_block, shift_block]
        + [VMEM] * 5,
        out_specs=[VMEM] * 2,
        scratch_shapes=[
            pltpu.VMEM((512, D), BF16),
            pltpu.VMEM((128, D), BF16),
            pltpu.VMEM((128, D), BF16),
            pltpu.VMEM((128, D), F32),
            pltpu.VMEM((LANES, WIDE), BF16),
        ],
        compiler_params=params(),
        cost_estimate=cost(4_000_000_000, 6_000_000),
        name="main",
    )(
        core, tok, cot, right, below, diag,
        w_mine, w_other, w_mine, w_other, bias_q, bias_s, pick, pick_quad, quad,
    )

    left = from_offset(quads[32:64], -1, 0)
    above = from_offset(quads[64:96], 0, -1)
    corner = from_offset(quads[96:128], -1, -1)
    grad_tokens = pl.pallas_call(
        plain_back,
        grid=(1,),
        out_shape=jax.ShapeDtypeStruct((128, D), BF16),
        in_specs=[SMEM] + [VMEM] * 5 + [plain_block, plain_block] + [VMEM] * 2,
        out_specs=VMEM,
        scratch_shapes=[
            pltpu.VMEM((128, D), BF16),
            pltpu.VMEM((128, D), BF16),
            pltpu.VMEM((128, D), F32),
            pltpu.VMEM((LANES, WIDE), BF16),
        ],
        compiler_params=params(),
        cost_estimate=cost(4_000_000_000, 4_000_000),
        name="plain_back",
    )(core, tok, quads[0:32], left, above, corner, w_mine, w_other, bias_p, pick_back)
    grad_plain, grad_shift = reduce_grads(local)
    return (grad_tokens.reshape(tokens.shape), grad_plain, grad_shift)


def solution(mesh):
    placed = (
        P(None, "freq", "tm", None),
        P(None, "freq", "tm", None),
        P(None, "freq"),
        P(None, "freq"),
        P("freq", None),
        P("freq", None),
        P(),
        P(),
    )
    return jax.shard_map(
        shards,
        mesh=mesh,
        in_specs=placed,
        out_specs=(P(None, "freq", "tm", None), P("freq", None), P("freq", None)),
        check_vma=False,
    )
```

time: 216 us -> 162 us (0.75)
  matrix products: 28.3 us -> 0 us
  local copies, waits for them, and re-layouts: 37.9 us -> 10.4 us
  waiting for transfers between devices: 29.4 us -> 3.13 us
  blocking collectives: 50.6 us -> 71.5 us
  Pallas kernels: 0 us -> 19.2 us
  other arithmetic: 19 us -> 4.63 us
  starting transfers between devices: 48.1 us -> 51 us
    dot_general x22 -> x0, matrix products: 25.2 us -> none  [the longest x2 5.16 us: offset_bias(): lax.dot_general(table, onehot, (((1,), (1,)), ((), ())), precision=lax.Pr...]
    all_to_all x2 -> x4, blocking collectives: 44 us -> 68.1 us  [swap(): return lax.all_to_all(value, axis, 0, 0, axis_index_groups=groups)]
    all_to_all x4 -> x2, waiting for transfers between devices: 23.8 us -> 1.05 us  [swap(): return lax.all_to_all(value, axis, 0, 0, axis_index_groups=groups)]
    pallas_call x0 -> x4, Pallas kernels: none -> 19.2 us  [the longest x1 10.3 us: shards(): pl.pallas_call(lambda *refs: main_kernel(grad_scale, *refs), grid=(1,), o...]
    reshape x9 -> x1, local copies, waits for them, and re-layouts: 11.9 us -> 0.02 us  [reduce_grads(): part = total(swap(part.reshape(8, 12, HALF), 'tm', tm_groups('z')))]
    unnamed x56 -> x34, local copies, waits for them, and re-layouts: 1.38 us -> 8.28 us
    convert_element_type x6 -> x0, local copies, waits for them, and re-layouts: 6.54 us -> none  [the longest x2 3.7 us: attend(): jnp.dot(normed.astype(jnp.bfloat16), w_qkv, preferred_element_type=jnp.fl...]
    ppermute x7, starting transfers between devices: 34.6 us -> 40.1 us  [the longest x6 32.7 us: from_offset(): return lax.ppermute(value, ('tm', 'freq'), pairs)]
  transfers between devices with their start and end apart: 11 -> 9, of which waited for: 6 -> 3; matrix products, arithmetic and copies ran while one was open for 22% -> 1% of each run, Pallas kernels for 0% -> 4%
where the time goes in v2:
time: 162 us; the launch traced here: 161 us
  blocking collectives  71.5 us (44%)
  starting transfers between devices  51 us (31%)
  Pallas kernels  19.2 us (12%)
  local copies, waits for them, and re-layouts  10.4 us (6%)
  other arithmetic  4.63 us (3%)
  waiting for transfers between devices  3.13 us (2%)
    all_to_all x4, blocking collectives, swap(): return lax.all_to_all(value, axis, 0, 0, axis_index_groups=groups)  68.1 us
    ppermute x6, starting transfers between devices, from_offset(): return lax.ppermute(value, ('tm', 'freq'), pairs)  32.7 us
    all_to_all x2, starting transfers between devices, swap(): return lax.all_to_all(value, axis, 0, 0, axis_index_groups=groups)  10.9 us
    pallas_call x1, Pallas kernels, shards(): pl.pallas_call(lambda *refs: main_kernel(grad_scale, *refs), grid=(1,), o...  10.3 us
    unnamed x34, local copies, waits for them, and re-layouts  8.28 us
    ppermute x1, starting transfers between devices, shards(): w_other = lax.ppermute(w_mine, 'tm', [(i, i ^ 1) for i in range(n_tm)])  7.36 us
    pallas_call x1, Pallas kernels, shards(): pl.pallas_call(plain_back, grid=(1,), out_shape=jax.ShapeDtypeStruct((128...  5.58 us
    reduce_sum x4, other arithmetic, total(): return jnp.sum(blocks.astype(F32), axis=0).astype(BF16)  3.79 us
  transfers between devices with their start and end apart: 9, of which 3 were waited for; matrix products, arithmetic and copies ran while one was open for 1% of the time, Pallas kernels for 4%

profile of v2, /device:TPU:1, one launch (start us, length us, event | category | flops | bytes accessed | tf_op | source)
XLA Modules:
  0.0 160.8 jit_solution(10485345760346871714)
XLA Ops:
  0.6 1.1 copy.24.qkv_p
  1.7 1.1 copy.25.qkv_s
  2.9 0.9 copy-done.3
  3.8 0.9 copy-done.5
  4.7 0.9 copy-done.7
  5.6 0.9 copy-done.8
  6.5 0.8 copy-done.9
  7.3 1.9 %prepare.1 = (bf16[8,384,384]{2,1,0:T(8,128)(2,1)}, bf16[160,768]{1,0:T(8,128)(2,1)}, bf16[160,768]{1,0:T(8,128)(2,1)}, bf16[160,768]{1,0:T(8,128)(2,1)}) custom-call(s32[1]{0:T(128)} %bitcast.core_ref.refs_0_, bf16[128,768]{1,0:T(8,128)(2,1)S(1)} %bitcast.16, bf16[128,768]{1,0:T(8,128)(2,1)S(1)} %bitcast.14, bf16[768,144]{1,0:T(8,128)(2,1)S(1)} %copy.24.qkv_p, ...), custom_call_target="tpu_custom_call" | custom-call | tf_op jit(solution)/shard_map/prepare/pallas_call | solution.py:400
  9.2 31.2 %all_to_all.30.refs_6_.refs_8_.wp_mine = bf16[8,384,384]{2,1,0:T(8,128)(2,1)S(1)} all-to-all(bf16[8,384,384]{2,1,0:T(8,128)(2,1)} %get-tuple-element.15), channel_id=1, replica_groups=mesh['tm'=64,'freq'=8] {'freq'}, dimensions={0} | all-to-all | bytes 4718592 | tf_op jit(solution)/shard_map/all_to_all | solution.py:352
  40.5 7.4 %collective-permute-start.3 = (bf16[8,384,384]{2,1,0:T(8,128)(2,1)S(1)}, bf16[8,384,384]{2,1,0:T(8,128)(2,1)}, u32[]{:S(2)}, u32[]{:S(2)}) collective-permute-start(bf16[8,384,384]{2,1,0:T(8,128)(2,1)S(1)} %all_to_all.30.refs_6_.refs_8_.wp_mine), channel_id=1, source_target_pairs={{0,8},{8,0},{16,24},{24,16},{32,40},{40,32},{48,56},{56,48},{64,72... | collective-permute-start | bytes 7077896 | tf_op jit(solution)/shard_map/ppermute | solution.py:414
  47.8 1.9 %collective-permute-start = (bf16[160,768]{1,0:T(8,128)(2,1)}, bf16[160,768]{1,0:T(8,128)(2,1)S(1)}, u32[]{:S(2)}, u32[]{:S(2)}) collective-permute-start(bf16[160,768]{1,0:T(8,128)(2,1)} %get-tuple-element.12), channel_id=1, source_target_pairs={{8,0},{9,1},{10,2},{11,3},{12,4},{13,5},{14,6},{15,7},{16,8},{17,9... | collective-permute-start | bytes 737288 | tf_op jit(solution)/shard_map/ppermute | solution.py:370
  49.8 3.1 %collective-permute-start.1 = (bf16[160,768]{1,0:T(8,128)(2,1)}, bf16[160,768]{1,0:T(8,128)(2,1)}, u32[]{:S(2)}, u32[]{:S(2)}) collective-permute-start(bf16[160,768]{1,0:T(8,128)(2,1)} %get-tuple-element.13), channel_id=1, source_target_pairs={{1,0},{2,1},{3,2},{4,3},{5,4},{6,5},{7,6},{0,7},{9,8},{10,9},{11,1... | collective-permute-start | bytes 737288 | tf_op jit(solution)/shard_map/ppermute | solution.py:370
  52.9 14.8 %collective-permute-start.2 = (bf16[160,768]{1,0:T(8,128)(2,1)}, bf16[160,768]{1,0:T(8,128)(2,1)}, u32[]{:S(2)}, u32[]{:S(2)}) collective-permute-start(bf16[160,768]{1,0:T(8,128)(2,1)} %get-tuple-element.14), channel_id=1, source_target_pairs={{9,0},{10,1},{11,2},{12,3},{13,4},{14,5},{15,6},{8,7},{17,8},{18,9... | collective-permute-start | bytes 737288 | tf_op jit(solution)/shard_map/ppermute | solution.py:370
  67.8 0.7 select_maximum_fusion.tables
  68.5 1.4 biases.1
  70.0 1.4 collective-permute-done.2.refs_5_
  71.5 0.9 copy-done.13
  72.4 0.8 copy-done.15
  73.1 10.3 %main.1 = (bf16[128,768]{1,0:T(8,128)(2,1)S(1)}, bf16[2,8,2,48,384]{4,3,2,1,0:T(8,128)(2,1)S(1)}) custom-call(s32[1]{0:T(128)} %bitcast.core_ref.refs_0_, bf16[128,768]{1,0:T(8,128)(2,1)S(1)} %bitcast.17, bf16[128,768]{1,0:T(8,128)(2,1)S(1)} %bitcast.15, bf16[160,768]{1,0:T(8,128)(2,1)S(1)} %collective-permute-done.refs_3_, ...), custom_call_target="tpu_custom_call" | custom-call | flops 4000000000 | bytes 6000000 | tf_op jit(solution)/shard_map/main/pallas_call | solution.py:431
  83.4 9.8 %all_to_all.31 = bf16[2,8,2,48,384]{4,3,2,1,0:T(8,128)(2,1)} all-to-all(bf16[2,8,2,48,384]{4,3,2,1,0:T(8,128)(2,1)S(1)} %get-tuple-element.20), channel_id=1, replica_groups={{0,8},{16,24},{32,40},{48,56},{64,72},{80,88},{96,104},{112,120},{128,1..., dimensions={0} | all-to-all | bytes 2359296 | tf_op jit(solution)/shard_map/all_to_all | solution.py:352
  93.2 2.6 %reduce_sum.48 = bf16[8,2,48,384]{3,2,1,0:T(8,128)(2,1)} reduce(bf16[2,8,2,48,384]{4,3,2,1,0:T(8,128)(2,1)} %all_to_all.31, bf16[]{:T(256)} %constant.44.clone.1), dimensions={0}, to_apply=%region_0.1 | reduce | flops 294912 | bytes 1769474 | tf_op jit(solution)/shard_map/reduce_sum | solution.py:356
  95.8 14.5 %all_to_all.32 = bf16[8,2,48,384]{3,2,1,0:T(8,128)(2,1)} all-to-all(bf16[8,2,48,384]{3,2,1,0:T(8,128)(2,1)} %reduce_sum.48), channel_id=1, replica_groups=mesh['tm'=64,'freq'=8] {'freq'}, dimensions={0} | all-to-all | bytes 1179648 | tf_op jit(solution)/shard_map/all_to_all | solution.py:352
  110.3 1.1 reduce_sum.49
  111.5 12.6 %all_to_all.33 = bf16[8,12,384]{2,1,0:T(8,128)(2,1)S(1)} all-to-all(bf16[8,12,384]{2,1,0:T(8,128)(2,1)S(1)} %reshape.27), channel_id=1, replica_groups={{0,64,128,192,256,320,384,448},{8,72,136,200,264,328,392,456},{16,80,14..., dimensions={0} | all-to-all | bytes 147456 | tf_op jit(solution)/shard_map/all_to_all | solution.py:352
  124.8 7.4 %all-to-all-start.4 = ((bf16[4,12,384]{2,1,0:T(8,128)(2,1)}), bf16[4,12,384]{2,1,0:T(8,128)(2,1)S(1)}, u32[]{:S(2)}, u32[]{:S(2)}) async-start(bf16[4,12,384]{2,1,0:T(8,128)(2,1)} %broadcast_in_dim.4), calls=%async_computation.4 | async-start | bytes 98304 | tf_op jit(solution)/shard_map/all_to_all | solution.py:352
  132.2 7.6 %collective-permute-start.4 = (bf16[32,768]{1,0:T(8,128)(2,1)S(1)}, bf16[32,768]{1,0:T(8,128)(2,1)S(1)}, u32[]{:S(2)}, u32[]{:S(2)}) collective-permute-start(bf16[32,768]{1,0:T(8,128)(2,1)S(1)} %get-tuple-element.25), channel_id=1, source_target_pairs={{504,0},{505,1},{506,2},{507,3},{508,4},{509,5},{510,6},{511,7},{0... | collective-permute-start | bytes 147464 | tf_op jit(solution)/shard_map/ppermute | solution.py:370
  139.8 2.4 %collective-permute-start.5 = (bf16[32,768]{1,0:T(8,128)(2,1)S(1)}, bf16[32,768]{1,0:T(8,128)(2,1)S(1)}, u32[]{:S(2)}, u32[]{:S(2)}) collective-permute-start(bf16[32,768]{1,0:T(8,128)(2,1)S(1)} %get-tuple-element.24), channel_id=1, source_target_pairs={{7,0},{0,1},{1,2},{2,3},{3,4},{4,5},{5,6},{6,7},{15,8},{8,9},{9,10... | collective-permute-start | bytes 147464 | tf_op jit(solution)/shard_map/ppermute | solution.py:370
  142.2 2.9 %collective-permute-start.6 = (bf16[32,768]{1,0:T(8,128)(2,1)S(1)}, bf16[32,768]{1,0:T(8,128)(2,1)S(1)}, u32[]{:S(2)}, u32[]{:S(2)}) collective-permute-start(bf16[32,768]{1,0:T(8,128)(2,1)S(1)} %get-tuple-element.23), channel_id=1, source_target_pairs={{511,0},{504,1},{505,2},{506,3},{507,4},{508,5},{509,6},{510,7},{7... | collective-permute-start | bytes 147464 | tf_op jit(solution)/shard_map/ppermute | solution.py:370
  145.8 3.5 %all-to-all-start.5 = ((bf16[8,12,384]{2,1,0:T(8,128)(2,1)}), bf16[8,12,384]{2,1,0:T(8,128)(2,1)S(1)}, u32[]{:S(2)}, u32[]{:S(2)}) async-start(bf16[8,12,384]{2,1,0:T(8,128)(2,1)} %broadcast_in_dim.5), calls=%async_computation.5 | async-start | bytes 196608 | tf_op jit(solution)/shard_map/all_to_all | solution.py:352
  150.0 5.6 %plain_back.1 = bf16[128,768]{1,0:T(8,128)(2,1)} custom-call(s32[1]{0:T(128)} %bitcast.core_ref.refs_0_, bf16[128,768]{1,0:T(8,128)(2,1)S(1)} %bitcast.18, bf16[32,768]{1,0:T(8,128)(2,1)S(1)} %get-tuple-element.26.g_own, bf16[32,768]{1,0:T(8,128)(2,1)S(1)} %collective-permute-done.4.g_left, bf16[32,768]{1,0:T(8,128)(2,1)S(1)} %collective-permute-done.5.g_above, ...), custom_call_target="tpu_custom_call" | custom-call | flops 4000000000 | bytes 4000000 | tf_op jit(solution)/shard_map/plain_back/pallas_call | solution.py:461
  155.6 1.1 all-to-all-done.5
  156.6 3.3 %all_gather.3 = bf16[2,2,48,384]{3,2,1,0:T(8,128)(2,1)S(1)} all-gather(bf16[1,2,48,384]{3,2,1,0:T(8,128)(2,1)S(1)} %all_gather_reshape.3), channel_id=1, replica_groups={{0,8},{16,24},{32,40},{48,56},{64,72},{80,88},{96,104},{112,120},{128,1..., dimensions={0}, use_global_device_ids=true | all-gather | bytes 221184 | tf_op jit(solution)/shard_map/all_gather | solution.py:379
  (43 shorter events, 2.9 us)
Async XLA Ops:
  2.9 0.9 copy-start.3
  3.8 0.9 copy-start.5
  4.7 0.9 copy-start.7
  5.6 0.9 copy-start.8
  6.5 0.8 copy-start.9
  9.2 59.3 %copy-start.2 = (bf16[256,1024]{1,0:T(8,128)(2,1)S(1)}, bf16[256,1024]{1,0:T(8,128)(2,1)}, u32[]{:S(2)}) copy-start(bf16[256,1024]{1,0:T(8,128)(2,1)} %constant.49.clone.pick) | copy-start | bytes 1572868
  9.2 62.2 %copy-start.4 = (bf16[2,8,8,768]{3,2,1,0:T(8,128)(2,1)S(1)}, bf16[2,8,8,768]{3,2,1,0:T(8,128)(2,1)}, u32[]{:S(2)}) copy-start(bf16[2,8,8,768]{3,2,1,0:T(8,128)(2,1)} %param.14) | copy-start | bytes 589828
  9.2 62.2 %copy-start.6 = (bf16[2,8,8,768]{3,2,1,0:T(8,128)(2,1)S(1)}, bf16[2,8,8,768]{3,2,1,0:T(8,128)(2,1)}, u32[]{:S(2)}) copy-start(bf16[2,8,8,768]{3,2,1,0:T(8,128)(2,1)} %param.13) | copy-start | bytes 589828
  9.2 62.2 %copy-start.10 = (bf16[128,128]{1,0:T(8,128)(2,1)S(1)}, bf16[128,128]{1,0:T(8,128)(2,1)}, u32[]{:S(2)}) copy-start(bf16[128,128]{1,0:T(8,128)(2,1)} %constant.46.clone.quad.refs_14_) | copy-start | bytes 98308
  40.5 31.0 %copy-start = (bf16[8,384,384]{2,1,0:T(8,128)(2,1)}, bf16[8,384,384]{2,1,0:T(8,128)(2,1)S(1)}, u32[]{:S(2)}) copy-start(bf16[8,384,384]{2,1,0:T(8,128)(2,1)S(1)} %all_to_all.30.refs_6_.refs_8_.wp_mine) | copy-start | bytes 7077892
  40.5 31.0 %collective-permute-start.3 = (bf16[8,384,384]{2,1,0:T(8,128)(2,1)S(1)}, bf16[8,384,384]{2,1,0:T(8,128)(2,1)}, u32[]{:S(2)}, u32[]{:S(2)}) collective-permute-start(bf16[8,384,384]{2,1,0:T(8,128)(2,1)S(1)} %all_to_all.30.refs_6_.refs_8_.wp_mine), channel_id=1, source_target_pairs={{0,8},{8,0},{16,24},{24,16},{32,40},{40,32},{48,56},{56,48},{64,72... | collective-permute-start | bytes 7077896 | tf_op jit(solution)/shard_map/ppermute | solution.py:414
  47.8 22.1 %collective-permute-start = (bf16[160,768]{1,0:T(8,128)(2,1)}, bf16[160,768]{1,0:T(8,128)(2,1)S(1)}, u32[]{:S(2)}, u32[]{:S(2)}) collective-permute-start(bf16[160,768]{1,0:T(8,128)(2,1)} %get-tuple-element.12), channel_id=1, source_target_pairs={{8,0},{9,1},{10,2},{11,3},{12,4},{13,5},{14,6},{15,7},{16,8},{17,9... | collective-permute-start | bytes 737288 | tf_op jit(solution)/shard_map/ppermute | solution.py:370
  49.8 20.2 %collective-permute-start.1 = (bf16[160,768]{1,0:T(8,128)(2,1)}, bf16[160,768]{1,0:T(8,128)(2,1)}, u32[]{:S(2)}, u32[]{:S(2)}) collective-permute-start(bf16[160,768]{1,0:T(8,128)(2,1)} %get-tuple-element.13), channel_id=1, source_target_pairs={{1,0},{2,1},{3,2},{4,3},{5,4},{6,5},{7,6},{0,7},{9,8},{10,9},{11,1... | collective-permute-start | bytes 737288 | tf_op jit(solution)/shard_map/ppermute | solution.py:370
  52.9 18.6 %collective-permute-start.2 = (bf16[160,768]{1,0:T(8,128)(2,1)}, bf16[160,768]{1,0:T(8,128)(2,1)}, u32[]{:S(2)}, u32[]{:S(2)}) collective-permute-start(bf16[160,768]{1,0:T(8,128)(2,1)} %get-tuple-element.14), channel_id=1, source_target_pairs={{9,0},{10,1},{11,2},{12,3},{13,4},{14,5},{15,6},{8,7},{17,8},{18,9... | collective-permute-start | bytes 737288 | tf_op jit(solution)/shard_map/ppermute | solution.py:370
  70.0 13.5 %copy-start.11 = (f32[64,768]{1,0:T(8,128)}, f32[64,768]{1,0:T(8,128)S(1)}, u32[]{:S(2)}) copy-start(f32[64,768]{1,0:T(8,128)S(1)} %get-tuple-element.19.bias_p) | copy-start | bytes 589828
  71.5 0.9 copy-start.13
  72.4 0.8 copy-start.15
  93.2 56.8 %copy-start.1 = (bf16[8,384,384]{2,1,0:T(8,128)(2,1)S(1)}, bf16[8,384,384]{2,1,0:T(8,128)(2,1)}, u32[]{:S(2)}) copy-start(bf16[8,384,384]{2,1,0:T(8,128)(2,1)} %copy-done) | copy-start | bytes 7077892
  93.2 56.8 %copy-start.12 = (f32[64,768]{1,0:T(8,128)S(1)}, f32[64,768]{1,0:T(8,128)}, u32[]{:S(2)}) copy-start(f32[64,768]{1,0:T(8,128)} %copy-done.11) | copy-start | bytes 589828
  93.2 56.8 %copy-start.14 = (bf16[128,128]{1,0:T(8,128)(2,1)S(1)}, bf16[128,128]{1,0:T(8,128)(2,1)}, u32[]{:S(2)}) copy-start(bf16[128,128]{1,0:T(8,128)(2,1)} %constant.48.clone.pick) | copy-start | bytes 98308
  124.8 20.3 %all-to-all-start.4 = ((bf16[4,12,384]{2,1,0:T(8,128)(2,1)}), bf16[4,12,384]{2,1,0:T(8,128)(2,1)S(1)}, u32[]{:S(2)}, u32[]{:S(2)}) async-start(bf16[4,12,384]{2,1,0:T(8,128)(2,1)} %broadcast_in_dim.4), calls=%async_computation.4 | async-start | bytes 98304 | tf_op jit(solution)/shard_map/all_to_all | solution.py:352
  132.2 17.2 %collective-permute-start.4 = (bf16[32,768]{1,0:T(8,128)(2,1)S(1)}, bf16[32,768]{1,0:T(8,128)(2,1)S(1)}, u32[]{:S(2)}, u32[]{:S(2)}) collective-permute-start(bf16[32,768]{1,0:T(8,128)(2,1)S(1)} %get-tuple-element.25), channel_id=1, source_target_pairs={{504,0},{505,1},{506,2},{507,3},{508,4},{509,5},{510,6},{511,7},{0... | collective-permute-start | bytes 147464 | tf_op jit(solution)/shard_map/ppermute | solution.py:370
  139.8 9.6 %collective-permute-start.5 = (bf16[32,768]{1,0:T(8,128)(2,1)S(1)}, bf16[32,768]{1,0:T(8,128)(2,1)S(1)}, u32[]{:S(2)}, u32[]{:S(2)}) collective-permute-start(bf16[32,768]{1,0:T(8,128)(2,1)S(1)} %get-tuple-element.24), channel_id=1, source_target_pairs={{7,0},{0,1},{1,2},{2,3},{3,4},{4,5},{5,6},{6,7},{15,8},{8,9},{9,10... | collective-permute-start | bytes 147464 | tf_op jit(solution)/shard_map/ppermute | solution.py:370
  142.2 7.8 %collective-permute-start.6 = (bf16[32,768]{1,0:T(8,128)(2,1)S(1)}, bf16[32,768]{1,0:T(8,128)(2,1)S(1)}, u32[]{:S(2)}, u32[]{:S(2)}) collective-permute-start(bf16[32,768]{1,0:T(8,128)(2,1)S(1)} %get-tuple-element.23), channel_id=1, source_target_pairs={{511,0},{504,1},{505,2},{506,3},{507,4},{508,5},{509,6},{510,7},{7... | collective-permute-start | bytes 147464 | tf_op jit(solution)/shard_map/ppermute | solution.py:370
  145.8 10.8 %all-to-all-start.5 = ((bf16[8,12,384]{2,1,0:T(8,128)(2,1)}), bf16[8,12,384]{2,1,0:T(8,128)(2,1)S(1)}, u32[]{:S(2)}, u32[]{:S(2)}) async-start(bf16[8,12,384]{2,1,0:T(8,128)(2,1)} %broadcast_in_dim.5), calls=%async_computation.5 | async-start | bytes 196608 | tf_op jit(solution)/shard_map/all_to_all | solution.py:352

commit v3 on v2

--- a/solution.py
+++ b/solution.py
@@ -111,24 +111,21 @@
     return (d_query, d_key, d_value)
 
 
-def prepare(core_ref, tok, cot, qkv_p, qkv_s, proj_p, proj_s, quad, out_w, out_r, out_b, out_d):
-    out_r[0:128] = tok[...]
-    out_b[0:128] = tok[...]
-    out_d[0:128] = tok[...]
+def prepare(core_ref, tok, cot, qkv_p, qkv_s, proj_p, proj_s, quad, out_w, out_r, out_b, out_d, block, sems):
+    start = pl.multiple_of(core_ref[0] * HALF, 128)
+    block[0:144] = qkv_p[:, pl.ds(start, HALF)]
+    block[144:192] = proj_p[:, pl.ds(start, HALF)]
+    block[192:336] = qkv_s[:, pl.ds(start, HALF)]
+    block[336:384] = proj_s[:, pl.ds(start, HALF)]
+    sends = [pltpu.make_async_copy(block, out_w.at[i], sems.at[i]) for i in range(8)]
+    for send in sends:
+        send.start()
     quads = dot(quad[...], cot[...]).astype(BF16)
-    out_r[128:160] = quads[64:96]
-    out_b[128:160] = quads[32:64]
-    out_d[128:160] = quads[0:32]
-    start = pl.multiple_of(core_ref[0] * HALF, 128)
-    first = qkv_p[pl.ds(start, HALF), :].astype(F32).T.astype(BF16)
-    third = qkv_s[pl.ds(start, HALF), :].astype(F32).T.astype(BF16)
-    second = proj_p[:, pl.ds(start, HALF)]
-    fourth = proj_s[:, pl.ds(start, HALF)]
-    for i in range(8):
-        out_w[i, 0:144] = first
-        out_w[i, 144:192] = second
-        out_w[i, 192:336] = third
-        out_w[i, 336:384] = fourth
+    for out, first in ((out_r, 64), (out_b, 32), (out_d, 0)):
+        out[0:128] = tok[...]
+        out[128:160] = quads[first : first + 32]
+    for send in sends:
+        send.wait()
 
 
 def biases(edge_ref, tables, pick, out_p, out_q, out_s, wide):
@@ -173,12 +170,12 @@
     return (mine, pl.multiple_of(HALF - mine, 128))
 
 
-def qkv_of(block):
-    return block[:, 0:SHARE].reshape(3 * WIDE, HALF)
-
-
-def proj_of(block):
-    return block[:, SHARE : SHARE + ROWS].reshape(WIDE, HALF)
+def qkv_of(ref, first):
+    return ref[:, first : first + SHARE].reshape(3 * WIDE, HALF)
+
+
+def proj_of(ref, first):
+    return ref[:, first + SHARE : first + SHARE + ROWS].reshape(WIDE, HALF)
 
 
 def input_grad(grad, normed, rstd, d_packed, w_mine, w_other, mine, other, sums):
@@ -201,17 +198,16 @@
     right,
     below,
     diag,
-    wp_mine,
-    wp_other,
-    ws_mine,
-    ws_other,
+    w_mine_ref,
+    w_other_ref,
     bias_q,
     bias_s,
     pick,
     pick_quad,
     quad,
     out_grad,
-    out_local,
+    out_keep,
+    out_send,
     rows,
     rows_small,
     grads,
@@ -233,7 +229,7 @@
     grads[...] = cot_in.astype(BF16)
     normed, _ = normalize(shifted)
     rows_small[...] = normed.astype(BF16)
-    w_mine, w_other = qkv_of(wp_mine[...]), qkv_of(wp_other[...])
+    w_mine, w_other = qkv_of(w_mine_ref, 0), qkv_of(w_other_ref, 0)
     query = project(rows_small, w_mine[:WIDE], w_other[:WIDE], mine, other).astype(BF16)
     key_value = project(rows, w_mine[WIDE:], w_other[WIDE:], mine, other).astype(BF16)
     at = lane((SPOTS, LANES))
@@ -259,14 +255,14 @@
         wide = jnp.concatenate([q.astype(BF16) for q in quarters], axis=0)
         mixed.append(fold(dot(wide, value, TN)).astype(BF16))
     mixed_plain = jnp.concatenate(mixed, axis=0)
-    sums[:, pl.ds(mine, HALF)] = dot(mixed_plain, proj_of(wp_mine[...]))
-    sums[:, pl.ds(other, HALF)] = dot(mixed_plain, proj_of(wp_other[...]))
+    sums[:, pl.ds(mine, HALF)] = dot(mixed_plain, proj_of(w_mine_ref, 0))
+    sums[:, pl.ds(other, HALF)] = dot(mixed_plain, proj_of(w_other_ref, 0))
     block_out = (shifted + sums[...]).astype(BF16).astype(F32)
     normed, rstd = normalize(block_out)
     rows_small[...] = normed.astype(BF16)
-    w_mine, w_other = qkv_of(ws_mine[...]), qkv_of(ws_other[...])
+    w_mine, w_other = qkv_of(w_mine_ref, 192), qkv_of(w_other_ref, 192)
     packed = project(rows_small, w_mine, w_other, mine, other).astype(BF16)
-    d_mixed = project(grads, proj_of(ws_mine[...]), proj_of(ws_other[...]), mine, other).astype(BF16)
+    d_mixed = project(grads, proj_of(w_mine_ref, 192), proj_of(w_other_ref, 192), mine, other).astype(BF16)
     mixed, d_packed = [], []
     for s in range(2):
         part = packed[s * SPOTS : (s + 1) * SPOTS]
@@ -284,24 +280,34 @@
         grads[...].astype(F32), normed, rstd, d_packed, w_mine, w_other, mine, other, sums
     )
     out_grad[...] = dot(quad[...], grad).astype(BF16)
-    local_plain = (dot(mixed_plain, grad, TN) * grad_scale).astype(BF16)
-    local_shift = (dot(mixed_shift, grads[...], TN) * grad_scale).astype(BF16)
-    for side in range(2):
-        for i in range(8):
-            at_rows = slice(i * ROWS, (i + 1) * ROWS)
-            at_lanes = slice(side * HALF, (side + 1) * HALF)
-            out_local[side, i, 0] = local_plain[at_rows, at_lanes]
-            out_local[side, i, 1] = local_shift[at_rows, at_lanes]
+    rows_small[...] = grad
+    for out, start in ((out_keep, mine), (out_send, other)):
+        part = dot(mixed_plain, rows_small[:, pl.ds(start, HALF)], TN) * grad_scale
+        out[:, 0] = part.astype(BF16).reshape(8, ROWS, HALF)
+        part = dot(mixed_shift, grads[:, pl.ds(start, HALF)], TN) * grad_scale
+        out[:, 1] = part.astype(BF16).reshape(8, ROWS, HALF)
+
+
+def sum_copies(parts, out):
+    value = jnp.sum(parts[...].astype(F32), axis=0).astype(BF16)
+    for i in range(out.shape[0]):
+        out[i] = value
+
+
+def finish(parts, out_plain, out_shift):
+    for i, out in enumerate((out_plain, out_shift)):
+        out[:, 0:HALF] = parts[0, i].astype(F32)
+        out[:, HALF:D] = parts[1, i].astype(F32)
 
 
 def plain_back(
-    core_ref, tok, g_own, g_left, g_above, g_diag, wp_mine, wp_other, bias_p, pick, out, rows, grads, sums, mask
+    core_ref, tok, g_own, g_left, g_above, g_diag, w_mine_ref, w_other_ref, bias_p, pick, out, rows, grads, sums, mask
 ):
     mine, other = sides(core_ref)
     mask[...] = head_mask()
     normed, rstd = normalize(tok[...].astype(F32))
     rows[...] = normed.astype(BF16)
-    w_mine, w_other = qkv_of(wp_mine[...]), qkv_of(wp_other[...])
+    w_mine, w_other = qkv_of(w_mine_ref, 0), qkv_of(w_other_ref, 0)
     packed = project(rows, w_mine, w_other, mine, other).astype(BF16)
     gathered = (
         dot(pick[:, 0:32], g_diag[...])
@@ -310,7 +316,7 @@
         + dot(pick[:, 96:128], g_own[...])
     )
     grads[...] = gathered.astype(BF16)
-    d_mixed = project(grads, proj_of(wp_mine[...]), proj_of(wp_other[...]), mine, other).astype(BF16)
+    d_mixed = project(grads, proj_of(w_mine_ref, 0), proj_of(w_other_ref, 0), mine, other).astype(BF16)
     d_packed = []
     for s in range(2):
         part = packed[s * SPOTS : (s + 1) * SPOTS]
@@ -329,8 +335,8 @@
 SMEM = pl.BlockSpec(memory_space=pltpu.SMEM)
 
 
-def params():
-    return pltpu.CompilerParams(vmem_limit_bytes=50 * 1024 * 1024)
+def params(size=32):
+    return pltpu.CompilerParams(vmem_limit_bytes=size * 1024 * 1024)
 
 
 def cost(flops, size):
@@ -356,10 +362,6 @@
     return jnp.sum(blocks.astype(F32), axis=0).astype(BF16)
 
 
-def copies(value, count):
-    return jnp.broadcast_to(value[None], (count,) + value.shape)
-
-
 def from_offset(value, along_tm, along_freq):
     n_tm, n_freq = lax.axis_size("tm"), lax.axis_size("freq")
     pairs = []
@@ -370,15 +372,19 @@
     return lax.ppermute(value, ("tm", "freq"), pairs)
 
 
-def reduce_grads(local):
-    part = total(swap(local, "tm", tm_groups("core")))
-    part = total(swap(part, "freq"))
-    part = total(swap(part.reshape(8, 12, HALF), "tm", tm_groups("z")))
-    part = total(swap(copies(part, 4), "tm", tm_groups("y_hi")))
-    part = swap(copies(part, 8), "tm", tm_groups("z")).reshape(2, ROWS, HALF)
-    part = lax.all_gather(part, "tm", axis_index_groups=tm_groups("core"))
-    part = jnp.concatenate([part[0], part[1]], axis=-1).astype(F32)
-    return (part[0], part[1])
+def other_core(value):
+    return lax.ppermute(value, "tm", [(i, i ^ 1) for i in range(lax.axis_size("tm"))])
+
+
+def summed(parts, count):
+    return pl.pallas_call(
+        sum_copies,
+        out_shape=jax.ShapeDtypeStruct((count,) + parts.shape[1:], BF16),
+        in_specs=[VMEM],
+        out_specs=VMEM,
+        compiler_params=params(),
+        name="sum_copies",
+    )(parts)
 
 
 def shards(
@@ -401,17 +407,16 @@
         prepare,
         out_shape=(jax.ShapeDtypeStruct((8, 384, HALF), BF16), message, message, message),
         in_specs=[SMEM] + [VMEM] * 7,
-        out_specs=[VMEM] * 4,
-        compiler_params=params(),
+        out_specs=[pl.BlockSpec(memory_space=pl.ANY)] + [VMEM] * 3,
+        scratch_shapes=[pltpu.VMEM((384, HALF), BF16), pltpu.SemaphoreType.DMA((8,))],
+        compiler_params=params(60),
         name="prepare",
-    )(core, tok, cot, qkv_plain, qkv_shift, proj_plain, proj_shift, quad)
+    )(core, tok, cot, qkv_plain.T, qkv_shift.T, proj_plain, proj_shift, quad)
 
     right = from_offset(to_left, 1, 0)
     below = from_offset(to_above, 0, 1)
     diag = from_offset(to_diag, 1, 1)
     w_mine = swap(weights, "freq")
-    n_tm = lax.axis_size("tm")
-    w_other = lax.ppermute(w_mine, "tm", [(i, i ^ 1) for i in range(n_tm)])
 
     tables = jnp.concatenate([table_plain, table_shift], axis=0)
     tables = jnp.pad(tables, ((0, 8), (0, 256 - REL)))
@@ -426,20 +431,19 @@
         name="biases",
     )(edge, tables, jnp.asarray(offset_pick(), BF16))
 
-    plain_block = pl.BlockSpec((8, 192, HALF), lambda i: (0, 0, 0))
-    shift_block = pl.BlockSpec((8, 192, HALF), lambda i: (0, 1, 0))
-    quads, local = pl.pallas_call(
+    w_mine, right, below, diag, bias_p, bias_q, bias_s = lax.optimization_barrier(
+        (w_mine, right, below, diag, bias_p, bias_q, bias_s)
+    )
+    w_other = other_core(w_mine)
+    quads, keep, send = pl.pallas_call(
         lambda *refs: main_kernel(grad_scale, *refs),
-        grid=(1,),
         out_shape=(
             jax.ShapeDtypeStruct((128, D), BF16),
-            jax.ShapeDtypeStruct((2, 8, 2, ROWS, HALF), BF16),
+            jax.ShapeDtypeStruct((8, 2, ROWS, HALF), BF16),
+            jax.ShapeDtypeStruct((8, 2, ROWS, HALF), BF16),
         ),
-        in_specs=[SMEM]
-        + [VMEM] * 5
-        + [plain_block, plain_block, shift_block, shift_block]
-        + [VMEM] * 5,
-        out_specs=[VMEM] * 2,
+        in_specs=[SMEM] + [VMEM] * 12,
+        out_specs=[VMEM] * 3,
         scratch_shapes=[
             pltpu.VMEM((512, D), BF16),
             pltpu.VMEM((128, D), BF16),
@@ -452,17 +456,23 @@
         name="main",
     )(
         core, tok, cot, right, below, diag,
-        w_mine, w_other, w_mine, w_other, bias_q, bias_s, pick, pick_quad, quad,
-    )
-
+        w_mine, w_other, bias_q, bias_s, pick, pick_quad, quad,
+    )
+
+    part = (keep.astype(F32) + other_core(send).astype(F32)).astype(BF16)
+    part, quads = lax.optimization_barrier((part, quads))
+    part = swap(part, "freq")
     left = from_offset(quads[32:64], -1, 0)
     above = from_offset(quads[64:96], 0, -1)
     corner = from_offset(quads[96:128], -1, -1)
+    part, left, above, corner = lax.optimization_barrier((part, left, above, corner))
+    part = total(part).reshape(8, 12, HALF)
+    part, left, above, corner = lax.optimization_barrier((part, left, above, corner))
+    part = swap(part, "tm", tm_groups("z"))
     grad_tokens = pl.pallas_call(
         plain_back,
-        grid=(1,),
         out_shape=jax.ShapeDtypeStruct((128, D), BF16),
-        in_specs=[SMEM] + [VMEM] * 5 + [plain_block, plain_block] + [VMEM] * 2,
+        in_specs=[SMEM] + [VMEM] * 9,
         out_specs=VMEM,
         scratch_shapes=[
             pltpu.VMEM((128, D), BF16),
@@ -474,7 +484,18 @@
         cost_estimate=cost(4_000_000_000, 4_000_000),
         name="plain_back",
     )(core, tok, quads[0:32], left, above, corner, w_mine, w_other, bias_p, pick_back)
-    grad_plain, grad_shift = reduce_grads(local)
+    part, grad_tokens = lax.optimization_barrier((part, grad_tokens))
+    part = swap(summed(part, 4), "tm", tm_groups("y_hi"))
+    part = swap(summed(part, 8), "tm", tm_groups("z")).reshape(2, ROWS, HALF)
+    part = lax.all_gather(part, "tm", axis_index_groups=tm_groups("core"))
+    grad_plain, grad_shift = pl.pallas_call(
+        finish,
+        out_shape=(jax.ShapeDtypeStruct((ROWS, D), F32),) * 2,
+        in_specs=[VMEM],
+        out_specs=[VMEM] * 2,
+        compiler_params=params(),
+        name="finish",
+    )(part)
     return (grad_tokens.reshape(tokens.shape), grad_plain, grad_shift)
 
 

time: 162 us -> 152 us (0.938)
  blocking collectives: 71.5 us -> 29.5 us
  waiting for transfers between devices: 3.13 us -> 34 us
  starting transfers between devices: 51 us -> 56.6 us
  local copies, waits for them, and re-layouts: 10.4 us -> 7.91 us
  other arithmetic: 4.63 us -> 2.93 us
    all_to_all x4 -> x2, blocking collectives: 68.1 us -> 22.4 us  [swap(): return lax.all_to_all(value, axis, 0, 0, axis_index_groups=groups)]
    ppermute x6, waiting for transfers between devices: 2.08 us -> 25.8 us  [from_offset(): return lax.ppermute(value, ('tm', 'freq'), pairs)]
    all_to_all x2 -> x3, starting transfers between devices: 10.9 us -> 20.5 us  [swap(): return lax.all_to_all(value, axis, 0, 0, axis_index_groups=groups)]
    ppermute x1 -> x2, waiting for transfers between devices: 0.01 us -> 6.36 us  [other_core(): lax.ppermute(value, 'tm', [(i, i ^ 1) for i in range(lax.axis_size('tm'))])]
    all_gather x1, blocking collectives: 3.33 us -> 7.16 us  [shards(): part = lax.all_gather(part, 'tm', axis_index_groups=tm_groups('core'))]
    ppermute x1 -> x2, starting transfers between devices: 7.36 us -> 4.07 us  [other_core(): lax.ppermute(value, 'tm', [(i, i ^ 1) for i in range(lax.axis_size('tm'))])]
    reduce_sum x4 -> x1, other arithmetic: 3.79 us -> 1.15 us  [total(): return jnp.sum(blocks.astype(F32), axis=0).astype(BF16)]
    pallas_call x1, Pallas kernels: 1.94 us -> 3.74 us  [shards(): pl.pallas_call(prepare, out_shape=(jax.ShapeDtypeStruct((8, 384, HALF), B...]
  transfers between devices with their start and end apart: 9 -> 11, of which waited for: 3 -> 7; matrix products, arithmetic and copies ran while one was open for 1% -> 1% of each run, Pallas kernels for 4% -> 4%
where the time goes in v3:
time: 152 us; the launch traced here: 151 us
  starting transfers between devices  56.6 us (37%)
  waiting for transfers between devices  34 us (22%)
  blocking collectives  29.5 us (19%)
  Pallas kernels  19.4 us (13%)
  local copies, waits for them, and re-layouts  7.91 us (5%)
  other arithmetic  2.93 us (2%)
    ppermute x6, starting transfers between devices, from_offset(): return lax.ppermute(value, ('tm', 'freq'), pairs)  32 us
    ppermute x6, waiting for transfers between devices, from_offset(): return lax.ppermute(value, ('tm', 'freq'), pairs)  25.8 us
    all_to_all x2, blocking collectives, swap(): return lax.all_to_all(value, axis, 0, 0, axis_index_groups=groups)  22.4 us
    all_to_all x3, starting transfers between devices, swap(): return lax.all_to_all(value, axis, 0, 0, axis_index_groups=groups)  20.5 us
    pallas_call x1, Pallas kernels, shards(): pl.pallas_call(lambda *refs: main_kernel(grad_scale, *refs), out_shape=(j...  9.34 us
    unnamed x30, local copies, waits for them, and re-layouts  7.22 us
    all_gather x1, blocking collectives, shards(): part = lax.all_gather(part, 'tm', axis_index_groups=tm_groups('core'))  7.16 us
    ppermute x2, waiting for transfers between devices, other_core(): lax.ppermute(value, 'tm', [(i, i ^ 1) for i in range(lax.axis_size('tm'))])  6.36 us
  transfers between devices with their start and end apart: 11, of which 7 were waited for; matrix products, arithmetic and copies ran while one was open for 1% of the time, Pallas kernels for 4%

profile of v3, /device:TPU:1, one launch (start us, length us, event | category | flops | bytes accessed | tf_op | source)
XLA Modules:
  0.0 151.3 jit_solution(14648119488632595894)
XLA Ops:
  0.6 3.7 %prepare.1 = (bf16[8,384,384]{2,1,0:T(8,128)(2,1)}, bf16[160,768]{1,0:T(8,128)(2,1)}, bf16[160,768]{1,0:T(8,128)(2,1)}, bf16[160,768]{1,0:T(8,128)(2,1)}) custom-call(s32[1]{0:T(128)} %bitcast.core_ref.refs_0_, bf16[128,768]{1,0:T(8,128)(2,1)} %bitcast.10, bf16[128,768]{1,0:T(8,128)(2,1)} %bitcast.8, bf16[144,768]{1,0:T(8,128)(2,1)} %bitcast.13, ...), custom_call_target="tpu_custom_call" | custom-call | tf_op jit(solution)/shard_map/prepare/pallas_call | solution.py:406
  4.4 6.0 %all-to-all-start = ((bf16[8,384,384]{2,1,0:T(8,128)(2,1)}), bf16[8,384,384]{2,1,0:T(8,128)(2,1)S(1)}, u32[]{:S(2)}, u32[]{:S(2)}) async-start(bf16[8,384,384]{2,1,0:T(8,128)(2,1)} %get-tuple-element.34), calls=%async_computation | async-start | bytes 4718592 | tf_op jit(solution)/shard_map/all_to_all | solution.py:358
  10.5 6.5 %collective-permute-start = (bf16[160,768]{1,0:T(8,128)(2,1)}, bf16[160,768]{1,0:T(8,128)(2,1)S(1)}, u32[]{:S(2)}, u32[]{:S(2)}) collective-permute-start(bf16[160,768]{1,0:T(8,128)(2,1)} %get-tuple-element.35), channel_id=1, source_target_pairs={{8,0},{9,1},{10,2},{11,3},{12,4},{13,5},{14,6},{15,7},{16,8},{17,9... | collective-permute-start | bytes 737288 | tf_op jit(solution)/shard_map/ppermute | solution.py:372
  17.0 5.7 %collective-permute-start.1 = (bf16[160,768]{1,0:T(8,128)(2,1)}, bf16[160,768]{1,0:T(8,128)(2,1)}, u32[]{:S(2)}, u32[]{:S(2)}) collective-permute-start(bf16[160,768]{1,0:T(8,128)(2,1)} %get-tuple-element.36), channel_id=1, source_target_pairs={{1,0},{2,1},{3,2},{4,3},{5,4},{6,5},{7,6},{0,7},{9,8},{10,9},{11,1... | collective-permute-start | bytes 737288 | tf_op jit(solution)/shard_map/ppermute | solution.py:372
  22.7 9.4 %collective-permute-start.2 = (bf16[160,768]{1,0:T(8,128)(2,1)}, bf16[160,768]{1,0:T(8,128)(2,1)}, u32[]{:S(2)}, u32[]{:S(2)}) collective-permute-start(bf16[160,768]{1,0:T(8,128)(2,1)} %get-tuple-element.37), channel_id=1, source_target_pairs={{9,0},{10,1},{11,2},{12,3},{13,4},{14,5},{15,6},{8,7},{17,8},{18,9... | collective-permute-start | bytes 737288 | tf_op jit(solution)/shard_map/ppermute | solution.py:372
  33.0 1.4 biases.1
  36.4 6.1 %collective-permute-done.1.refs_4_ = bf16[160,768]{1,0:T(8,128)(2,1)} collective-permute-done((bf16[160,768]{1,0:T(8,128)(2,1)}, bf16[160,768]{1,0:T(8,128)(2,1)}, u32[]{:S(2)}, u32[]{:S(2)}) %collective-permute-start.1) | collective-permute-done | bytes 245792 | tf_op jit(solution)/shard_map/ppermute | solution.py:372
  42.5 17.4 %collective-permute-done.2.refs_5_ = bf16[160,768]{1,0:T(8,128)(2,1)} collective-permute-done((bf16[160,768]{1,0:T(8,128)(2,1)}, bf16[160,768]{1,0:T(8,128)(2,1)}, u32[]{:S(2)}, u32[]{:S(2)}) %collective-permute-start.2) | collective-permute-done | bytes 245792 | tf_op jit(solution)/shard_map/ppermute | solution.py:372
  59.9 1.9 %collective-permute-start.3 = (bf16[8,384,384]{2,1,0:T(8,128)(2,1)S(1)}, bf16[8,384,384]{2,1,0:T(8,128)(2,1)S(1)}, u32[]{:S(2)}, u32[]{:S(2)}) collective-permute-start(bf16[8,384,384]{2,1,0:T(8,128)(2,1)S(1)} %all-to-all-done.refs_6_.w_mine_ref), channel_id=1, source_target_pairs={{0,8},{8,0},{16,24},{24,16},{32,40},{40,32},{48,56},{56,48},{64,72... | collective-permute-start | bytes 7077896 | tf_op jit(solution)/shard_map/ppermute | solution.py:376
  61.8 4.5 %collective-permute-done.3.refs_7_.w_other_ref = bf16[8,384,384]{2,1,0:T(8,128)(2,1)S(1)} collective-permute-done((bf16[8,384,384]{2,1,0:T(8,128)(2,1)S(1)}, bf16[8,384,384]{2,1,0:T(8,128)(2,1)S(1)}, u32[]{:S(2)}, u32[]{:S(2)}) %collective-permute-start.3) | collective-permute-done | bytes 2359328 | tf_op jit(solution)/shard_map/ppermute | solution.py:376
  66.3 0.9 copy-done.9
  67.2 0.9 copy-done.11
  68.2 0.9 copy-done.12
  69.1 0.8 copy-done.14
  69.8 9.3 %main.1 = (bf16[128,768]{1,0:T(8,128)(2,1)S(1)}, bf16[8,2,48,384]{3,2,1,0:T(8,128)(2,1)S(1)}, bf16[8,2,48,384]{3,2,1,0:T(8,128)(2,1)S(1)}) custom-call(s32[1]{0:T(128)} %bitcast.core_ref.refs_0_, bf16[128,768]{1,0:T(8,128)(2,1)S(1)} %bitcast.11, bf16[128,768]{1,0:T(8,128)(2,1)S(1)} %bitcast.9, bf16[160,768]{1,0:T(8,128)(2,1)S(1)} %collective-permute-done.refs_3_, ...), custom_call_target="tpu_custom_call" | custom-call | flops 4000000000 | bytes 6000000 | tf_op jit(solution)/shard_map/main/pallas_call | solution.py:438
  79.2 2.2 %collective-permute-start.4 = (bf16[8,2,48,384]{3,2,1,0:T(8,128)(2,1)S(1)}, bf16[8,2,48,384]{3,2,1,0:T(8,128)(2,1)S(1)}, u32[]{:S(2)}, u32[]{:S(2)}) collective-permute-start(bf16[8,2,48,384]{3,2,1,0:T(8,128)(2,1)S(1)} %get-tuple-element.48), channel_id=1, source_target_pairs={{0,8},{8,0},{16,24},{24,16},{32,40},{40,32},{48,56},{56,48},{64,72... | collective-permute-start | bytes 1769480 | tf_op jit(solution)/shard_map/ppermute | solution.py:376
  81.4 1.9 %collective-permute-done.4 = bf16[8,2,48,384]{3,2,1,0:T(8,128)(2,1)S(1)} collective-permute-done((bf16[8,2,48,384]{3,2,1,0:T(8,128)(2,1)S(1)}, bf16[8,2,48,384]{3,2,1,0:T(8,128)(2,1)S(1)}, u32[]{:S(2)}, u32[]{:S(2)}) %collective-permute-start.4) | collective-permute-done | bytes 589856 | tf_op jit(solution)/shard_map/ppermute | solution.py:376
  83.2 1.0 add_convert_fusion
  84.2 4.2 %all-to-all-start.1 = ((bf16[8,2,48,384]{3,2,1,0:T(8,128)(2,1)}), bf16[8,2,48,384]{3,2,1,0:T(8,128)(2,1)}, u32[]{:S(2)}, u32[]{:S(2)}) async-start(bf16[8,2,48,384]{3,2,1,0:T(8,128)(2,1)} %add_convert_fusion), calls=%async_computation.1 | async-start | bytes 1179648 | tf_op jit(solution)/shard_map/all_to_all | solution.py:358
  88.4 4.9 %collective-permute-start.7 = (bf16[32,768]{1,0:T(8,128)(2,1)S(1)}, bf16[32,768]{1,0:T(8,128)(2,1)S(1)}, u32[]{:S(2)}, u32[]{:S(2)}) collective-permute-start(bf16[32,768]{1,0:T(8,128)(2,1)S(1)} %get-tuple-element.66), channel_id=1, source_target_pairs={{511,0},{504,1},{505,2},{506,3},{507,4},{508,5},{509,6},{510,7},{7... | collective-permute-start | bytes 147464 | tf_op jit(solution)/shard_map/ppermute | solution.py:372
  93.3 2.2 %collective-permute-start.6 = (bf16[32,768]{1,0:T(8,128)(2,1)S(1)}, bf16[32,768]{1,0:T(8,128)(2,1)S(1)}, u32[]{:S(2)}, u32[]{:S(2)}) collective-permute-start(bf16[32,768]{1,0:T(8,128)(2,1)S(1)} %get-tuple-element.67), channel_id=1, source_target_pairs={{7,0},{0,1},{1,2},{2,3},{3,4},{4,5},{5,6},{6,7},{15,8},{8,9},{9,10... | collective-permute-start | bytes 147464 | tf_op jit(solution)/shard_map/ppermute | solution.py:372
  95.5 3.3 %collective-permute-start.5 = (bf16[32,768]{1,0:T(8,128)(2,1)S(1)}, bf16[32,768]{1,0:T(8,128)(2,1)S(1)}, u32[]{:S(2)}, u32[]{:S(2)}) collective-permute-start(bf16[32,768]{1,0:T(8,128)(2,1)S(1)} %get-tuple-element.68), channel_id=1, source_target_pairs={{504,0},{505,1},{506,2},{507,3},{508,4},{509,5},{510,6},{511,7},{0... | collective-permute-start | bytes 147464 | tf_op jit(solution)/shard_map/ppermute | solution.py:372
  98.7 1.3 collective-permute-done.7.g_diag
  100.0 1.1 collective-permute-done.6.g_above
  101.1 1.1 reduce_sum.12
  102.9 10.4 %all-to-all-start.2 = ((bf16[8,12,384]{2,1,0:T(8,128)(2,1)}), bf16[8,12,384]{2,1,0:T(8,128)(2,1)S(1)}, u32[]{:S(2)}, u32[]{:S(2)}) async-start(bf16[8,12,384]{2,1,0:T(8,128)(2,1)} %reshape.24), calls=%async_computation.2 | async-start | bytes 196608 | tf_op jit(solution)/shard_map/all_to_all | solution.py:358
  113.3 1.7 %copy-done.5 = bf16[8,384,384]{2,1,0:T(8,128)(2,1)S(1)} copy-done((bf16[8,384,384]{2,1,0:T(8,128)(2,1)S(1)}, bf16[8,384,384]{2,1,0:T(8,128)(2,1)}, u32[]{:S(2)}) %copy-start.5) | copy-done | bytes 2359320
  115.0 4.2 %plain_back.1 = bf16[128,768]{1,0:T(8,128)(2,1)} custom-call(s32[1]{0:T(128)} %bitcast.core_ref.refs_0_, bf16[128,768]{1,0:T(8,128)(2,1)S(1)} %bitcast.12, bf16[32,768]{1,0:T(8,128)(2,1)S(1)} %get-tuple-element.65.g_own, bf16[32,768]{1,0:T(8,128)(2,1)S(1)} %collective-permute-done.5.g_left, bf16[32,768]{1,0:T(8,128)(2,1)S(1)} %collective-permute-done.6.g_above, ...), custom_call_target="tpu_custom_call" | custom-call | flops 4000000000 | bytes 4000000 | tf_op jit(solution)/shard_map/plain_back/pallas_call | solution.py:472
  119.1 1.8 %all-to-all-done.2.parts = bf16[8,12,384]{2,1,0:T(8,128)(2,1)S(1)} async-done(((bf16[8,12,384]{2,1,0:T(8,128)(2,1)}), bf16[8,12,384]{2,1,0:T(8,128)(2,1)S(1)}, u32[]{:S(2)}, u32[]{:S(2)}) %all-to-all-start.2) | async-done | bytes 73760 | tf_op jit(solution)/shard_map/all_to_all | solution.py:358
  121.0 10.1 %all_to_all.25.parts = bf16[4,12,384]{2,1,0:T(8,128)(2,1)S(1)} all-to-all(bf16[4,12,384]{2,1,0:T(8,128)(2,1)S(1)} %sum_copies.2), channel_id=1, replica_groups={{0,16,32,48},{8,24,40,56},{64,80,96,112},{72,88,104,120},{128,144,160,1..., dimensions={0} | all-to-all | bytes 73728 | tf_op jit(solution)/shard_map/all_to_all | solution.py:358
  131.1 12.3 %all_to_all.26 = bf16[8,12,384]{2,1,0:T(8,128)(2,1)S(1)} all-to-all(bf16[8,12,384]{2,1,0:T(8,128)(2,1)S(1)} %sum_copies.3), channel_id=1, replica_groups={{0,64,128,192,256,320,384,448},{8,72,136,200,264,328,392,456},{16,80,14..., dimensions={0} | all-to-all | bytes 147456 | tf_op jit(solution)/shard_map/all_to_all | solution.py:358
  143.4 7.2 %all_gather.3.parts = bf16[2,2,48,384]{3,2,1,0:T(8,128)(2,1)S(1)} all-gather(bf16[1,2,48,384]{3,2,1,0:T(8,128)(2,1)S(1)} %all_gather_reshape.3), channel_id=1, replica_groups={{0,8},{16,24},{32,40},{48,56},{64,72},{80,88},{96,104},{112,120},{128,1..., dimensions={0}, use_global_device_ids=true | all-gather | bytes 221184 | tf_op jit(solution)/shard_map/all_gather | solution.py:490
  (37 shorter events, 4.3 us)
Async XLA Ops:
  4.4 28.6 %copy-start = (bf16[256,1024]{1,0:T(8,128)(2,1)S(1)}, bf16[256,1024]{1,0:T(8,128)(2,1)}, u32[]{:S(2)}) copy-start(bf16[256,1024]{1,0:T(8,128)(2,1)} %constant.46.clone.pick) | copy-start | bytes 1572868
  4.4 61.9 %copy-start.1 = (bf16[2,8,8,768]{3,2,1,0:T(8,128)(2,1)S(1)}, bf16[2,8,8,768]{3,2,1,0:T(8,128)(2,1)}, u32[]{:S(2)}) copy-start(bf16[2,8,8,768]{3,2,1,0:T(8,128)(2,1)} %param.14) | copy-start | bytes 589828
  4.4 61.9 %copy-start.2 = (bf16[2,8,8,768]{3,2,1,0:T(8,128)(2,1)S(1)}, bf16[2,8,8,768]{3,2,1,0:T(8,128)(2,1)}, u32[]{:S(2)}) copy-start(bf16[2,8,8,768]{3,2,1,0:T(8,128)(2,1)} %param.13) | copy-start | bytes 589828
  4.4 61.9 %copy-start.3 = (bf16[128,128]{1,0:T(8,128)(2,1)S(1)}, bf16[128,128]{1,0:T(8,128)(2,1)}, u32[]{:S(2)}) copy-start(bf16[128,128]{1,0:T(8,128)(2,1)} %constant.43.clone.quad.refs_12_) | copy-start | bytes 98308
  4.4 55.4 %all-to-all-start = ((bf16[8,384,384]{2,1,0:T(8,128)(2,1)}), bf16[8,384,384]{2,1,0:T(8,128)(2,1)S(1)}, u32[]{:S(2)}, u32[]{:S(2)}) async-start(bf16[8,384,384]{2,1,0:T(8,128)(2,1)} %get-tuple-element.34), calls=%async_computation | async-start | bytes 4718592 | tf_op jit(solution)/shard_map/all_to_all | solution.py:358
  10.5 26.0 %collective-permute-start = (bf16[160,768]{1,0:T(8,128)(2,1)}, bf16[160,768]{1,0:T(8,128)(2,1)S(1)}, u32[]{:S(2)}, u32[]{:S(2)}) collective-permute-start(bf16[160,768]{1,0:T(8,128)(2,1)} %get-tuple-element.35), channel_id=1, source_target_pairs={{8,0},{9,1},{10,2},{11,3},{12,4},{13,5},{14,6},{15,7},{16,8},{17,9... | collective-permute-start | bytes 737288 | tf_op jit(solution)/shard_map/ppermute | solution.py:372
  17.0 25.5 %collective-permute-start.1 = (bf16[160,768]{1,0:T(8,128)(2,1)}, bf16[160,768]{1,0:T(8,128)(2,1)}, u32[]{:S(2)}, u32[]{:S(2)}) collective-permute-start(bf16[160,768]{1,0:T(8,128)(2,1)} %get-tuple-element.36), channel_id=1, source_target_pairs={{1,0},{2,1},{3,2},{4,3},{5,4},{6,5},{7,6},{0,7},{9,8},{10,9},{11,1... | collective-permute-start | bytes 737288 | tf_op jit(solution)/shard_map/ppermute | solution.py:372
  22.7 37.2 %collective-permute-start.2 = (bf16[160,768]{1,0:T(8,128)(2,1)}, bf16[160,768]{1,0:T(8,128)(2,1)}, u32[]{:S(2)}, u32[]{:S(2)}) collective-permute-start(bf16[160,768]{1,0:T(8,128)(2,1)} %get-tuple-element.37), channel_id=1, source_target_pairs={{9,0},{10,1},{11,2},{12,3},{13,4},{14,5},{15,6},{8,7},{17,8},{18,9... | collective-permute-start | bytes 737288 | tf_op jit(solution)/shard_map/ppermute | solution.py:372
  34.4 0.7 copy-start.6
  35.1 0.7 copy-start.8
  35.8 0.7 copy-start.10
  59.9 6.4 %collective-permute-start.3 = (bf16[8,384,384]{2,1,0:T(8,128)(2,1)S(1)}, bf16[8,384,384]{2,1,0:T(8,128)(2,1)S(1)}, u32[]{:S(2)}, u32[]{:S(2)}) collective-permute-start(bf16[8,384,384]{2,1,0:T(8,128)(2,1)S(1)} %all-to-all-done.refs_6_.w_mine_ref), channel_id=1, source_target_pairs={{0,8},{8,0},{16,24},{24,16},{32,40},{40,32},{48,56},{56,48},{64,72... | collective-permute-start | bytes 7077896 | tf_op jit(solution)/shard_map/ppermute | solution.py:376
  66.3 0.9 copy-start.9
  67.2 0.9 copy-start.11
  68.1 0.9 copy-start.12
  69.1 0.8 copy-start.14
  69.8 9.3 %copy-start.4 = (bf16[8,384,384]{2,1,0:T(8,128)(2,1)}, bf16[8,384,384]{2,1,0:T(8,128)(2,1)S(1)}, u32[]{:S(2)}) copy-start(bf16[8,384,384]{2,1,0:T(8,128)(2,1)S(1)} %collective-permute-done.3.refs_7_.w_other_ref) | copy-start | bytes 7077892
  79.2 34.1 %copy-start.7 = (f32[64,768]{1,0:T(8,128)S(1)}, f32[64,768]{1,0:T(8,128)}, u32[]{:S(2)}) copy-start(f32[64,768]{1,0:T(8,128)} %copy-done.6) | copy-start | bytes 589828
  79.2 34.1 %copy-start.13 = (bf16[128,128]{1,0:T(8,128)(2,1)S(1)}, bf16[128,128]{1,0:T(8,128)(2,1)}, u32[]{:S(2)}) copy-start(bf16[128,128]{1,0:T(8,128)(2,1)} %constant.45.clone.pick) | copy-start | bytes 98308
  79.2 4.0 %collective-permute-start.4 = (bf16[8,2,48,384]{3,2,1,0:T(8,128)(2,1)S(1)}, bf16[8,2,48,384]{3,2,1,0:T(8,128)(2,1)S(1)}, u32[]{:S(2)}, u32[]{:S(2)}) collective-permute-start(bf16[8,2,48,384]{3,2,1,0:T(8,128)(2,1)S(1)} %get-tuple-element.48), channel_id=1, source_target_pairs={{0,8},{8,0},{16,24},{24,16},{32,40},{40,32},{48,56},{56,48},{64,72... | collective-permute-start | bytes 1769480 | tf_op jit(solution)/shard_map/ppermute | solution.py:376
  84.2 16.9 %all-to-all-start.1 = ((bf16[8,2,48,384]{3,2,1,0:T(8,128)(2,1)}), bf16[8,2,48,384]{3,2,1,0:T(8,128)(2,1)}, u32[]{:S(2)}, u32[]{:S(2)}) async-start(bf16[8,2,48,384]{3,2,1,0:T(8,128)(2,1)} %add_convert_fusion), calls=%async_computation.1 | async-start | bytes 1179648 | tf_op jit(solution)/shard_map/all_to_all | solution.py:358
  88.4 11.6 %collective-permute-start.7 = (bf16[32,768]{1,0:T(8,128)(2,1)S(1)}, bf16[32,768]{1,0:T(8,128)(2,1)S(1)}, u32[]{:S(2)}, u32[]{:S(2)}) collective-permute-start(bf16[32,768]{1,0:T(8,128)(2,1)S(1)} %get-tuple-element.66), channel_id=1, source_target_pairs={{511,0},{504,1},{505,2},{506,3},{507,4},{508,5},{509,6},{510,7},{7... | collective-permute-start | bytes 147464 | tf_op jit(solution)/shard_map/ppermute | solution.py:372
  93.3 7.8 %collective-permute-start.6 = (bf16[32,768]{1,0:T(8,128)(2,1)S(1)}, bf16[32,768]{1,0:T(8,128)(2,1)S(1)}, u32[]{:S(2)}, u32[]{:S(2)}) collective-permute-start(bf16[32,768]{1,0:T(8,128)(2,1)S(1)} %get-tuple-element.67), channel_id=1, source_target_pairs={{7,0},{0,1},{1,2},{2,3},{3,4},{4,5},{5,6},{6,7},{15,8},{8,9},{9,10... | collective-permute-start | bytes 147464 | tf_op jit(solution)/shard_map/ppermute | solution.py:372
  95.5 5.6 %collective-permute-start.5 = (bf16[32,768]{1,0:T(8,128)(2,1)S(1)}, bf16[32,768]{1,0:T(8,128)(2,1)S(1)}, u32[]{:S(2)}, u32[]{:S(2)}) collective-permute-start(bf16[32,768]{1,0:T(8,128)(2,1)S(1)} %get-tuple-element.68), channel_id=1, source_target_pairs={{504,0},{505,1},{506,2},{507,3},{508,4},{509,5},{510,6},{511,7},{0... | collective-permute-start | bytes 147464 | tf_op jit(solution)/shard_map/ppermute | solution.py:372
  102.9 18.0 %all-to-all-start.2 = ((bf16[8,12,384]{2,1,0:T(8,128)(2,1)}), bf16[8,12,384]{2,1,0:T(8,128)(2,1)S(1)}, u32[]{:S(2)}, u32[]{:S(2)}) async-start(bf16[8,12,384]{2,1,0:T(8,128)(2,1)} %reshape.24), calls=%async_computation.2 | async-start | bytes 196608 | tf_op jit(solution)/shard_map/all_to_all | solution.py:358
  113.3 1.7 %copy-start.5 = (bf16[8,384,384]{2,1,0:T(8,128)(2,1)S(1)}, bf16[8,384,384]{2,1,0:T(8,128)(2,1)}, u32[]{:S(2)}) copy-start(bf16[8,384,384]{2,1,0:T(8,128)(2,1)} %copy-done.4) | copy-start | bytes 7077892

commit v4 on v3

--- a/solution.py
+++ b/solution.py
@@ -2,7 +2,6 @@
 
 import jax
 import jax.numpy as jnp
-import numpy as np
 from jax import lax
 from jax.experimental import pallas as pl
 from jax.experimental.pallas import tpu as pltpu
@@ -32,36 +31,11 @@
 BF16 = jnp.bfloat16
 
 
-def shifted_pick():
-    pick = np.zeros((2 * SPOTS, 4 * 2 * SPOTS), np.float32)
-    for s in range(2):
-        for a in range(WIN):
-            for b in range(WIN):
-                window = 2 * (a >= 4) + (b >= 4)
-                source = window * 128 + s * SPOTS + (a ^ 4) * WIN + (b ^ 4)
-                pick[s * SPOTS + a * WIN + b, source] = 1.0
-    return pick
-
-
-def quadrant_pick():
-    pick = np.zeros((2 * SPOTS, 2 * SPOTS), np.float32)
-    for quad in range(4):
-        for s in range(2):
-            for a in range(4):
-                for b in range(4):
-                    row = quad * 32 + s * 16 + a * 4 + b
-                    spot = (a + 4 * (quad // 2)) * WIN + b + 4 * (quad % 2)
-                    pick[row, s * SPOTS + spot] = 1.0
-    return pick
-
-
 def offset_pick():
-    pick = np.zeros((256, WIN * 128), np.float32)
-    for d in range(WIN):
-        for row in range(15):
-            for b in range(WIN):
-                pick[row * 15 + b - d + 7, d * 128 + row * WIN + b] = 1.0
-    return pick
+    column = lane((256, WIN * 128))
+    entry = ((column >> 3) & 15) * 15 + (column & 7) - (column >> 7) + 7
+    row = lax.broadcasted_iota(jnp.int32, (256, WIN * 128), 0)
+    return jnp.where(row == entry, 1.0, 0.0).astype(BF16)
 
 
 def dot(left, right, dims=NN):
@@ -76,6 +50,15 @@
 
 def lane(shape):
     return lax.broadcasted_iota(jnp.int32, shape, len(shape) - 1)
+
+
+def quadrant_pick(transposed=False):
+    row = lax.broadcasted_iota(jnp.int32, (128, 128), 1 if transposed else 0)
+    column = lax.broadcasted_iota(jnp.int32, (128, 128), 0 if transposed else 1)
+    high = (row & 64) >> 1
+    low = (row & 32) >> 3
+    spot = high + low + ((row & 12) << 1) + (row & 3) + ((row & 16) << 2)
+    return jnp.where(spot == column, 1.0, 0.0).astype(BF16)
 
 
 def head_mask():
@@ -111,7 +94,7 @@
     return (d_query, d_key, d_value)
 
 
-def prepare(core_ref, tok, cot, qkv_p, qkv_s, proj_p, proj_s, quad, out_w, out_r, out_b, out_d, block, sems):
+def prepare(core_ref, cot, qkv_p, qkv_s, proj_p, proj_s, out_w, out_o, out_r, out_b, out_d, block, sems):
     start = pl.multiple_of(core_ref[0] * HALF, 128)
     block[0:144] = qkv_p[:, pl.ds(start, HALF)]
     block[144:192] = proj_p[:, pl.ds(start, HALF)]
@@ -120,21 +103,23 @@
     sends = [pltpu.make_async_copy(block, out_w.at[i], sems.at[i]) for i in range(8)]
     for send in sends:
         send.start()
-    quads = dot(quad[...], cot[...]).astype(BF16)
-    for out, first in ((out_r, 64), (out_b, 32), (out_d, 0)):
-        out[0:128] = tok[...]
-        out[128:160] = quads[first : first + 32]
+    quads = dot(quadrant_pick(), cot[...]).astype(BF16)
+    for out, first in ((out_o, 96), (out_r, 64), (out_b, 32), (out_d, 0)):
+        out[...] = quads[first : first + 32]
     for send in sends:
         send.wait()
 
 
-def biases(edge_ref, tables, pick, out_p, out_q, out_s, wide):
+def biases(edge_ref, table_p, table_s, out_p, out_s, tables, wide):
+    tables[...] = jnp.zeros_like(tables)
+    tables[0:HEADS, 0:REL] = table_p[...]
+    tables[HEADS : 2 * HEADS, 0:REL] = table_s[...]
     values = tables[...]
     high = values.astype(BF16)
     rest = values - high.astype(F32)
     middle = rest.astype(BF16)
     low = (rest - middle.astype(F32)).astype(BF16)
-    ones = pick[...]
+    ones = offset_pick()
     spread = (dot(high, ones) + dot(middle, ones)) + dot(low, ones)
     for row in range(2 * HEADS):
         for d in range(WIN):
@@ -149,10 +134,6 @@
                 second = pltpu.roll(wide[even + WIN : even + 2 * WIN], (SPOTS - move) % 128, 1)
                 out[c * WIN : (c + 1) * WIN, pair * 128 : (pair + 1) * 128] = jnp.where(left, first, second)
     at = lane((SPOTS, LANES))
-    plain = out_p[...]
-    turned = jnp.where((at & 4) != 0, pltpu.roll(plain, 4, 1), pltpu.roll(plain, LANES - 4, 1))
-    turned = jnp.where((at & 32) != 0, pltpu.roll(turned, 32, 1), pltpu.roll(turned, LANES - 32, 1))
-    out_q[...] = turned
     key_at = lax.broadcasted_iota(jnp.int32, (SPOTS, LANES), 0)
     cross = at ^ key_at
     barred = (cross & 32) * edge_ref[0] + (cross & 4) * edge_ref[1]
@@ -190,25 +171,55 @@
     return (grad + d_input).astype(BF16)
 
 
+def plain_forward(
+    core_ref, tok, w_mine_ref, w_other_ref, bias_p, out_o, out_r, out_b, out_d, rows, sums, mask
+):
+    mine, other = sides(core_ref)
+    mask[...] = head_mask()
+    inputs = tok[...].astype(F32)
+    rows[...] = normalize(inputs)[0].astype(BF16)
+    w_mine, w_other = qkv_of(w_mine_ref, 0), qkv_of(w_other_ref, 0)
+    packed = project(rows, w_mine, w_other, mine, other).astype(BF16)
+    mixed = []
+    for s in range(2):
+        part = packed[s * SPOTS : (s + 1) * SPOTS]
+        query, key, value = part[:, :WIDE], part[:, WIDE : 2 * WIDE], part[:, 2 * WIDE :]
+        probs = softmax_down(dot(key, expand(query, mask), NT) * SCALE + bias_p[...])
+        mixed.append(fold(dot(probs.astype(BF16), value, TN)).astype(BF16))
+    mixed = jnp.concatenate(mixed, axis=0)
+    sums[:, pl.ds(mine, HALF)] = dot(mixed, proj_of(w_mine_ref, 0))
+    sums[:, pl.ds(other, HALF)] = dot(mixed, proj_of(w_other_ref, 0))
+    block_out = (inputs + sums[...]).astype(BF16)
+    pick = quadrant_pick()
+    outs = (out_d, out_b, out_r, out_o)
+    for whole, first in ((block_out, 0), (mixed, D)):
+        quads = dot(pick, whole).astype(BF16)
+        for i, out in enumerate(outs):
+            out[:, first : first + whole.shape[1]] = quads[i * 32 : (i + 1) * 32]
+
+
 def main_kernel(
     grad_scale,
     core_ref,
-    tok,
-    cot,
+    cot_own,
+    cot_right,
+    cot_below,
+    cot_diag,
+    own,
     right,
     below,
     diag,
     w_mine_ref,
     w_other_ref,
-    bias_q,
     bias_s,
-    pick,
-    pick_quad,
-    quad,
-    out_grad,
+    out_own,
+    out_right,
+    out_below,
+    out_diag,
     out_keep,
     out_send,
-    rows,
+    staged,
+    staged_cot,
     rows_small,
     grads,
     sums,
@@ -216,48 +227,15 @@
 ):
     mine, other = sides(core_ref)
     mask[...] = head_mask()
-    sources = (tok, right, below, diag)
-    for w, source in enumerate(sources):
-        for s in range(2):
-            normed, _ = normalize(source[s * SPOTS : (s + 1) * SPOTS].astype(F32))
-            rows[s * 256 + w * SPOTS : s * 256 + (w + 1) * SPOTS] = normed.astype(BF16)
-    shifted = dot(pick[:, 0:128], tok[...])
-    cot_in = dot(pick[:, 0:128], cot[...])
-    for w in range(1, 4):
-        shifted = shifted + dot(pick[:, w * 128 : (w + 1) * 128], sources[w][0:128])
-        cot_in = cot_in + dot(pick_quad[:, (w - 1) * 32 : w * 32], sources[w][128:160])
-    grads[...] = cot_in.astype(BF16)
-    normed, _ = normalize(shifted)
-    rows_small[...] = normed.astype(BF16)
-    w_mine, w_other = qkv_of(w_mine_ref, 0), qkv_of(w_other_ref, 0)
-    query = project(rows_small, w_mine[:WIDE], w_other[:WIDE], mine, other).astype(BF16)
-    key_value = project(rows, w_mine[WIDE:], w_other[WIDE:], mine, other).astype(BF16)
-    at = lane((SPOTS, LANES))
-    lower = (at & 32) != 0
-    later = (at & 4) != 0
-    mixed = []
-    for s in range(2):
-        key = key_value[s * 256 : (s + 1) * 256, :WIDE]
-        value = key_value[s * 256 : (s + 1) * 256, WIDE:]
-        full = dot(key, expand(query[s * SPOTS : (s + 1) * SPOTS], mask), NT)
-        scores = jnp.where(
-            lower,
-            jnp.where(later, full[192:256], full[128:192]),
-            jnp.where(later, full[64:128], full[0:64]),
-        )
-        probs = softmax_down(scores * SCALE + bias_q[...])
-        quarters = [
-            jnp.where(lower | later, 0.0, probs),
-            jnp.where(lower, 0.0, jnp.where(later, probs, 0.0)),
-            jnp.where(lower, jnp.where(later, 0.0, probs), 0.0),
-            jnp.where(lower & later, probs, 0.0),
-        ]
-        wide = jnp.concatenate([q.astype(BF16) for q in quarters], axis=0)
-        mixed.append(fold(dot(wide, value, TN)).astype(BF16))
-    mixed_plain = jnp.concatenate(mixed, axis=0)
-    sums[:, pl.ds(mine, HALF)] = dot(mixed_plain, proj_of(w_mine_ref, 0))
-    sums[:, pl.ds(other, HALF)] = dot(mixed_plain, proj_of(w_other_ref, 0))
-    block_out = (shifted + sums[...]).astype(BF16).astype(F32)
+    for i, (part, cot) in enumerate(
+        ((own, cot_own), (right, cot_right), (below, cot_below), (diag, cot_diag))
+    ):
+        staged[i * 32 : (i + 1) * 32] = part[...]
+        staged_cot[i * 32 : (i + 1) * 32] = cot[...]
+    pick = quadrant_pick(True)
+    grads[...] = dot(pick, staged_cot[...]).astype(BF16)
+    block_out = dot(pick, staged[:, 0:D])
+    mixed_plain = dot(pick, staged[:, D : D + WIDE]).astype(BF16)
     normed, rstd = normalize(block_out)
     rows_small[...] = normed.astype(BF16)
     w_mine, w_other = qkv_of(w_mine_ref, 192), qkv_of(w_other_ref, 192)
@@ -279,7 +257,9 @@
     grad = input_grad(
         grads[...].astype(F32), normed, rstd, d_packed, w_mine, w_other, mine, other, sums
     )
-    out_grad[...] = dot(quad[...], grad).astype(BF16)
+    quads = dot(quadrant_pick(), grad).astype(BF16)
+    for i, out in enumerate((out_own, out_right, out_below, out_diag)):
+        out[...] = quads[i * 32 : (i + 1) * 32]
     rows_small[...] = grad
     for out, start in ((out_keep, mine), (out_send, other)):
         part = dot(mixed_plain, rows_small[:, pl.ds(start, HALF)], TN) * grad_scale
@@ -301,7 +281,7 @@
 
 
 def plain_back(
-    core_ref, tok, g_own, g_left, g_above, g_diag, w_mine_ref, w_other_ref, bias_p, pick, out, rows, grads, sums, mask
+    core_ref, tok, g_own, g_left, g_above, g_diag, w_mine_ref, w_other_ref, bias_p, out, staged, rows, grads, sums, mask
 ):
     mine, other = sides(core_ref)
     mask[...] = head_mask()
@@ -309,12 +289,9 @@
     rows[...] = normed.astype(BF16)
     w_mine, w_other = qkv_of(w_mine_ref, 0), qkv_of(w_other_ref, 0)
     packed = project(rows, w_mine, w_other, mine, other).astype(BF16)
-    gathered = (
-        dot(pick[:, 0:32], g_diag[...])
-        + dot(pick[:, 32:64], g_above[...])
-        + dot(pick[:, 64:96], g_left[...])
-        + dot(pick[:, 96:128], g_own[...])
-    )
+    for i, part in enumerate((g_diag, g_above, g_left, g_own)):
+        staged[i * 32 : (i + 1) * 32] = part[...]
+    gathered = dot(quadrant_pick(True), staged[...])
     grads[...] = gathered.astype(BF16)
     d_mixed = project(grads, proj_of(w_mine_ref, 0), proj_of(w_other_ref, 0), mine, other).astype(BF16)
     d_packed = []
@@ -395,57 +372,67 @@
     last_time = lax.axis_index("tm") == lax.axis_size("tm") - 1
     edge = jnp.stack([last_freq, last_time]).astype(jnp.int32)
     grad_scale = 1.0 / math.sqrt(128 * lax.axis_size("tm") * lax.axis_size("freq"))
-    pick = jnp.asarray(shifted_pick(), BF16)
-    quad = jnp.asarray(quadrant_pick(), BF16)
-    pick_quad = jnp.asarray(quadrant_pick()[32:].T, BF16)
-    pick_back = jnp.asarray(quadrant_pick().T, BF16)
     tok = tokens.reshape(128, D)
     cot = cotangent.reshape(128, D)
 
-    message = jax.ShapeDtypeStruct((160, D), BF16)
-    weights, to_left, to_above, to_diag = pl.pallas_call(
+    piece = jax.ShapeDtypeStruct((32, D), BF16)
+    weights, cot_own, to_left, to_above, to_diag = pl.pallas_call(
         prepare,
-        out_shape=(jax.ShapeDtypeStruct((8, 384, HALF), BF16), message, message, message),
-        in_specs=[SMEM] + [VMEM] * 7,
-        out_specs=[pl.BlockSpec(memory_space=pl.ANY)] + [VMEM] * 3,
+        out_shape=(jax.ShapeDtypeStruct((8, 384, HALF), BF16), piece, piece, piece, piece),
+        in_specs=[SMEM] + [VMEM] * 5,
+        out_specs=[pl.BlockSpec(memory_space=pl.ANY)] + [VMEM] * 4,
         scratch_shapes=[pltpu.VMEM((384, HALF), BF16), pltpu.SemaphoreType.DMA((8,))],
         compiler_params=params(60),
         name="prepare",
-    )(core, tok, cot, qkv_plain.T, qkv_shift.T, proj_plain, proj_shift, quad)
-
+    )(core, cot, qkv_plain.T, qkv_shift.T, proj_plain, proj_shift)
+
+    w_mine = swap(weights, "freq")
+    cot_right = from_offset(to_left, 1, 0)
+    cot_below = from_offset(to_above, 0, 1)
+    cot_diag = from_offset(to_diag, 1, 1)
+
+    table = jax.ShapeDtypeStruct((SPOTS, LANES), F32)
+    bias_p, bias_s = pl.pallas_call(
+        biases,
+        out_shape=(table, table),
+        in_specs=[SMEM, VMEM, VMEM],
+        out_specs=[VMEM] * 2,
+        scratch_shapes=[pltpu.VMEM((32, 256), F32), pltpu.VMEM((2 * HEADS * WIN, 128), F32)],
+        compiler_params=params(),
+        name="biases",
+    )(edge, table_plain, table_shift)
+
+    w_mine, bias_p, bias_s, cot_right, cot_below, cot_diag = lax.optimization_barrier(
+        (w_mine, bias_p, bias_s, cot_right, cot_below, cot_diag)
+    )
+    w_other = other_core(w_mine)
+    packet = jax.ShapeDtypeStruct((32, D + WIDE), BF16)
+    own, to_left, to_above, to_diag = pl.pallas_call(
+        plain_forward,
+        out_shape=(packet,) * 4,
+        in_specs=[SMEM] + [VMEM] * 4,
+        out_specs=[VMEM] * 4,
+        scratch_shapes=[
+            pltpu.VMEM((128, D), BF16),
+            pltpu.VMEM((128, D), F32),
+            pltpu.VMEM((LANES, WIDE), BF16),
+        ],
+        compiler_params=params(),
+        cost_estimate=cost(1_000_000_000, 4_000_000),
+        name="plain_forward",
+    )(core, tok, w_mine, w_other, bias_p)
     right = from_offset(to_left, 1, 0)
     below = from_offset(to_above, 0, 1)
     diag = from_offset(to_diag, 1, 1)
-    w_mine = swap(weights, "freq")
-
-    tables = jnp.concatenate([table_plain, table_shift], axis=0)
-    tables = jnp.pad(tables, ((0, 8), (0, 256 - REL)))
-    table = jax.ShapeDtypeStruct((SPOTS, LANES), F32)
-    bias_p, bias_q, bias_s = pl.pallas_call(
-        biases,
-        out_shape=(table, table, table),
-        in_specs=[SMEM, VMEM, VMEM],
-        out_specs=[VMEM] * 3,
-        scratch_shapes=[pltpu.VMEM((2 * HEADS * WIN, 128), F32)],
-        compiler_params=params(),
-        name="biases",
-    )(edge, tables, jnp.asarray(offset_pick(), BF16))
-
-    w_mine, right, below, diag, bias_p, bias_q, bias_s = lax.optimization_barrier(
-        (w_mine, right, below, diag, bias_p, bias_q, bias_s)
-    )
-    w_other = other_core(w_mine)
-    quads, keep, send = pl.pallas_call(
+    half = jax.ShapeDtypeStruct((8, 2, ROWS, HALF), BF16)
+    g_own, to_right, to_below, to_diag, keep, send = pl.pallas_call(
         lambda *refs: main_kernel(grad_scale, *refs),
-        out_shape=(
-            jax.ShapeDtypeStruct((128, D), BF16),
-            jax.ShapeDtypeStruct((8, 2, ROWS, HALF), BF16),
-            jax.ShapeDtypeStruct((8, 2, ROWS, HALF), BF16),
-        ),
-        in_specs=[SMEM] + [VMEM] * 12,
-        out_specs=[VMEM] * 3,
+        out_shape=(piece,) * 4 + (half, half),
+        in_specs=[SMEM] + [VMEM] * 11,
+        out_specs=[VMEM] * 6,
         scratch_shapes=[
-            pltpu.VMEM((512, D), BF16),
+            pltpu.VMEM((128, D + WIDE), BF16),
+            pltpu.VMEM((128, D), BF16),
             pltpu.VMEM((128, D), BF16),
             pltpu.VMEM((128, D), BF16),
             pltpu.VMEM((128, D), F32),
@@ -455,26 +442,28 @@
         cost_estimate=cost(4_000_000_000, 6_000_000),
         name="main",
     )(
-        core, tok, cot, right, below, diag,
-        w_mine, w_other, bias_q, bias_s, pick, pick_quad, quad,
+        core, cot_own, cot_right, cot_below, cot_diag,
+        own, right, below, diag, w_mine, w_other, bias_s,
     )
 
     part = (keep.astype(F32) + other_core(send).astype(F32)).astype(BF16)
-    part, quads = lax.optimization_barrier((part, quads))
+    part, to_right, to_below, to_diag = lax.optimization_barrier(
+        (part, to_right, to_below, to_diag)
+    )
     part = swap(part, "freq")
-    left = from_offset(quads[32:64], -1, 0)
-    above = from_offset(quads[64:96], 0, -1)
-    corner = from_offset(quads[96:128], -1, -1)
+    left = from_offset(to_right, -1, 0)
+    above = from_offset(to_below, 0, -1)
+    corner = from_offset(to_diag, -1, -1)
+    part = swap(total(part).reshape(8, 12, HALF), "tm", tm_groups("z"))
     part, left, above, corner = lax.optimization_barrier((part, left, above, corner))
-    part = total(part).reshape(8, 12, HALF)
-    part, left, above, corner = lax.optimization_barrier((part, left, above, corner))
-    part = swap(part, "tm", tm_groups("z"))
+    part = swap(summed(part, 4), "tm", tm_groups("y_hi"))
     grad_tokens = pl.pallas_call(
         plain_back,
         out_shape=jax.ShapeDtypeStruct((128, D), BF16),
-        in_specs=[SMEM] + [VMEM] * 9,
+        in_specs=[SMEM] + [VMEM] * 8,
         out_specs=VMEM,
         scratch_shapes=[
+            pltpu.VMEM((128, D), BF16),
             pltpu.VMEM((128, D), BF16),
             pltpu.VMEM((128, D), BF16),
             pltpu.VMEM((128, D), F32),
@@ -483,9 +472,8 @@
         compiler_params=params(),
         cost_estimate=cost(4_000_000_000, 4_000_000),
         name="plain_back",
-    )(core, tok, quads[0:32], left, above, corner, w_mine, w_other, bias_p, pick_back)
+    )(core, tok, g_own, left, above, corner, w_mine, w_other, bias_p)
     part, grad_tokens = lax.optimization_barrier((part, grad_tokens))
-    part = swap(summed(part, 4), "tm", tm_groups("y_hi"))
     part = swap(summed(part, 8), "tm", tm_groups("z")).reshape(2, ROWS, HALF)
     part = lax.all_gather(part, "tm", axis_index_groups=tm_groups("core"))
     grad_plain, grad_shift = pl.pallas_call(

time: 152 us -> 151 us (level)
  starting transfers between devices: 56.6 us -> 71.5 us
  waiting for transfers between devices: 34 us -> 24.3 us
  local copies, waits for them, and re-layouts: 7.91 us -> 2.39 us
  blocking collectives: 29.5 us -> 33.4 us
  Pallas kernels: 19.4 us -> 16.7 us
  other arithmetic: 2.93 us -> 1.37 us
    ppermute x6 -> x9, starting transfers between devices: 32 us -> 50.3 us  [from_offset(): return lax.ppermute(value, ('tm', 'freq'), pairs)]
    ppermute x6 -> x9, waiting for transfers between devices: 25.8 us -> 16.9 us  [from_offset(): return lax.ppermute(value, ('tm', 'freq'), pairs)]
    unnamed x30 -> x18, local copies, waits for them, and re-layouts: 7.22 us -> 1.71 us
    all_to_all x2, blocking collectives: 22.4 us -> 27.9 us  [swap(): return lax.all_to_all(value, axis, 0, 0, axis_index_groups=groups)]
    all_to_all x3, starting transfers between devices: 20.5 us -> 15.2 us  [swap(): return lax.all_to_all(value, axis, 0, 0, axis_index_groups=groups)]
    pallas_call x2 -> x3, Pallas kernels: 10.7 us -> 7.91 us  [the longest x1 4.34 us: shards(): pl.pallas_call(lambda *refs: main_kernel(grad_scale, *refs), out_shape=(p...]
    ppermute x2, starting transfers between devices: 4.07 us -> 6.08 us  [other_core(): lax.ppermute(value, 'tm', [(i, i ^ 1) for i in range(lax.axis_size('tm'))])]
    all_gather x1, blocking collectives: 7.16 us -> 5.5 us  [shards(): part = lax.all_gather(part, 'tm', axis_index_groups=tm_groups('core'))]
  transfers between devices with their start and end apart: 11 -> 14, of which waited for: 7 -> 8; matrix products, arithmetic and copies ran while one was open for 1% -> 0% of each run, Pallas kernels for 4% -> 3%
where the time goes in v4:
time: 151 us
  starting transfers between devices  71.5 us (47%)
  blocking collectives  33.4 us (22%)
  waiting for transfers between devices  24.3 us (16%)
  Pallas kernels  16.7 us (11%)
  local copies, waits for them, and re-layouts  2.39 us (2%)
    ppermute x9, starting transfers between devices, from_offset(): return lax.ppermute(value, ('tm', 'freq'), pairs)  50.3 us
    all_to_all x2, blocking collectives, swap(): return lax.all_to_all(value, axis, 0, 0, axis_index_groups=groups)  27.9 us
    ppermute x9, waiting for transfers between devices, from_offset(): return lax.ppermute(value, ('tm', 'freq'), pairs)  16.9 us
    all_to_all x3, starting transfers between devices, swap(): return lax.all_to_all(value, axis, 0, 0, axis_index_groups=groups)  15.2 us
    ppermute x2, waiting for transfers between devices, other_core(): lax.ppermute(value, 'tm', [(i, i ^ 1) for i in range(lax.axis_size('tm'))])  6.11 us
    ppermute x2, starting transfers between devices, other_core(): lax.ppermute(value, 'tm', [(i, i ^ 1) for i in range(lax.axis_size('tm'))])  6.08 us
    all_gather x1, blocking collectives, shards(): part = lax.all_gather(part, 'tm', axis_index_groups=tm_groups('core'))  5.5 us
    pallas_call x1, Pallas kernels, shards(): pl.pallas_call(lambda *refs: main_kernel(grad_scale, *refs), out_shape=(p...  4.34 us
  transfers between devices with their start and end apart: 14, of which 8 were waited for; matrix products, arithmetic and copies ran while one was open for 0% of the time, Pallas kernels for 3%

profile of v4, /device:TPU:1, one launch (start us, length us, event | category | flops | bytes accessed | tf_op | source)
XLA Modules:
  0.0 150.5 jit_solution(9519353658778428603)
XLA Ops:
  0.6 3.5 %prepare.1 = (bf16[8,384,384]{2,1,0:T(8,128)(2,1)}, bf16[32,768]{1,0:T(8,128)(2,1)}, bf16[32,768]{1,0:T(8,128)(2,1)}, bf16[32,768]{1,0:T(8,128)(2,1)}, bf16[32,768]{1,0:T(8,128)(2,1)}) custom-call(s32[1]{0:T(128)} %bitcast.core_ref.refs_0_, bf16[128,768]{1,0:T(8,128)(2,1)} %bitcast.12, bf16[144,768]{1,0:T(8,128)(2,1)} %bitcast.10, ...), custom_call_target="tpu_custom_call" | custom-call | tf_op jit(solution)/shard_map/prepare/pallas_call | solution.py:379
  4.2 6.0 %all-to-all-start = ((bf16[8,384,384]{2,1,0:T(8,128)(2,1)}), bf16[8,384,384]{2,1,0:T(8,128)(2,1)S(1)}, u32[]{:S(2)}, u32[]{:S(2)}) async-start(bf16[8,384,384]{2,1,0:T(8,128)(2,1)} %get-tuple-element.39), calls=%async_computation | async-start | bytes 4718592 | tf_op jit(solution)/shard_map/all_to_all | solution.py:335
  10.2 6.6 %collective-permute-start = (bf16[32,768]{1,0:T(8,128)(2,1)S(1)}, bf16[32,768]{1,0:T(8,128)(2,1)S(1)}, u32[]{:S(2)}, u32[]{:S(2)}) collective-permute-start(bf16[32,768]{1,0:T(8,128)(2,1)S(1)} %copy-done.8), channel_id=1, source_target_pairs={{8,0},{9,1},{10,2},{11,3},{12,4},{13,5},{14,6},{15,7},{16,8},{17,9... | collective-permute-start | bytes 147464 | tf_op jit(solution)/shard_map/ppermute | solution.py:349
  16.8 5.7 %collective-permute-start.1 = (bf16[32,768]{1,0:T(8,128)(2,1)S(1)}, bf16[32,768]{1,0:T(8,128)(2,1)S(1)}, u32[]{:S(2)}, u32[]{:S(2)}) collective-permute-start(bf16[32,768]{1,0:T(8,128)(2,1)S(1)} %copy-done.7), channel_id=1, source_target_pairs={{1,0},{2,1},{3,2},{4,3},{5,4},{6,5},{7,6},{0,7},{9,8},{10,9},{11,1... | collective-permute-start | bytes 147464 | tf_op jit(solution)/shard_map/ppermute | solution.py:349
  22.5 9.4 %collective-permute-start.2 = (bf16[32,768]{1,0:T(8,128)(2,1)S(1)}, bf16[32,768]{1,0:T(8,128)(2,1)S(1)}, u32[]{:S(2)}, u32[]{:S(2)}) collective-permute-start(bf16[32,768]{1,0:T(8,128)(2,1)S(1)} %copy-done.6), channel_id=1, source_target_pairs={{9,0},{10,1},{11,2},{12,3},{13,4},{14,5},{15,6},{8,7},{17,8},{18,9... | collective-permute-start | bytes 147464 | tf_op jit(solution)/shard_map/ppermute | solution.py:349
  32.1 1.2 biases.1
  33.3 2.2 %collective-permute-done.1.refs_3_ = bf16[32,768]{1,0:T(8,128)(2,1)S(1)} collective-permute-done((bf16[32,768]{1,0:T(8,128)(2,1)S(1)}, bf16[32,768]{1,0:T(8,128)(2,1)S(1)}, u32[]{:S(2)}, u32[]{:S(2)}) %collective-permute-start.1) | collective-permute-done | bytes 49184 | tf_op jit(solution)/shard_map/ppermute | solution.py:349
  35.5 8.8 %collective-permute-done.2.refs_4_ = bf16[32,768]{1,0:T(8,128)(2,1)S(1)} collective-permute-done((bf16[32,768]{1,0:T(8,128)(2,1)S(1)}, bf16[32,768]{1,0:T(8,128)(2,1)S(1)}, u32[]{:S(2)}, u32[]{:S(2)}) %collective-permute-start.2) | collective-permute-done | bytes 49184 | tf_op jit(solution)/shard_map/ppermute | solution.py:349
  44.3 1.9 %collective-permute-start.3 = (bf16[8,384,384]{2,1,0:T(8,128)(2,1)S(1)}, bf16[8,384,384]{2,1,0:T(8,128)(2,1)S(1)}, u32[]{:S(2)}, u32[]{:S(2)}) collective-permute-start(bf16[8,384,384]{2,1,0:T(8,128)(2,1)S(1)} %all-to-all-done.w_mine_ref.refs_9_), channel_id=1, source_target_pairs={{0,8},{8,0},{16,24},{24,16},{32,40},{40,32},{48,56},{56,48},{64,72... | collective-permute-start | bytes 7077896 | tf_op jit(solution)/shard_map/ppermute | solution.py:353
  46.2 4.5 %collective-permute-done.3.w_other_ref.refs_10_ = bf16[8,384,384]{2,1,0:T(8,128)(2,1)S(1)} collective-permute-done((bf16[8,384,384]{2,1,0:T(8,128)(2,1)S(1)}, bf16[8,384,384]{2,1,0:T(8,128)(2,1)S(1)}, u32[]{:S(2)}, u32[]{:S(2)}) %collective-permute-start.3) | collective-permute-done | bytes 2359328 | tf_op jit(solution)/shard_map/ppermute | solution.py:353
  50.7 2.4 %plain_forward.1 = (bf16[32,1152]{1,0:T(8,128)(2,1)S(1)}, bf16[32,1152]{1,0:T(8,128)(2,1)S(1)}, bf16[32,1152]{1,0:T(8,128)(2,1)S(1)}, bf16[32,1152]{1,0:T(8,128)(2,1)S(1)}) custom-call(s32[1]{0:T(128)} %bitcast.core_ref.refs_0_, bf16[128,768]{1,0:T(8,128)(2,1)S(1)} %bitcast.8, bf16[8,384,384]{2,1,0:T(8,128)(2,1)S(1)} %all-to-all-done.w_mine_ref.refs_9_, ...), custom_call_target="tpu_custom_call" | custom-call | flops 1000000000 | bytes 4000000 | tf_op jit(solution)/shard_map/plain_forward/pallas_call | solution.py:410
  53.0 2.0 %collective-permute-start.4 = (bf16[32,1152]{1,0:T(8,128)(2,1)S(1)}, bf16[32,1152]{1,0:T(8,128)(2,1)S(1)}, u32[]{:S(2)}, u32[]{:S(2)}) collective-permute-start(bf16[32,1152]{1,0:T(8,128)(2,1)S(1)} %get-tuple-element.51), channel_id=1, source_target_pairs={{8,0},{9,1},{10,2},{11,3},{12,4},{13,5},{14,6},{15,7},{16,8},{17,9... | collective-permute-start | bytes 221192 | tf_op jit(solution)/shard_map/ppermute | solution.py:349
  55.1 2.4 %collective-permute-start.5 = (bf16[32,1152]{1,0:T(8,128)(2,1)S(1)}, bf16[32,1152]{1,0:T(8,128)(2,1)S(1)}, u32[]{:S(2)}, u32[]{:S(2)}) collective-permute-start(bf16[32,1152]{1,0:T(8,128)(2,1)S(1)} %get-tuple-element.52), channel_id=1, source_target_pairs={{1,0},{2,1},{3,2},{4,3},{5,4},{6,5},{7,6},{0,7},{9,8},{10,9},{11,1... | collective-permute-start | bytes 221192 | tf_op jit(solution)/shard_map/ppermute | solution.py:349
  57.5 13.9 %collective-permute-start.6 = (bf16[32,1152]{1,0:T(8,128)(2,1)S(1)}, bf16[32,1152]{1,0:T(8,128)(2,1)S(1)}, u32[]{:S(2)}, u32[]{:S(2)}) collective-permute-start(bf16[32,1152]{1,0:T(8,128)(2,1)S(1)} %get-tuple-element.53), channel_id=1, source_target_pairs={{9,0},{10,1},{11,2},{12,3},{13,4},{14,5},{15,6},{8,7},{17,8},{18,9... | collective-permute-start | bytes 221192 | tf_op jit(solution)/shard_map/ppermute | solution.py:349
  71.4 1.4 collective-permute-done.6.refs_8_
  72.7 4.3 %main.1 = (bf16[32,768]{1,0:T(8,128)(2,1)S(1)}, bf16[32,768]{1,0:T(8,128)(2,1)S(1)}, bf16[32,768]{1,0:T(8,128)(2,1)S(1)}, bf16[32,768]{1,0:T(8,128)(2,1)S(1)}, b...) custom-call(s32[1]{0:T(128)} %bitcast.core_ref.refs_0_, bf16[32,768]{1,0:T(8,128)(2,1)S(1)} %copy-done.5, ...), custom_call_target="tpu_custom_call" | custom-call | flops 4000000000 | bytes 6000000 | tf_op jit(solution)/shard_map/main/pallas_call | solution.py:428
  77.1 4.2 %collective-permute-start.7 = (bf16[8,2,48,384]{3,2,1,0:T(8,128)(2,1)S(1)}, bf16[8,2,48,384]{3,2,1,0:T(8,128)(2,1)S(1)}, u32[]{:S(2)}, u32[]{:S(2)}) collective-permute-start(bf16[8,2,48,384]{3,2,1,0:T(8,128)(2,1)S(1)} %get-tuple-element.56), channel_id=1, source_target_pairs={{0,8},{8,0},{16,24},{24,16},{32,40},{40,32},{48,56},{56,48},{64,72... | collective-permute-start | bytes 1769480 | tf_op jit(solution)/shard_map/ppermute | solution.py:353
  81.3 1.6 %collective-permute-done.7 = bf16[8,2,48,384]{3,2,1,0:T(8,128)(2,1)S(1)} collective-permute-done((bf16[8,2,48,384]{3,2,1,0:T(8,128)(2,1)S(1)}, bf16[8,2,48,384]{3,2,1,0:T(8,128)(2,1)S(1)}, u32[]{:S(2)}, u32[]{:S(2)}) %collective-permute-start.7) | collective-permute-done | bytes 589856 | tf_op jit(solution)/shard_map/ppermute | solution.py:353
  83.0 13.7 %all_to_all.25 = bf16[8,2,48,384]{3,2,1,0:T(8,128)(2,1)} all-to-all(bf16[8,2,48,384]{3,2,1,0:T(8,128)(2,1)S(1)} %add_convert_fusion), channel_id=1, replica_groups=mesh['tm'=64,'freq'=8] {'freq'}, dimensions={0} | all-to-all | bytes 1179648 | tf_op jit(solution)/shard_map/all_to_all | solution.py:335
  96.8 1.1 reduce_sum.12
  98.6 4.2 %all-to-all-start.2 = ((bf16[8,12,384]{2,1,0:T(8,128)(2,1)}), bf16[8,12,384]{2,1,0:T(8,128)(2,1)S(1)}, u32[]{:S(2)}, u32[]{:S(2)}) async-start(bf16[8,12,384]{2,1,0:T(8,128)(2,1)} %reshape.24), calls=%async_computation.2 | async-start | bytes 196608 | tf_op jit(solution)/shard_map/all_to_all | solution.py:335
  102.7 5.0 %collective-permute-start.8 = (bf16[32,768]{1,0:T(8,128)(2,1)S(1)}, bf16[32,768]{1,0:T(8,128)(2,1)S(1)}, u32[]{:S(2)}, u32[]{:S(2)}) collective-permute-start(bf16[32,768]{1,0:T(8,128)(2,1)S(1)} %get-tuple-element.61), channel_id=1, source_target_pairs={{504,0},{505,1},{506,2},{507,3},{508,4},{509,5},{510,6},{511,7},{0... | collective-permute-start | bytes 147464 | tf_op jit(solution)/shard_map/ppermute | solution.py:349
  107.8 2.4 %collective-permute-start.9 = (bf16[32,768]{1,0:T(8,128)(2,1)S(1)}, bf16[32,768]{1,0:T(8,128)(2,1)S(1)}, u32[]{:S(2)}, u32[]{:S(2)}) collective-permute-start(bf16[32,768]{1,0:T(8,128)(2,1)S(1)} %get-tuple-element.62), channel_id=1, source_target_pairs={{7,0},{0,1},{1,2},{2,3},{3,4},{4,5},{5,6},{6,7},{15,8},{8,9},{9,10... | collective-permute-start | bytes 147464 | tf_op jit(solution)/shard_map/ppermute | solution.py:349
  110.1 2.9 %collective-permute-start.10 = (bf16[32,768]{1,0:T(8,128)(2,1)S(1)}, bf16[32,768]{1,0:T(8,128)(2,1)S(1)}, u32[]{:S(2)}, u32[]{:S(2)}) collective-permute-start(bf16[32,768]{1,0:T(8,128)(2,1)S(1)} %get-tuple-element.63), channel_id=1, source_target_pairs={{511,0},{504,1},{505,2},{506,3},{507,4},{508,5},{509,6},{510,7},{7... | collective-permute-start | bytes 147464 | tf_op jit(solution)/shard_map/ppermute | solution.py:349
  113.1 1.6 %collective-permute-done.9.g_above = bf16[32,768]{1,0:T(8,128)(2,1)S(1)} collective-permute-done((bf16[32,768]{1,0:T(8,128)(2,1)S(1)}, bf16[32,768]{1,0:T(8,128)(2,1)S(1)}, u32[]{:S(2)}, u32[]{:S(2)}) %collective-permute-start.9) | collective-permute-done | bytes 49184 | tf_op jit(solution)/shard_map/ppermute | solution.py:349
  114.7 3.0 %collective-permute-done.10.g_diag = bf16[32,768]{1,0:T(8,128)(2,1)S(1)} collective-permute-done((bf16[32,768]{1,0:T(8,128)(2,1)S(1)}, bf16[32,768]{1,0:T(8,128)(2,1)S(1)}, u32[]{:S(2)}, u32[]{:S(2)}) %collective-permute-start.10) | collective-permute-done | bytes 49184 | tf_op jit(solution)/shard_map/ppermute | solution.py:349
  118.3 5.0 %all-to-all-start.3 = ((bf16[4,12,384]{2,1,0:T(8,128)(2,1)}), bf16[4,12,384]{2,1,0:T(8,128)(2,1)S(1)}, u32[]{:S(2)}, u32[]{:S(2)}) async-start(bf16[4,12,384]{2,1,0:T(8,128)(2,1)} %sum_copies.2), calls=%async_computation.3 | async-start | bytes 98304 | tf_op jit(solution)/shard_map/all_to_all | solution.py:335
  123.3 1.7 %copy-done.1 = bf16[8,384,384]{2,1,0:T(8,128)(2,1)S(1)} copy-done((bf16[8,384,384]{2,1,0:T(8,128)(2,1)S(1)}, bf16[8,384,384]{2,1,0:T(8,128)(2,1)}, u32[]{:S(2)}) %copy-start.1) | copy-done | bytes 2359320
  125.0 3.9 %plain_back.1 = bf16[128,768]{1,0:T(8,128)(2,1)} custom-call(s32[1]{0:T(128)} %bitcast.core_ref.refs_0_, bf16[128,768]{1,0:T(8,128)(2,1)S(1)} %bitcast.9, bf16[32,768]{1,0:T(8,128)(2,1)S(1)} %get-tuple-element.65.g_own, bf16[32,768]{1,0:T(8,128)(2,1)S(1)} %collective-permute-done.8.g_left, bf16[32,768]{1,0:T(8,128)(2,1)S(1)} %collective-permute-done.9.g_above, ...), custom_call_target="tpu_custom_call" | custom-call | flops 4000000000 | bytes 4000000 | tf_op jit(solution)/shard_map/plain_back/pallas_call | solution.py:460
  128.9 1.3 all-to-all-done.3.parts
  130.2 14.1 %all_to_all.26 = bf16[8,12,384]{2,1,0:T(8,128)(2,1)S(1)} all-to-all(bf16[8,12,384]{2,1,0:T(8,128)(2,1)S(1)} %sum_copies.3), channel_id=1, replica_groups={{0,64,128,192,256,320,384,448},{8,72,136,200,264,328,392,456},{16,80,14..., dimensions={0} | all-to-all | bytes 147456 | tf_op jit(solution)/shard_map/all_to_all | solution.py:335
  144.3 5.5 %all_gather.3.parts = bf16[2,2,48,384]{3,2,1,0:T(8,128)(2,1)S(1)} all-gather(bf16[1,2,48,384]{3,2,1,0:T(8,128)(2,1)S(1)} %all_gather_reshape.3), channel_id=1, replica_groups={{0,8},{16,24},{32,40},{48,56},{64,72},{80,88},{96,104},{112,120},{128,1..., dimensions={0}, use_global_device_ids=true | all-gather | bytes 221184 | tf_op jit(solution)/shard_map/all_gather | solution.py:478
  (30 shorter events, 2.3 us)
Async XLA Ops:
  4.2 6.1 %copy-start.8 = (bf16[32,768]{1,0:T(8,128)(2,1)S(1)}, bf16[32,768]{1,0:T(8,128)(2,1)}, u32[]{:S(2)}) copy-start(bf16[32,768]{1,0:T(8,128)(2,1)} %get-tuple-element.42) | copy-start | bytes 147460
  4.2 12.6 %copy-start.7 = (bf16[32,768]{1,0:T(8,128)(2,1)S(1)}, bf16[32,768]{1,0:T(8,128)(2,1)}, u32[]{:S(2)}) copy-start(bf16[32,768]{1,0:T(8,128)(2,1)} %get-tuple-element.43) | copy-start | bytes 147460
  4.2 18.3 %copy-start.6 = (bf16[32,768]{1,0:T(8,128)(2,1)S(1)}, bf16[32,768]{1,0:T(8,128)(2,1)}, u32[]{:S(2)}) copy-start(bf16[32,768]{1,0:T(8,128)(2,1)} %get-tuple-element.44) | copy-start | bytes 147460
  4.2 27.9 %copy-start.3 = (f32[12,225]{1,0:T(8,128)S(1)}, f32[12,225]{1,0:T(8,128)}, u32[]{:S(2)}) copy-start(f32[12,225]{1,0:T(8,128)} %table_p.1) | copy-start | bytes 32404
  4.2 27.8 %copy-start.4 = (f32[12,225]{1,0:T(8,128)S(1)}, f32[12,225]{1,0:T(8,128)}, u32[]{:S(2)}) copy-start(f32[12,225]{1,0:T(8,128)} %table_s.1) | copy-start | bytes 32404
  4.2 46.5 %copy-start.2 = (bf16[2,8,8,768]{3,2,1,0:T(8,128)(2,1)S(1)}, bf16[2,8,8,768]{3,2,1,0:T(8,128)(2,1)}, u32[]{:S(2)}) copy-start(bf16[2,8,8,768]{3,2,1,0:T(8,128)(2,1)} %param.8) | copy-start | bytes 589828
  4.2 40.0 %all-to-all-start = ((bf16[8,384,384]{2,1,0:T(8,128)(2,1)}), bf16[8,384,384]{2,1,0:T(8,128)(2,1)S(1)}, u32[]{:S(2)}, u32[]{:S(2)}) async-start(bf16[8,384,384]{2,1,0:T(8,128)(2,1)} %get-tuple-element.39), calls=%async_computation | async-start | bytes 4718592 | tf_op jit(solution)/shard_map/all_to_all | solution.py:335
  10.2 23.0 %collective-permute-start = (bf16[32,768]{1,0:T(8,128)(2,1)S(1)}, bf16[32,768]{1,0:T(8,128)(2,1)S(1)}, u32[]{:S(2)}, u32[]{:S(2)}) collective-permute-start(bf16[32,768]{1,0:T(8,128)(2,1)S(1)} %copy-done.8), channel_id=1, source_target_pairs={{8,0},{9,1},{10,2},{11,3},{12,4},{13,5},{14,6},{15,7},{16,8},{17,9... | collective-permute-start | bytes 147464 | tf_op jit(solution)/shard_map/ppermute | solution.py:349
  16.8 18.7 %collective-permute-start.1 = (bf16[32,768]{1,0:T(8,128)(2,1)S(1)}, bf16[32,768]{1,0:T(8,128)(2,1)S(1)}, u32[]{:S(2)}, u32[]{:S(2)}) collective-permute-start(bf16[32,768]{1,0:T(8,128)(2,1)S(1)} %copy-done.7), channel_id=1, source_target_pairs={{1,0},{2,1},{3,2},{4,3},{5,4},{6,5},{7,6},{0,7},{9,8},{10,9},{11,1... | collective-permute-start | bytes 147464 | tf_op jit(solution)/shard_map/ppermute | solution.py:349
  22.5 21.8 %collective-permute-start.2 = (bf16[32,768]{1,0:T(8,128)(2,1)S(1)}, bf16[32,768]{1,0:T(8,128)(2,1)S(1)}, u32[]{:S(2)}, u32[]{:S(2)}) collective-permute-start(bf16[32,768]{1,0:T(8,128)(2,1)S(1)} %copy-done.6), channel_id=1, source_target_pairs={{9,0},{10,1},{11,2},{12,3},{13,4},{14,5},{15,6},{8,7},{17,8},{18,9... | collective-permute-start | bytes 147464 | tf_op jit(solution)/shard_map/ppermute | solution.py:349
  44.3 6.4 %collective-permute-start.3 = (bf16[8,384,384]{2,1,0:T(8,128)(2,1)S(1)}, bf16[8,384,384]{2,1,0:T(8,128)(2,1)S(1)}, u32[]{:S(2)}, u32[]{:S(2)}) collective-permute-start(bf16[8,384,384]{2,1,0:T(8,128)(2,1)S(1)} %all-to-all-done.w_mine_ref.refs_9_), channel_id=1, source_target_pairs={{0,8},{8,0},{16,24},{24,16},{32,40},{40,32},{48,56},{56,48},{64,72... | collective-permute-start | bytes 7077896 | tf_op jit(solution)/shard_map/ppermute | solution.py:353
  50.7 22.1 %copy-start = (bf16[8,384,384]{2,1,0:T(8,128)(2,1)}, bf16[8,384,384]{2,1,0:T(8,128)(2,1)S(1)}, u32[]{:S(2)}) copy-start(bf16[8,384,384]{2,1,0:T(8,128)(2,1)S(1)} %collective-permute-done.3.w_other_ref.refs_10_) | copy-start | bytes 7077892
  50.7 22.1 %copy-start.5 = (bf16[32,768]{1,0:T(8,128)(2,1)S(1)}, bf16[32,768]{1,0:T(8,128)(2,1)}, u32[]{:S(2)}) copy-start(bf16[32,768]{1,0:T(8,128)(2,1)} %get-tuple-element.38.refs_1_) | copy-start | bytes 147460
  53.0 18.3 %collective-permute-start.4 = (bf16[32,1152]{1,0:T(8,128)(2,1)S(1)}, bf16[32,1152]{1,0:T(8,128)(2,1)S(1)}, u32[]{:S(2)}, u32[]{:S(2)}) collective-permute-start(bf16[32,1152]{1,0:T(8,128)(2,1)S(1)} %get-tuple-element.51), channel_id=1, source_target_pairs={{8,0},{9,1},{10,2},{11,3},{12,4},{13,5},{14,6},{15,7},{16,8},{17,9... | collective-permute-start | bytes 221192 | tf_op jit(solution)/shard_map/ppermute | solution.py:349
  55.1 16.3 %collective-permute-start.5 = (bf16[32,1152]{1,0:T(8,128)(2,1)S(1)}, bf16[32,1152]{1,0:T(8,128)(2,1)S(1)}, u32[]{:S(2)}, u32[]{:S(2)}) collective-permute-start(bf16[32,1152]{1,0:T(8,128)(2,1)S(1)} %get-tuple-element.52), channel_id=1, source_target_pairs={{1,0},{2,1},{3,2},{4,3},{5,4},{6,5},{7,6},{0,7},{9,8},{10,9},{11,1... | collective-permute-start | bytes 221192 | tf_op jit(solution)/shard_map/ppermute | solution.py:349
  57.5 15.3 %collective-permute-start.6 = (bf16[32,1152]{1,0:T(8,128)(2,1)S(1)}, bf16[32,1152]{1,0:T(8,128)(2,1)S(1)}, u32[]{:S(2)}, u32[]{:S(2)}) collective-permute-start(bf16[32,1152]{1,0:T(8,128)(2,1)S(1)} %get-tuple-element.53), channel_id=1, source_target_pairs={{9,0},{10,1},{11,2},{12,3},{13,4},{14,5},{15,6},{8,7},{17,8},{18,9... | collective-permute-start | bytes 221192 | tf_op jit(solution)/shard_map/ppermute | solution.py:349
  77.1 5.8 %collective-permute-start.7 = (bf16[8,2,48,384]{3,2,1,0:T(8,128)(2,1)S(1)}, bf16[8,2,48,384]{3,2,1,0:T(8,128)(2,1)S(1)}, u32[]{:S(2)}, u32[]{:S(2)}) collective-permute-start(bf16[8,2,48,384]{3,2,1,0:T(8,128)(2,1)S(1)} %get-tuple-element.56), channel_id=1, source_target_pairs={{0,8},{8,0},{16,24},{24,16},{32,40},{40,32},{48,56},{56,48},{64,72... | collective-permute-start | bytes 1769480 | tf_op jit(solution)/shard_map/ppermute | solution.py:353
  98.6 19.1 %all-to-all-start.2 = ((bf16[8,12,384]{2,1,0:T(8,128)(2,1)}), bf16[8,12,384]{2,1,0:T(8,128)(2,1)S(1)}, u32[]{:S(2)}, u32[]{:S(2)}) async-start(bf16[8,12,384]{2,1,0:T(8,128)(2,1)} %reshape.24), calls=%async_computation.2 | async-start | bytes 196608 | tf_op jit(solution)/shard_map/all_to_all | solution.py:335
  102.7 10.3 %collective-permute-start.8 = (bf16[32,768]{1,0:T(8,128)(2,1)S(1)}, bf16[32,768]{1,0:T(8,128)(2,1)S(1)}, u32[]{:S(2)}, u32[]{:S(2)}) collective-permute-start(bf16[32,768]{1,0:T(8,128)(2,1)S(1)} %get-tuple-element.61), channel_id=1, source_target_pairs={{504,0},{505,1},{506,2},{507,3},{508,4},{509,5},{510,6},{511,7},{0... | collective-permute-start | bytes 147464 | tf_op jit(solution)/shard_map/ppermute | solution.py:349
  107.8 6.9 %collective-permute-start.9 = (bf16[32,768]{1,0:T(8,128)(2,1)S(1)}, bf16[32,768]{1,0:T(8,128)(2,1)S(1)}, u32[]{:S(2)}, u32[]{:S(2)}) collective-permute-start(bf16[32,768]{1,0:T(8,128)(2,1)S(1)} %get-tuple-element.62), channel_id=1, source_target_pairs={{7,0},{0,1},{1,2},{2,3},{3,4},{4,5},{5,6},{6,7},{15,8},{8,9},{9,10... | collective-permute-start | bytes 147464 | tf_op jit(solution)/shard_map/ppermute | solution.py:349
  110.1 7.5 %collective-permute-start.10 = (bf16[32,768]{1,0:T(8,128)(2,1)S(1)}, bf16[32,768]{1,0:T(8,128)(2,1)S(1)}, u32[]{:S(2)}, u32[]{:S(2)}) collective-permute-start(bf16[32,768]{1,0:T(8,128)(2,1)S(1)} %get-tuple-element.63), channel_id=1, source_target_pairs={{511,0},{504,1},{505,2},{506,3},{507,4},{508,5},{509,6},{510,7},{7... | collective-permute-start | bytes 147464 | tf_op jit(solution)/shard_map/ppermute | solution.py:349
  118.3 11.9 %all-to-all-start.3 = ((bf16[4,12,384]{2,1,0:T(8,128)(2,1)}), bf16[4,12,384]{2,1,0:T(8,128)(2,1)S(1)}, u32[]{:S(2)}, u32[]{:S(2)}) async-start(bf16[4,12,384]{2,1,0:T(8,128)(2,1)} %sum_copies.2), calls=%async_computation.3 | async-start | bytes 98304 | tf_op jit(solution)/shard_map/all_to_all | solution.py:335
  123.3 1.7 %copy-start.1 = (bf16[8,384,384]{2,1,0:T(8,128)(2,1)S(1)}, bf16[8,384,384]{2,1,0:T(8,128)(2,1)}, u32[]{:S(2)}) copy-start(bf16[8,384,384]{2,1,0:T(8,128)(2,1)} %copy-done) | copy-start | bytes 7077892

commit v5 on v4

--- a/solution.py
+++ b/solution.py
@@ -94,23 +94,29 @@
     return (d_query, d_key, d_value)
 
 
-def prepare(core_ref, cot, qkv_p, qkv_s, proj_p, proj_s, out_w, out_o, out_r, out_b, out_d, block, sems):
+def copy_all(pairs, sems, first=0):
+    moves = [
+        pltpu.make_async_copy(source, target, sems.at[first + i])
+        for i, (source, target) in enumerate(pairs)
+    ]
+    for move in moves:
+        move.start()
+    return moves
+
+
+def wait_all(moves):
+    for move in moves:
+        move.wait()
+
+
+def prepare(core_ref, qkv, proj, out, block, sems):
     start = pl.multiple_of(core_ref[0] * HALF, 128)
-    block[0:144] = qkv_p[:, pl.ds(start, HALF)]
-    block[144:192] = proj_p[:, pl.ds(start, HALF)]
-    block[192:336] = qkv_s[:, pl.ds(start, HALF)]
-    block[336:384] = proj_s[:, pl.ds(start, HALF)]
-    sends = [pltpu.make_async_copy(block, out_w.at[i], sems.at[i]) for i in range(8)]
-    for send in sends:
-        send.start()
-    quads = dot(quadrant_pick(), cot[...]).astype(BF16)
-    for out, first in ((out_o, 96), (out_r, 64), (out_b, 32), (out_d, 0)):
-        out[...] = quads[first : first + 32]
-    for send in sends:
-        send.wait()
-
-
-def biases(edge_ref, table_p, table_s, out_p, out_s, tables, wide):
+    block[0:SHARE] = qkv[:, pl.ds(start, HALF)]
+    block[SHARE : SHARE + ROWS] = proj[:, pl.ds(start, HALF)]
+    wait_all(copy_all([(block, out.at[i]) for i in range(8)], sems))
+
+
+def biases(edge_ref, table_p, table_s, to_p, to_s, out_p, out_s, tables, wide, sems):
     tables[...] = jnp.zeros_like(tables)
     tables[0:HEADS, 0:REL] = table_p[...]
     tables[HEADS : 2 * HEADS, 0:REL] = table_s[...]
@@ -138,6 +144,7 @@
     cross = at ^ key_at
     barred = (cross & 32) * edge_ref[0] + (cross & 4) * edge_ref[1]
     out_s[...] = jnp.where(barred != 0, NEG, out_s[...])
+    wait_all(copy_all([(out_p, to_p), (out_s, to_s)], sems))
 
 
 def project(rows_ref, w_mine, w_other, mine, other):
@@ -151,12 +158,12 @@
     return (mine, pl.multiple_of(HALF - mine, 128))
 
 
-def qkv_of(ref, first):
-    return ref[:, first : first + SHARE].reshape(3 * WIDE, HALF)
-
-
-def proj_of(ref, first):
-    return ref[:, first + SHARE : first + SHARE + ROWS].reshape(WIDE, HALF)
+def qkv_of(ref):
+    return ref[:, 0:SHARE].reshape(3 * WIDE, HALF)
+
+
+def proj_of(ref):
+    return ref[:, SHARE : SHARE + ROWS].reshape(WIDE, HALF)
 
 
 def input_grad(grad, normed, rstd, d_packed, w_mine, w_other, mine, other, sums):
@@ -172,14 +179,34 @@
 
 
 def plain_forward(
-    core_ref, tok, w_mine_ref, w_other_ref, bias_p, out_o, out_r, out_b, out_d, rows, sums, mask
+    core_ref,
+    tok_far,
+    cot_far,
+    bias_far,
+    w_mine_ref,
+    w_other_ref,
+    out_o,
+    out_r,
+    out_b,
+    out_d,
+    tok,
+    cot,
+    bias_p,
+    packets,
+    rows,
+    sums,
+    mask,
+    sems,
 ):
     mine, other = sides(core_ref)
+    loads = copy_all([(tok_far, tok), (bias_far, bias_p), (cot_far, cot)], sems)
     mask[...] = head_mask()
+    loads[0].wait()
     inputs = tok[...].astype(F32)
     rows[...] = normalize(inputs)[0].astype(BF16)
-    w_mine, w_other = qkv_of(w_mine_ref, 0), qkv_of(w_other_ref, 0)
+    w_mine, w_other = qkv_of(w_mine_ref), qkv_of(w_other_ref)
     packed = project(rows, w_mine, w_other, mine, other).astype(BF16)
+    loads[1].wait()
     mixed = []
     for s in range(2):
         part = packed[s * SPOTS : (s + 1) * SPOTS]
@@ -187,60 +214,56 @@
         probs = softmax_down(dot(key, expand(query, mask), NT) * SCALE + bias_p[...])
         mixed.append(fold(dot(probs.astype(BF16), value, TN)).astype(BF16))
     mixed = jnp.concatenate(mixed, axis=0)
-    sums[:, pl.ds(mine, HALF)] = dot(mixed, proj_of(w_mine_ref, 0))
-    sums[:, pl.ds(other, HALF)] = dot(mixed, proj_of(w_other_ref, 0))
+    sums[:, pl.ds(mine, HALF)] = dot(mixed, proj_of(w_mine_ref))
+    sums[:, pl.ds(other, HALF)] = dot(mixed, proj_of(w_other_ref))
     block_out = (inputs + sums[...]).astype(BF16)
     pick = quadrant_pick()
+    loads[2].wait()
+    for whole, first in ((block_out, 0), (mixed, D), (cot[...], D + WIDE)):
+        packets[:, first : first + whole.shape[1]] = dot(pick, whole).astype(BF16)
     outs = (out_d, out_b, out_r, out_o)
-    for whole, first in ((block_out, 0), (mixed, D)):
-        quads = dot(pick, whole).astype(BF16)
-        for i, out in enumerate(outs):
-            out[:, first : first + whole.shape[1]] = quads[i * 32 : (i + 1) * 32]
+    wait_all(copy_all([(packets.at[i * 32 : (i + 1) * 32], out) for i, out in enumerate(outs)], sems, 3))
 
 
 def main_kernel(
     grad_scale,
     core_ref,
-    cot_own,
-    cot_right,
-    cot_below,
-    cot_diag,
-    own,
+    own_far,
+    bias_far,
     right,
     below,
     diag,
     w_mine_ref,
     w_other_ref,
+    to_own,
+    to_column,
+    to_below,
+    to_local,
     bias_s,
-    out_own,
-    out_right,
-    out_below,
-    out_diag,
-    out_keep,
-    out_send,
+    quads,
+    out_local,
     staged,
-    staged_cot,
     rows_small,
     grads,
     sums,
     mask,
+    sems,
 ):
     mine, other = sides(core_ref)
+    loads = copy_all([(own_far, staged.at[0:32]), (bias_far, bias_s)], sems)
     mask[...] = head_mask()
-    for i, (part, cot) in enumerate(
-        ((own, cot_own), (right, cot_right), (below, cot_below), (diag, cot_diag))
-    ):
+    for i, part in ((1, right), (2, below), (3, diag)):
         staged[i * 32 : (i + 1) * 32] = part[...]
-        staged_cot[i * 32 : (i + 1) * 32] = cot[...]
+    wait_all(loads)
     pick = quadrant_pick(True)
-    grads[...] = dot(pick, staged_cot[...]).astype(BF16)
+    grads[...] = dot(pick, staged[:, D + WIDE :]).astype(BF16)
     block_out = dot(pick, staged[:, 0:D])
     mixed_plain = dot(pick, staged[:, D : D + WIDE]).astype(BF16)
     normed, rstd = normalize(block_out)
     rows_small[...] = normed.astype(BF16)
-    w_mine, w_other = qkv_of(w_mine_ref, 192), qkv_of(w_other_ref, 192)
+    w_mine, w_other = qkv_of(w_mine_ref), qkv_of(w_other_ref)
     packed = project(rows_small, w_mine, w_other, mine, other).astype(BF16)
-    d_mixed = project(grads, proj_of(w_mine_ref, 192), proj_of(w_other_ref, 192), mine, other).astype(BF16)
+    d_mixed = project(grads, proj_of(w_mine_ref), proj_of(w_other_ref), mine, other).astype(BF16)
     mixed, d_packed = [], []
     for s in range(2):
         part = packed[s * SPOTS : (s + 1) * SPOTS]
@@ -257,15 +280,36 @@
     grad = input_grad(
         grads[...].astype(F32), normed, rstd, d_packed, w_mine, w_other, mine, other, sums
     )
-    quads = dot(quadrant_pick(), grad).astype(BF16)
-    for i, out in enumerate((out_own, out_right, out_below, out_diag)):
-        out[...] = quads[i * 32 : (i + 1) * 32]
-    rows_small[...] = grad
-    for out, start in ((out_keep, mine), (out_send, other)):
-        part = dot(mixed_plain, rows_small[:, pl.ds(start, HALF)], TN) * grad_scale
-        out[:, 0] = part.astype(BF16).reshape(8, ROWS, HALF)
-        part = dot(mixed_shift, grads[:, pl.ds(start, HALF)], TN) * grad_scale
-        out[:, 1] = part.astype(BF16).reshape(8, ROWS, HALF)
+    quads[...] = dot(quadrant_pick(), grad).astype(BF16)
+    stores = copy_all(
+        [
+            (quads.at[0:32], to_own),
+            (quads.at[32:64], to_column.at[0:32]),
+            (quads.at[96:128], to_column.at[32:64]),
+            (quads.at[64:96], to_below),
+        ],
+        sems,
+        2,
+    )
+    local_shift = dot(mixed_shift, grads[...], TN) * grad_scale
+    out_local[:, 1] = local_shift.astype(BF16).reshape(8, ROWS, D)
+    local_plain = dot(mixed_plain, grad, TN) * grad_scale
+    out_local[:, 0] = local_plain.astype(BF16).reshape(8, ROWS, D)
+    wait_all(copy_all([(out_local, to_local)], sems, 6))
+    wait_all(stores)
+
+
+def sum_split(core_ref, parts, out_keep, out_send, total):
+    mine, other = sides(core_ref)
+    total[...] = jnp.sum(parts[...].astype(F32), axis=0)
+    out_keep[...] = total[:, :, pl.ds(mine, HALF)]
+    out_send[...] = total[:, :, pl.ds(other, HALF)].astype(BF16)
+
+
+def pair_copies(keep, arrived, out):
+    value = (keep[...] + arrived[...].astype(F32)).astype(BF16)
+    for i in range(out.shape[0]):
+        out[i] = value
 
 
 def sum_copies(parts, out):
@@ -281,19 +325,50 @@
 
 
 def plain_back(
-    core_ref, tok, g_own, g_left, g_above, g_diag, w_mine_ref, w_other_ref, bias_p, out, staged, rows, grads, sums, mask
+    core_ref,
+    tok_far,
+    own_far,
+    bias_far,
+    mine_far,
+    other_far,
+    column,
+    row,
+    out,
+    tok,
+    bias_p,
+    w_mine_ref,
+    w_other_ref,
+    staged,
+    rows,
+    grads,
+    sums,
+    mask,
+    sems,
 ):
     mine, other = sides(core_ref)
+    loads = copy_all(
+        [
+            (tok_far, tok),
+            (mine_far, w_mine_ref),
+            (other_far, w_other_ref),
+            (own_far, staged.at[96:128]),
+            (bias_far, bias_p),
+        ],
+        sems,
+    )
     mask[...] = head_mask()
+    staged[0:32] = row[32:64]
+    staged[32:64] = row[0:32]
+    staged[64:96] = column[0:32]
+    loads[0].wait()
     normed, rstd = normalize(tok[...].astype(F32))
     rows[...] = normed.astype(BF16)
-    w_mine, w_other = qkv_of(w_mine_ref, 0), qkv_of(w_other_ref, 0)
+    wait_all(loads[1:])
+    w_mine, w_other = qkv_of(w_mine_ref), qkv_of(w_other_ref)
     packed = project(rows, w_mine, w_other, mine, other).astype(BF16)
-    for i, part in enumerate((g_diag, g_above, g_left, g_own)):
-        staged[i * 32 : (i + 1) * 32] = part[...]
     gathered = dot(quadrant_pick(True), staged[...])
     grads[...] = gathered.astype(BF16)
-    d_mixed = project(grads, proj_of(w_mine_ref, 0), proj_of(w_other_ref, 0), mine, other).astype(BF16)
+    d_mixed = project(grads, proj_of(w_mine_ref), proj_of(w_other_ref), mine, other).astype(BF16)
     d_packed = []
     for s in range(2):
         part = packed[s * SPOTS : (s + 1) * SPOTS]
@@ -310,10 +385,15 @@
 
 VMEM = pl.BlockSpec(memory_space=pltpu.VMEM)
 SMEM = pl.BlockSpec(memory_space=pltpu.SMEM)
+HBM = pl.BlockSpec(memory_space=pltpu.HBM)
 
 
 def params(size=32):
     return pltpu.CompilerParams(vmem_limit_bytes=size * 1024 * 1024)
+
+
+def far(value):
+    return pltpu.with_memory_space_constraint(value, pltpu.HBM)
 
 
 def cost(flops, size):
@@ -333,10 +413,6 @@
 
 def swap(value, axis, groups=None):
     return lax.all_to_all(value, axis, 0, 0, axis_index_groups=groups)
-
-
-def total(blocks):
-    return jnp.sum(blocks.astype(F32), axis=0).astype(BF16)
 
 
 def from_offset(value, along_tm, along_freq):
@@ -375,106 +451,144 @@
     tok = tokens.reshape(128, D)
     cot = cotangent.reshape(128, D)
 
-    piece = jax.ShapeDtypeStruct((32, D), BF16)
-    weights, cot_own, to_left, to_above, to_diag = pl.pallas_call(
-        prepare,
-        out_shape=(jax.ShapeDtypeStruct((8, 384, HALF), BF16), piece, piece, piece, piece),
-        in_specs=[SMEM] + [VMEM] * 5,
-        out_specs=[pl.BlockSpec(memory_space=pl.ANY)] + [VMEM] * 4,
-        scratch_shapes=[pltpu.VMEM((384, HALF), BF16), pltpu.SemaphoreType.DMA((8,))],
-        compiler_params=params(60),
-        name="prepare",
-    )(core, cot, qkv_plain.T, qkv_shift.T, proj_plain, proj_shift)
-
-    w_mine = swap(weights, "freq")
-    cot_right = from_offset(to_left, 1, 0)
-    cot_below = from_offset(to_above, 0, 1)
-    cot_diag = from_offset(to_diag, 1, 1)
-
-    table = jax.ShapeDtypeStruct((SPOTS, LANES), F32)
+    def share(qkv, proj):
+        return pl.pallas_call(
+            prepare,
+            out_shape=pltpu.HBM((8, SHARE + ROWS, HALF), BF16),
+            in_specs=[SMEM, VMEM, VMEM],
+            out_specs=HBM,
+            scratch_shapes=[
+                pltpu.VMEM((SHARE + ROWS, HALF), BF16),
+                pltpu.SemaphoreType.DMA((8,)),
+            ],
+            compiler_params=params(60),
+            name="prepare",
+        )(core, qkv.T, proj)
+
+    first_mine = swap(share(qkv_plain, proj_plain), "freq")
+    second_share = share(qkv_shift, proj_shift)
+    table = pltpu.HBM((SPOTS, LANES), F32)
     bias_p, bias_s = pl.pallas_call(
         biases,
         out_shape=(table, table),
         in_specs=[SMEM, VMEM, VMEM],
-        out_specs=[VMEM] * 2,
-        scratch_shapes=[pltpu.VMEM((32, 256), F32), pltpu.VMEM((2 * HEADS * WIN, 128), F32)],
+        out_specs=[HBM] * 2,
+        scratch_shapes=[
+            pltpu.VMEM((SPOTS, LANES), F32),
+            pltpu.VMEM((SPOTS, LANES), F32),
+            pltpu.VMEM((32, 256), F32),
+            pltpu.VMEM((2 * HEADS * WIN, 128), F32),
+            pltpu.SemaphoreType.DMA((2,)),
+        ],
         compiler_params=params(),
         name="biases",
     )(edge, table_plain, table_shift)
 
-    w_mine, bias_p, bias_s, cot_right, cot_below, cot_diag = lax.optimization_barrier(
-        (w_mine, bias_p, bias_s, cot_right, cot_below, cot_diag)
-    )
-    w_other = other_core(w_mine)
-    packet = jax.ShapeDtypeStruct((32, D + WIDE), BF16)
+    first_mine, second_share, bias_p, bias_s = lax.optimization_barrier(
+        (first_mine, second_share, bias_p, bias_s)
+    )
+    second_mine = swap(second_share, "freq")
+    first_other = other_core(first_mine)
+    packet = pltpu.HBM((32, 2 * D + WIDE), BF16)
     own, to_left, to_above, to_diag = pl.pallas_call(
         plain_forward,
         out_shape=(packet,) * 4,
-        in_specs=[SMEM] + [VMEM] * 4,
-        out_specs=[VMEM] * 4,
+        in_specs=[SMEM] + [HBM] * 3 + [VMEM] * 2,
+        out_specs=[HBM] * 4,
         scratch_shapes=[
+            pltpu.VMEM((128, D), BF16),
+            pltpu.VMEM((128, D), BF16),
+            pltpu.VMEM((SPOTS, LANES), F32),
+            pltpu.VMEM((128, 2 * D + WIDE), BF16),
             pltpu.VMEM((128, D), BF16),
             pltpu.VMEM((128, D), F32),
             pltpu.VMEM((LANES, WIDE), BF16),
+            pltpu.SemaphoreType.DMA((7,)),
         ],
         compiler_params=params(),
-        cost_estimate=cost(1_000_000_000, 4_000_000),
+        cost_estimate=cost(1_000_000, 1_000_000),
         name="plain_forward",
-    )(core, tok, w_mine, w_other, bias_p)
+    )(core, far(tok), far(cot), far(bias_p), first_mine, first_other)
     right = from_offset(to_left, 1, 0)
     below = from_offset(to_above, 0, 1)
     diag = from_offset(to_diag, 1, 1)
-    half = jax.ShapeDtypeStruct((8, 2, ROWS, HALF), BF16)
-    g_own, to_right, to_below, to_diag, keep, send = pl.pallas_call(
+    second_mine, right, below, diag = lax.optimization_barrier(
+        (second_mine, right, below, diag)
+    )
+    second_other = other_core(second_mine)
+    piece = pltpu.HBM((32, D), BF16)
+    column = pltpu.HBM((64, D), BF16)
+    local = pltpu.HBM((8, 2, ROWS, D), BF16)
+    g_own, to_right, to_below, local = pl.pallas_call(
         lambda *refs: main_kernel(grad_scale, *refs),
-        out_shape=(piece,) * 4 + (half, half),
-        in_specs=[SMEM] + [VMEM] * 11,
-        out_specs=[VMEM] * 6,
+        out_shape=(piece, column, piece, local),
+        in_specs=[SMEM] + [HBM] * 2 + [VMEM] * 5,
+        out_specs=[HBM] * 4,
         scratch_shapes=[
-            pltpu.VMEM((128, D + WIDE), BF16),
-            pltpu.VMEM((128, D), BF16),
+            pltpu.VMEM((SPOTS, LANES), F32),
+            pltpu.VMEM((128, D), BF16),
+            pltpu.VMEM((8, 2, ROWS, D), BF16),
+            pltpu.VMEM((128, 2 * D + WIDE), BF16),
             pltpu.VMEM((128, D), BF16),
             pltpu.VMEM((128, D), BF16),
             pltpu.VMEM((128, D), F32),
             pltpu.VMEM((LANES, WIDE), BF16),
+            pltpu.SemaphoreType.DMA((7,)),
         ],
         compiler_params=params(),
-        cost_estimate=cost(4_000_000_000, 6_000_000),
+        cost_estimate=cost(1_000_000, 1_000_000),
         name="main",
-    )(
-        core, cot_own, cot_right, cot_below, cot_diag,
-        own, right, below, diag, w_mine, w_other, bias_s,
-    )
-
-    part = (keep.astype(F32) + other_core(send).astype(F32)).astype(BF16)
-    part, to_right, to_below, to_diag = lax.optimization_barrier(
-        (part, to_right, to_below, to_diag)
-    )
-    part = swap(part, "freq")
-    left = from_offset(to_right, -1, 0)
-    above = from_offset(to_below, 0, -1)
-    corner = from_offset(to_diag, -1, -1)
-    part = swap(total(part).reshape(8, 12, HALF), "tm", tm_groups("z"))
-    part, left, above, corner = lax.optimization_barrier((part, left, above, corner))
+    )(core, far(own), far(bias_s), right, below, diag, second_mine, second_other)
+
+    local, to_right, to_below = lax.optimization_barrier((local, to_right, to_below))
+    part = swap(local, "freq")
+    column = from_offset(to_right, -1, 0)
+    half = (2, ROWS, HALF)
+    keep, send = pl.pallas_call(
+        sum_split,
+        out_shape=(jax.ShapeDtypeStruct(half, F32), jax.ShapeDtypeStruct(half, BF16)),
+        in_specs=[SMEM, VMEM],
+        out_specs=[VMEM] * 2,
+        scratch_shapes=[pltpu.VMEM((2, ROWS, D), F32)],
+        compiler_params=params(),
+        name="sum_split",
+    )(core, part)
+    part = pl.pallas_call(
+        pair_copies,
+        out_shape=jax.ShapeDtypeStruct((8,) + half, BF16),
+        in_specs=[VMEM] * 2,
+        out_specs=VMEM,
+        compiler_params=params(),
+        name="pair_copies",
+    )(keep, other_core(send))
+    part, column, to_below = lax.optimization_barrier((part, column, to_below))
+    part = swap(part, "tm", tm_groups("z"))
+    row = from_offset(jnp.concatenate([to_below, column[32:64]], axis=0), 0, -1)
+    part, row = lax.optimization_barrier((part, row))
     part = swap(summed(part, 4), "tm", tm_groups("y_hi"))
     grad_tokens = pl.pallas_call(
         plain_back,
         out_shape=jax.ShapeDtypeStruct((128, D), BF16),
-        in_specs=[SMEM] + [VMEM] * 8,
+        in_specs=[SMEM] + [HBM] * 5 + [VMEM] * 2,
         out_specs=VMEM,
         scratch_shapes=[
             pltpu.VMEM((128, D), BF16),
+            pltpu.VMEM((SPOTS, LANES), F32),
+            pltpu.VMEM((8, SHARE + ROWS, HALF), BF16),
+            pltpu.VMEM((8, SHARE + ROWS, HALF), BF16),
+            pltpu.VMEM((128, D), BF16),
             pltpu.VMEM((128, D), BF16),
             pltpu.VMEM((128, D), BF16),
             pltpu.VMEM((128, D), F32),
             pltpu.VMEM((LANES, WIDE), BF16),
+            pltpu.SemaphoreType.DMA((5,)),
         ],
         compiler_params=params(),
         cost_estimate=cost(4_000_000_000, 4_000_000),
         name="plain_back",
-    )(core, tok, g_own, left, above, corner, w_mine, w_other, bias_p)
+    )(core, far(tok), far(g_own), far(bias_p), far(first_mine), far(first_other), column, row)
     part, grad_tokens = lax.optimization_barrier((part, grad_tokens))
-    part = swap(summed(part, 8), "tm", tm_groups("z")).reshape(2, ROWS, HALF)
+    part = summed(part, 1)[0]
     part = lax.all_gather(part, "tm", axis_index_groups=tm_groups("core"))
     grad_plain, grad_shift = pl.pallas_call(
         finish,

time: 151 us -> 147 us (0.974)
  blocking collectives: 33.4 us -> 4.71 us
  waiting for transfers between devices: 24.3 us -> 51.6 us
  Pallas kernels: 16.7 us -> 25.3 us
  starting transfers between devices: 71.5 us -> 63.3 us
  local copies, waits for them, and re-layouts: 2.39 us -> 0.03 us
    all_to_all x3 -> x5, waiting for transfers between devices: 1.29 us -> 38.1 us  [swap(): return lax.all_to_all(value, axis, 0, 0, axis_index_groups=groups)]
    all_to_all x2 -> x0, blocking collectives: 27.9 us -> none  [swap(): return lax.all_to_all(value, axis, 0, 0, axis_index_groups=groups)]
    ppermute x9 -> x5, starting transfers between devices: 50.3 us -> 26.2 us  [from_offset(): return lax.ppermute(value, ('tm', 'freq'), pairs)]
    ppermute x2 -> x3, starting transfers between devices: 6.08 us -> 15.6 us  [other_core(): lax.ppermute(value, 'tm', [(i, i ^ 1) for i in range(lax.axis_size('tm'))])]
    ppermute x9 -> x5, waiting for transfers between devices: 16.9 us -> 7.74 us  [from_offset(): return lax.ppermute(value, ('tm', 'freq'), pairs)]
    all_to_all x3 -> x5, starting transfers between devices: 15.2 us -> 21.5 us  [swap(): return lax.all_to_all(value, axis, 0, 0, axis_index_groups=groups)]
    pallas_call x1, Pallas kernels: 2.35 us -> 4.53 us  [shards(): pl.pallas_call(plain_forward, out_shape=(packet,) * 4, in_specs=[SMEM] +...]
    pallas_call x1, Pallas kernels: 4.34 us -> 6.39 us  [shards(): pl.pallas_call(lambda *refs: main_kernel(grad_scale, *refs), out_shape=(p...]
  transfers between devices with their start and end apart: 14 -> 13, of which waited for: 8 -> 9; matrix products, arithmetic and copies ran while one was open for 0% -> 0% of each run, Pallas kernels for 3% -> 10%
where the time goes in v5:
time: 147 us; the launch traced here: 146 us
  starting transfers between devices  63.3 us (43%)
  waiting for transfers between devices  51.6 us (35%)
  Pallas kernels  25.3 us (17%)
  blocking collectives  4.71 us (3%)
    all_to_all x5, waiting for transfers between devices, swap(): return lax.all_to_all(value, axis, 0, 0, axis_index_groups=groups)  38.1 us
    ppermute x5, starting transfers between devices, from_offset(): return lax.ppermute(value, ('tm', 'freq'), pairs)  26.2 us
    all_to_all x5, starting transfers between devices, swap(): return lax.all_to_all(value, axis, 0, 0, axis_index_groups=groups)  21.5 us
    ppermute x3, starting transfers between devices, other_core(): lax.ppermute(value, 'tm', [(i, i ^ 1) for i in range(lax.axis_size('tm'))])  15.6 us
    ppermute x5, waiting for transfers between devices, from_offset(): return lax.ppermute(value, ('tm', 'freq'), pairs)  7.74 us
    pallas_call x1, Pallas kernels, shards(): pl.pallas_call(lambda *refs: main_kernel(grad_scale, *refs), out_shape=(p...  6.39 us
    ppermute x3, waiting for transfers between devices, other_core(): lax.ppermute(value, 'tm', [(i, i ^ 1) for i in range(lax.axis_size('tm'))])  5.79 us
    pallas_call x1, Pallas kernels, shards(): pl.pallas_call(plain_back, out_shape=jax.ShapeDtypeStruct((128, D), BF16)...  5.54 us
  transfers between devices with their start and end apart: 13, of which 9 were waited for; matrix products, arithmetic and copies ran while one was open for 0% of the time, Pallas kernels for 10%

profile of v5, /device:TPU:1, one launch (start us, length us, event | category | flops | bytes accessed | tf_op | source)
XLA Modules:
  0.0 145.9 jit_solution(11047569184909235853)
XLA Ops:
  0.6 2.1 %prepare.2 = bf16[8,192,384]{2,1,0:T(8,128)(2,1)} custom-call(s32[1]{0:T(128)} %bitcast.core_ref.refs_0_, bf16[144,768]{1,0:T(8,128)(2,1)} %bitcast.8, bf16[48,768]{1,0:T(8,128)(2,1)} %proj.2), custom_call_target="tpu_custom_call" | custom-call | tf_op jit(solution)/shard_map/prepare/pallas_call | solution.py:455
  2.8 5.9 %all-to-all-start = ((bf16[8,192,384]{2,1,0:T(8,128)(2,1)}), bf16[8,192,384]{2,1,0:T(8,128)(2,1)S(1)}, u32[]{:S(2)}, u32[]{:S(2)}) async-start(bf16[8,192,384]{2,1,0:T(8,128)(2,1)} %prepare.2), calls=%async_computation | async-start | bytes 2359296 | tf_op jit(solution)/shard_map/all_to_all | solution.py:415
  8.7 2.1 %prepare.3 = bf16[8,192,384]{2,1,0:T(8,128)(2,1)} custom-call(s32[1]{0:T(128)} %bitcast.core_ref.refs_0_, bf16[144,768]{1,0:T(8,128)(2,1)} %bitcast.9, bf16[48,768]{1,0:T(8,128)(2,1)} %proj.3), custom_call_target="tpu_custom_call" | custom-call | tf_op jit(solution)/shard_map/prepare/pallas_call | solution.py:455
  10.9 2.0 %biases.1 = (f32[64,768]{1,0:T(8,128)}, f32[64,768]{1,0:T(8,128)}) custom-call(s32[2]{0:T(128)S(1)} %add_convert_fusion.edge_ref, f32[12,225]{1,0:T(8,128)S(1)} %copy-done.2, f32[12,225]{1,0:T(8,128)S(1)} %copy-done.3), custom_call_target="tpu_custom_call" | custom-call | tf_op jit(solution)/shard_map/biases/pallas_call | solution.py:471
  12.8 8.5 %all-to-all-done.w_mine_ref.mine_far = bf16[8,192,384]{2,1,0:T(8,128)(2,1)S(1)} async-done(((bf16[8,192,384]{2,1,0:T(8,128)(2,1)}), bf16[8,192,384]{2,1,0:T(8,128)(2,1)S(1)}, u32[]{:S(2)}, u32[]{:S(2)}) %all-to-all-start) | async-done | bytes 1179680 | tf_op jit(solution)/shard_map/all_to_all | solution.py:415
  21.4 3.9 %all-to-all-start.1 = ((bf16[8,192,384]{2,1,0:T(8,128)(2,1)}), bf16[8,192,384]{2,1,0:T(8,128)(2,1)S(1)}, u32[]{:S(2)}, u32[]{:S(2)}) async-start(bf16[8,192,384]{2,1,0:T(8,128)(2,1)} %prepare.3), calls=%async_computation.1 | async-start | bytes 2359296 | tf_op jit(solution)/shard_map/all_to_all | solution.py:415
  25.2 7.1 %collective-permute-start = (bf16[8,192,384]{2,1,0:T(8,128)(2,1)S(1)}, bf16[8,192,384]{2,1,0:T(8,128)(2,1)S(1)}, u32[]{:S(2)}, u32[]{:S(2)}) collective-permute-start(bf16[8,192,384]{2,1,0:T(8,128)(2,1)S(1)} %all-to-all-done.w_mine_ref.mine_far), channel_id=1, source_target_pairs={{0,8},{8,0},{16,24},{24,16},{32,40},{40,32},{48,56},{56,48},{64,72... | collective-permute-start | bytes 3538952 | tf_op jit(solution)/shard_map/ppermute | solution.py:429
  32.3 2.5 %collective-permute-done.w_other_ref.other_far = bf16[8,192,384]{2,1,0:T(8,128)(2,1)S(1)} collective-permute-done((bf16[8,192,384]{2,1,0:T(8,128)(2,1)S(1)}, bf16[8,192,384]{2,1,0:T(8,128)(2,1)S(1)}, u32[]{:S(2)}, u32[]{:S(2)}) %collective-permute-start) | collective-permute-done | bytes 1179680 | tf_op jit(solution)/shard_map/ppermute | solution.py:429
  34.7 4.5 %plain_forward.1 = (bf16[32,1920]{1,0:T(8,128)(2,1)}, bf16[32,1920]{1,0:T(8,128)(2,1)}, bf16[32,1920]{1,0:T(8,128)(2,1)}, bf16[32,1920]{1,0:T(8,128)(2,1)}) custom-call(s32[1]{0:T(128)} %bitcast.core_ref.refs_0_, bf16[128,768]{1,0:T(8,128)(2,1)} %bitcast.11, bf16[128,768]{1,0:T(8,128)(2,1)} %bitcast.10, f32[64,768]{1,0:T(8,128)} %get-tuple-element.37.bias_far, ...), custom_call_target="tpu_custom_call" | custom-call | flops 1000000 | bytes 1000000 | tf_op jit(solution)/shard_map/plain_forward/pallas_call | solution.py:493
  39.3 2.3 %collective-permute-start.1 = (bf16[32,1920]{1,0:T(8,128)(2,1)}, bf16[32,1920]{1,0:T(8,128)(2,1)S(1)}, u32[]{:S(2)}, u32[]{:S(2)}) collective-permute-start(bf16[32,1920]{1,0:T(8,128)(2,1)} %get-tuple-element.42), channel_id=1, source_target_pairs={{8,0},{9,1},{10,2},{11,3},{12,4},{13,5},{14,6},{15,7},{16,8},{17,9... | collective-permute-start | bytes 368648 | tf_op jit(solution)/shard_map/ppermute | solution.py:425
  41.6 5.7 %collective-permute-start.2 = (bf16[32,1920]{1,0:T(8,128)(2,1)}, bf16[32,1920]{1,0:T(8,128)(2,1)S(1)}, u32[]{:S(2)}, u32[]{:S(2)}) collective-permute-start(bf16[32,1920]{1,0:T(8,128)(2,1)} %get-tuple-element.43), channel_id=1, source_target_pairs={{1,0},{2,1},{3,2},{4,3},{5,4},{6,5},{7,6},{0,7},{9,8},{10,9},{11,1... | collective-permute-start | bytes 368648 | tf_op jit(solution)/shard_map/ppermute | solution.py:425
  47.3 13.9 %collective-permute-start.3 = (bf16[32,1920]{1,0:T(8,128)(2,1)}, bf16[32,1920]{1,0:T(8,128)(2,1)S(1)}, u32[]{:S(2)}, u32[]{:S(2)}) collective-permute-start(bf16[32,1920]{1,0:T(8,128)(2,1)} %get-tuple-element.44), channel_id=1, source_target_pairs={{9,0},{10,1},{11,2},{12,3},{13,4},{14,5},{15,6},{8,7},{17,8},{18,9... | collective-permute-start | bytes 368648 | tf_op jit(solution)/shard_map/ppermute | solution.py:425
  61.2 2.1 %collective-permute-done.3.refs_5_ = bf16[32,1920]{1,0:T(8,128)(2,1)S(1)} collective-permute-done((bf16[32,1920]{1,0:T(8,128)(2,1)}, bf16[32,1920]{1,0:T(8,128)(2,1)S(1)}, u32[]{:S(2)}, u32[]{:S(2)}) %collective-permute-start.3) | collective-permute-done | bytes 122912 | tf_op jit(solution)/shard_map/ppermute | solution.py:425
  63.3 5.3 %collective-permute-start.4 = (bf16[8,192,384]{2,1,0:T(8,128)(2,1)S(1)}, bf16[8,192,384]{2,1,0:T(8,128)(2,1)S(1)}, u32[]{:S(2)}, u32[]{:S(2)}) collective-permute-start(bf16[8,192,384]{2,1,0:T(8,128)(2,1)S(1)} %all-to-all-done.1.refs_6_), channel_id=1, source_target_pairs={{0,8},{8,0},{16,24},{24,16},{32,40},{40,32},{48,56},{56,48},{64,72... | collective-permute-start | bytes 3538952 | tf_op jit(solution)/shard_map/ppermute | solution.py:429
  68.6 2.5 %collective-permute-done.4.refs_7_ = bf16[8,192,384]{2,1,0:T(8,128)(2,1)S(1)} collective-permute-done((bf16[8,192,384]{2,1,0:T(8,128)(2,1)S(1)}, bf16[8,192,384]{2,1,0:T(8,128)(2,1)S(1)}, u32[]{:S(2)}, u32[]{:S(2)}) %collective-permute-start.4) | collective-permute-done | bytes 1179680 | tf_op jit(solution)/shard_map/ppermute | solution.py:429
  71.1 6.4 %main.1 = (bf16[32,768]{1,0:T(8,128)(2,1)}, bf16[64,768]{1,0:T(8,128)(2,1)}, bf16[32,768]{1,0:T(8,128)(2,1)}, bf16[8,2,48,768]{3,2,1,0:T(8,128)(2,1)}) custom-call(s32[1]{0:T(128)} %bitcast.core_ref.refs_0_, bf16[32,1920]{1,0:T(8,128)(2,1)} %get-tuple-element.39.refs_1_, f32[64,768]{1,0:T(8,128)} %get-tuple-element.40.refs_2_, ...), custom_call_target="tpu_custom_call" | custom-call | flops 1000000 | bytes 1000000 | tf_op jit(solution)/shard_map/main/pallas_call | solution.py:522
  77.5 3.7 %all-to-all-start.2 = ((bf16[8,2,48,768]{3,2,1,0:T(8,128)(2,1)}), bf16[8,2,48,768]{3,2,1,0:T(8,128)(2,1)S(1)}, u32[]{:S(2)}, u32[]{:S(2)}) async-start(bf16[8,2,48,768]{3,2,1,0:T(8,128)(2,1)} %get-tuple-element.52), calls=%async_computation.2 | async-start | bytes 2359296 | tf_op jit(solution)/shard_map/all_to_all | solution.py:415
  81.2 1.9 %collective-permute-start.6 = (bf16[64,768]{1,0:T(8,128)(2,1)S(1)}, bf16[64,768]{1,0:T(8,128)(2,1)S(1)}, u32[]{:S(2)}, u32[]{:S(2)}) collective-permute-start(bf16[64,768]{1,0:T(8,128)(2,1)S(1)} %copy-done.5), channel_id=1, source_target_pairs={{504,0},{505,1},{506,2},{507,3},{508,4},{509,5},{510,6},{511,7},{0... | collective-permute-start | bytes 294920 | tf_op jit(solution)/shard_map/ppermute | solution.py:425
  83.2 14.9 %all-to-all-done.2.parts = bf16[8,2,48,768]{3,2,1,0:T(8,128)(2,1)S(1)} async-done(((bf16[8,2,48,768]{3,2,1,0:T(8,128)(2,1)}), bf16[8,2,48,768]{3,2,1,0:T(8,128)(2,1)S(1)}, u32[]{:S(2)}, u32[]{:S(2)}) %all-to-all-start.2) | async-done | bytes 1179680 | tf_op jit(solution)/shard_map/all_to_all | solution.py:415
  98.3 3.2 %collective-permute-start.5 = (bf16[2,48,384]{2,1,0:T(8,128)(2,1)S(1)}, bf16[2,48,384]{2,1,0:T(8,128)(2,1)S(1)}, u32[]{:S(2)}, u32[]{:S(2)}) collective-permute-start(bf16[2,48,384]{2,1,0:T(8,128)(2,1)S(1)} %get-tuple-element.54), channel_id=1, source_target_pairs={{0,8},{8,0},{16,24},{24,16},{32,40},{40,32},{48,56},{56,48},{64,72... | collective-permute-start | bytes 221192 | tf_op jit(solution)/shard_map/ppermute | solution.py:429
  101.5 0.9 collective-permute-done.5.arrived
  102.4 0.9 pair_copies.1
  103.3 3.5 %all-to-all-start.3 = ((bf16[8,2,48,384]{3,2,1,0:T(8,128)(2,1)}), bf16[8,2,48,384]{3,2,1,0:T(8,128)(2,1)S(1)}, u32[]{:S(2)}, u32[]{:S(2)}) async-start(bf16[8,2,48,384]{3,2,1,0:T(8,128)(2,1)} %pair_copies.1), calls=%async_computation.3 | async-start | bytes 1179648 | tf_op jit(solution)/shard_map/all_to_all | solution.py:415
  106.9 2.4 %collective-permute-start.7 = (bf16[64,768]{1,0:T(8,128)(2,1)S(1)}, bf16[64,768]{1,0:T(8,128)(2,1)S(1)}, u32[]{:S(2)}, u32[]{:S(2)}) collective-permute-start(bf16[64,768]{1,0:T(8,128)(2,1)S(1)} %pad_maximum_fusion), channel_id=1, source_target_pairs={{7,0},{0,1},{1,2},{2,3},{3,4},{4,5},{5,6},{6,7},{15,8},{8,9},{9,10... | collective-permute-start | bytes 294920 | tf_op jit(solution)/shard_map/ppermute | solution.py:425
  109.3 5.6 %collective-permute-done.7.row = bf16[64,768]{1,0:T(8,128)(2,1)S(1)} collective-permute-done((bf16[64,768]{1,0:T(8,128)(2,1)S(1)}, bf16[64,768]{1,0:T(8,128)(2,1)S(1)}, u32[]{:S(2)}, u32[]{:S(2)}) %collective-permute-start.7) | collective-permute-done | bytes 98336 | tf_op jit(solution)/shard_map/ppermute | solution.py:425
  114.9 11.3 %all-to-all-done.3.parts = bf16[8,2,48,384]{3,2,1,0:T(8,128)(2,1)S(1)} async-done(((bf16[8,2,48,384]{3,2,1,0:T(8,128)(2,1)}), bf16[8,2,48,384]{3,2,1,0:T(8,128)(2,1)S(1)}, u32[]{:S(2)}, u32[]{:S(2)}) %all-to-all-start.3) | async-done | bytes 589856 | tf_op jit(solution)/shard_map/all_to_all | solution.py:415
  126.2 0.8 sum_copies.2
  127.0 4.5 %all-to-all-start.4 = ((bf16[4,2,48,384]{3,2,1,0:T(8,128)(2,1)}), bf16[4,2,48,384]{3,2,1,0:T(8,128)(2,1)S(1)}, u32[]{:S(2)}, u32[]{:S(2)}) async-start(bf16[4,2,48,384]{3,2,1,0:T(8,128)(2,1)} %sum_copies.2), calls=%async_computation.4 | async-start | bytes 589824 | tf_op jit(solution)/shard_map/all_to_all | solution.py:415
  131.5 5.5 %plain_back.1 = bf16[128,768]{1,0:T(8,128)(2,1)} custom-call(s32[1]{0:T(128)} %bitcast.core_ref.refs_0_, bf16[128,768]{1,0:T(8,128)(2,1)} %bitcast.12, bf16[32,768]{1,0:T(8,128)(2,1)} %get-tuple-element.61.own_far, f32[64,768]{1,0:T(8,128)} %get-tuple-element.37.bias_far, bf16[8,192,384]{2,1,0:T(8,128)(2,1)} %copy-done, bf16[8,192,384]{2,1,0:T(8,128)(2,1)} %copy-done.1, ...), custom_call_target="tpu_custom_call" | custom-call | flops 4000000000 | bytes 4000000 | tf_op jit(solution)/shard_map/plain_back/pallas_call | solution.py:569
  137.0 3.4 %all-to-all-done.4.parts = bf16[4,2,48,384]{3,2,1,0:T(8,128)(2,1)S(1)} async-done(((bf16[4,2,48,384]{3,2,1,0:T(8,128)(2,1)}), bf16[4,2,48,384]{3,2,1,0:T(8,128)(2,1)S(1)}, u32[]{:S(2)}, u32[]{:S(2)}) %all-to-all-start.4) | async-done | bytes 294944 | tf_op jit(solution)/shard_map/all_to_all | solution.py:415
  140.5 4.7 %all_gather.3.parts = bf16[2,2,48,384]{3,2,1,0:T(8,128)(2,1)S(1)} all-gather(bf16[1,2,48,384]{3,2,1,0:T(8,128)(2,1)S(1)} %sum_copies.3), channel_id=1, replica_groups={{0,8},{16,24},{32,40},{48,56},{64,72},{80,88},{96,104},{112,120},{128,1..., dimensions={0}, use_global_device_ids=true | all-gather | bytes 221184 | tf_op jit(solution)/shard_map/all_gather | solution.py:592
  145.2 0.7 finish.1
  (21 shorter events, 0.4 us)
Async XLA Ops:
  2.8 18.6 %all-to-all-start = ((bf16[8,192,384]{2,1,0:T(8,128)(2,1)}), bf16[8,192,384]{2,1,0:T(8,128)(2,1)S(1)}, u32[]{:S(2)}, u32[]{:S(2)}) async-start(bf16[8,192,384]{2,1,0:T(8,128)(2,1)} %prepare.2), calls=%async_computation | async-start | bytes 2359296 | tf_op jit(solution)/shard_map/all_to_all | solution.py:415
  8.7 2.2 %copy-start.2 = (f32[12,225]{1,0:T(8,128)S(1)}, f32[12,225]{1,0:T(8,128)}, u32[]{:S(2)}) copy-start(f32[12,225]{1,0:T(8,128)} %table_p.1) | copy-start | bytes 32404
  8.7 2.2 %copy-start.3 = (f32[12,225]{1,0:T(8,128)S(1)}, f32[12,225]{1,0:T(8,128)}, u32[]{:S(2)}) copy-start(f32[12,225]{1,0:T(8,128)} %table_s.1) | copy-start | bytes 32404
  21.4 13.4 %copy-start = (bf16[8,192,384]{2,1,0:T(8,128)(2,1)}, bf16[8,192,384]{2,1,0:T(8,128)(2,1)S(1)}, u32[]{:S(2)}) copy-start(bf16[8,192,384]{2,1,0:T(8,128)(2,1)S(1)} %all-to-all-done.w_mine_ref.mine_far) | copy-start | bytes 3538948
  21.4 42.0 %all-to-all-start.1 = ((bf16[8,192,384]{2,1,0:T(8,128)(2,1)}), bf16[8,192,384]{2,1,0:T(8,128)(2,1)S(1)}, u32[]{:S(2)}, u32[]{:S(2)}) async-start(bf16[8,192,384]{2,1,0:T(8,128)(2,1)} %prepare.3), calls=%async_computation.1 | async-start | bytes 2359296 | tf_op jit(solution)/shard_map/all_to_all | solution.py:415
  25.2 9.5 %collective-permute-start = (bf16[8,192,384]{2,1,0:T(8,128)(2,1)S(1)}, bf16[8,192,384]{2,1,0:T(8,128)(2,1)S(1)}, u32[]{:S(2)}, u32[]{:S(2)}) collective-permute-start(bf16[8,192,384]{2,1,0:T(8,128)(2,1)S(1)} %all-to-all-done.w_mine_ref.mine_far), channel_id=1, source_target_pairs={{0,8},{8,0},{16,24},{24,16},{32,40},{40,32},{48,56},{56,48},{64,72... | collective-permute-start | bytes 3538952 | tf_op jit(solution)/shard_map/ppermute | solution.py:429
  34.7 4.5 %copy-start.1 = (bf16[8,192,384]{2,1,0:T(8,128)(2,1)}, bf16[8,192,384]{2,1,0:T(8,128)(2,1)S(1)}, u32[]{:S(2)}) copy-start(bf16[8,192,384]{2,1,0:T(8,128)(2,1)S(1)} %collective-permute-done.w_other_ref.other_far) | copy-start | bytes 3538948
  39.3 21.9 %collective-permute-start.1 = (bf16[32,1920]{1,0:T(8,128)(2,1)}, bf16[32,1920]{1,0:T(8,128)(2,1)S(1)}, u32[]{:S(2)}, u32[]{:S(2)}) collective-permute-start(bf16[32,1920]{1,0:T(8,128)(2,1)} %get-tuple-element.42), channel_id=1, source_target_pairs={{8,0},{9,1},{10,2},{11,3},{12,4},{13,5},{14,6},{15,7},{16,8},{17,9... | collective-permute-start | bytes 368648 | tf_op jit(solution)/shard_map/ppermute | solution.py:425
  41.6 19.6 %collective-permute-start.2 = (bf16[32,1920]{1,0:T(8,128)(2,1)}, bf16[32,1920]{1,0:T(8,128)(2,1)S(1)}, u32[]{:S(2)}, u32[]{:S(2)}) collective-permute-start(bf16[32,1920]{1,0:T(8,128)(2,1)} %get-tuple-element.43), channel_id=1, source_target_pairs={{1,0},{2,1},{3,2},{4,3},{5,4},{6,5},{7,6},{0,7},{9,8},{10,9},{11,1... | collective-permute-start | bytes 368648 | tf_op jit(solution)/shard_map/ppermute | solution.py:425
  47.3 16.1 %collective-permute-start.3 = (bf16[32,1920]{1,0:T(8,128)(2,1)}, bf16[32,1920]{1,0:T(8,128)(2,1)S(1)}, u32[]{:S(2)}, u32[]{:S(2)}) collective-permute-start(bf16[32,1920]{1,0:T(8,128)(2,1)} %get-tuple-element.44), channel_id=1, source_target_pairs={{9,0},{10,1},{11,2},{12,3},{13,4},{14,5},{15,6},{8,7},{17,8},{18,9... | collective-permute-start | bytes 368648 | tf_op jit(solution)/shard_map/ppermute | solution.py:425
  63.3 7.8 %collective-permute-start.4 = (bf16[8,192,384]{2,1,0:T(8,128)(2,1)S(1)}, bf16[8,192,384]{2,1,0:T(8,128)(2,1)S(1)}, u32[]{:S(2)}, u32[]{:S(2)}) collective-permute-start(bf16[8,192,384]{2,1,0:T(8,128)(2,1)S(1)} %all-to-all-done.1.refs_6_), channel_id=1, source_target_pairs={{0,8},{8,0},{16,24},{24,16},{32,40},{40,32},{48,56},{56,48},{64,72... | collective-permute-start | bytes 3538952 | tf_op jit(solution)/shard_map/ppermute | solution.py:429
  77.5 3.7 %copy-start.5 = (bf16[64,768]{1,0:T(8,128)(2,1)S(1)}, bf16[64,768]{1,0:T(8,128)(2,1)}, u32[]{:S(2)}) copy-start(bf16[64,768]{1,0:T(8,128)(2,1)} %get-tuple-element.55) | copy-start | bytes 294916
  77.5 20.6 %all-to-all-start.2 = ((bf16[8,2,48,768]{3,2,1,0:T(8,128)(2,1)}), bf16[8,2,48,768]{3,2,1,0:T(8,128)(2,1)S(1)}, u32[]{:S(2)}, u32[]{:S(2)}) async-start(bf16[8,2,48,768]{3,2,1,0:T(8,128)(2,1)} %get-tuple-element.52), calls=%async_computation.2 | async-start | bytes 2359296 | tf_op jit(solution)/shard_map/all_to_all | solution.py:415
  81.2 22.1 %collective-permute-start.6 = (bf16[64,768]{1,0:T(8,128)(2,1)S(1)}, bf16[64,768]{1,0:T(8,128)(2,1)S(1)}, u32[]{:S(2)}, u32[]{:S(2)}) collective-permute-start(bf16[64,768]{1,0:T(8,128)(2,1)S(1)} %copy-done.5), channel_id=1, source_target_pairs={{504,0},{505,1},{506,2},{507,3},{508,4},{509,5},{510,6},{511,7},{0... | collective-permute-start | bytes 294920 | tf_op jit(solution)/shard_map/ppermute | solution.py:425
  98.3 8.6 %copy-start.4 = (bf16[32,768]{1,0:T(8,128)(2,1)S(1)}, bf16[32,768]{1,0:T(8,128)(2,1)}, u32[]{:S(2)}) copy-start(bf16[32,768]{1,0:T(8,128)(2,1)} %get-tuple-element.58) | copy-start | bytes 147460
  98.3 4.1 %collective-permute-start.5 = (bf16[2,48,384]{2,1,0:T(8,128)(2,1)S(1)}, bf16[2,48,384]{2,1,0:T(8,128)(2,1)S(1)}, u32[]{:S(2)}, u32[]{:S(2)}) collective-permute-start(bf16[2,48,384]{2,1,0:T(8,128)(2,1)S(1)} %get-tuple-element.54), channel_id=1, source_target_pairs={{0,8},{8,0},{16,24},{24,16},{32,40},{40,32},{48,56},{56,48},{64,72... | collective-permute-start | bytes 221192 | tf_op jit(solution)/shard_map/ppermute | solution.py:429
  103.3 22.9 %all-to-all-start.3 = ((bf16[8,2,48,384]{3,2,1,0:T(8,128)(2,1)}), bf16[8,2,48,384]{3,2,1,0:T(8,128)(2,1)S(1)}, u32[]{:S(2)}, u32[]{:S(2)}) async-start(bf16[8,2,48,384]{3,2,1,0:T(8,128)(2,1)} %pair_copies.1), calls=%async_computation.3 | async-start | bytes 1179648 | tf_op jit(solution)/shard_map/all_to_all | solution.py:415
  106.9 8.0 %collective-permute-start.7 = (bf16[64,768]{1,0:T(8,128)(2,1)S(1)}, bf16[64,768]{1,0:T(8,128)(2,1)S(1)}, u32[]{:S(2)}, u32[]{:S(2)}) collective-permute-start(bf16[64,768]{1,0:T(8,128)(2,1)S(1)} %pad_maximum_fusion), channel_id=1, source_target_pairs={{7,0},{0,1},{1,2},{2,3},{3,4},{4,5},{5,6},{6,7},{15,8},{8,9},{9,10... | collective-permute-start | bytes 294920 | tf_op jit(solution)/shard_map/ppermute | solution.py:425
  127.0 13.4 %all-to-all-start.4 = ((bf16[4,2,48,384]{3,2,1,0:T(8,128)(2,1)}), bf16[4,2,48,384]{3,2,1,0:T(8,128)(2,1)S(1)}, u32[]{:S(2)}, u32[]{:S(2)}) async-start(bf16[4,2,48,384]{3,2,1,0:T(8,128)(2,1)} %sum_copies.2), calls=%async_computation.4 | async-start | bytes 589824 | tf_op jit(solution)/shard_map/all_to_all | solution.py:415

commit v6 on v5

--- a/solution.py
+++ b/solution.py
@@ -109,11 +109,13 @@
         move.wait()
 
 
-def prepare(core_ref, qkv, proj, out, block, sems):
+def prepare(core_ref, qkv, proj, out, sems):
     start = pl.multiple_of(core_ref[0] * HALF, 128)
-    block[0:SHARE] = qkv[:, pl.ds(start, HALF)]
-    block[SHARE : SHARE + ROWS] = proj[:, pl.ds(start, HALF)]
-    wait_all(copy_all([(block, out.at[i]) for i in range(8)], sems))
+    pairs = []
+    for i in range(8):
+        pairs.append((qkv.at[:, pl.ds(start, HALF)], out.at[i, 0:SHARE]))
+        pairs.append((proj.at[:, pl.ds(start, HALF)], out.at[i, SHARE : SHARE + ROWS]))
+    wait_all(copy_all(pairs, sems))
 
 
 def biases(edge_ref, table_p, table_s, to_p, to_s, out_p, out_s, tables, wide, sems):
@@ -192,7 +194,8 @@
     tok,
     cot,
     bias_p,
-    packets,
+    own,
+    above,
     rows,
     sums,
     mask,
@@ -220,9 +223,10 @@
     pick = quadrant_pick()
     loads[2].wait()
     for whole, first in ((block_out, 0), (mixed, D), (cot[...], D + WIDE)):
-        packets[:, first : first + whole.shape[1]] = dot(pick, whole).astype(BF16)
-    outs = (out_d, out_b, out_r, out_o)
-    wait_all(copy_all([(packets.at[i * 32 : (i + 1) * 32], out) for i, out in enumerate(outs)], sems, 3))
+        quads = dot(pick, whole).astype(BF16)
+        for i, out in enumerate((out_d, above, out_r, own)):
+            out[:, first : first + whole.shape[1]] = quads[i * 32 : (i + 1) * 32]
+    wait_all(copy_all([(own, out_o), (above, out_b)], sems, 3))
 
 
 def main_kernel(
@@ -241,7 +245,8 @@
     to_local,
     bias_s,
     quads,
-    out_local,
+    out_plain,
+    out_shift,
     staged,
     rows_small,
     grads,
@@ -264,18 +269,24 @@
     w_mine, w_other = qkv_of(w_mine_ref), qkv_of(w_other_ref)
     packed = project(rows_small, w_mine, w_other, mine, other).astype(BF16)
     d_mixed = project(grads, proj_of(w_mine_ref), proj_of(w_other_ref), mine, other).astype(BF16)
-    mixed, d_packed = [], []
+    mixed, forward, d_packed = [], [], []
     for s in range(2):
         part = packed[s * SPOTS : (s + 1) * SPOTS]
         query, key, value = part[:, :WIDE], part[:, WIDE : 2 * WIDE], part[:, 2 * WIDE :]
         query_wide = expand(query, mask)
         probs = softmax_down(dot(key, query_wide, NT) * SCALE + bias_s[...])
         mixed.append(fold(dot(probs.astype(BF16), value, TN)).astype(BF16))
+        forward.append((query, key, value, query_wide, probs))
+    mixed_shift = jnp.concatenate(mixed, axis=0)
+    local_shift = dot(mixed_shift, grads[...], TN) * grad_scale
+    out_shift[...] = local_shift.astype(BF16).reshape(8, ROWS, D)
+    early = copy_all([(out_shift, to_local.at[:, 1])], sems, 6)
+    for s in range(2):
+        query, key, value, query_wide, probs = forward[s]
         back = attention_back(
             query, key, value, d_mixed[s * SPOTS : (s + 1) * SPOTS], probs, query_wide, mask
         )
         d_packed.append(jnp.concatenate(back, axis=1))
-    mixed_shift = jnp.concatenate(mixed, axis=0)
     d_packed = jnp.concatenate(d_packed, axis=0)
     grad = input_grad(
         grads[...].astype(F32), normed, rstd, d_packed, w_mine, w_other, mine, other, sums
@@ -291,12 +302,10 @@
         sems,
         2,
     )
-    local_shift = dot(mixed_shift, grads[...], TN) * grad_scale
-    out_local[:, 1] = local_shift.astype(BF16).reshape(8, ROWS, D)
     local_plain = dot(mixed_plain, grad, TN) * grad_scale
-    out_local[:, 0] = local_plain.astype(BF16).reshape(8, ROWS, D)
-    wait_all(copy_all([(out_local, to_local)], sems, 6))
-    wait_all(stores)
+    out_plain[...] = local_plain.astype(BF16).reshape(8, ROWS, D)
+    stores += copy_all([(out_plain, to_local.at[:, 0])], sems, 7)
+    wait_all(stores + early)
 
 
 def sum_split(core_ref, parts, out_keep, out_send, total):
@@ -455,15 +464,12 @@
         return pl.pallas_call(
             prepare,
             out_shape=pltpu.HBM((8, SHARE + ROWS, HALF), BF16),
-            in_specs=[SMEM, VMEM, VMEM],
+            in_specs=[SMEM, HBM, HBM],
             out_specs=HBM,
-            scratch_shapes=[
-                pltpu.VMEM((SHARE + ROWS, HALF), BF16),
-                pltpu.SemaphoreType.DMA((8,)),
-            ],
-            compiler_params=params(60),
+            scratch_shapes=[pltpu.SemaphoreType.DMA((16,))],
+            compiler_params=params(),
             name="prepare",
-        )(core, qkv.T, proj)
+        )(core, far(qkv.T), far(proj))
 
     first_mine = swap(share(qkv_plain, proj_plain), "freq")
     second_share = share(qkv_shift, proj_shift)
@@ -487,23 +493,25 @@
     first_mine, second_share, bias_p, bias_s = lax.optimization_barrier(
         (first_mine, second_share, bias_p, bias_s)
     )
+    first_other = other_core(first_mine)
     second_mine = swap(second_share, "freq")
-    first_other = other_core(first_mine)
     packet = pltpu.HBM((32, 2 * D + WIDE), BF16)
+    near = jax.ShapeDtypeStruct((32, 2 * D + WIDE), BF16)
     own, to_left, to_above, to_diag = pl.pallas_call(
         plain_forward,
-        out_shape=(packet,) * 4,
+        out_shape=(packet, near, packet, near),
         in_specs=[SMEM] + [HBM] * 3 + [VMEM] * 2,
-        out_specs=[HBM] * 4,
+        out_specs=[HBM, VMEM, HBM, VMEM],
         scratch_shapes=[
             pltpu.VMEM((128, D), BF16),
             pltpu.VMEM((128, D), BF16),
             pltpu.VMEM((SPOTS, LANES), F32),
-            pltpu.VMEM((128, 2 * D + WIDE), BF16),
+            pltpu.VMEM((32, 2 * D + WIDE), BF16),
+            pltpu.VMEM((32, 2 * D + WIDE), BF16),
             pltpu.VMEM((128, D), BF16),
             pltpu.VMEM((128, D), F32),
             pltpu.VMEM((LANES, WIDE), BF16),
-            pltpu.SemaphoreType.DMA((7,)),
+            pltpu.SemaphoreType.DMA((5,)),
         ],
         compiler_params=params(),
         cost_estimate=cost(1_000_000, 1_000_000),
@@ -512,9 +520,7 @@
     right = from_offset(to_left, 1, 0)
     below = from_offset(to_above, 0, 1)
     diag = from_offset(to_diag, 1, 1)
-    second_mine, right, below, diag = lax.optimization_barrier(
-        (second_mine, right, below, diag)
-    )
+    second_mine, right, diag = lax.optimization_barrier((second_mine, right, diag))
     second_other = other_core(second_mine)
     piece = pltpu.HBM((32, D), BF16)
     column = pltpu.HBM((64, D), BF16)
@@ -527,13 +533,14 @@
         scratch_shapes=[
             pltpu.VMEM((SPOTS, LANES), F32),
             pltpu.VMEM((128, D), BF16),
-            pltpu.VMEM((8, 2, ROWS, D), BF16),
+            pltpu.VMEM((8, ROWS, D), BF16),
+            pltpu.VMEM((8, ROWS, D), BF16),
             pltpu.VMEM((128, 2 * D + WIDE), BF16),
             pltpu.VMEM((128, D), BF16),
             pltpu.VMEM((128, D), BF16),
             pltpu.VMEM((128, D), F32),
             pltpu.VMEM((LANES, WIDE), BF16),
-            pltpu.SemaphoreType.DMA((7,)),
+            pltpu.SemaphoreType.DMA((8,)),
         ],
         compiler_params=params(),
         cost_estimate=cost(1_000_000, 1_000_000),

time: 147 us -> 208 us (1.41)
  Pallas kernels: 25.3 us -> 95.1 us
  waiting for transfers between devices: 51.6 us -> 43.4 us
    pallas_call x2, Pallas kernels: 4.22 us -> 74 us  [share(): pl.pallas_call(prepare, out_shape=pltpu.HBM((8, SHARE + ROWS, HALF), BF16...]
    all_to_all x5, waiting for transfers between devices: 38.1 us -> 29.6 us  [swap(): return lax.all_to_all(value, axis, 0, 0, axis_index_groups=groups)]
    ppermute x5, waiting for transfers between devices: 7.74 us -> 10.4 us  [from_offset(): return lax.ppermute(value, ('tm', 'freq'), pairs)]
    ppermute x3, waiting for transfers between devices: 5.79 us -> 3.35 us  [other_core(): lax.ppermute(value, 'tm', [(i, i ^ 1) for i in range(lax.axis_size('tm'))])]
    all_to_all x5, starting transfers between devices: 21.5 us -> 23.6 us  [swap(): return lax.all_to_all(value, axis, 0, 0, axis_index_groups=groups)]
    ppermute x3, starting transfers between devices: 15.6 us -> 13.5 us  [other_core(): lax.ppermute(value, 'tm', [(i, i ^ 1) for i in range(lax.axis_size('tm'))])]
  transfers between devices with their start and end apart: 13 -> 13, of which waited for: 9 -> 8; matrix products, arithmetic and copies ran while one was open for 0% -> 0% of each run, Pallas kernels for 10% -> 24%
where the time goes in v6:
time: 208 us; the launch traced here: 207 us
  Pallas kernels  95.1 us (46%)
  starting transfers between devices  63.7 us (31%)
  waiting for transfers between devices  43.4 us (21%)
  blocking collectives  3.55 us (2%)
    pallas_call x2, Pallas kernels, share(): pl.pallas_call(prepare, out_shape=pltpu.HBM((8, SHARE + ROWS, HALF), BF16...  74 us
    all_to_all x5, waiting for transfers between devices, swap(): return lax.all_to_all(value, axis, 0, 0, axis_index_groups=groups)  29.6 us
    ppermute x5, starting transfers between devices, from_offset(): return lax.ppermute(value, ('tm', 'freq'), pairs)  26.6 us
    all_to_all x5, starting transfers between devices, swap(): return lax.all_to_all(value, axis, 0, 0, axis_index_groups=groups)  23.6 us
    ppermute x3, starting transfers between devices, other_core(): lax.ppermute(value, 'tm', [(i, i ^ 1) for i in range(lax.axis_size('tm'))])  13.5 us
    ppermute x5, waiting for transfers between devices, from_offset(): return lax.ppermute(value, ('tm', 'freq'), pairs)  10.4 us
    pallas_call x1, Pallas kernels, shards(): pl.pallas_call(lambda *refs: main_kernel(grad_scale, *refs), out_shape=(p...  6.54 us
    pallas_call x1, Pallas kernels, shards(): pl.pallas_call(plain_back, out_shape=jax.ShapeDtypeStruct((128, D), BF16)...  5.55 us
  transfers between devices with their start and end apart: 13, of which 8 were waited for; matrix products, arithmetic and copies ran while one was open for 0% of the time, Pallas kernels for 24%

profile of v6, /device:TPU:1, one launch (start us, length us, event | category | flops | bytes accessed | tf_op | source)
XLA Modules:
  0.0 206.8 jit_solution(3057213175647338827)
XLA Ops:
  0.6 37.0 %prepare.2 = bf16[8,192,384]{2,1,0:T(8,128)(2,1)} custom-call(s32[1]{0:T(128)} %bitcast.core_ref.refs_0_, bf16[144,768]{1,0:T(8,128)(2,1)} %bitcast.8, bf16[48,768]{1,0:T(8,128)(2,1)} %proj.2), custom_call_target="tpu_custom_call" | custom-call | tf_op jit(solution)/shard_map/prepare/pallas_call | solution.py:464
  37.6 5.9 %all-to-all-start = ((bf16[8,192,384]{2,1,0:T(8,128)(2,1)}), bf16[8,192,384]{2,1,0:T(8,128)(2,1)S(1)}, u32[]{:S(2)}, u32[]{:S(2)}) async-start(bf16[8,192,384]{2,1,0:T(8,128)(2,1)} %prepare.2), calls=%async_computation | async-start | bytes 2359296 | tf_op jit(solution)/shard_map/all_to_all | solution.py:424
  43.5 37.0 %prepare.3 = bf16[8,192,384]{2,1,0:T(8,128)(2,1)} custom-call(s32[1]{0:T(128)} %bitcast.core_ref.refs_0_, bf16[144,768]{1,0:T(8,128)(2,1)} %bitcast.9, bf16[48,768]{1,0:T(8,128)(2,1)} %proj.3), custom_call_target="tpu_custom_call" | custom-call | tf_op jit(solution)/shard_map/prepare/pallas_call | solution.py:464
  80.6 2.0 biases.1
  82.6 5.1 %all-to-all-start.1 = ((bf16[8,192,384]{2,1,0:T(8,128)(2,1)}), bf16[8,192,384]{2,1,0:T(8,128)(2,1)S(1)}, u32[]{:S(2)}, u32[]{:S(2)}) async-start(bf16[8,192,384]{2,1,0:T(8,128)(2,1)} %prepare.3), calls=%async_computation.1 | async-start | bytes 2359296 | tf_op jit(solution)/shard_map/all_to_all | solution.py:424
  87.7 7.0 %collective-permute-start = (bf16[8,192,384]{2,1,0:T(8,128)(2,1)S(1)}, bf16[8,192,384]{2,1,0:T(8,128)(2,1)S(1)}, u32[]{:S(2)}, u32[]{:S(2)}) collective-permute-start(bf16[8,192,384]{2,1,0:T(8,128)(2,1)S(1)} %all-to-all-done.w_mine_ref.mine_far), channel_id=1, source_target_pairs={{0,8},{8,0},{16,24},{24,16},{32,40},{40,32},{48,56},{56,48},{64,72... | collective-permute-start | bytes 3538952 | tf_op jit(solution)/shard_map/ppermute | solution.py:438
  94.7 2.5 %collective-permute-done.w_other_ref.other_far = bf16[8,192,384]{2,1,0:T(8,128)(2,1)S(1)} collective-permute-done((bf16[8,192,384]{2,1,0:T(8,128)(2,1)S(1)}, bf16[8,192,384]{2,1,0:T(8,128)(2,1)S(1)}, u32[]{:S(2)}, u32[]{:S(2)}) %collective-permute-start) | collective-permute-done | bytes 1179680 | tf_op jit(solution)/shard_map/ppermute | solution.py:438
  97.2 4.4 %plain_forward.1 = (bf16[32,1920]{1,0:T(8,128)(2,1)}, bf16[32,1920]{1,0:T(8,128)(2,1)S(1)}, bf16[32,1920]{1,0:T(8,128)(2,1)}, bf16[32,1920]{1,0:T(8,128)(2,1)S(1)}) custom-call(s32[1]{0:T(128)} %bitcast.core_ref.refs_0_, bf16[128,768]{1,0:T(8,128)(2,1)} %bitcast.11, bf16[128,768]{1,0:T(8,128)(2,1)} %bitcast.10, f32[64,768]{1,0:T(8,128)} %get-tuple-element.36.bias_far, ...), custom_call_target="tpu_custom_call" | custom-call | flops 1000000 | bytes 1000000 | tf_op jit(solution)/shard_map/plain_forward/pallas_call | solution.py:500
  101.6 2.3 %collective-permute-start.1 = (bf16[32,1920]{1,0:T(8,128)(2,1)S(1)}, bf16[32,1920]{1,0:T(8,128)(2,1)S(1)}, u32[]{:S(2)}, u32[]{:S(2)}) collective-permute-start(bf16[32,1920]{1,0:T(8,128)(2,1)S(1)} %get-tuple-element.41), channel_id=1, source_target_pairs={{8,0},{9,1},{10,2},{11,3},{12,4},{13,5},{14,6},{15,7},{16,8},{17,9... | collective-permute-start | bytes 368648 | tf_op jit(solution)/shard_map/ppermute | solution.py:434
  103.9 13.7 %collective-permute-start.2 = (bf16[32,1920]{1,0:T(8,128)(2,1)S(1)}, bf16[32,1920]{1,0:T(8,128)(2,1)S(1)}, u32[]{:S(2)}, u32[]{:S(2)}) collective-permute-start(bf16[32,1920]{1,0:T(8,128)(2,1)S(1)} %get-tuple-element.42), channel_id=1, source_target_pairs={{9,0},{10,1},{11,2},{12,3},{13,4},{14,5},{15,6},{8,7},{17,8},{18,9... | collective-permute-start | bytes 368648 | tf_op jit(solution)/shard_map/ppermute | solution.py:434
  117.6 1.8 collective-permute-done.2.refs_5_
  119.5 2.2 %collective-permute-start.4 = (bf16[8,192,384]{2,1,0:T(8,128)(2,1)S(1)}, bf16[8,192,384]{2,1,0:T(8,128)(2,1)S(1)}, u32[]{:S(2)}, u32[]{:S(2)}) collective-permute-start(bf16[8,192,384]{2,1,0:T(8,128)(2,1)S(1)} %all-to-all-done.1.refs_6_), channel_id=1, source_target_pairs={{0,8},{8,0},{16,24},{24,16},{32,40},{40,32},{48,56},{56,48},{64,72... | collective-permute-start | bytes 3538952 | tf_op jit(solution)/shard_map/ppermute | solution.py:438
  121.7 6.3 %collective-permute-start.3 = (bf16[32,1920]{1,0:T(8,128)(2,1)}, bf16[32,1920]{1,0:T(8,128)(2,1)S(1)}, u32[]{:S(2)}, u32[]{:S(2)}) collective-permute-start(bf16[32,1920]{1,0:T(8,128)(2,1)} %get-tuple-element.44), channel_id=1, source_target_pairs={{1,0},{2,1},{3,2},{4,3},{5,4},{6,5},{7,6},{0,7},{9,8},{10,9},{11,1... | collective-permute-start | bytes 368648 | tf_op jit(solution)/shard_map/ppermute | solution.py:434
  127.9 3.0 %collective-permute-done.3.refs_4_ = bf16[32,1920]{1,0:T(8,128)(2,1)S(1)} collective-permute-done((bf16[32,1920]{1,0:T(8,128)(2,1)}, bf16[32,1920]{1,0:T(8,128)(2,1)S(1)}, u32[]{:S(2)}, u32[]{:S(2)}) %collective-permute-start.3) | collective-permute-done | bytes 122912 | tf_op jit(solution)/shard_map/ppermute | solution.py:434
  131.0 6.5 %main.1 = (bf16[32,768]{1,0:T(8,128)(2,1)}, bf16[64,768]{1,0:T(8,128)(2,1)}, bf16[32,768]{1,0:T(8,128)(2,1)}, bf16[8,2,48,768]{3,2,1,0:T(8,128)(2,1)}) custom-call(s32[1]{0:T(128)} %bitcast.core_ref.refs_0_, bf16[32,1920]{1,0:T(8,128)(2,1)} %get-tuple-element.38.refs_1_, f32[64,768]{1,0:T(8,128)} %get-tuple-element.39.refs_2_, ...), custom_call_target="tpu_custom_call" | custom-call | flops 1000000 | bytes 1000000 | tf_op jit(solution)/shard_map/main/pallas_call | solution.py:528
  137.5 5.6 %all-to-all-start.2 = ((bf16[8,2,48,768]{3,2,1,0:T(8,128)(2,1)}), bf16[8,2,48,768]{3,2,1,0:T(8,128)(2,1)S(1)}, u32[]{:S(2)}, u32[]{:S(2)}) async-start(bf16[8,2,48,768]{3,2,1,0:T(8,128)(2,1)} %get-tuple-element.50), calls=%async_computation.2 | async-start | bytes 2359296 | tf_op jit(solution)/shard_map/all_to_all | solution.py:424
  143.2 1.9 collective-permute-start.6
  145.1 13.8 %all-to-all-done.2.parts = bf16[8,2,48,768]{3,2,1,0:T(8,128)(2,1)S(1)} async-done(((bf16[8,2,48,768]{3,2,1,0:T(8,128)(2,1)}), bf16[8,2,48,768]{3,2,1,0:T(8,128)(2,1)S(1)}, u32[]{:S(2)}, u32[]{:S(2)}) %all-to-all-start.2) | async-done | bytes 1179680 | tf_op jit(solution)/shard_map/all_to_all | solution.py:424
  158.9 0.2 sum_split.1
  159.2 4.3 %collective-permute-start.5 = (bf16[2,48,384]{2,1,0:T(8,128)(2,1)S(1)}, bf16[2,48,384]{2,1,0:T(8,128)(2,1)S(1)}, u32[]{:S(2)}, u32[]{:S(2)}) collective-permute-start(bf16[2,48,384]{2,1,0:T(8,128)(2,1)S(1)} %get-tuple-element.52), channel_id=1, source_target_pairs={{0,8},{8,0},{16,24},{24,16},{32,40},{40,32},{48,56},{56,48},{64,72... | collective-permute-start | bytes 221192 | tf_op jit(solution)/shard_map/ppermute | solution.py:438
  163.5 0.9 collective-permute-done.5.arrived
  164.4 0.9 pair_copies.1
  165.3 3.5 %all-to-all-start.3 = ((bf16[8,2,48,384]{3,2,1,0:T(8,128)(2,1)}), bf16[8,2,48,384]{3,2,1,0:T(8,128)(2,1)S(1)}, u32[]{:S(2)}, u32[]{:S(2)}) async-start(bf16[8,2,48,384]{3,2,1,0:T(8,128)(2,1)} %pair_copies.1), calls=%async_computation.3 | async-start | bytes 1179648 | tf_op jit(solution)/shard_map/all_to_all | solution.py:424
  168.9 2.5 %collective-permute-start.7 = (bf16[64,768]{1,0:T(8,128)(2,1)S(1)}, bf16[64,768]{1,0:T(8,128)(2,1)S(1)}, u32[]{:S(2)}, u32[]{:S(2)}) collective-permute-start(bf16[64,768]{1,0:T(8,128)(2,1)S(1)} %pad_maximum_fusion), channel_id=1, source_target_pairs={{7,0},{0,1},{1,2},{2,3},{3,4},{4,5},{5,6},{6,7},{15,8},{8,9},{9,10... | collective-permute-start | bytes 294920 | tf_op jit(solution)/shard_map/ppermute | solution.py:434
  171.4 5.5 %collective-permute-done.7.row = bf16[64,768]{1,0:T(8,128)(2,1)S(1)} collective-permute-done((bf16[64,768]{1,0:T(8,128)(2,1)S(1)}, bf16[64,768]{1,0:T(8,128)(2,1)S(1)}, u32[]{:S(2)}, u32[]{:S(2)}) %collective-permute-start.7) | collective-permute-done | bytes 98336 | tf_op jit(solution)/shard_map/ppermute | solution.py:434
  176.9 11.3 %all-to-all-done.3.parts = bf16[8,2,48,384]{3,2,1,0:T(8,128)(2,1)S(1)} async-done(((bf16[8,2,48,384]{3,2,1,0:T(8,128)(2,1)}), bf16[8,2,48,384]{3,2,1,0:T(8,128)(2,1)S(1)}, u32[]{:S(2)}, u32[]{:S(2)}) %all-to-all-start.3) | async-done | bytes 589856 | tf_op jit(solution)/shard_map/all_to_all | solution.py:424
  188.2 0.8 sum_copies.2
  189.0 3.5 %all-to-all-start.4 = ((bf16[4,2,48,384]{3,2,1,0:T(8,128)(2,1)}), bf16[4,2,48,384]{3,2,1,0:T(8,128)(2,1)S(1)}, u32[]{:S(2)}, u32[]{:S(2)}) async-start(bf16[4,2,48,384]{3,2,1,0:T(8,128)(2,1)} %sum_copies.2), calls=%async_computation.4 | async-start | bytes 589824 | tf_op jit(solution)/shard_map/all_to_all | solution.py:424
  192.4 5.6 %plain_back.1 = bf16[128,768]{1,0:T(8,128)(2,1)} custom-call(s32[1]{0:T(128)} %bitcast.core_ref.refs_0_, bf16[128,768]{1,0:T(8,128)(2,1)} %bitcast.12, bf16[32,768]{1,0:T(8,128)(2,1)} %get-tuple-element.59.own_far, f32[64,768]{1,0:T(8,128)} %get-tuple-element.36.bias_far, bf16[8,192,384]{2,1,0:T(8,128)(2,1)} %copy-done, bf16[8,192,384]{2,1,0:T(8,128)(2,1)} %copy-done.1, ...), custom_call_target="tpu_custom_call" | custom-call | flops 4000000000 | bytes 4000000 | tf_op jit(solution)/shard_map/plain_back/pallas_call | solution.py:576
  198.0 4.5 %all-to-all-done.4.parts = bf16[4,2,48,384]{3,2,1,0:T(8,128)(2,1)S(1)} async-done(((bf16[4,2,48,384]{3,2,1,0:T(8,128)(2,1)}), bf16[4,2,48,384]{3,2,1,0:T(8,128)(2,1)S(1)}, u32[]{:S(2)}, u32[]{:S(2)}) %all-to-all-start.4) | async-done | bytes 294944 | tf_op jit(solution)/shard_map/all_to_all | solution.py:424
  202.6 3.5 %all_gather.3.parts = bf16[2,2,48,384]{3,2,1,0:T(8,128)(2,1)S(1)} all-gather(bf16[1,2,48,384]{3,2,1,0:T(8,128)(2,1)S(1)} %sum_copies.3), channel_id=1, replica_groups={{0,8},{16,24},{32,40},{48,56},{64,72},{80,88},{96,104},{112,120},{128,1..., dimensions={0}, use_global_device_ids=true | all-gather | bytes 221184 | tf_op jit(solution)/shard_map/all_gather | solution.py:599
  206.1 0.7 finish.1
  (21 shorter events, 0.2 us)
Async XLA Ops:
  37.6 45.0 %all-to-all-start = ((bf16[8,192,384]{2,1,0:T(8,128)(2,1)}), bf16[8,192,384]{2,1,0:T(8,128)(2,1)S(1)}, u32[]{:S(2)}, u32[]{:S(2)}) async-start(bf16[8,192,384]{2,1,0:T(8,128)(2,1)} %prepare.2), calls=%async_computation | async-start | bytes 2359296 | tf_op jit(solution)/shard_map/all_to_all | solution.py:424
  43.5 37.1 %copy-start.2 = (f32[12,225]{1,0:T(8,128)S(1)}, f32[12,225]{1,0:T(8,128)}, u32[]{:S(2)}) copy-start(f32[12,225]{1,0:T(8,128)} %table_p.1) | copy-start | bytes 32404
  43.5 37.1 %copy-start.3 = (f32[12,225]{1,0:T(8,128)S(1)}, f32[12,225]{1,0:T(8,128)}, u32[]{:S(2)}) copy-start(f32[12,225]{1,0:T(8,128)} %table_s.1) | copy-start | bytes 32404
  82.6 14.6 %copy-start = (bf16[8,192,384]{2,1,0:T(8,128)(2,1)}, bf16[8,192,384]{2,1,0:T(8,128)(2,1)S(1)}, u32[]{:S(2)}) copy-start(bf16[8,192,384]{2,1,0:T(8,128)(2,1)S(1)} %all-to-all-done.w_mine_ref.mine_far) | copy-start | bytes 3538948
  82.6 36.8 %all-to-all-start.1 = ((bf16[8,192,384]{2,1,0:T(8,128)(2,1)}), bf16[8,192,384]{2,1,0:T(8,128)(2,1)S(1)}, u32[]{:S(2)}, u32[]{:S(2)}) async-start(bf16[8,192,384]{2,1,0:T(8,128)(2,1)} %prepare.3), calls=%async_computation.1 | async-start | bytes 2359296 | tf_op jit(solution)/shard_map/all_to_all | solution.py:424
  87.7 9.4 %collective-permute-start = (bf16[8,192,384]{2,1,0:T(8,128)(2,1)S(1)}, bf16[8,192,384]{2,1,0:T(8,128)(2,1)S(1)}, u32[]{:S(2)}, u32[]{:S(2)}) collective-permute-start(bf16[8,192,384]{2,1,0:T(8,128)(2,1)S(1)} %all-to-all-done.w_mine_ref.mine_far), channel_id=1, source_target_pairs={{0,8},{8,0},{16,24},{24,16},{32,40},{40,32},{48,56},{56,48},{64,72... | collective-permute-start | bytes 3538952 | tf_op jit(solution)/shard_map/ppermute | solution.py:438
  97.2 4.4 %copy-start.1 = (bf16[8,192,384]{2,1,0:T(8,128)(2,1)}, bf16[8,192,384]{2,1,0:T(8,128)(2,1)S(1)}, u32[]{:S(2)}) copy-start(bf16[8,192,384]{2,1,0:T(8,128)(2,1)S(1)} %collective-permute-done.w_other_ref.other_far) | copy-start | bytes 3538948
  101.6 16.0 %collective-permute-start.1 = (bf16[32,1920]{1,0:T(8,128)(2,1)S(1)}, bf16[32,1920]{1,0:T(8,128)(2,1)S(1)}, u32[]{:S(2)}, u32[]{:S(2)}) collective-permute-start(bf16[32,1920]{1,0:T(8,128)(2,1)S(1)} %get-tuple-element.41), channel_id=1, source_target_pairs={{8,0},{9,1},{10,2},{11,3},{12,4},{13,5},{14,6},{15,7},{16,8},{17,9... | collective-permute-start | bytes 368648 | tf_op jit(solution)/shard_map/ppermute | solution.py:434
  103.9 15.5 %collective-permute-start.2 = (bf16[32,1920]{1,0:T(8,128)(2,1)S(1)}, bf16[32,1920]{1,0:T(8,128)(2,1)S(1)}, u32[]{:S(2)}, u32[]{:S(2)}) collective-permute-start(bf16[32,1920]{1,0:T(8,128)(2,1)S(1)} %get-tuple-element.42), channel_id=1, source_target_pairs={{9,0},{10,1},{11,2},{12,3},{13,4},{14,5},{15,6},{8,7},{17,8},{18,9... | collective-permute-start | bytes 368648 | tf_op jit(solution)/shard_map/ppermute | solution.py:434
  119.5 11.5 %collective-permute-start.4 = (bf16[8,192,384]{2,1,0:T(8,128)(2,1)S(1)}, bf16[8,192,384]{2,1,0:T(8,128)(2,1)S(1)}, u32[]{:S(2)}, u32[]{:S(2)}) collective-permute-start(bf16[8,192,384]{2,1,0:T(8,128)(2,1)S(1)} %all-to-all-done.1.refs_6_), channel_id=1, source_target_pairs={{0,8},{8,0},{16,24},{24,16},{32,40},{40,32},{48,56},{56,48},{64,72... | collective-permute-start | bytes 3538952 | tf_op jit(solution)/shard_map/ppermute | solution.py:438
  121.7 9.3 %collective-permute-start.3 = (bf16[32,1920]{1,0:T(8,128)(2,1)}, bf16[32,1920]{1,0:T(8,128)(2,1)S(1)}, u32[]{:S(2)}, u32[]{:S(2)}) collective-permute-start(bf16[32,1920]{1,0:T(8,128)(2,1)} %get-tuple-element.44), channel_id=1, source_target_pairs={{1,0},{2,1},{3,2},{4,3},{5,4},{6,5},{7,6},{0,7},{9,8},{10,9},{11,1... | collective-permute-start | bytes 368648 | tf_op jit(solution)/shard_map/ppermute | solution.py:434
  137.5 5.7 %copy-start.5 = (bf16[64,768]{1,0:T(8,128)(2,1)S(1)}, bf16[64,768]{1,0:T(8,128)(2,1)}, u32[]{:S(2)}) copy-start(bf16[64,768]{1,0:T(8,128)(2,1)} %get-tuple-element.53) | copy-start | bytes 294916
  137.5 21.4 %all-to-all-start.2 = ((bf16[8,2,48,768]{3,2,1,0:T(8,128)(2,1)}), bf16[8,2,48,768]{3,2,1,0:T(8,128)(2,1)S(1)}, u32[]{:S(2)}, u32[]{:S(2)}) async-start(bf16[8,2,48,768]{3,2,1,0:T(8,128)(2,1)} %get-tuple-element.50), calls=%async_computation.2 | async-start | bytes 2359296 | tf_op jit(solution)/shard_map/all_to_all | solution.py:424
  143.2 22.1 %collective-permute-start.6 = (bf16[64,768]{1,0:T(8,128)(2,1)S(1)}, bf16[64,768]{1,0:T(8,128)(2,1)S(1)}, u32[]{:S(2)}, u32[]{:S(2)}) collective-permute-start(bf16[64,768]{1,0:T(8,128)(2,1)S(1)} %copy-done.5), channel_id=1, source_target_pairs={{504,0},{505,1},{506,2},{507,3},{508,4},{509,5},{510,6},{511,7},{0... | collective-permute-start | bytes 294920 | tf_op jit(solution)/shard_map/ppermute | solution.py:434
  159.2 9.7 %copy-start.4 = (bf16[32,768]{1,0:T(8,128)(2,1)S(1)}, bf16[32,768]{1,0:T(8,128)(2,1)}, u32[]{:S(2)}) copy-start(bf16[32,768]{1,0:T(8,128)(2,1)} %get-tuple-element.56) | copy-start | bytes 147460
  159.2 5.2 %collective-permute-start.5 = (bf16[2,48,384]{2,1,0:T(8,128)(2,1)S(1)}, bf16[2,48,384]{2,1,0:T(8,128)(2,1)S(1)}, u32[]{:S(2)}, u32[]{:S(2)}) collective-permute-start(bf16[2,48,384]{2,1,0:T(8,128)(2,1)S(1)} %get-tuple-element.52), channel_id=1, source_target_pairs={{0,8},{8,0},{16,24},{24,16},{32,40},{40,32},{48,56},{56,48},{64,72... | collective-permute-start | bytes 221192 | tf_op jit(solution)/shard_map/ppermute | solution.py:438
  165.3 22.9 %all-to-all-start.3 = ((bf16[8,2,48,384]{3,2,1,0:T(8,128)(2,1)}), bf16[8,2,48,384]{3,2,1,0:T(8,128)(2,1)S(1)}, u32[]{:S(2)}, u32[]{:S(2)}) async-start(bf16[8,2,48,384]{3,2,1,0:T(8,128)(2,1)} %pair_copies.1), calls=%async_computation.3 | async-start | bytes 1179648 | tf_op jit(solution)/shard_map/all_to_all | solution.py:424
  168.9 8.0 %collective-permute-start.7 = (bf16[64,768]{1,0:T(8,128)(2,1)S(1)}, bf16[64,768]{1,0:T(8,128)(2,1)S(1)}, u32[]{:S(2)}, u32[]{:S(2)}) collective-permute-start(bf16[64,768]{1,0:T(8,128)(2,1)S(1)} %pad_maximum_fusion), channel_id=1, source_target_pairs={{7,0},{0,1},{1,2},{2,3},{3,4},{4,5},{5,6},{6,7},{15,8},{8,9},{9,10... | collective-permute-start | bytes 294920 | tf_op jit(solution)/shard_map/ppermute | solution.py:434
  189.0 13.5 %all-to-all-start.4 = ((bf16[4,2,48,384]{3,2,1,0:T(8,128)(2,1)}), bf16[4,2,48,384]{3,2,1,0:T(8,128)(2,1)S(1)}, u32[]{:S(2)}, u32[]{:S(2)}) async-start(bf16[4,2,48,384]{3,2,1,0:T(8,128)(2,1)} %sum_copies.2), calls=%async_computation.4 | async-start | bytes 589824 | tf_op jit(solution)/shard_map/all_to_all | solution.py:424

commit v7 on v5

--- a/solution.py
+++ b/solution.py
@@ -109,11 +109,14 @@
         move.wait()
 
 
-def prepare(core_ref, qkv, proj, out, block, sems):
+def prepare(core_ref, qkv_p, proj_p, qkv_s, proj_s, out_first, out_second, block, second, sems):
     start = pl.multiple_of(core_ref[0] * HALF, 128)
-    block[0:SHARE] = qkv[:, pl.ds(start, HALF)]
-    block[SHARE : SHARE + ROWS] = proj[:, pl.ds(start, HALF)]
-    wait_all(copy_all([(block, out.at[i]) for i in range(8)], sems))
+    second[0:SHARE] = qkv_s[:, pl.ds(start, HALF)]
+    second[SHARE : SHARE + ROWS] = proj_s[:, pl.ds(start, HALF)]
+    block[0:SHARE] = qkv_p[:, pl.ds(start, HALF)]
+    block[SHARE : SHARE + ROWS] = proj_p[:, pl.ds(start, HALF)]
+    moves = [(second, out_second)] + [(block, out_first.at[i]) for i in range(8)]
+    wait_all(copy_all(moves, sems))
 
 
 def biases(edge_ref, table_p, table_s, to_p, to_s, out_p, out_s, tables, wide, sems):
@@ -230,15 +233,16 @@
     core_ref,
     own_far,
     bias_far,
+    mine_far,
     right,
     below,
     diag,
-    w_mine_ref,
     w_other_ref,
     to_own,
     to_column,
     to_below,
     to_local,
+    w_mine_ref,
     bias_s,
     quads,
     out_local,
@@ -250,17 +254,20 @@
     sems,
 ):
     mine, other = sides(core_ref)
-    loads = copy_all([(own_far, staged.at[0:32]), (bias_far, bias_s)], sems)
+    loads = copy_all(
+        [(own_far, staged.at[0:32]), (mine_far, w_mine_ref), (bias_far, bias_s)], sems
+    )
     mask[...] = head_mask()
     for i, part in ((1, right), (2, below), (3, diag)):
         staged[i * 32 : (i + 1) * 32] = part[...]
-    wait_all(loads)
+    loads[0].wait()
     pick = quadrant_pick(True)
     grads[...] = dot(pick, staged[:, D + WIDE :]).astype(BF16)
     block_out = dot(pick, staged[:, 0:D])
     mixed_plain = dot(pick, staged[:, D : D + WIDE]).astype(BF16)
     normed, rstd = normalize(block_out)
     rows_small[...] = normed.astype(BF16)
+    wait_all(loads[1:])
     w_mine, w_other = qkv_of(w_mine_ref), qkv_of(w_other_ref)
     packed = project(rows_small, w_mine, w_other, mine, other).astype(BF16)
     d_mixed = project(grads, proj_of(w_mine_ref), proj_of(w_other_ref), mine, other).astype(BF16)
@@ -289,13 +296,13 @@
             (quads.at[64:96], to_below),
         ],
         sems,
-        2,
+        3,
     )
     local_shift = dot(mixed_shift, grads[...], TN) * grad_scale
     out_local[:, 1] = local_shift.astype(BF16).reshape(8, ROWS, D)
     local_plain = dot(mixed_plain, grad, TN) * grad_scale
     out_local[:, 0] = local_plain.astype(BF16).reshape(8, ROWS, D)
-    wait_all(copy_all([(out_local, to_local)], sems, 6))
+    wait_all(copy_all([(out_local, to_local)], sems, 7))
     wait_all(stores)
 
 
@@ -451,22 +458,25 @@
     tok = tokens.reshape(128, D)
     cot = cotangent.reshape(128, D)
 
-    def share(qkv, proj):
-        return pl.pallas_call(
-            prepare,
-            out_shape=pltpu.HBM((8, SHARE + ROWS, HALF), BF16),
-            in_specs=[SMEM, VMEM, VMEM],
-            out_specs=HBM,
-            scratch_shapes=[
-                pltpu.VMEM((SHARE + ROWS, HALF), BF16),
-                pltpu.SemaphoreType.DMA((8,)),
-            ],
-            compiler_params=params(60),
-            name="prepare",
-        )(core, qkv.T, proj)
-
-    first_mine = swap(share(qkv_plain, proj_plain), "freq")
-    second_share = share(qkv_shift, proj_shift)
+    first_share, second_share = pl.pallas_call(
+        prepare,
+        out_shape=(
+            pltpu.HBM((8, SHARE + ROWS, HALF), BF16),
+            pltpu.HBM((SHARE + ROWS, HALF), BF16),
+        ),
+        in_specs=[SMEM] + [VMEM] * 4,
+        out_specs=[HBM] * 2,
+        scratch_shapes=[
+            pltpu.VMEM((SHARE + ROWS, HALF), BF16),
+            pltpu.VMEM((SHARE + ROWS, HALF), BF16),
+            pltpu.SemaphoreType.DMA((9,)),
+        ],
+        compiler_params=params(60),
+        name="prepare",
+    )(core, qkv_plain.T, proj_plain, qkv_shift.T, proj_shift)
+    second_mine = lax.all_gather(second_share, "freq")
+    first_mine = swap(first_share, "freq")
+
     table = pltpu.HBM((SPOTS, LANES), F32)
     bias_p, bias_s = pl.pallas_call(
         biases,
@@ -484,10 +494,7 @@
         name="biases",
     )(edge, table_plain, table_shift)
 
-    first_mine, second_share, bias_p, bias_s = lax.optimization_barrier(
-        (first_mine, second_share, bias_p, bias_s)
-    )
-    second_mine = swap(second_share, "freq")
+    first_mine, bias_p, bias_s = lax.optimization_barrier((first_mine, bias_p, bias_s))
     first_other = other_core(first_mine)
     packet = pltpu.HBM((32, 2 * D + WIDE), BF16)
     own, to_left, to_above, to_diag = pl.pallas_call(
@@ -522,9 +529,10 @@
     g_own, to_right, to_below, local = pl.pallas_call(
         lambda *refs: main_kernel(grad_scale, *refs),
         out_shape=(piece, column, piece, local),
-        in_specs=[SMEM] + [HBM] * 2 + [VMEM] * 5,
+        in_specs=[SMEM] + [HBM] * 3 + [VMEM] * 4,
         out_specs=[HBM] * 4,
         scratch_shapes=[
+            pltpu.VMEM((8, SHARE + ROWS, HALF), BF16),
             pltpu.VMEM((SPOTS, LANES), F32),
             pltpu.VMEM((128, D), BF16),
             pltpu.VMEM((8, 2, ROWS, D), BF16),
@@ -533,12 +541,12 @@
             pltpu.VMEM((128, D), BF16),
             pltpu.VMEM((128, D), F32),
             pltpu.VMEM((LANES, WIDE), BF16),
-            pltpu.SemaphoreType.DMA((7,)),
+            pltpu.SemaphoreType.DMA((8,)),
         ],
         compiler_params=params(),
         cost_estimate=cost(1_000_000, 1_000_000),
         name="main",
-    )(core, far(own), far(bias_s), right, below, diag, second_mine, second_other)
+    )(core, far(own), far(bias_s), far(second_mine), right, below, diag, second_other)
 
     local, to_right, to_below = lax.optimization_barrier((local, to_right, to_below))
     part = swap(local, "freq")

time: 147 us -> 169 us (1.15)
  between operations: 0.88 us -> 14.2 us
  waiting for transfers between devices: 51.6 us -> 58.8 us
  starting transfers between devices: 63.3 us -> 66.5 us
  Pallas kernels: 25.3 us -> 23.4 us
    all_gather x0 -> x1, waiting for transfers between devices: none -> 10.1 us  [shards(): second_mine = lax.all_gather(second_share, 'freq')]
    all_to_all x5 -> x4, starting transfers between devices: 21.5 us -> 24.5 us  [swap(): return lax.all_to_all(value, axis, 0, 0, axis_index_groups=groups)]
    ppermute x5, waiting for transfers between devices: 7.74 us -> 5.34 us  [from_offset(): return lax.ppermute(value, ('tm', 'freq'), pairs)]
    pallas_call x2 -> x1, Pallas kernels: 4.22 us -> 2.27 us  [shards(): pl.pallas_call(prepare, out_shape=(pltpu.HBM((8, SHARE + ROWS, HALF), BF1...]
    all_to_all x5 -> x4, waiting for transfers between devices: 38.1 us -> 36.6 us  [swap(): return lax.all_to_all(value, axis, 0, 0, axis_index_groups=groups)]
  transfers between devices with their start and end apart: 13 -> 13, of which waited for: 9 -> 9; matrix products, arithmetic and copies ran while one was open for 0% -> 0% of each run, Pallas kernels for 10% -> 8%
where the time goes in v7:
time: 169 us; the launch traced here: 168 us
  starting transfers between devices  66.5 us (39%)
  waiting for transfers between devices  58.8 us (35%)
  Pallas kernels  23.4 us (14%)
  between operations  14.2 us (8%)
  blocking collectives  4.73 us (3%)
    all_to_all x4, waiting for transfers between devices, swap(): return lax.all_to_all(value, axis, 0, 0, axis_index_groups=groups)  36.6 us
    ppermute x5, starting transfers between devices, from_offset(): return lax.ppermute(value, ('tm', 'freq'), pairs)  26.7 us
    all_to_all x4, starting transfers between devices, swap(): return lax.all_to_all(value, axis, 0, 0, axis_index_groups=groups)  24.5 us
    ppermute x3, starting transfers between devices, other_core(): lax.ppermute(value, 'tm', [(i, i ^ 1) for i in range(lax.axis_size('tm'))])  15.3 us
    all_gather x1, waiting for transfers between devices, shards(): second_mine = lax.all_gather(second_share, 'freq')  10.1 us
    pallas_call x1, Pallas kernels, shards(): pl.pallas_call(lambda *refs: main_kernel(grad_scale, *refs), out_shape=(p...  6.4 us
    ppermute x3, waiting for transfers between devices, other_core(): lax.ppermute(value, 'tm', [(i, i ^ 1) for i in range(lax.axis_size('tm'))])  6.01 us
    pallas_call x1, Pallas kernels, shards(): pl.pallas_call(plain_back, out_shape=jax.ShapeDtypeStruct((128, D), BF16)...  5.55 us
  transfers between devices with their start and end apart: 13, of which 9 were waited for; matrix products, arithmetic and copies ran while one was open for 0% of the time, Pallas kernels for 8%

profile of v7, /device:TPU:1, one launch (start us, length us, event | category | flops | bytes accessed | tf_op | source)
XLA Modules:
  0.0 167.7 jit_solution(929245333173125061)
XLA Ops:
  7.2 2.3 %prepare.1 = (bf16[8,192,384]{2,1,0:T(8,128)(2,1)}, bf16[192,384]{1,0:T(8,128)(2,1)}) custom-call(s32[1]{0:T(128)} %bitcast.core_ref.refs_0_, bf16[144,768]{1,0:T(8,128)(2,1)} %bitcast.11, bf16[48,768]{1,0:T(8,128)(2,1)} %proj_p.1, bf16[144,768]{1,0:T(8,128)(2,1)} %bitcast.12, bf16[48,768]{1,0:T(8,128)(2,1)} %proj_s.1), custom_call_target="tpu_custom_call" | custom-call | tf_op jit(solution)/shard_map/prepare/pallas_call | solution.py:461
  9.5 5.9 %all-to-all-start = ((bf16[8,192,384]{2,1,0:T(8,128)(2,1)}), bf16[8,192,384]{2,1,0:T(8,128)(2,1)S(1)}, u32[]{:S(2)}, u32[]{:S(2)}) async-start(bf16[8,192,384]{2,1,0:T(8,128)(2,1)} %get-tuple-element.36), calls=%async_computation | async-start | bytes 2359296 | tf_op jit(solution)/shard_map/all_to_all | solution.py:422
  15.4 0.7 all-gather.3.cloned.1.call-update
  16.2 2.0 %biases.1 = (f32[64,768]{1,0:T(8,128)}, f32[64,768]{1,0:T(8,128)}) custom-call(s32[2]{0:T(128)S(1)} %add_convert_fusion.edge_ref, f32[12,225]{1,0:T(8,128)S(1)} %copy-done.2, f32[12,225]{1,0:T(8,128)S(1)} %copy-done.3), custom_call_target="tpu_custom_call" | custom-call | tf_op jit(solution)/shard_map/biases/pallas_call | solution.py:481
  18.2 9.9 %all-to-all-done.w_mine_ref.mine_far = bf16[8,192,384]{2,1,0:T(8,128)(2,1)S(1)} async-done(((bf16[8,192,384]{2,1,0:T(8,128)(2,1)}), bf16[8,192,384]{2,1,0:T(8,128)(2,1)S(1)}, u32[]{:S(2)}, u32[]{:S(2)}) %all-to-all-start) | async-done | bytes 1179680 | tf_op jit(solution)/shard_map/all_to_all | solution.py:422
  28.1 7.3 %collective-permute-start = (bf16[8,192,384]{2,1,0:T(8,128)(2,1)S(1)}, bf16[8,192,384]{2,1,0:T(8,128)(2,1)S(1)}, u32[]{:S(2)}, u32[]{:S(2)}) collective-permute-start(bf16[8,192,384]{2,1,0:T(8,128)(2,1)S(1)} %all-to-all-done.w_mine_ref.mine_far), channel_id=1, source_target_pairs={{0,8},{8,0},{16,24},{24,16},{32,40},{40,32},{48,56},{56,48},{64,72... | collective-permute-start | bytes 3538952 | tf_op jit(solution)/shard_map/ppermute | solution.py:436
  35.4 2.5 %collective-permute-done.w_other_ref.other_far = bf16[8,192,384]{2,1,0:T(8,128)(2,1)S(1)} collective-permute-done((bf16[8,192,384]{2,1,0:T(8,128)(2,1)S(1)}, bf16[8,192,384]{2,1,0:T(8,128)(2,1)S(1)}, u32[]{:S(2)}, u32[]{:S(2)}) %collective-permute-start) | collective-permute-done | bytes 1179680 | tf_op jit(solution)/shard_map/ppermute | solution.py:436
  37.9 4.5 %plain_forward.1 = (bf16[32,1920]{1,0:T(8,128)(2,1)}, bf16[32,1920]{1,0:T(8,128)(2,1)}, bf16[32,1920]{1,0:T(8,128)(2,1)}, bf16[32,1920]{1,0:T(8,128)(2,1)}) custom-call(s32[1]{0:T(128)} %bitcast.core_ref.refs_0_, bf16[128,768]{1,0:T(8,128)(2,1)} %bitcast.14, bf16[128,768]{1,0:T(8,128)(2,1)} %bitcast.13, f32[64,768]{1,0:T(8,128)} %get-tuple-element.39.bias_far, ...), custom_call_target="tpu_custom_call" | custom-call | flops 1000000 | bytes 1000000 | tf_op jit(solution)/shard_map/plain_forward/pallas_call | solution.py:500
  42.4 2.3 %collective-permute-start.1 = (bf16[32,1920]{1,0:T(8,128)(2,1)}, bf16[32,1920]{1,0:T(8,128)(2,1)S(1)}, u32[]{:S(2)}, u32[]{:S(2)}) collective-permute-start(bf16[32,1920]{1,0:T(8,128)(2,1)} %get-tuple-element.44), channel_id=1, source_target_pairs={{8,0},{9,1},{10,2},{11,3},{12,4},{13,5},{14,6},{15,7},{16,8},{17,9... | collective-permute-start | bytes 368648 | tf_op jit(solution)/shard_map/ppermute | solution.py:432
  44.7 3.1 %collective-permute-start.2 = (bf16[32,1920]{1,0:T(8,128)(2,1)}, bf16[32,1920]{1,0:T(8,128)(2,1)S(1)}, u32[]{:S(2)}, u32[]{:S(2)}) collective-permute-start(bf16[32,1920]{1,0:T(8,128)(2,1)} %get-tuple-element.45), channel_id=1, source_target_pairs={{1,0},{2,1},{3,2},{4,3},{5,4},{6,5},{7,6},{0,7},{9,8},{10,9},{11,1... | collective-permute-start | bytes 368648 | tf_op jit(solution)/shard_map/ppermute | solution.py:432
  47.8 14.1 %collective-permute-start.3 = (bf16[32,1920]{1,0:T(8,128)(2,1)}, bf16[32,1920]{1,0:T(8,128)(2,1)S(1)}, u32[]{:S(2)}, u32[]{:S(2)}) collective-permute-start(bf16[32,1920]{1,0:T(8,128)(2,1)} %get-tuple-element.46), channel_id=1, source_target_pairs={{9,0},{10,1},{11,2},{12,3},{13,4},{14,5},{15,6},{8,7},{17,8},{18,9... | collective-permute-start | bytes 368648 | tf_op jit(solution)/shard_map/ppermute | solution.py:432
  61.9 10.1 %all-gather.3.cloned.1.call-done = bf16[1536,384]{1,0:T(8,128)(2,1)} async-done(((bf16[192,384]{1,0:T(8,128)(2,1)}), bf16[1536,384]{1,0:T(8,128)(2,1)}) %all-gather.3.cloned.1.call-update) | async-done | bytes 1179664 | tf_op jit(solution)/shard_map/all_gather | solution.py:477
  72.1 4.4 %collective-permute-start.4 = (bf16[8,192,384]{2,1,0:T(8,128)(2,1)}, bf16[8,192,384]{2,1,0:T(8,128)(2,1)S(1)}, u32[]{:S(2)}, u32[]{:S(2)}) collective-permute-start(bf16[8,192,384]{2,1,0:T(8,128)(2,1)} %bitcast.9), channel_id=1, source_target_pairs={{0,8},{8,0},{16,24},{24,16},{32,40},{40,32},{48,56},{56,48},{64,72... | collective-permute-start | bytes 3538952 | tf_op jit(solution)/shard_map/ppermute | solution.py:436
  76.4 2.7 %collective-permute-done.4.refs_7_ = bf16[8,192,384]{2,1,0:T(8,128)(2,1)S(1)} collective-permute-done((bf16[8,192,384]{2,1,0:T(8,128)(2,1)}, bf16[8,192,384]{2,1,0:T(8,128)(2,1)S(1)}, u32[]{:S(2)}, u32[]{:S(2)}) %collective-permute-start.4) | collective-permute-done | bytes 1179680 | tf_op jit(solution)/shard_map/ppermute | solution.py:436
  79.1 6.4 %main.1 = (bf16[32,768]{1,0:T(8,128)(2,1)}, bf16[64,768]{1,0:T(8,128)(2,1)}, bf16[32,768]{1,0:T(8,128)(2,1)}, bf16[8,2,48,768]{3,2,1,0:T(8,128)(2,1)}) custom-call(s32[1]{0:T(128)} %bitcast.core_ref.refs_0_, bf16[32,1920]{1,0:T(8,128)(2,1)} %get-tuple-element.41.refs_1_, f32[64,768]{1,0:T(8,128)} %get-tuple-element.42.refs_2_, ...), custom_call_target="tpu_custom_call" | custom-call | flops 1000000 | bytes 1000000 | tf_op jit(solution)/shard_map/main/pallas_call | solution.py:529
  85.5 4.2 %all-to-all-start.1 = ((bf16[8,2,48,768]{3,2,1,0:T(8,128)(2,1)}), bf16[8,2,48,768]{3,2,1,0:T(8,128)(2,1)S(1)}, u32[]{:S(2)}, u32[]{:S(2)}) async-start(bf16[8,2,48,768]{3,2,1,0:T(8,128)(2,1)} %get-tuple-element.54), calls=%async_computation.1 | async-start | bytes 2359296 | tf_op jit(solution)/shard_map/all_to_all | solution.py:422
  89.7 4.8 %collective-permute-start.6 = (bf16[64,768]{1,0:T(8,128)(2,1)S(1)}, bf16[64,768]{1,0:T(8,128)(2,1)S(1)}, u32[]{:S(2)}, u32[]{:S(2)}) collective-permute-start(bf16[64,768]{1,0:T(8,128)(2,1)S(1)} %copy-done.5), channel_id=1, source_target_pairs={{504,0},{505,1},{506,2},{507,3},{508,4},{509,5},{510,6},{511,7},{0... | collective-permute-start | bytes 294920 | tf_op jit(solution)/shard_map/ppermute | solution.py:432
  94.5 11.8 %all-to-all-done.1.parts = bf16[8,2,48,768]{3,2,1,0:T(8,128)(2,1)S(1)} async-done(((bf16[8,2,48,768]{3,2,1,0:T(8,128)(2,1)}), bf16[8,2,48,768]{3,2,1,0:T(8,128)(2,1)S(1)}, u32[]{:S(2)}, u32[]{:S(2)}) %all-to-all-start.1) | async-done | bytes 1179680 | tf_op jit(solution)/shard_map/all_to_all | solution.py:422
  106.3 0.2 sum_split.1
  106.6 3.6 %collective-permute-start.5 = (bf16[2,48,384]{2,1,0:T(8,128)(2,1)S(1)}, bf16[2,48,384]{2,1,0:T(8,128)(2,1)S(1)}, u32[]{:S(2)}, u32[]{:S(2)}) collective-permute-start(bf16[2,48,384]{2,1,0:T(8,128)(2,1)S(1)} %get-tuple-element.56), channel_id=1, source_target_pairs={{0,8},{8,0},{16,24},{24,16},{32,40},{40,32},{48,56},{56,48},{64,72... | collective-permute-start | bytes 221192 | tf_op jit(solution)/shard_map/ppermute | solution.py:436
  110.1 0.9 collective-permute-done.5.arrived
  111.0 0.9 pair_copies.1
  111.9 8.9 %all-to-all-start.2 = ((bf16[8,2,48,384]{3,2,1,0:T(8,128)(2,1)}), bf16[8,2,48,384]{3,2,1,0:T(8,128)(2,1)S(1)}, u32[]{:S(2)}, u32[]{:S(2)}) async-start(bf16[8,2,48,384]{3,2,1,0:T(8,128)(2,1)} %pair_copies.1), calls=%async_computation.2 | async-start | bytes 1179648 | tf_op jit(solution)/shard_map/all_to_all | solution.py:422
  120.8 2.4 %collective-permute-start.7 = (bf16[64,768]{1,0:T(8,128)(2,1)S(1)}, bf16[64,768]{1,0:T(8,128)(2,1)S(1)}, u32[]{:S(2)}, u32[]{:S(2)}) collective-permute-start(bf16[64,768]{1,0:T(8,128)(2,1)S(1)} %pad_maximum_fusion), channel_id=1, source_target_pairs={{7,0},{0,1},{1,2},{2,3},{3,4},{4,5},{5,6},{6,7},{15,8},{8,9},{9,10... | collective-permute-start | bytes 294920 | tf_op jit(solution)/shard_map/ppermute | solution.py:432
  123.3 5.3 %collective-permute-done.7.row = bf16[64,768]{1,0:T(8,128)(2,1)S(1)} collective-permute-done((bf16[64,768]{1,0:T(8,128)(2,1)S(1)}, bf16[64,768]{1,0:T(8,128)(2,1)S(1)}, u32[]{:S(2)}, u32[]{:S(2)}) %collective-permute-start.7) | collective-permute-done | bytes 98336 | tf_op jit(solution)/shard_map/ppermute | solution.py:432
  128.6 11.6 %all-to-all-done.2.parts = bf16[8,2,48,384]{3,2,1,0:T(8,128)(2,1)S(1)} async-done(((bf16[8,2,48,384]{3,2,1,0:T(8,128)(2,1)}), bf16[8,2,48,384]{3,2,1,0:T(8,128)(2,1)S(1)}, u32[]{:S(2)}, u32[]{:S(2)}) %all-to-all-start.2) | async-done | bytes 589856 | tf_op jit(solution)/shard_map/all_to_all | solution.py:422
  140.1 0.8 sum_copies.2
  141.0 5.5 %all-to-all-start.3 = ((bf16[4,2,48,384]{3,2,1,0:T(8,128)(2,1)}), bf16[4,2,48,384]{3,2,1,0:T(8,128)(2,1)S(1)}, u32[]{:S(2)}, u32[]{:S(2)}) async-start(bf16[4,2,48,384]{3,2,1,0:T(8,128)(2,1)} %sum_copies.2), calls=%async_computation.3 | async-start | bytes 589824 | tf_op jit(solution)/shard_map/all_to_all | solution.py:422
  146.4 5.5 %plain_back.1 = bf16[128,768]{1,0:T(8,128)(2,1)} custom-call(s32[1]{0:T(128)} %bitcast.core_ref.refs_0_, bf16[128,768]{1,0:T(8,128)(2,1)} %bitcast.15, bf16[32,768]{1,0:T(8,128)(2,1)} %get-tuple-element.63.own_far, f32[64,768]{1,0:T(8,128)} %get-tuple-element.39.bias_far, bf16[8,192,384]{2,1,0:T(8,128)(2,1)} %copy-done, bf16[8,192,384]{2,1,0:T(8,128)(2,1)} %copy-done.1, ...), custom_call_target="tpu_custom_call" | custom-call | flops 4000000000 | bytes 4000000 | tf_op jit(solution)/shard_map/plain_back/pallas_call | solution.py:577
  152.0 3.4 %all-to-all-done.3.parts = bf16[4,2,48,384]{3,2,1,0:T(8,128)(2,1)S(1)} async-done(((bf16[4,2,48,384]{3,2,1,0:T(8,128)(2,1)}), bf16[4,2,48,384]{3,2,1,0:T(8,128)(2,1)S(1)}, u32[]{:S(2)}, u32[]{:S(2)}) %all-to-all-start.3) | async-done | bytes 294944 | tf_op jit(solution)/shard_map/all_to_all | solution.py:422
  155.4 4.7 %all_gather.11.parts = bf16[2,2,48,384]{3,2,1,0:T(8,128)(2,1)S(1)} all-gather(bf16[1,2,48,384]{3,2,1,0:T(8,128)(2,1)S(1)} %sum_copies.3), channel_id=1, replica_groups={{0,8},{16,24},{32,40},{48,56},{64,72},{80,88},{96,104},{112,120},{128,1..., dimensions={0}, use_global_device_ids=true | all-gather | bytes 221184 | tf_op jit(solution)/shard_map/all_gather | solution.py:600
  160.1 0.7 finish.1
  (21 shorter events, 0.2 us)
Async XLA Ops:
  9.5 6.7 %copy-start.2 = (f32[12,225]{1,0:T(8,128)S(1)}, f32[12,225]{1,0:T(8,128)}, u32[]{:S(2)}) copy-start(f32[12,225]{1,0:T(8,128)} %table_p.1) | copy-start | bytes 32404
  9.5 6.7 %copy-start.3 = (f32[12,225]{1,0:T(8,128)S(1)}, f32[12,225]{1,0:T(8,128)}, u32[]{:S(2)}) copy-start(f32[12,225]{1,0:T(8,128)} %table_s.1) | copy-start | bytes 32404
  9.5 18.6 %all-to-all-start = ((bf16[8,192,384]{2,1,0:T(8,128)(2,1)}), bf16[8,192,384]{2,1,0:T(8,128)(2,1)S(1)}, u32[]{:S(2)}, u32[]{:S(2)}) async-start(bf16[8,192,384]{2,1,0:T(8,128)(2,1)} %get-tuple-element.36), calls=%async_computation | async-start | bytes 2359296 | tf_op jit(solution)/shard_map/all_to_all | solution.py:422
  15.4 56.7 %all-gather.3.cloned.1.call-start = ((), (), s32[]{:S(2)}) async-start(), calls=%async_computation.4 | async-start | bytes 1327104 | tf_op jit(solution)/shard_map/all_gather | solution.py:477
  28.1 14.3 %copy-start = (bf16[8,192,384]{2,1,0:T(8,128)(2,1)}, bf16[8,192,384]{2,1,0:T(8,128)(2,1)S(1)}, u32[]{:S(2)}) copy-start(bf16[8,192,384]{2,1,0:T(8,128)(2,1)S(1)} %all-to-all-done.w_mine_ref.mine_far) | copy-start | bytes 3538948
  28.1 9.8 %collective-permute-start = (bf16[8,192,384]{2,1,0:T(8,128)(2,1)S(1)}, bf16[8,192,384]{2,1,0:T(8,128)(2,1)S(1)}, u32[]{:S(2)}, u32[]{:S(2)}) collective-permute-start(bf16[8,192,384]{2,1,0:T(8,128)(2,1)S(1)} %all-to-all-done.w_mine_ref.mine_far), channel_id=1, source_target_pairs={{0,8},{8,0},{16,24},{24,16},{32,40},{40,32},{48,56},{56,48},{64,72... | collective-permute-start | bytes 3538952 | tf_op jit(solution)/shard_map/ppermute | solution.py:436
  37.9 4.5 %copy-start.1 = (bf16[8,192,384]{2,1,0:T(8,128)(2,1)}, bf16[8,192,384]{2,1,0:T(8,128)(2,1)S(1)}, u32[]{:S(2)}) copy-start(bf16[8,192,384]{2,1,0:T(8,128)(2,1)S(1)} %collective-permute-done.w_other_ref.other_far) | copy-start | bytes 3538948
  42.4 29.7 %collective-permute-start.1 = (bf16[32,1920]{1,0:T(8,128)(2,1)}, bf16[32,1920]{1,0:T(8,128)(2,1)S(1)}, u32[]{:S(2)}, u32[]{:S(2)}) collective-permute-start(bf16[32,1920]{1,0:T(8,128)(2,1)} %get-tuple-element.44), channel_id=1, source_target_pairs={{8,0},{9,1},{10,2},{11,3},{12,4},{13,5},{14,6},{15,7},{16,8},{17,9... | collective-permute-start | bytes 368648 | tf_op jit(solution)/shard_map/ppermute | solution.py:432
  44.7 27.4 %collective-permute-start.2 = (bf16[32,1920]{1,0:T(8,128)(2,1)}, bf16[32,1920]{1,0:T(8,128)(2,1)S(1)}, u32[]{:S(2)}, u32[]{:S(2)}) collective-permute-start(bf16[32,1920]{1,0:T(8,128)(2,1)} %get-tuple-element.45), channel_id=1, source_target_pairs={{1,0},{2,1},{3,2},{4,3},{5,4},{6,5},{7,6},{0,7},{9,8},{10,9},{11,1... | collective-permute-start | bytes 368648 | tf_op jit(solution)/shard_map/ppermute | solution.py:432
  47.8 24.3 %collective-permute-start.3 = (bf16[32,1920]{1,0:T(8,128)(2,1)}, bf16[32,1920]{1,0:T(8,128)(2,1)S(1)}, u32[]{:S(2)}, u32[]{:S(2)}) collective-permute-start(bf16[32,1920]{1,0:T(8,128)(2,1)} %get-tuple-element.46), channel_id=1, source_target_pairs={{9,0},{10,1},{11,2},{12,3},{13,4},{14,5},{15,6},{8,7},{17,8},{18,9... | collective-permute-start | bytes 368648 | tf_op jit(solution)/shard_map/ppermute | solution.py:432
  72.1 7.0 %collective-permute-start.4 = (bf16[8,192,384]{2,1,0:T(8,128)(2,1)}, bf16[8,192,384]{2,1,0:T(8,128)(2,1)S(1)}, u32[]{:S(2)}, u32[]{:S(2)}) collective-permute-start(bf16[8,192,384]{2,1,0:T(8,128)(2,1)} %bitcast.9), channel_id=1, source_target_pairs={{0,8},{8,0},{16,24},{24,16},{32,40},{40,32},{48,56},{56,48},{64,72... | collective-permute-start | bytes 3538952 | tf_op jit(solution)/shard_map/ppermute | solution.py:436
  85.5 4.2 %copy-start.5 = (bf16[64,768]{1,0:T(8,128)(2,1)S(1)}, bf16[64,768]{1,0:T(8,128)(2,1)}, u32[]{:S(2)}) copy-start(bf16[64,768]{1,0:T(8,128)(2,1)} %get-tuple-element.57) | copy-start | bytes 294916
  85.5 20.8 %all-to-all-start.1 = ((bf16[8,2,48,768]{3,2,1,0:T(8,128)(2,1)}), bf16[8,2,48,768]{3,2,1,0:T(8,128)(2,1)S(1)}, u32[]{:S(2)}, u32[]{:S(2)}) async-start(bf16[8,2,48,768]{3,2,1,0:T(8,128)(2,1)} %get-tuple-element.54), calls=%async_computation.1 | async-start | bytes 2359296 | tf_op jit(solution)/shard_map/all_to_all | solution.py:422
  89.7 22.2 %collective-permute-start.6 = (bf16[64,768]{1,0:T(8,128)(2,1)S(1)}, bf16[64,768]{1,0:T(8,128)(2,1)S(1)}, u32[]{:S(2)}, u32[]{:S(2)}) collective-permute-start(bf16[64,768]{1,0:T(8,128)(2,1)S(1)} %copy-done.5), channel_id=1, source_target_pairs={{504,0},{505,1},{506,2},{507,3},{508,4},{509,5},{510,6},{511,7},{0... | collective-permute-start | bytes 294920 | tf_op jit(solution)/shard_map/ppermute | solution.py:432
  106.5 14.2 %copy-start.4 = (bf16[32,768]{1,0:T(8,128)(2,1)S(1)}, bf16[32,768]{1,0:T(8,128)(2,1)}, u32[]{:S(2)}) copy-start(bf16[32,768]{1,0:T(8,128)(2,1)} %get-tuple-element.60) | copy-start | bytes 147460
  106.6 4.5 %collective-permute-start.5 = (bf16[2,48,384]{2,1,0:T(8,128)(2,1)S(1)}, bf16[2,48,384]{2,1,0:T(8,128)(2,1)S(1)}, u32[]{:S(2)}, u32[]{:S(2)}) collective-permute-start(bf16[2,48,384]{2,1,0:T(8,128)(2,1)S(1)} %get-tuple-element.56), channel_id=1, source_target_pairs={{0,8},{8,0},{16,24},{24,16},{32,40},{40,32},{48,56},{56,48},{64,72... | collective-permute-start | bytes 221192 | tf_op jit(solution)/shard_map/ppermute | solution.py:436
  111.9 28.3 %all-to-all-start.2 = ((bf16[8,2,48,384]{3,2,1,0:T(8,128)(2,1)}), bf16[8,2,48,384]{3,2,1,0:T(8,128)(2,1)S(1)}, u32[]{:S(2)}, u32[]{:S(2)}) async-start(bf16[8,2,48,384]{3,2,1,0:T(8,128)(2,1)} %pair_copies.1), calls=%async_computation.2 | async-start | bytes 1179648 | tf_op jit(solution)/shard_map/all_to_all | solution.py:422
  120.8 7.8 %collective-permute-start.7 = (bf16[64,768]{1,0:T(8,128)(2,1)S(1)}, bf16[64,768]{1,0:T(8,128)(2,1)S(1)}, u32[]{:S(2)}, u32[]{:S(2)}) collective-permute-start(bf16[64,768]{1,0:T(8,128)(2,1)S(1)} %pad_maximum_fusion), channel_id=1, source_target_pairs={{7,0},{0,1},{1,2},{2,3},{3,4},{4,5},{5,6},{6,7},{15,8},{8,9},{9,10... | collective-permute-start | bytes 294920 | tf_op jit(solution)/shard_map/ppermute | solution.py:432
  141.0 14.4 %all-to-all-start.3 = ((bf16[4,2,48,384]{3,2,1,0:T(8,128)(2,1)}), bf16[4,2,48,384]{3,2,1,0:T(8,128)(2,1)S(1)}, u32[]{:S(2)}, u32[]{:S(2)}) async-start(bf16[4,2,48,384]{3,2,1,0:T(8,128)(2,1)} %sum_copies.2), calls=%async_computation.3 | async-start | bytes 589824 | tf_op jit(solution)/shard_map/all_to_all | solution.py:422
Sparse Core Ops, SparseCore 0:
  18.8 53.1 all-gather.2

commit v8 on v5

--- a/solution.py
+++ b/solution.py
@@ -238,10 +238,10 @@
     to_own,
     to_column,
     to_below,
-    to_local,
+    out_keep,
+    out_send,
     bias_s,
     quads,
-    out_local,
     staged,
     rows_small,
     grads,
@@ -291,25 +291,13 @@
         sems,
         2,
     )
-    local_shift = dot(mixed_shift, grads[...], TN) * grad_scale
-    out_local[:, 1] = local_shift.astype(BF16).reshape(8, ROWS, D)
-    local_plain = dot(mixed_plain, grad, TN) * grad_scale
-    out_local[:, 0] = local_plain.astype(BF16).reshape(8, ROWS, D)
-    wait_all(copy_all([(out_local, to_local)], sems, 6))
+    rows_small[...] = grad
+    for out, start in ((out_send, other), (out_keep, mine)):
+        part = dot(mixed_shift, grads[:, pl.ds(start, HALF)], TN) * grad_scale
+        out[:, 1] = part.astype(BF16).reshape(8, ROWS, HALF)
+        part = dot(mixed_plain, rows_small[:, pl.ds(start, HALF)], TN) * grad_scale
+        out[:, 0] = part.astype(BF16).reshape(8, ROWS, HALF)
     wait_all(stores)
-
-
-def sum_split(core_ref, parts, out_keep, out_send, total):
-    mine, other = sides(core_ref)
-    total[...] = jnp.sum(parts[...].astype(F32), axis=0)
-    out_keep[...] = total[:, :, pl.ds(mine, HALF)]
-    out_send[...] = total[:, :, pl.ds(other, HALF)].astype(BF16)
-
-
-def pair_copies(keep, arrived, out):
-    value = (keep[...] + arrived[...].astype(F32)).astype(BF16)
-    for i in range(out.shape[0]):
-        out[i] = value
 
 
 def sum_copies(parts, out):
@@ -518,54 +506,36 @@
     second_other = other_core(second_mine)
     piece = pltpu.HBM((32, D), BF16)
     column = pltpu.HBM((64, D), BF16)
-    local = pltpu.HBM((8, 2, ROWS, D), BF16)
-    g_own, to_right, to_below, local = pl.pallas_call(
+    local = jax.ShapeDtypeStruct((8, 2, ROWS, HALF), BF16)
+    g_own, to_right, to_below, keep, send = pl.pallas_call(
         lambda *refs: main_kernel(grad_scale, *refs),
-        out_shape=(piece, column, piece, local),
+        out_shape=(piece, column, piece, local, local),
         in_specs=[SMEM] + [HBM] * 2 + [VMEM] * 5,
-        out_specs=[HBM] * 4,
+        out_specs=[HBM] * 3 + [VMEM] * 2,
         scratch_shapes=[
             pltpu.VMEM((SPOTS, LANES), F32),
             pltpu.VMEM((128, D), BF16),
-            pltpu.VMEM((8, 2, ROWS, D), BF16),
             pltpu.VMEM((128, 2 * D + WIDE), BF16),
             pltpu.VMEM((128, D), BF16),
             pltpu.VMEM((128, D), BF16),
             pltpu.VMEM((128, D), F32),
             pltpu.VMEM((LANES, WIDE), BF16),
-            pltpu.SemaphoreType.DMA((7,)),
+            pltpu.SemaphoreType.DMA((6,)),
         ],
         compiler_params=params(),
         cost_estimate=cost(1_000_000, 1_000_000),
         name="main",
     )(core, far(own), far(bias_s), right, below, diag, second_mine, second_other)
 
-    local, to_right, to_below = lax.optimization_barrier((local, to_right, to_below))
-    part = swap(local, "freq")
+    part = (keep.astype(F32) + other_core(send).astype(F32)).astype(BF16)
+    part, to_right, to_below = lax.optimization_barrier((part, to_right, to_below))
+    part = swap(part, "freq")
     column = from_offset(to_right, -1, 0)
-    half = (2, ROWS, HALF)
-    keep, send = pl.pallas_call(
-        sum_split,
-        out_shape=(jax.ShapeDtypeStruct(half, F32), jax.ShapeDtypeStruct(half, BF16)),
-        in_specs=[SMEM, VMEM],
-        out_specs=[VMEM] * 2,
-        scratch_shapes=[pltpu.VMEM((2, ROWS, D), F32)],
-        compiler_params=params(),
-        name="sum_split",
-    )(core, part)
-    part = pl.pallas_call(
-        pair_copies,
-        out_shape=jax.ShapeDtypeStruct((8,) + half, BF16),
-        in_specs=[VMEM] * 2,
-        out_specs=VMEM,
-        compiler_params=params(),
-        name="pair_copies",
-    )(keep, other_core(send))
     part, column, to_below = lax.optimization_barrier((part, column, to_below))
-    part = swap(part, "tm", tm_groups("z"))
+    part = swap(summed(part, 4), "tm", tm_groups("y_hi"))
     row = from_offset(jnp.concatenate([to_below, column[32:64]], axis=0), 0, -1)
     part, row = lax.optimization_barrier((part, row))
-    part = swap(summed(part, 4), "tm", tm_groups("y_hi"))
+    part = swap(summed(part, 8), "tm", tm_groups("z"))
     grad_tokens = pl.pallas_call(
         plain_back,
         out_shape=jax.ShapeDtypeStruct((128, D), BF16),

time: 147 us -> 140 us (0.952)
  waiting for transfers between devices: 51.6 us -> 42.1 us
  starting transfers between devices: 63.3 us -> 65 us
    all_to_all x5, waiting for transfers between devices: 38.1 us -> 20.6 us  [swap(): return lax.all_to_all(value, axis, 0, 0, axis_index_groups=groups)]
    ppermute x5, waiting for transfers between devices: 7.74 us -> 15 us  [from_offset(): return lax.ppermute(value, ('tm', 'freq'), pairs)]
    all_to_all x5, starting transfers between devices: 21.5 us -> 23.9 us  [swap(): return lax.all_to_all(value, axis, 0, 0, axis_index_groups=groups)]
where the time goes in v8:
time: 140 us; the launch traced here: 139 us
  starting transfers between devices  65 us (46%)
  waiting for transfers between devices  42.1 us (30%)
  Pallas kernels  24.5 us (18%)
  blocking collectives  5.27 us (4%)
    ppermute x5, starting transfers between devices, from_offset(): return lax.ppermute(value, ('tm', 'freq'), pairs)  26.4 us
    all_to_all x5, starting transfers between devices, swap(): return lax.all_to_all(value, axis, 0, 0, axis_index_groups=groups)  23.9 us
    all_to_all x5, waiting for transfers between devices, swap(): return lax.all_to_all(value, axis, 0, 0, axis_index_groups=groups)  20.6 us
    ppermute x5, waiting for transfers between devices, from_offset(): return lax.ppermute(value, ('tm', 'freq'), pairs)  15 us
    ppermute x3, starting transfers between devices, other_core(): lax.ppermute(value, 'tm', [(i, i ^ 1) for i in range(lax.axis_size('tm'))])  14.6 us
    ppermute x3, waiting for transfers between devices, other_core(): lax.ppermute(value, 'tm', [(i, i ^ 1) for i in range(lax.axis_size('tm'))])  6.51 us
    pallas_call x1, Pallas kernels, shards(): pl.pallas_call(lambda *refs: main_kernel(grad_scale, *refs), out_shape=(p...  5.74 us
    pallas_call x1, Pallas kernels, shards(): pl.pallas_call(plain_back, out_shape=jax.ShapeDtypeStruct((128, D), BF16)...  5.55 us
  transfers between devices with their start and end apart: 13, of which 9 were waited for; matrix products, arithmetic and copies ran while one was open for 0% of the time, Pallas kernels for 10%

profile of v8, /device:TPU:1, one launch (start us, length us, event | category | flops | bytes accessed | tf_op | source)
XLA Modules:
  0.0 138.8 jit_solution(4283263832067935975)
XLA Ops:
  0.6 2.1 %prepare.2 = bf16[8,192,384]{2,1,0:T(8,128)(2,1)} custom-call(s32[1]{0:T(128)} %bitcast.core_ref.refs_0_, bf16[144,768]{1,0:T(8,128)(2,1)} %bitcast.8, bf16[48,768]{1,0:T(8,128)(2,1)} %proj.2), custom_call_target="tpu_custom_call" | custom-call | tf_op jit(solution)/shard_map/prepare/pallas_call | solution.py:443
  2.8 5.9 %all-to-all-start = ((bf16[8,192,384]{2,1,0:T(8,128)(2,1)}), bf16[8,192,384]{2,1,0:T(8,128)(2,1)S(1)}, u32[]{:S(2)}, u32[]{:S(2)}) async-start(bf16[8,192,384]{2,1,0:T(8,128)(2,1)} %prepare.2), calls=%async_computation | async-start | bytes 2359296 | tf_op jit(solution)/shard_map/all_to_all | solution.py:403
  8.7 2.1 %prepare.3 = bf16[8,192,384]{2,1,0:T(8,128)(2,1)} custom-call(s32[1]{0:T(128)} %bitcast.core_ref.refs_0_, bf16[144,768]{1,0:T(8,128)(2,1)} %bitcast.9, bf16[48,768]{1,0:T(8,128)(2,1)} %proj.3), custom_call_target="tpu_custom_call" | custom-call | tf_op jit(solution)/shard_map/prepare/pallas_call | solution.py:443
  10.9 2.0 %biases.1 = (f32[64,768]{1,0:T(8,128)}, f32[64,768]{1,0:T(8,128)}) custom-call(s32[2]{0:T(128)S(1)} %add_convert_fusion.1.edge_ref, f32[12,225]{1,0:T(8,128)S(1)} %copy-done.2, f32[12,225]{1,0:T(8,128)S(1)} %copy-done.3), custom_call_target="tpu_custom_call" | custom-call | tf_op jit(solution)/shard_map/biases/pallas_call | solution.py:459
  12.9 8.5 %all-to-all-done.w_mine_ref.mine_far = bf16[8,192,384]{2,1,0:T(8,128)(2,1)S(1)} async-done(((bf16[8,192,384]{2,1,0:T(8,128)(2,1)}), bf16[8,192,384]{2,1,0:T(8,128)(2,1)S(1)}, u32[]{:S(2)}, u32[]{:S(2)}) %all-to-all-start) | async-done | bytes 1179680 | tf_op jit(solution)/shard_map/all_to_all | solution.py:403
  21.4 3.9 %all-to-all-start.1 = ((bf16[8,192,384]{2,1,0:T(8,128)(2,1)}), bf16[8,192,384]{2,1,0:T(8,128)(2,1)S(1)}, u32[]{:S(2)}, u32[]{:S(2)}) async-start(bf16[8,192,384]{2,1,0:T(8,128)(2,1)} %prepare.3), calls=%async_computation.1 | async-start | bytes 2359296 | tf_op jit(solution)/shard_map/all_to_all | solution.py:403
  25.2 7.1 %collective-permute-start = (bf16[8,192,384]{2,1,0:T(8,128)(2,1)S(1)}, bf16[8,192,384]{2,1,0:T(8,128)(2,1)S(1)}, u32[]{:S(2)}, u32[]{:S(2)}) collective-permute-start(bf16[8,192,384]{2,1,0:T(8,128)(2,1)S(1)} %all-to-all-done.w_mine_ref.mine_far), channel_id=1, source_target_pairs={{0,8},{8,0},{16,24},{24,16},{32,40},{40,32},{48,56},{56,48},{64,72... | collective-permute-start | bytes 3538952 | tf_op jit(solution)/shard_map/ppermute | solution.py:417
  32.3 2.5 %collective-permute-done.w_other_ref.other_far = bf16[8,192,384]{2,1,0:T(8,128)(2,1)S(1)} collective-permute-done((bf16[8,192,384]{2,1,0:T(8,128)(2,1)S(1)}, bf16[8,192,384]{2,1,0:T(8,128)(2,1)S(1)}, u32[]{:S(2)}, u32[]{:S(2)}) %collective-permute-start) | collective-permute-done | bytes 1179680 | tf_op jit(solution)/shard_map/ppermute | solution.py:417
  34.7 4.5 %plain_forward.1 = (bf16[32,1920]{1,0:T(8,128)(2,1)}, bf16[32,1920]{1,0:T(8,128)(2,1)}, bf16[32,1920]{1,0:T(8,128)(2,1)}, bf16[32,1920]{1,0:T(8,128)(2,1)}) custom-call(s32[1]{0:T(128)} %bitcast.core_ref.refs_0_, bf16[128,768]{1,0:T(8,128)(2,1)} %bitcast.11, bf16[128,768]{1,0:T(8,128)(2,1)} %bitcast.10, f32[64,768]{1,0:T(8,128)} %get-tuple-element.36.bias_far, ...), custom_call_target="tpu_custom_call" | custom-call | flops 1000000 | bytes 1000000 | tf_op jit(solution)/shard_map/plain_forward/pallas_call | solution.py:481
  39.3 2.3 %collective-permute-start.1 = (bf16[32,1920]{1,0:T(8,128)(2,1)}, bf16[32,1920]{1,0:T(8,128)(2,1)S(1)}, u32[]{:S(2)}, u32[]{:S(2)}) collective-permute-start(bf16[32,1920]{1,0:T(8,128)(2,1)} %get-tuple-element.41), channel_id=1, source_target_pairs={{8,0},{9,1},{10,2},{11,3},{12,4},{13,5},{14,6},{15,7},{16,8},{17,9... | collective-permute-start | bytes 368648 | tf_op jit(solution)/shard_map/ppermute | solution.py:413
  41.6 5.7 %collective-permute-start.2 = (bf16[32,1920]{1,0:T(8,128)(2,1)}, bf16[32,1920]{1,0:T(8,128)(2,1)S(1)}, u32[]{:S(2)}, u32[]{:S(2)}) collective-permute-start(bf16[32,1920]{1,0:T(8,128)(2,1)} %get-tuple-element.42), channel_id=1, source_target_pairs={{1,0},{2,1},{3,2},{4,3},{5,4},{6,5},{7,6},{0,7},{9,8},{10,9},{11,1... | collective-permute-start | bytes 368648 | tf_op jit(solution)/shard_map/ppermute | solution.py:413
  47.3 13.9 %collective-permute-start.3 = (bf16[32,1920]{1,0:T(8,128)(2,1)}, bf16[32,1920]{1,0:T(8,128)(2,1)S(1)}, u32[]{:S(2)}, u32[]{:S(2)}) collective-permute-start(bf16[32,1920]{1,0:T(8,128)(2,1)} %get-tuple-element.43), channel_id=1, source_target_pairs={{9,0},{10,1},{11,2},{12,3},{13,4},{14,5},{15,6},{8,7},{17,8},{18,9... | collective-permute-start | bytes 368648 | tf_op jit(solution)/shard_map/ppermute | solution.py:413
  61.2 2.1 %collective-permute-done.3.refs_5_ = bf16[32,1920]{1,0:T(8,128)(2,1)S(1)} collective-permute-done((bf16[32,1920]{1,0:T(8,128)(2,1)}, bf16[32,1920]{1,0:T(8,128)(2,1)S(1)}, u32[]{:S(2)}, u32[]{:S(2)}) %collective-permute-start.3) | collective-permute-done | bytes 122912 | tf_op jit(solution)/shard_map/ppermute | solution.py:413
  63.3 5.3 %collective-permute-start.4 = (bf16[8,192,384]{2,1,0:T(8,128)(2,1)S(1)}, bf16[8,192,384]{2,1,0:T(8,128)(2,1)S(1)}, u32[]{:S(2)}, u32[]{:S(2)}) collective-permute-start(bf16[8,192,384]{2,1,0:T(8,128)(2,1)S(1)} %all-to-all-done.1.refs_6_), channel_id=1, source_target_pairs={{0,8},{8,0},{16,24},{24,16},{32,40},{40,32},{48,56},{56,48},{64,72... | collective-permute-start | bytes 3538952 | tf_op jit(solution)/shard_map/ppermute | solution.py:417
  68.6 2.5 %collective-permute-done.4.refs_7_ = bf16[8,192,384]{2,1,0:T(8,128)(2,1)S(1)} collective-permute-done((bf16[8,192,384]{2,1,0:T(8,128)(2,1)S(1)}, bf16[8,192,384]{2,1,0:T(8,128)(2,1)S(1)}, u32[]{:S(2)}, u32[]{:S(2)}) %collective-permute-start.4) | collective-permute-done | bytes 1179680 | tf_op jit(solution)/shard_map/ppermute | solution.py:417
  71.1 5.7 %main.1 = (bf16[32,768]{1,0:T(8,128)(2,1)}, bf16[64,768]{1,0:T(8,128)(2,1)}, bf16[32,768]{1,0:T(8,128)(2,1)}, bf16[8,2,48,384]{3,2,1,0:T(8,128)(2,1)S(1)}, bf16[8,2,48,384]{3,2,1,0:T(8,128)(2,1)S(1)}) custom-call(s32[1]{0:T(128)} %bitcast.core_ref.refs_0_, bf16[32,1920]{1,0:T(8,128)(2,1)} %get-tuple-element.38.refs_1_, f32[64,768]{1,0:T(8,128)} %get-tuple-element.39.refs_2_, ...), custom_call_target="tpu_custom_call" | custom-call | flops 1000000 | bytes 1000000 | tf_op jit(solution)/shard_map/main/pallas_call | solution.py:510
  76.8 2.3 %collective-permute-start.5 = (bf16[8,2,48,384]{3,2,1,0:T(8,128)(2,1)S(1)}, bf16[8,2,48,384]{3,2,1,0:T(8,128)(2,1)S(1)}, u32[]{:S(2)}, u32[]{:S(2)}) collective-permute-start(bf16[8,2,48,384]{3,2,1,0:T(8,128)(2,1)S(1)} %get-tuple-element.49), channel_id=1, source_target_pairs={{0,8},{8,0},{16,24},{24,16},{32,40},{40,32},{48,56},{56,48},{64,72... | collective-permute-start | bytes 1769480 | tf_op jit(solution)/shard_map/ppermute | solution.py:417
  79.1 1.6 %collective-permute-done.5 = bf16[8,2,48,384]{3,2,1,0:T(8,128)(2,1)S(1)} collective-permute-done((bf16[8,2,48,384]{3,2,1,0:T(8,128)(2,1)S(1)}, bf16[8,2,48,384]{3,2,1,0:T(8,128)(2,1)S(1)}, u32[]{:S(2)}, u32[]{:S(2)}) %collective-permute-start.5) | collective-permute-done | bytes 589856 | tf_op jit(solution)/shard_map/ppermute | solution.py:417
  80.7 1.0 add_convert_fusion
  81.7 3.7 %all-to-all-start.2 = ((bf16[8,2,48,384]{3,2,1,0:T(8,128)(2,1)}), bf16[8,2,48,384]{3,2,1,0:T(8,128)(2,1)S(1)}, u32[]{:S(2)}, u32[]{:S(2)}) async-start(bf16[8,2,48,384]{3,2,1,0:T(8,128)(2,1)} %add_convert_fusion), calls=%async_computation.2 | async-start | bytes 1179648 | tf_op jit(solution)/shard_map/all_to_all | solution.py:403
  85.4 1.9 %collective-permute-start.6 = (bf16[64,768]{1,0:T(8,128)(2,1)S(1)}, bf16[64,768]{1,0:T(8,128)(2,1)S(1)}, u32[]{:S(2)}, u32[]{:S(2)}) collective-permute-start(bf16[64,768]{1,0:T(8,128)(2,1)S(1)} %copy-done.5), channel_id=1, source_target_pairs={{504,0},{505,1},{506,2},{507,3},{508,4},{509,5},{510,6},{511,7},{0... | collective-permute-start | bytes 294920 | tf_op jit(solution)/shard_map/ppermute | solution.py:413
  87.3 6.7 %collective-permute-done.6.column = bf16[64,768]{1,0:T(8,128)(2,1)S(1)} collective-permute-done((bf16[64,768]{1,0:T(8,128)(2,1)S(1)}, bf16[64,768]{1,0:T(8,128)(2,1)S(1)}, u32[]{:S(2)}, u32[]{:S(2)}) %collective-permute-start.6) | collective-permute-done | bytes 98336 | tf_op jit(solution)/shard_map/ppermute | solution.py:413
  94.1 1.5 %all-to-all-done.2.parts = bf16[8,2,48,384]{3,2,1,0:T(8,128)(2,1)S(1)} async-done(((bf16[8,2,48,384]{3,2,1,0:T(8,128)(2,1)}), bf16[8,2,48,384]{3,2,1,0:T(8,128)(2,1)S(1)}, u32[]{:S(2)}, u32[]{:S(2)}) %all-to-all-start.2) | async-done | bytes 589856 | tf_op jit(solution)/shard_map/all_to_all | solution.py:403
  95.6 0.8 sum_copies.3
  96.4 3.5 %all-to-all-start.3 = ((bf16[4,2,48,384]{3,2,1,0:T(8,128)(2,1)}), bf16[4,2,48,384]{3,2,1,0:T(8,128)(2,1)S(1)}, u32[]{:S(2)}, u32[]{:S(2)}) async-start(bf16[4,2,48,384]{3,2,1,0:T(8,128)(2,1)} %sum_copies.3), calls=%async_computation.3 | async-start | bytes 589824 | tf_op jit(solution)/shard_map/all_to_all | solution.py:403
  99.9 2.6 %collective-permute-start.7 = (bf16[64,768]{1,0:T(8,128)(2,1)S(1)}, bf16[64,768]{1,0:T(8,128)(2,1)S(1)}, u32[]{:S(2)}, u32[]{:S(2)}) collective-permute-start(bf16[64,768]{1,0:T(8,128)(2,1)S(1)} %pad_maximum_fusion), channel_id=1, source_target_pairs={{7,0},{0,1},{1,2},{2,3},{3,4},{4,5},{5,6},{6,7},{15,8},{8,9},{9,10... | collective-permute-start | bytes 294920 | tf_op jit(solution)/shard_map/ppermute | solution.py:413
  102.5 6.1 %collective-permute-done.7.row = bf16[64,768]{1,0:T(8,128)(2,1)S(1)} collective-permute-done((bf16[64,768]{1,0:T(8,128)(2,1)S(1)}, bf16[64,768]{1,0:T(8,128)(2,1)S(1)}, u32[]{:S(2)}, u32[]{:S(2)}) %collective-permute-start.7) | collective-permute-done | bytes 98336 | tf_op jit(solution)/shard_map/ppermute | solution.py:413
  108.7 0.9 sum_copies.4
  109.5 7.0 %all-to-all-start.4 = ((bf16[8,2,48,384]{3,2,1,0:T(8,128)(2,1)}), bf16[8,2,48,384]{3,2,1,0:T(8,128)(2,1)S(1)}, u32[]{:S(2)}, u32[]{:S(2)}) async-start(bf16[8,2,48,384]{3,2,1,0:T(8,128)(2,1)} %sum_copies.4), calls=%async_computation.4 | async-start | bytes 1179648 | tf_op jit(solution)/shard_map/all_to_all | solution.py:403
  116.6 5.5 %plain_back.1 = bf16[128,768]{1,0:T(8,128)(2,1)} custom-call(s32[1]{0:T(128)} %bitcast.core_ref.refs_0_, bf16[128,768]{1,0:T(8,128)(2,1)} %bitcast.12, bf16[32,768]{1,0:T(8,128)(2,1)} %get-tuple-element.59.own_far, f32[64,768]{1,0:T(8,128)} %get-tuple-element.36.bias_far, bf16[8,192,384]{2,1,0:T(8,128)(2,1)} %copy-done, bf16[8,192,384]{2,1,0:T(8,128)(2,1)} %copy-done.1, ...), custom_call_target="tpu_custom_call" | custom-call | flops 4000000000 | bytes 4000000 | tf_op jit(solution)/shard_map/plain_back/pallas_call | solution.py:539
  122.2 10.6 %all-to-all-done.4.parts = bf16[8,2,48,384]{3,2,1,0:T(8,128)(2,1)S(1)} async-done(((bf16[8,2,48,384]{3,2,1,0:T(8,128)(2,1)}), bf16[8,2,48,384]{3,2,1,0:T(8,128)(2,1)S(1)}, u32[]{:S(2)}, u32[]{:S(2)}) %all-to-all-start.4) | async-done | bytes 589856 | tf_op jit(solution)/shard_map/all_to_all | solution.py:403
  132.8 5.3 %all_gather.3.parts = bf16[2,2,48,384]{3,2,1,0:T(8,128)(2,1)S(1)} all-gather(bf16[1,2,48,384]{3,2,1,0:T(8,128)(2,1)S(1)} %sum_copies.5), channel_id=1, replica_groups={{0,8},{16,24},{32,40},{48,56},{64,72},{80,88},{96,104},{112,120},{128,1..., dimensions={0}, use_global_device_ids=true | all-gather | bytes 221184 | tf_op jit(solution)/shard_map/all_gather | solution.py:562
  (21 shorter events, 0.9 us)
Async XLA Ops:
  2.8 18.6 %all-to-all-start = ((bf16[8,192,384]{2,1,0:T(8,128)(2,1)}), bf16[8,192,384]{2,1,0:T(8,128)(2,1)S(1)}, u32[]{:S(2)}, u32[]{:S(2)}) async-start(bf16[8,192,384]{2,1,0:T(8,128)(2,1)} %prepare.2), calls=%async_computation | async-start | bytes 2359296 | tf_op jit(solution)/shard_map/all_to_all | solution.py:403
  8.7 2.2 %copy-start.2 = (f32[12,225]{1,0:T(8,128)S(1)}, f32[12,225]{1,0:T(8,128)}, u32[]{:S(2)}) copy-start(f32[12,225]{1,0:T(8,128)} %table_p.1) | copy-start | bytes 32404
  8.7 2.2 %copy-start.3 = (f32[12,225]{1,0:T(8,128)S(1)}, f32[12,225]{1,0:T(8,128)}, u32[]{:S(2)}) copy-start(f32[12,225]{1,0:T(8,128)} %table_s.1) | copy-start | bytes 32404
  21.4 13.4 %copy-start = (bf16[8,192,384]{2,1,0:T(8,128)(2,1)}, bf16[8,192,384]{2,1,0:T(8,128)(2,1)S(1)}, u32[]{:S(2)}) copy-start(bf16[8,192,384]{2,1,0:T(8,128)(2,1)S(1)} %all-to-all-done.w_mine_ref.mine_far) | copy-start | bytes 3538948
  21.4 42.0 %all-to-all-start.1 = ((bf16[8,192,384]{2,1,0:T(8,128)(2,1)}), bf16[8,192,384]{2,1,0:T(8,128)(2,1)S(1)}, u32[]{:S(2)}, u32[]{:S(2)}) async-start(bf16[8,192,384]{2,1,0:T(8,128)(2,1)} %prepare.3), calls=%async_computation.1 | async-start | bytes 2359296 | tf_op jit(solution)/shard_map/all_to_all | solution.py:403
  25.2 9.5 %collective-permute-start = (bf16[8,192,384]{2,1,0:T(8,128)(2,1)S(1)}, bf16[8,192,384]{2,1,0:T(8,128)(2,1)S(1)}, u32[]{:S(2)}, u32[]{:S(2)}) collective-permute-start(bf16[8,192,384]{2,1,0:T(8,128)(2,1)S(1)} %all-to-all-done.w_mine_ref.mine_far), channel_id=1, source_target_pairs={{0,8},{8,0},{16,24},{24,16},{32,40},{40,32},{48,56},{56,48},{64,72... | collective-permute-start | bytes 3538952 | tf_op jit(solution)/shard_map/ppermute | solution.py:417
  34.7 4.5 %copy-start.1 = (bf16[8,192,384]{2,1,0:T(8,128)(2,1)}, bf16[8,192,384]{2,1,0:T(8,128)(2,1)S(1)}, u32[]{:S(2)}) copy-start(bf16[8,192,384]{2,1,0:T(8,128)(2,1)S(1)} %collective-permute-done.w_other_ref.other_far) | copy-start | bytes 3538948
  39.3 21.9 %collective-permute-start.1 = (bf16[32,1920]{1,0:T(8,128)(2,1)}, bf16[32,1920]{1,0:T(8,128)(2,1)S(1)}, u32[]{:S(2)}, u32[]{:S(2)}) collective-permute-start(bf16[32,1920]{1,0:T(8,128)(2,1)} %get-tuple-element.41), channel_id=1, source_target_pairs={{8,0},{9,1},{10,2},{11,3},{12,4},{13,5},{14,6},{15,7},{16,8},{17,9... | collective-permute-start | bytes 368648 | tf_op jit(solution)/shard_map/ppermute | solution.py:413
  41.6 19.6 %collective-permute-start.2 = (bf16[32,1920]{1,0:T(8,128)(2,1)}, bf16[32,1920]{1,0:T(8,128)(2,1)S(1)}, u32[]{:S(2)}, u32[]{:S(2)}) collective-permute-start(bf16[32,1920]{1,0:T(8,128)(2,1)} %get-tuple-element.42), channel_id=1, source_target_pairs={{1,0},{2,1},{3,2},{4,3},{5,4},{6,5},{7,6},{0,7},{9,8},{10,9},{11,1... | collective-permute-start | bytes 368648 | tf_op jit(solution)/shard_map/ppermute | solution.py:413
  47.3 16.1 %collective-permute-start.3 = (bf16[32,1920]{1,0:T(8,128)(2,1)}, bf16[32,1920]{1,0:T(8,128)(2,1)S(1)}, u32[]{:S(2)}, u32[]{:S(2)}) collective-permute-start(bf16[32,1920]{1,0:T(8,128)(2,1)} %get-tuple-element.43), channel_id=1, source_target_pairs={{9,0},{10,1},{11,2},{12,3},{13,4},{14,5},{15,6},{8,7},{17,8},{18,9... | collective-permute-start | bytes 368648 | tf_op jit(solution)/shard_map/ppermute | solution.py:413
  63.3 7.7 %collective-permute-start.4 = (bf16[8,192,384]{2,1,0:T(8,128)(2,1)S(1)}, bf16[8,192,384]{2,1,0:T(8,128)(2,1)S(1)}, u32[]{:S(2)}, u32[]{:S(2)}) collective-permute-start(bf16[8,192,384]{2,1,0:T(8,128)(2,1)S(1)} %all-to-all-done.1.refs_6_), channel_id=1, source_target_pairs={{0,8},{8,0},{16,24},{24,16},{32,40},{40,32},{48,56},{56,48},{64,72... | collective-permute-start | bytes 3538952 | tf_op jit(solution)/shard_map/ppermute | solution.py:417
  76.8 3.9 %collective-permute-start.5 = (bf16[8,2,48,384]{3,2,1,0:T(8,128)(2,1)S(1)}, bf16[8,2,48,384]{3,2,1,0:T(8,128)(2,1)S(1)}, u32[]{:S(2)}, u32[]{:S(2)}) collective-permute-start(bf16[8,2,48,384]{3,2,1,0:T(8,128)(2,1)S(1)} %get-tuple-element.49), channel_id=1, source_target_pairs={{0,8},{8,0},{16,24},{24,16},{32,40},{40,32},{48,56},{56,48},{64,72... | collective-permute-start | bytes 1769480 | tf_op jit(solution)/shard_map/ppermute | solution.py:417
  80.7 4.7 %copy-start.5 = (bf16[64,768]{1,0:T(8,128)(2,1)S(1)}, bf16[64,768]{1,0:T(8,128)(2,1)}, u32[]{:S(2)}) copy-start(bf16[64,768]{1,0:T(8,128)(2,1)} %get-tuple-element.53) | copy-start | bytes 294916
  81.7 18.1 %copy-start.4 = (bf16[32,768]{1,0:T(8,128)(2,1)S(1)}, bf16[32,768]{1,0:T(8,128)(2,1)}, u32[]{:S(2)}) copy-start(bf16[32,768]{1,0:T(8,128)(2,1)} %get-tuple-element.56) | copy-start | bytes 147460
  81.7 13.9 %all-to-all-start.2 = ((bf16[8,2,48,384]{3,2,1,0:T(8,128)(2,1)}), bf16[8,2,48,384]{3,2,1,0:T(8,128)(2,1)S(1)}, u32[]{:S(2)}, u32[]{:S(2)}) async-start(bf16[8,2,48,384]{3,2,1,0:T(8,128)(2,1)} %add_convert_fusion), calls=%async_computation.2 | async-start | bytes 1179648 | tf_op jit(solution)/shard_map/all_to_all | solution.py:403
  85.4 8.7 %collective-permute-start.6 = (bf16[64,768]{1,0:T(8,128)(2,1)S(1)}, bf16[64,768]{1,0:T(8,128)(2,1)S(1)}, u32[]{:S(2)}, u32[]{:S(2)}) collective-permute-start(bf16[64,768]{1,0:T(8,128)(2,1)S(1)} %copy-done.5), channel_id=1, source_target_pairs={{504,0},{505,1},{506,2},{507,3},{508,4},{509,5},{510,6},{511,7},{0... | collective-permute-start | bytes 294920 | tf_op jit(solution)/shard_map/ppermute | solution.py:413
  96.4 12.3 %all-to-all-start.3 = ((bf16[4,2,48,384]{3,2,1,0:T(8,128)(2,1)}), bf16[4,2,48,384]{3,2,1,0:T(8,128)(2,1)S(1)}, u32[]{:S(2)}, u32[]{:S(2)}) async-start(bf16[4,2,48,384]{3,2,1,0:T(8,128)(2,1)} %sum_copies.3), calls=%async_computation.3 | async-start | bytes 589824 | tf_op jit(solution)/shard_map/all_to_all | solution.py:403
  99.9 8.8 %collective-permute-start.7 = (bf16[64,768]{1,0:T(8,128)(2,1)S(1)}, bf16[64,768]{1,0:T(8,128)(2,1)S(1)}, u32[]{:S(2)}, u32[]{:S(2)}) collective-permute-start(bf16[64,768]{1,0:T(8,128)(2,1)S(1)} %pad_maximum_fusion), channel_id=1, source_target_pairs={{7,0},{0,1},{1,2},{2,3},{3,4},{4,5},{5,6},{6,7},{15,8},{8,9},{9,10... | collective-permute-start | bytes 294920 | tf_op jit(solution)/shard_map/ppermute | solution.py:413
  109.5 23.2 %all-to-all-start.4 = ((bf16[8,2,48,384]{3,2,1,0:T(8,128)(2,1)}), bf16[8,2,48,384]{3,2,1,0:T(8,128)(2,1)S(1)}, u32[]{:S(2)}, u32[]{:S(2)}) async-start(bf16[8,2,48,384]{3,2,1,0:T(8,128)(2,1)} %sum_copies.4), calls=%async_computation.4 | async-start | bytes 1179648 | tf_op jit(solution)/shard_map/all_to_all | solution.py:403

commit v9 on v8

--- a/solution.py
+++ b/solution.py
@@ -494,7 +494,7 @@
             pltpu.SemaphoreType.DMA((7,)),
         ],
         compiler_params=params(),
-        cost_estimate=cost(1_000_000, 1_000_000),
+        cost_estimate=cost(20_000_000_000, 1_000_000),
         name="plain_forward",
     )(core, far(tok), far(cot), far(bias_p), first_mine, first_other)
     right = from_offset(to_left, 1, 0)

time: 140 us -> 138 us (0.986)
  waiting for transfers between devices: 42.1 us -> 39.6 us
    ppermute x3, waiting for transfers between devices: 6.51 us -> 4.06 us  [other_core(): lax.ppermute(value, 'tm', [(i, i ^ 1) for i in range(lax.axis_size('tm'))])]
    all_to_all x5, waiting for transfers between devices: 20.6 us -> 18.9 us  [swap(): return lax.all_to_all(value, axis, 0, 0, axis_index_groups=groups)]
    ppermute x5, waiting for transfers between devices: 15 us -> 16.6 us  [from_offset(): return lax.ppermute(value, ('tm', 'freq'), pairs)]
  transfers between devices with their start and end apart: 13 -> 13, of which waited for: 9 -> 8; matrix products, arithmetic and copies ran while one was open for 0% -> 0% of each run, Pallas kernels for 10% -> 10%
where the time goes in v9:
time: 138 us; the launch traced here: 137 us
  starting transfers between devices  64.7 us (47%)
  waiting for transfers between devices  39.6 us (29%)
  Pallas kernels  24.5 us (18%)
  blocking collectives  6.49 us (5%)
    ppermute x5, starting transfers between devices, from_offset(): return lax.ppermute(value, ('tm', 'freq'), pairs)  25.5 us
    all_to_all x5, starting transfers between devices, swap(): return lax.all_to_all(value, axis, 0, 0, axis_index_groups=groups)  24.1 us
    all_to_all x5, waiting for transfers between devices, swap(): return lax.all_to_all(value, axis, 0, 0, axis_index_groups=groups)  18.9 us
    ppermute x5, waiting for transfers between devices, from_offset(): return lax.ppermute(value, ('tm', 'freq'), pairs)  16.6 us
    ppermute x3, starting transfers between devices, other_core(): lax.ppermute(value, 'tm', [(i, i ^ 1) for i in range(lax.axis_size('tm'))])  15 us
    all_gather x1, blocking collectives, shards(): part = lax.all_gather(part, 'tm', axis_index_groups=tm_groups('core'))  6.49 us
    pallas_call x1, Pallas kernels, shards(): pl.pallas_call(lambda *refs: main_kernel(grad_scale, *refs), out_shape=(p...  5.74 us
    pallas_call x1, Pallas kernels, shards(): pl.pallas_call(plain_back, out_shape=jax.ShapeDtypeStruct((128, D), BF16)...  5.54 us
  transfers between devices with their start and end apart: 13, of which 8 were waited for; matrix products, arithmetic and copies ran while one was open for 0% of the time, Pallas kernels for 10%

profile of v9, /device:TPU:1, one launch (start us, length us, event | category | flops | bytes accessed | tf_op | source)
XLA Modules:
  0.0 137.3 jit_solution(2882732694400874491)
XLA Ops:
  0.6 2.1 %prepare.2 = bf16[8,192,384]{2,1,0:T(8,128)(2,1)} custom-call(s32[1]{0:T(128)} %bitcast.core_ref.refs_0_, bf16[144,768]{1,0:T(8,128)(2,1)} %bitcast.8, bf16[48,768]{1,0:T(8,128)(2,1)} %proj.2), custom_call_target="tpu_custom_call" | custom-call | tf_op jit(solution)/shard_map/prepare/pallas_call | solution.py:443
  2.8 5.9 %all-to-all-start = ((bf16[8,192,384]{2,1,0:T(8,128)(2,1)}), bf16[8,192,384]{2,1,0:T(8,128)(2,1)S(1)}, u32[]{:S(2)}, u32[]{:S(2)}) async-start(bf16[8,192,384]{2,1,0:T(8,128)(2,1)} %prepare.2), calls=%async_computation | async-start | bytes 2359296 | tf_op jit(solution)/shard_map/all_to_all | solution.py:403
  8.7 2.1 %prepare.3 = bf16[8,192,384]{2,1,0:T(8,128)(2,1)} custom-call(s32[1]{0:T(128)} %bitcast.core_ref.refs_0_, bf16[144,768]{1,0:T(8,128)(2,1)} %bitcast.9, bf16[48,768]{1,0:T(8,128)(2,1)} %proj.3), custom_call_target="tpu_custom_call" | custom-call | tf_op jit(solution)/shard_map/prepare/pallas_call | solution.py:443
  10.9 2.0 %biases.1 = (f32[64,768]{1,0:T(8,128)}, f32[64,768]{1,0:T(8,128)}) custom-call(s32[2]{0:T(128)S(1)} %add_convert_fusion.1.edge_ref, f32[12,225]{1,0:T(8,128)S(1)} %copy-done.1, f32[12,225]{1,0:T(8,128)S(1)} %copy-done.2), custom_call_target="tpu_custom_call" | custom-call | tf_op jit(solution)/shard_map/biases/pallas_call | solution.py:459
  12.9 8.5 %all-to-all-done.w_mine_ref.mine_far = bf16[8,192,384]{2,1,0:T(8,128)(2,1)S(1)} async-done(((bf16[8,192,384]{2,1,0:T(8,128)(2,1)}), bf16[8,192,384]{2,1,0:T(8,128)(2,1)S(1)}, u32[]{:S(2)}, u32[]{:S(2)}) %all-to-all-start) | async-done | bytes 1179680 | tf_op jit(solution)/shard_map/all_to_all | solution.py:403
  21.4 7.3 %collective-permute-start = (bf16[8,192,384]{2,1,0:T(8,128)(2,1)S(1)}, bf16[8,192,384]{2,1,0:T(8,128)(2,1)S(1)}, u32[]{:S(2)}, u32[]{:S(2)}) collective-permute-start(bf16[8,192,384]{2,1,0:T(8,128)(2,1)S(1)} %all-to-all-done.w_mine_ref.mine_far), channel_id=1, source_target_pairs={{0,8},{8,0},{16,24},{24,16},{32,40},{40,32},{48,56},{56,48},{64,72... | collective-permute-start | bytes 3538952 | tf_op jit(solution)/shard_map/ppermute | solution.py:417
  28.7 3.6 %all-to-all-start.1 = ((bf16[8,192,384]{2,1,0:T(8,128)(2,1)}), bf16[8,192,384]{2,1,0:T(8,128)(2,1)S(1)}, u32[]{:S(2)}, u32[]{:S(2)}) async-start(bf16[8,192,384]{2,1,0:T(8,128)(2,1)} %prepare.3), calls=%async_computation.1 | async-start | bytes 2359296 | tf_op jit(solution)/shard_map/all_to_all | solution.py:403
  32.3 4.5 %plain_forward.1 = (bf16[32,1920]{1,0:T(8,128)(2,1)}, bf16[32,1920]{1,0:T(8,128)(2,1)}, bf16[32,1920]{1,0:T(8,128)(2,1)}, bf16[32,1920]{1,0:T(8,128)(2,1)}) custom-call(s32[1]{0:T(128)} %bitcast.core_ref.refs_0_, bf16[128,768]{1,0:T(8,128)(2,1)} %bitcast.11, bf16[128,768]{1,0:T(8,128)(2,1)} %bitcast.10, f32[64,768]{1,0:T(8,128)} %get-tuple-element.36.bias_far, ...), custom_call_target="tpu_custom_call" | custom-call | flops 20000000000 | bytes 1000000 | tf_op jit(solution)/shard_map/plain_forward/pallas_call | solution.py:481
  36.9 1.9 %collective-permute-start.1 = (bf16[32,1920]{1,0:T(8,128)(2,1)}, bf16[32,1920]{1,0:T(8,128)(2,1)S(1)}, u32[]{:S(2)}, u32[]{:S(2)}) collective-permute-start(bf16[32,1920]{1,0:T(8,128)(2,1)} %get-tuple-element.41), channel_id=1, source_target_pairs={{8,0},{9,1},{10,2},{11,3},{12,4},{13,5},{14,6},{15,7},{16,8},{17,9... | collective-permute-start | bytes 368648 | tf_op jit(solution)/shard_map/ppermute | solution.py:413
  38.8 5.7 %collective-permute-start.2 = (bf16[32,1920]{1,0:T(8,128)(2,1)}, bf16[32,1920]{1,0:T(8,128)(2,1)S(1)}, u32[]{:S(2)}, u32[]{:S(2)}) collective-permute-start(bf16[32,1920]{1,0:T(8,128)(2,1)} %get-tuple-element.42), channel_id=1, source_target_pairs={{1,0},{2,1},{3,2},{4,3},{5,4},{6,5},{7,6},{0,7},{9,8},{10,9},{11,1... | collective-permute-start | bytes 368648 | tf_op jit(solution)/shard_map/ppermute | solution.py:413
  44.5 14.0 %collective-permute-start.3 = (bf16[32,1920]{1,0:T(8,128)(2,1)}, bf16[32,1920]{1,0:T(8,128)(2,1)S(1)}, u32[]{:S(2)}, u32[]{:S(2)}) collective-permute-start(bf16[32,1920]{1,0:T(8,128)(2,1)} %get-tuple-element.43), channel_id=1, source_target_pairs={{9,0},{10,1},{11,2},{12,3},{13,4},{14,5},{15,6},{8,7},{17,8},{18,9... | collective-permute-start | bytes 368648 | tf_op jit(solution)/shard_map/ppermute | solution.py:413
  58.5 2.1 %collective-permute-done.3.refs_5_ = bf16[32,1920]{1,0:T(8,128)(2,1)S(1)} collective-permute-done((bf16[32,1920]{1,0:T(8,128)(2,1)}, bf16[32,1920]{1,0:T(8,128)(2,1)S(1)}, u32[]{:S(2)}, u32[]{:S(2)}) %collective-permute-start.3) | collective-permute-done | bytes 122912 | tf_op jit(solution)/shard_map/ppermute | solution.py:413
  60.6 5.4 %collective-permute-start.4 = (bf16[8,192,384]{2,1,0:T(8,128)(2,1)S(1)}, bf16[8,192,384]{2,1,0:T(8,128)(2,1)S(1)}, u32[]{:S(2)}, u32[]{:S(2)}) collective-permute-start(bf16[8,192,384]{2,1,0:T(8,128)(2,1)S(1)} %all-to-all-done.1.refs_6_), channel_id=1, source_target_pairs={{0,8},{8,0},{16,24},{24,16},{32,40},{40,32},{48,56},{56,48},{64,72... | collective-permute-start | bytes 3538952 | tf_op jit(solution)/shard_map/ppermute | solution.py:417
  66.0 2.5 %collective-permute-done.4.refs_7_ = bf16[8,192,384]{2,1,0:T(8,128)(2,1)S(1)} collective-permute-done((bf16[8,192,384]{2,1,0:T(8,128)(2,1)S(1)}, bf16[8,192,384]{2,1,0:T(8,128)(2,1)S(1)}, u32[]{:S(2)}, u32[]{:S(2)}) %collective-permute-start.4) | collective-permute-done | bytes 1179680 | tf_op jit(solution)/shard_map/ppermute | solution.py:417
  68.5 5.7 %main.1 = (bf16[32,768]{1,0:T(8,128)(2,1)}, bf16[64,768]{1,0:T(8,128)(2,1)}, bf16[32,768]{1,0:T(8,128)(2,1)}, bf16[8,2,48,384]{3,2,1,0:T(8,128)(2,1)S(1)}, bf16[8,2,48,384]{3,2,1,0:T(8,128)(2,1)S(1)}) custom-call(s32[1]{0:T(128)} %bitcast.core_ref.refs_0_, bf16[32,1920]{1,0:T(8,128)(2,1)} %get-tuple-element.38.refs_1_, f32[64,768]{1,0:T(8,128)} %get-tuple-element.39.refs_2_, ...), custom_call_target="tpu_custom_call" | custom-call | flops 1000000 | bytes 1000000 | tf_op jit(solution)/shard_map/main/pallas_call | solution.py:510
  74.2 2.3 %collective-permute-start.5 = (bf16[8,2,48,384]{3,2,1,0:T(8,128)(2,1)S(1)}, bf16[8,2,48,384]{3,2,1,0:T(8,128)(2,1)S(1)}, u32[]{:S(2)}, u32[]{:S(2)}) collective-permute-start(bf16[8,2,48,384]{3,2,1,0:T(8,128)(2,1)S(1)} %get-tuple-element.49), channel_id=1, source_target_pairs={{0,8},{8,0},{16,24},{24,16},{32,40},{40,32},{48,56},{56,48},{64,72... | collective-permute-start | bytes 1769480 | tf_op jit(solution)/shard_map/ppermute | solution.py:417
  76.5 1.6 %collective-permute-done.5 = bf16[8,2,48,384]{3,2,1,0:T(8,128)(2,1)S(1)} collective-permute-done((bf16[8,2,48,384]{3,2,1,0:T(8,128)(2,1)S(1)}, bf16[8,2,48,384]{3,2,1,0:T(8,128)(2,1)S(1)}, u32[]{:S(2)}, u32[]{:S(2)}) %collective-permute-start.5) | collective-permute-done | bytes 589856 | tf_op jit(solution)/shard_map/ppermute | solution.py:417
  78.1 1.0 add_convert_fusion
  79.1 3.7 %all-to-all-start.2 = ((bf16[8,2,48,384]{3,2,1,0:T(8,128)(2,1)}), bf16[8,2,48,384]{3,2,1,0:T(8,128)(2,1)S(1)}, u32[]{:S(2)}, u32[]{:S(2)}) async-start(bf16[8,2,48,384]{3,2,1,0:T(8,128)(2,1)} %add_convert_fusion), calls=%async_computation.2 | async-start | bytes 1179648 | tf_op jit(solution)/shard_map/all_to_all | solution.py:403
  82.8 1.9 %collective-permute-start.6 = (bf16[64,768]{1,0:T(8,128)(2,1)S(1)}, bf16[64,768]{1,0:T(8,128)(2,1)S(1)}, u32[]{:S(2)}, u32[]{:S(2)}) collective-permute-start(bf16[64,768]{1,0:T(8,128)(2,1)S(1)} %copy-done.5), channel_id=1, source_target_pairs={{504,0},{505,1},{506,2},{507,3},{508,4},{509,5},{510,6},{511,7},{0... | collective-permute-start | bytes 294920 | tf_op jit(solution)/shard_map/ppermute | solution.py:413
  84.7 7.2 %collective-permute-done.6.column = bf16[64,768]{1,0:T(8,128)(2,1)S(1)} collective-permute-done((bf16[64,768]{1,0:T(8,128)(2,1)S(1)}, bf16[64,768]{1,0:T(8,128)(2,1)S(1)}, u32[]{:S(2)}, u32[]{:S(2)}) %collective-permute-start.6) | collective-permute-done | bytes 98336 | tf_op jit(solution)/shard_map/ppermute | solution.py:413
  91.9 1.0 all-to-all-done.2.parts
  93.0 0.8 sum_copies.3
  93.8 3.5 %all-to-all-start.3 = ((bf16[4,2,48,384]{3,2,1,0:T(8,128)(2,1)}), bf16[4,2,48,384]{3,2,1,0:T(8,128)(2,1)S(1)}, u32[]{:S(2)}, u32[]{:S(2)}) async-start(bf16[4,2,48,384]{3,2,1,0:T(8,128)(2,1)} %sum_copies.3), calls=%async_computation.3 | async-start | bytes 589824 | tf_op jit(solution)/shard_map/all_to_all | solution.py:403
  97.3 2.0 %collective-permute-start.7 = (bf16[64,768]{1,0:T(8,128)(2,1)S(1)}, bf16[64,768]{1,0:T(8,128)(2,1)S(1)}, u32[]{:S(2)}, u32[]{:S(2)}) collective-permute-start(bf16[64,768]{1,0:T(8,128)(2,1)S(1)} %pad_maximum_fusion), channel_id=1, source_target_pairs={{7,0},{0,1},{1,2},{2,3},{3,4},{4,5},{5,6},{6,7},{15,8},{8,9},{9,10... | collective-permute-start | bytes 294920 | tf_op jit(solution)/shard_map/ppermute | solution.py:413
  99.3 7.2 %collective-permute-done.7.row = bf16[64,768]{1,0:T(8,128)(2,1)S(1)} collective-permute-done((bf16[64,768]{1,0:T(8,128)(2,1)S(1)}, bf16[64,768]{1,0:T(8,128)(2,1)S(1)}, u32[]{:S(2)}, u32[]{:S(2)}) %collective-permute-start.7) | collective-permute-done | bytes 98336 | tf_op jit(solution)/shard_map/ppermute | solution.py:413
  106.6 0.9 sum_copies.4
  107.5 7.6 %all-to-all-start.4 = ((bf16[8,2,48,384]{3,2,1,0:T(8,128)(2,1)}), bf16[8,2,48,384]{3,2,1,0:T(8,128)(2,1)S(1)}, u32[]{:S(2)}, u32[]{:S(2)}) async-start(bf16[8,2,48,384]{3,2,1,0:T(8,128)(2,1)} %sum_copies.4), calls=%async_computation.4 | async-start | bytes 1179648 | tf_op jit(solution)/shard_map/all_to_all | solution.py:403
  115.0 5.5 %plain_back.1 = bf16[128,768]{1,0:T(8,128)(2,1)} custom-call(s32[1]{0:T(128)} %bitcast.core_ref.refs_0_, bf16[128,768]{1,0:T(8,128)(2,1)} %bitcast.12, bf16[32,768]{1,0:T(8,128)(2,1)} %get-tuple-element.59.own_far, f32[64,768]{1,0:T(8,128)} %get-tuple-element.36.bias_far, bf16[8,192,384]{2,1,0:T(8,128)(2,1)} %copy-done, bf16[8,192,384]{2,1,0:T(8,128)(2,1)} %copy-done.3, ...), custom_call_target="tpu_custom_call" | custom-call | flops 4000000000 | bytes 4000000 | tf_op jit(solution)/shard_map/plain_back/pallas_call | solution.py:539
  120.6 9.4 %all-to-all-done.4.parts = bf16[8,2,48,384]{3,2,1,0:T(8,128)(2,1)S(1)} async-done(((bf16[8,2,48,384]{3,2,1,0:T(8,128)(2,1)}), bf16[8,2,48,384]{3,2,1,0:T(8,128)(2,1)S(1)}, u32[]{:S(2)}, u32[]{:S(2)}) %all-to-all-start.4) | async-done | bytes 589856 | tf_op jit(solution)/shard_map/all_to_all | solution.py:403
  130.1 6.5 %all_gather.3.parts = bf16[2,2,48,384]{3,2,1,0:T(8,128)(2,1)S(1)} all-gather(bf16[1,2,48,384]{3,2,1,0:T(8,128)(2,1)S(1)} %sum_copies.5), channel_id=1, replica_groups={{0,8},{16,24},{32,40},{48,56},{64,72},{80,88},{96,104},{112,120},{128,1..., dimensions={0}, use_global_device_ids=true | all-gather | bytes 221184 | tf_op jit(solution)/shard_map/all_gather | solution.py:562
  136.5 0.7 finish.1
  (21 shorter events, 0.2 us)
Async XLA Ops:
  2.8 18.6 %all-to-all-start = ((bf16[8,192,384]{2,1,0:T(8,128)(2,1)}), bf16[8,192,384]{2,1,0:T(8,128)(2,1)S(1)}, u32[]{:S(2)}, u32[]{:S(2)}) async-start(bf16[8,192,384]{2,1,0:T(8,128)(2,1)} %prepare.2), calls=%async_computation | async-start | bytes 2359296 | tf_op jit(solution)/shard_map/all_to_all | solution.py:403
  8.7 2.2 %copy-start.1 = (f32[12,225]{1,0:T(8,128)S(1)}, f32[12,225]{1,0:T(8,128)}, u32[]{:S(2)}) copy-start(f32[12,225]{1,0:T(8,128)} %table_p.1) | copy-start | bytes 32404
  8.7 2.2 %copy-start.2 = (f32[12,225]{1,0:T(8,128)S(1)}, f32[12,225]{1,0:T(8,128)}, u32[]{:S(2)}) copy-start(f32[12,225]{1,0:T(8,128)} %table_s.1) | copy-start | bytes 32404
  21.4 11.0 %copy-start = (bf16[8,192,384]{2,1,0:T(8,128)(2,1)}, bf16[8,192,384]{2,1,0:T(8,128)(2,1)S(1)}, u32[]{:S(2)}) copy-start(bf16[8,192,384]{2,1,0:T(8,128)(2,1)S(1)} %all-to-all-done.w_mine_ref.mine_far) | copy-start | bytes 3538948
  21.4 10.9 %collective-permute-start = (bf16[8,192,384]{2,1,0:T(8,128)(2,1)S(1)}, bf16[8,192,384]{2,1,0:T(8,128)(2,1)S(1)}, u32[]{:S(2)}, u32[]{:S(2)}) collective-permute-start(bf16[8,192,384]{2,1,0:T(8,128)(2,1)S(1)} %all-to-all-done.w_mine_ref.mine_far), channel_id=1, source_target_pairs={{0,8},{8,0},{16,24},{24,16},{32,40},{40,32},{48,56},{56,48},{64,72... | collective-permute-start | bytes 3538952 | tf_op jit(solution)/shard_map/ppermute | solution.py:417
  28.7 31.9 %all-to-all-start.1 = ((bf16[8,192,384]{2,1,0:T(8,128)(2,1)}), bf16[8,192,384]{2,1,0:T(8,128)(2,1)S(1)}, u32[]{:S(2)}, u32[]{:S(2)}) async-start(bf16[8,192,384]{2,1,0:T(8,128)(2,1)} %prepare.3), calls=%async_computation.1 | async-start | bytes 2359296 | tf_op jit(solution)/shard_map/all_to_all | solution.py:403
  32.3 4.6 %copy-start.3 = (bf16[8,192,384]{2,1,0:T(8,128)(2,1)}, bf16[8,192,384]{2,1,0:T(8,128)(2,1)S(1)}, u32[]{:S(2)}) copy-start(bf16[8,192,384]{2,1,0:T(8,128)(2,1)S(1)} %collective-permute-done.w_other_ref.other_far) | copy-start | bytes 3538948
  36.9 21.6 %collective-permute-start.1 = (bf16[32,1920]{1,0:T(8,128)(2,1)}, bf16[32,1920]{1,0:T(8,128)(2,1)S(1)}, u32[]{:S(2)}, u32[]{:S(2)}) collective-permute-start(bf16[32,1920]{1,0:T(8,128)(2,1)} %get-tuple-element.41), channel_id=1, source_target_pairs={{8,0},{9,1},{10,2},{11,3},{12,4},{13,5},{14,6},{15,7},{16,8},{17,9... | collective-permute-start | bytes 368648 | tf_op jit(solution)/shard_map/ppermute | solution.py:413
  38.8 19.7 %collective-permute-start.2 = (bf16[32,1920]{1,0:T(8,128)(2,1)}, bf16[32,1920]{1,0:T(8,128)(2,1)S(1)}, u32[]{:S(2)}, u32[]{:S(2)}) collective-permute-start(bf16[32,1920]{1,0:T(8,128)(2,1)} %get-tuple-element.42), channel_id=1, source_target_pairs={{1,0},{2,1},{3,2},{4,3},{5,4},{6,5},{7,6},{0,7},{9,8},{10,9},{11,1... | collective-permute-start | bytes 368648 | tf_op jit(solution)/shard_map/ppermute | solution.py:413
  44.5 16.1 %collective-permute-start.3 = (bf16[32,1920]{1,0:T(8,128)(2,1)}, bf16[32,1920]{1,0:T(8,128)(2,1)S(1)}, u32[]{:S(2)}, u32[]{:S(2)}) collective-permute-start(bf16[32,1920]{1,0:T(8,128)(2,1)} %get-tuple-element.43), channel_id=1, source_target_pairs={{9,0},{10,1},{11,2},{12,3},{13,4},{14,5},{15,6},{8,7},{17,8},{18,9... | collective-permute-start | bytes 368648 | tf_op jit(solution)/shard_map/ppermute | solution.py:413
  60.6 7.8 %collective-permute-start.4 = (bf16[8,192,384]{2,1,0:T(8,128)(2,1)S(1)}, bf16[8,192,384]{2,1,0:T(8,128)(2,1)S(1)}, u32[]{:S(2)}, u32[]{:S(2)}) collective-permute-start(bf16[8,192,384]{2,1,0:T(8,128)(2,1)S(1)} %all-to-all-done.1.refs_6_), channel_id=1, source_target_pairs={{0,8},{8,0},{16,24},{24,16},{32,40},{40,32},{48,56},{56,48},{64,72... | collective-permute-start | bytes 3538952 | tf_op jit(solution)/shard_map/ppermute | solution.py:417
  74.2 3.9 %collective-permute-start.5 = (bf16[8,2,48,384]{3,2,1,0:T(8,128)(2,1)S(1)}, bf16[8,2,48,384]{3,2,1,0:T(8,128)(2,1)S(1)}, u32[]{:S(2)}, u32[]{:S(2)}) collective-permute-start(bf16[8,2,48,384]{3,2,1,0:T(8,128)(2,1)S(1)} %get-tuple-element.49), channel_id=1, source_target_pairs={{0,8},{8,0},{16,24},{24,16},{32,40},{40,32},{48,56},{56,48},{64,72... | collective-permute-start | bytes 1769480 | tf_op jit(solution)/shard_map/ppermute | solution.py:417
  78.1 4.7 %copy-start.5 = (bf16[64,768]{1,0:T(8,128)(2,1)S(1)}, bf16[64,768]{1,0:T(8,128)(2,1)}, u32[]{:S(2)}) copy-start(bf16[64,768]{1,0:T(8,128)(2,1)} %get-tuple-element.53) | copy-start | bytes 294916
  79.1 18.1 %copy-start.4 = (bf16[32,768]{1,0:T(8,128)(2,1)S(1)}, bf16[32,768]{1,0:T(8,128)(2,1)}, u32[]{:S(2)}) copy-start(bf16[32,768]{1,0:T(8,128)(2,1)} %get-tuple-element.56) | copy-start | bytes 147460
  79.1 13.9 %all-to-all-start.2 = ((bf16[8,2,48,384]{3,2,1,0:T(8,128)(2,1)}), bf16[8,2,48,384]{3,2,1,0:T(8,128)(2,1)S(1)}, u32[]{:S(2)}, u32[]{:S(2)}) async-start(bf16[8,2,48,384]{3,2,1,0:T(8,128)(2,1)} %add_convert_fusion), calls=%async_computation.2 | async-start | bytes 1179648 | tf_op jit(solution)/shard_map/all_to_all | solution.py:403
  82.8 9.1 %collective-permute-start.6 = (bf16[64,768]{1,0:T(8,128)(2,1)S(1)}, bf16[64,768]{1,0:T(8,128)(2,1)S(1)}, u32[]{:S(2)}, u32[]{:S(2)}) collective-permute-start(bf16[64,768]{1,0:T(8,128)(2,1)S(1)} %copy-done.5), channel_id=1, source_target_pairs={{504,0},{505,1},{506,2},{507,3},{508,4},{509,5},{510,6},{511,7},{0... | collective-permute-start | bytes 294920 | tf_op jit(solution)/shard_map/ppermute | solution.py:413
  93.8 12.8 %all-to-all-start.3 = ((bf16[4,2,48,384]{3,2,1,0:T(8,128)(2,1)}), bf16[4,2,48,384]{3,2,1,0:T(8,128)(2,1)S(1)}, u32[]{:S(2)}, u32[]{:S(2)}) async-start(bf16[4,2,48,384]{3,2,1,0:T(8,128)(2,1)} %sum_copies.3), calls=%async_computation.3 | async-start | bytes 589824 | tf_op jit(solution)/shard_map/all_to_all | solution.py:403
  97.3 9.3 %collective-permute-start.7 = (bf16[64,768]{1,0:T(8,128)(2,1)S(1)}, bf16[64,768]{1,0:T(8,128)(2,1)S(1)}, u32[]{:S(2)}, u32[]{:S(2)}) collective-permute-start(bf16[64,768]{1,0:T(8,128)(2,1)S(1)} %pad_maximum_fusion), channel_id=1, source_target_pairs={{7,0},{0,1},{1,2},{2,3},{3,4},{4,5},{5,6},{6,7},{15,8},{8,9},{9,10... | collective-permute-start | bytes 294920 | tf_op jit(solution)/shard_map/ppermute | solution.py:413
  107.5 22.5 %all-to-all-start.4 = ((bf16[8,2,48,384]{3,2,1,0:T(8,128)(2,1)}), bf16[8,2,48,384]{3,2,1,0:T(8,128)(2,1)S(1)}, u32[]{:S(2)}, u32[]{:S(2)}) async-start(bf16[8,2,48,384]{3,2,1,0:T(8,128)(2,1)} %sum_copies.4), calls=%async_computation.4 | async-start | bytes 1179648 | tf_op jit(solution)/shard_map/all_to_all | solution.py:403

commit v10 on v8

--- a/solution.py
+++ b/solution.py
@@ -18,6 +18,7 @@
 HALF = D // 2
 SHARE = 144
 ROWS = 48
+PART = SHARE + ROWS
 
 NEG = -1e30
 EPS = 1e-05
@@ -109,10 +110,11 @@
         move.wait()
 
 
-def prepare(core_ref, qkv, proj, out, block, sems):
+def prepare(core_ref, qkv_p, proj_p, qkv_s, proj_s, out, block, sems):
     start = pl.multiple_of(core_ref[0] * HALF, 128)
-    block[0:SHARE] = qkv[:, pl.ds(start, HALF)]
-    block[SHARE : SHARE + ROWS] = proj[:, pl.ds(start, HALF)]
+    for first, qkv, proj in ((0, qkv_p, proj_p), (PART, qkv_s, proj_s)):
+        block[first : first + SHARE] = qkv[:, pl.ds(start, HALF)]
+        block[first + SHARE : first + PART] = proj[:, pl.ds(start, HALF)]
     wait_all(copy_all([(block, out.at[i]) for i in range(8)], sems))
 
 
@@ -158,12 +160,12 @@
     return (mine, pl.multiple_of(HALF - mine, 128))
 
 
-def qkv_of(ref):
-    return ref[:, 0:SHARE].reshape(3 * WIDE, HALF)
-
-
-def proj_of(ref):
-    return ref[:, SHARE : SHARE + ROWS].reshape(WIDE, HALF)
+def qkv_of(ref, first=0):
+    return ref[:, first : first + SHARE].reshape(3 * WIDE, HALF)
+
+
+def proj_of(ref, first=0):
+    return ref[:, first + SHARE : first + PART].reshape(WIDE, HALF)
 
 
 def input_grad(grad, normed, rstd, d_packed, w_mine, w_other, mine, other, sums):
@@ -178,69 +180,90 @@
     return (grad + d_input).astype(BF16)
 
 
-def plain_forward(
+def plain_begin(
     core_ref,
     tok_far,
     cot_far,
-    bias_far,
+    bias_p_far,
+    bias_s_far,
+    w_mine_ref,
+    out_tok,
+    out_cot,
+    out_rows,
+    out_part,
+    out_bias_p,
+    out_bias_s,
+    cot,
+    sems,
+):
+    mine, _ = sides(core_ref)
+    loads = copy_all(
+        [(tok_far, out_tok), (cot_far, cot), (bias_p_far, out_bias_p), (bias_s_far, out_bias_s)],
+        sems,
+    )
+    loads[0].wait()
+    out_rows[...] = normalize(out_tok[...].astype(F32))[0].astype(BF16)
+    out_part[...] = dot(out_rows[:, pl.ds(mine, HALF)], qkv_of(w_mine_ref), NT)
+    loads[1].wait()
+    out_cot[...] = dot(quadrant_pick(), cot[...]).astype(BF16)
+    wait_all(loads[2:])
+
+
+def plain_forward(
+    core_ref,
+    tok,
+    cot_quads,
+    rows,
+    part,
+    bias_p,
     w_mine_ref,
     w_other_ref,
     out_o,
     out_r,
     out_b,
     out_d,
-    tok,
-    cot,
-    bias_p,
-    packets,
-    rows,
     sums,
     mask,
-    sems,
 ):
     mine, other = sides(core_ref)
-    loads = copy_all([(tok_far, tok), (bias_far, bias_p), (cot_far, cot)], sems)
     mask[...] = head_mask()
-    loads[0].wait()
-    inputs = tok[...].astype(F32)
-    rows[...] = normalize(inputs)[0].astype(BF16)
-    w_mine, w_other = qkv_of(w_mine_ref), qkv_of(w_other_ref)
-    packed = project(rows, w_mine, w_other, mine, other).astype(BF16)
-    loads[1].wait()
+    packed = part[...] + dot(rows[:, pl.ds(other, HALF)], qkv_of(w_other_ref), NT)
+    packed = packed.astype(BF16)
     mixed = []
     for s in range(2):
-        part = packed[s * SPOTS : (s + 1) * SPOTS]
-        query, key, value = part[:, :WIDE], part[:, WIDE : 2 * WIDE], part[:, 2 * WIDE :]
+        block = packed[s * SPOTS : (s + 1) * SPOTS]
+        query, key, value = block[:, :WIDE], block[:, WIDE : 2 * WIDE], block[:, 2 * WIDE :]
         probs = softmax_down(dot(key, expand(query, mask), NT) * SCALE + bias_p[...])
         mixed.append(fold(dot(probs.astype(BF16), value, TN)).astype(BF16))
     mixed = jnp.concatenate(mixed, axis=0)
     sums[:, pl.ds(mine, HALF)] = dot(mixed, proj_of(w_mine_ref))
     sums[:, pl.ds(other, HALF)] = dot(mixed, proj_of(w_other_ref))
-    block_out = (inputs + sums[...]).astype(BF16)
+    block_out = (tok[...].astype(F32) + sums[...]).astype(BF16)
     pick = quadrant_pick()
-    loads[2].wait()
-    for whole, first in ((block_out, 0), (mixed, D), (cot[...], D + WIDE)):
-        packets[:, first : first + whole.shape[1]] = dot(pick, whole).astype(BF16)
     outs = (out_d, out_b, out_r, out_o)
-    wait_all(copy_all([(packets.at[i * 32 : (i + 1) * 32], out) for i, out in enumerate(outs)], sems, 3))
+    for whole, first in ((block_out, 0), (mixed, D)):
+        quads = dot(pick, whole).astype(BF16)
+        for i, out in enumerate(outs):
+            out[:, first : first + whole.shape[1]] = quads[i * 32 : (i + 1) * 32]
+    for i, out in enumerate(outs):
+        out[:, D + WIDE :] = cot_quads[i * 32 : (i + 1) * 32]
 
 
 def main_kernel(
     grad_scale,
     core_ref,
-    own_far,
-    bias_far,
+    own,
     right,
     below,
     diag,
     w_mine_ref,
     w_other_ref,
+    bias_s,
     to_own,
     to_column,
     to_below,
     out_keep,
     out_send,
-    bias_s,
     quads,
     staged,
     rows_small,
@@ -250,20 +273,18 @@
     sems,
 ):
     mine, other = sides(core_ref)
-    loads = copy_all([(own_far, staged.at[0:32]), (bias_far, bias_s)], sems)
     mask[...] = head_mask()
-    for i, part in ((1, right), (2, below), (3, diag)):
+    for i, part in enumerate((own, right, below, diag)):
         staged[i * 32 : (i + 1) * 32] = part[...]
-    wait_all(loads)
     pick = quadrant_pick(True)
     grads[...] = dot(pick, staged[:, D + WIDE :]).astype(BF16)
     block_out = dot(pick, staged[:, 0:D])
     mixed_plain = dot(pick, staged[:, D : D + WIDE]).astype(BF16)
     normed, rstd = normalize(block_out)
     rows_small[...] = normed.astype(BF16)
-    w_mine, w_other = qkv_of(w_mine_ref), qkv_of(w_other_ref)
+    w_mine, w_other = qkv_of(w_mine_ref, PART), qkv_of(w_other_ref, PART)
     packed = project(rows_small, w_mine, w_other, mine, other).astype(BF16)
-    d_mixed = project(grads, proj_of(w_mine_ref), proj_of(w_other_ref), mine, other).astype(BF16)
+    d_mixed = project(grads, proj_of(w_mine_ref, PART), proj_of(w_other_ref, PART), mine, other).astype(BF16)
     mixed, d_packed = [], []
     for s in range(2):
         part = packed[s * SPOTS : (s + 1) * SPOTS]
@@ -289,7 +310,6 @@
             (quads.at[64:96], to_below),
         ],
         sems,
-        2,
     )
     rows_small[...] = grad
     for out, start in ((out_send, other), (out_keep, mine)):
@@ -337,8 +357,8 @@
     loads = copy_all(
         [
             (tok_far, tok),
-            (mine_far, w_mine_ref),
-            (other_far, w_other_ref),
+            (mine_far.at[:, 0:PART], w_mine_ref),
+            (other_far.at[:, 0:PART], w_other_ref),
             (own_far, staged.at[96:128]),
             (bias_far, bias_p),
         ],
@@ -439,22 +459,17 @@
     tok = tokens.reshape(128, D)
     cot = cotangent.reshape(128, D)
 
-    def share(qkv, proj):
-        return pl.pallas_call(
-            prepare,
-            out_shape=pltpu.HBM((8, SHARE + ROWS, HALF), BF16),
-            in_specs=[SMEM, VMEM, VMEM],
-            out_specs=HBM,
-            scratch_shapes=[
-                pltpu.VMEM((SHARE + ROWS, HALF), BF16),
-                pltpu.SemaphoreType.DMA((8,)),
-            ],
-            compiler_params=params(60),
-            name="prepare",
-        )(core, qkv.T, proj)
-
-    first_mine = swap(share(qkv_plain, proj_plain), "freq")
-    second_share = share(qkv_shift, proj_shift)
+    shares = pl.pallas_call(
+        prepare,
+        out_shape=pltpu.HBM((8, 2 * PART, HALF), BF16),
+        in_specs=[SMEM] + [VMEM] * 4,
+        out_specs=HBM,
+        scratch_shapes=[pltpu.VMEM((2 * PART, HALF), BF16), pltpu.SemaphoreType.DMA((8,))],
+        compiler_params=params(60),
+        name="prepare",
+    )(core, qkv_plain.T, proj_plain, qkv_shift.T, proj_shift)
+    w_mine = swap(shares, "freq")
+
     table = pltpu.HBM((SPOTS, LANES), F32)
     bias_p, bias_s = pl.pallas_call(
         biases,
@@ -472,60 +487,62 @@
         name="biases",
     )(edge, table_plain, table_shift)
 
-    first_mine, second_share, bias_p, bias_s = lax.optimization_barrier(
-        (first_mine, second_share, bias_p, bias_s)
-    )
-    second_mine = swap(second_share, "freq")
-    first_other = other_core(first_mine)
-    packet = pltpu.HBM((32, 2 * D + WIDE), BF16)
+    w_mine, bias_p, bias_s = lax.optimization_barrier((w_mine, bias_p, bias_s))
+    w_other = other_core(w_mine)
+    tile = jax.ShapeDtypeStruct((128, D), BF16)
+    near_table = jax.ShapeDtypeStruct((SPOTS, LANES), F32)
+    near_tok, near_cot, rows, part, near_p, near_s = pl.pallas_call(
+        plain_begin,
+        out_shape=(
+            tile,
+            tile,
+            tile,
+            jax.ShapeDtypeStruct((128, 3 * WIDE), F32),
+            near_table,
+            near_table,
+        ),
+        in_specs=[SMEM] + [HBM] * 4 + [VMEM],
+        out_specs=[VMEM] * 6,
+        scratch_shapes=[pltpu.VMEM((128, D), BF16), pltpu.SemaphoreType.DMA((4,))],
+        compiler_params=params(),
+        cost_estimate=cost(5_000_000_000, 1_000_000),
+        name="plain_begin",
+    )(core, far(tok), far(cot), far(bias_p), far(bias_s), w_mine)
+    packet = jax.ShapeDtypeStruct((32, 2 * D + WIDE), BF16)
     own, to_left, to_above, to_diag = pl.pallas_call(
         plain_forward,
         out_shape=(packet,) * 4,
-        in_specs=[SMEM] + [HBM] * 3 + [VMEM] * 2,
-        out_specs=[HBM] * 4,
-        scratch_shapes=[
-            pltpu.VMEM((128, D), BF16),
-            pltpu.VMEM((128, D), BF16),
-            pltpu.VMEM((SPOTS, LANES), F32),
-            pltpu.VMEM((128, 2 * D + WIDE), BF16),
-            pltpu.VMEM((128, D), BF16),
-            pltpu.VMEM((128, D), F32),
-            pltpu.VMEM((LANES, WIDE), BF16),
-            pltpu.SemaphoreType.DMA((7,)),
-        ],
+        in_specs=[SMEM] + [VMEM] * 7,
+        out_specs=[VMEM] * 4,
+        scratch_shapes=[pltpu.VMEM((128, D), F32), pltpu.VMEM((LANES, WIDE), BF16)],
         compiler_params=params(),
         cost_estimate=cost(1_000_000, 1_000_000),
         name="plain_forward",
-    )(core, far(tok), far(cot), far(bias_p), first_mine, first_other)
+    )(core, near_tok, near_cot, rows, part, near_p, w_mine, w_other)
     right = from_offset(to_left, 1, 0)
     below = from_offset(to_above, 0, 1)
     diag = from_offset(to_diag, 1, 1)
-    second_mine, right, below, diag = lax.optimization_barrier(
-        (second_mine, right, below, diag)
-    )
-    second_other = other_core(second_mine)
     piece = pltpu.HBM((32, D), BF16)
     column = pltpu.HBM((64, D), BF16)
     local = jax.ShapeDtypeStruct((8, 2, ROWS, HALF), BF16)
     g_own, to_right, to_below, keep, send = pl.pallas_call(
         lambda *refs: main_kernel(grad_scale, *refs),
         out_shape=(piece, column, piece, local, local),
-        in_specs=[SMEM] + [HBM] * 2 + [VMEM] * 5,
+        in_specs=[SMEM] + [VMEM] * 7,
         out_specs=[HBM] * 3 + [VMEM] * 2,
         scratch_shapes=[
-            pltpu.VMEM((SPOTS, LANES), F32),
             pltpu.VMEM((128, D), BF16),
             pltpu.VMEM((128, 2 * D + WIDE), BF16),
             pltpu.VMEM((128, D), BF16),
             pltpu.VMEM((128, D), BF16),
             pltpu.VMEM((128, D), F32),
             pltpu.VMEM((LANES, WIDE), BF16),
-            pltpu.SemaphoreType.DMA((6,)),
+            pltpu.SemaphoreType.DMA((4,)),
         ],
         compiler_params=params(),
         cost_estimate=cost(1_000_000, 1_000_000),
         name="main",
-    )(core, far(own), far(bias_s), right, below, diag, second_mine, second_other)
+    )(core, own, right, below, diag, w_mine, w_other, near_s)
 
     part = (keep.astype(F32) + other_core(send).astype(F32)).astype(BF16)
     part, to_right, to_below = lax.optimization_barrier((part, to_right, to_below))
@@ -556,7 +573,7 @@
         compiler_params=params(),
         cost_estimate=cost(4_000_000_000, 4_000_000),
         name="plain_back",
-    )(core, far(tok), far(g_own), far(bias_p), far(first_mine), far(first_other), column, row)
+    )(core, far(tok), far(g_own), far(bias_p), far(w_mine), far(w_other), column, row)
     part, grad_tokens = lax.optimization_barrier((part, grad_tokens))
     part = summed(part, 1)[0]
     part = lax.all_gather(part, "tm", axis_index_groups=tm_groups("core"))

time: 140 us -> 139 us (level)
  waiting for transfers between devices: 42.1 us -> 52.8 us
  starting transfers between devices: 65 us -> 55.1 us
  Pallas kernels: 24.5 us -> 21.1 us
  blocking collectives: 5.27 us -> 6.98 us
    all_to_all x5 -> x4, waiting for transfers between devices: 20.6 us -> 33.4 us  [swap(): return lax.all_to_all(value, axis, 0, 0, axis_index_groups=groups)]
    all_to_all x5 -> x4, starting transfers between devices: 23.9 us -> 18.9 us  [swap(): return lax.all_to_all(value, axis, 0, 0, axis_index_groups=groups)]
    ppermute x3 -> x2, starting transfers between devices: 14.6 us -> 11.9 us  [other_core(): lax.ppermute(value, 'tm', [(i, i ^ 1) for i in range(lax.axis_size('tm'))])]
    pallas_call x1, Pallas kernels: 4.53 us -> 1.91 us  [shards(): pl.pallas_call(plain_forward, out_shape=(packet,) * 4, in_specs=[SMEM] +...]
    ppermute x3 -> x2, waiting for transfers between devices: 6.51 us -> 3.99 us  [other_core(): lax.ppermute(value, 'tm', [(i, i ^ 1) for i in range(lax.axis_size('tm'))])]
    ppermute x5, starting transfers between devices: 26.4 us -> 24.3 us  [from_offset(): return lax.ppermute(value, ('tm', 'freq'), pairs)]
    all_gather x1, blocking collectives: 5.27 us -> 6.98 us  [shards(): part = lax.all_gather(part, 'tm', axis_index_groups=tm_groups('core'))]
  transfers between devices with their start and end apart: 13 -> 11, of which waited for: 9 -> 8; matrix products, arithmetic and copies ran while one was open for 0% -> 0% of each run, Pallas kernels for 10% -> 7%
where the time goes in v10:
time: 139 us; the launch traced here: 138 us
  starting transfers between devices  55.1 us (40%)
  waiting for transfers between devices  52.8 us (38%)
  Pallas kernels  21.1 us (15%)
  blocking collectives  6.98 us (5%)
    all_to_all x4, waiting for transfers between devices, swap(): return lax.all_to_all(value, axis, 0, 0, axis_index_groups=groups)  33.4 us
    ppermute x5, starting transfers between devices, from_offset(): return lax.ppermute(value, ('tm', 'freq'), pairs)  24.3 us
    all_to_all x4, starting transfers between devices, swap(): return lax.all_to_all(value, axis, 0, 0, axis_index_groups=groups)  18.9 us
    ppermute x5, waiting for transfers between devices, from_offset(): return lax.ppermute(value, ('tm', 'freq'), pairs)  15.4 us
    ppermute x2, starting transfers between devices, other_core(): lax.ppermute(value, 'tm', [(i, i ^ 1) for i in range(lax.axis_size('tm'))])  11.9 us
    all_gather x1, blocking collectives, shards(): part = lax.all_gather(part, 'tm', axis_index_groups=tm_groups('core'))  6.98 us
    pallas_call x1, Pallas kernels, shards(): pl.pallas_call(plain_back, out_shape=jax.ShapeDtypeStruct((128, D), BF16)...  5.54 us
    pallas_call x1, Pallas kernels, shards(): pl.pallas_call(lambda *refs: main_kernel(grad_scale, *refs), out_shape=(p...  4.77 us
  transfers between devices with their start and end apart: 11, of which 8 were waited for; matrix products, arithmetic and copies ran while one was open for 0% of the time, Pallas kernels for 7%

profile of v10, /device:TPU:1, one launch (start us, length us, event | category | flops | bytes accessed | tf_op | source)
XLA Modules:
  0.0 138.0 jit_solution(6053221681446049173)
XLA Ops:
  0.6 2.7 %prepare.1 = bf16[8,384,384]{2,1,0:T(8,128)(2,1)} custom-call(s32[1]{0:T(128)} %bitcast.core_ref.refs_0_, bf16[144,768]{1,0:T(8,128)(2,1)} %bitcast.8, bf16[48,768]{1,0:T(8,128)(2,1)} %proj_p.1, bf16[144,768]{1,0:T(8,128)(2,1)} %bitcast.9, bf16[48,768]{1,0:T(8,128)(2,1)} %proj_s.1), custom_call_target="tpu_custom_call" | custom-call | tf_op jit(solution)/shard_map/prepare/pallas_call | solution.py:462
  3.3 5.9 %all-to-all-start = ((bf16[8,384,384]{2,1,0:T(8,128)(2,1)}), bf16[8,384,384]{2,1,0:T(8,128)(2,1)S(1)}, u32[]{:S(2)}, u32[]{:S(2)}) async-start(bf16[8,384,384]{2,1,0:T(8,128)(2,1)} %prepare.1), calls=%async_computation | async-start | bytes 4718592 | tf_op jit(solution)/shard_map/all_to_all | solution.py:423
  9.2 0.1 add_convert_fusion.1.edge_ref
  9.3 2.0 %biases.1 = (f32[64,768]{1,0:T(8,128)}, f32[64,768]{1,0:T(8,128)}) custom-call(s32[2]{0:T(128)S(1)} %add_convert_fusion.1.edge_ref, f32[12,225]{1,0:T(8,128)S(1)} %copy-done.2, f32[12,225]{1,0:T(8,128)S(1)} %copy-done.3), custom_call_target="tpu_custom_call" | custom-call | tf_op jit(solution)/shard_map/biases/pallas_call | solution.py:474
  11.3 23.2 %all-to-all-done.w_mine_ref.refs_5_.mine_far = bf16[8,384,384]{2,1,0:T(8,128)(2,1)S(1)} async-done(((bf16[8,384,384]{2,1,0:T(8,128)(2,1)}), bf16[8,384,384]{2,1,0:T(8,128)(2,1)S(1)}, u32[]{:S(2)}, u32[]{:S(2)}) %all-to-all-start) | async-done | bytes 2359328 | tf_op jit(solution)/shard_map/all_to_all | solution.py:423
  34.5 7.3 %collective-permute-start = (bf16[8,384,384]{2,1,0:T(8,128)(2,1)S(1)}, bf16[8,384,384]{2,1,0:T(8,128)(2,1)S(1)}, u32[]{:S(2)}, u32[]{:S(2)}) collective-permute-start(bf16[8,384,384]{2,1,0:T(8,128)(2,1)S(1)} %all-to-all-done.w_mine_ref.refs_5_.mine_far), channel_id=1, source_target_pairs={{0,8},{8,0},{16,24},{24,16},{32,40},{40,32},{48,56},{56,48},{64,72... | collective-permute-start | bytes 7077896 | tf_op jit(solution)/shard_map/ppermute | solution.py:437
  41.9 1.8 %plain_begin.1 = (bf16[128,768]{1,0:T(8,128)(2,1)S(1)}, bf16[128,768]{1,0:T(8,128)(2,1)S(1)}, bf16[128,768]{1,0:T(8,128)(2,1)S(1)}, f32[128,1152]{1,0:T(8,128)S(...) custom-call(s32[1]{0:T(128)} %bitcast.core_ref.refs_0_, bf16[128,768]{1,0:T(8,128)(2,1)} %bitcast.11, ...), custom_call_target="tpu_custom_call" | custom-call | flops 5000000000 | bytes 1000000 | tf_op jit(solution)/shard_map/plain_begin/pallas_call | solution.py:494
  43.6 2.4 %collective-permute-done.w_other_ref.refs_6_.other_far = bf16[8,384,384]{2,1,0:T(8,128)(2,1)S(1)} collective-permute-done((bf16[8,384,384]{2,1,0:T(8,128)(2,1)S(1)}, bf16[8,384,384]{2,1,0:T(8,128)(2,1)S(1)}, u32[]{:S(2)}, u32[]{:S(2)}) %collective-permute-start) | collective-permute-done | bytes 2359328 | tf_op jit(solution)/shard_map/ppermute | solution.py:437
  46.0 1.9 %plain_forward.1 = (bf16[32,1920]{1,0:T(8,128)(2,1)S(1)}, bf16[32,1920]{1,0:T(8,128)(2,1)S(1)}, bf16[32,1920]{1,0:T(8,128)(2,1)S(1)}, bf16[32,1920]{1,0:T(8,128)(2,1)S(1)}) custom-call(s32[1]{0:T(128)} %bitcast.core_ref.refs_0_, bf16[128,768]{1,0:T(8,128)(2,1)S(1)} %get-tuple-element.40.tok, bf16[128,768]{1,0:T(8,128)(2,1)S(1)} %get-tuple-element.41.cot_quads, ...), custom_call_target="tpu_custom_call" | custom-call | flops 1000000 | bytes 1000000 | tf_op jit(solution)/shard_map/plain_forward/pallas_call | solution.py:512
  47.9 2.3 %collective-permute-start.1 = (bf16[32,1920]{1,0:T(8,128)(2,1)S(1)}, bf16[32,1920]{1,0:T(8,128)(2,1)S(1)}, u32[]{:S(2)}, u32[]{:S(2)}) collective-permute-start(bf16[32,1920]{1,0:T(8,128)(2,1)S(1)} %get-tuple-element.46), channel_id=1, source_target_pairs={{8,0},{9,1},{10,2},{11,3},{12,4},{13,5},{14,6},{15,7},{16,8},{17,9... | collective-permute-start | bytes 368648 | tf_op jit(solution)/shard_map/ppermute | solution.py:433
  50.2 3.0 %collective-permute-start.2 = (bf16[32,1920]{1,0:T(8,128)(2,1)S(1)}, bf16[32,1920]{1,0:T(8,128)(2,1)S(1)}, u32[]{:S(2)}, u32[]{:S(2)}) collective-permute-start(bf16[32,1920]{1,0:T(8,128)(2,1)S(1)} %get-tuple-element.47), channel_id=1, source_target_pairs={{1,0},{2,1},{3,2},{4,3},{5,4},{6,5},{7,6},{0,7},{9,8},{10,9},{11,1... | collective-permute-start | bytes 368648 | tf_op jit(solution)/shard_map/ppermute | solution.py:433
  53.3 14.9 %collective-permute-start.3 = (bf16[32,1920]{1,0:T(8,128)(2,1)S(1)}, bf16[32,1920]{1,0:T(8,128)(2,1)S(1)}, u32[]{:S(2)}, u32[]{:S(2)}) collective-permute-start(bf16[32,1920]{1,0:T(8,128)(2,1)S(1)} %get-tuple-element.48), channel_id=1, source_target_pairs={{9,0},{10,1},{11,2},{12,3},{13,4},{14,5},{15,6},{8,7},{17,8},{18,9... | collective-permute-start | bytes 368648 | tf_op jit(solution)/shard_map/ppermute | solution.py:433
  68.2 1.8 %collective-permute-done.3.refs_4_ = bf16[32,1920]{1,0:T(8,128)(2,1)S(1)} collective-permute-done((bf16[32,1920]{1,0:T(8,128)(2,1)S(1)}, bf16[32,1920]{1,0:T(8,128)(2,1)S(1)}, u32[]{:S(2)}, u32[]{:S(2)}) %collective-permute-start.3) | collective-permute-done | bytes 122912 | tf_op jit(solution)/shard_map/ppermute | solution.py:433
  70.0 4.8 %main.1 = (bf16[32,768]{1,0:T(8,128)(2,1)}, bf16[64,768]{1,0:T(8,128)(2,1)}, bf16[32,768]{1,0:T(8,128)(2,1)}, bf16[8,2,48,384]{3,2,1,0:T(8,128)(2,1)S(1)}, bf16[8,2,48,384]{3,2,1,0:T(8,128)(2,1)S(1)}) custom-call(s32[1]{0:T(128)} %bitcast.core_ref.refs_0_, bf16[32,1920]{1,0:T(8,128)(2,1)S(1)} %get-tuple-element.45.refs_1_, ...), custom_call_target="tpu_custom_call" | custom-call | flops 1000000 | bytes 1000000 | tf_op jit(solution)/shard_map/main/pallas_call | solution.py:528
  74.8 4.6 %collective-permute-start.4 = (bf16[8,2,48,384]{3,2,1,0:T(8,128)(2,1)S(1)}, bf16[8,2,48,384]{3,2,1,0:T(8,128)(2,1)S(1)}, u32[]{:S(2)}, u32[]{:S(2)}) collective-permute-start(bf16[8,2,48,384]{3,2,1,0:T(8,128)(2,1)S(1)} %get-tuple-element.51), channel_id=1, source_target_pairs={{0,8},{8,0},{16,24},{24,16},{32,40},{40,32},{48,56},{56,48},{64,72... | collective-permute-start | bytes 1769480 | tf_op jit(solution)/shard_map/ppermute | solution.py:437
  79.4 1.6 %collective-permute-done.4 = bf16[8,2,48,384]{3,2,1,0:T(8,128)(2,1)S(1)} collective-permute-done((bf16[8,2,48,384]{3,2,1,0:T(8,128)(2,1)S(1)}, bf16[8,2,48,384]{3,2,1,0:T(8,128)(2,1)S(1)}, u32[]{:S(2)}, u32[]{:S(2)}) %collective-permute-start.4) | collective-permute-done | bytes 589856 | tf_op jit(solution)/shard_map/ppermute | solution.py:437
  81.0 1.0 add_convert_fusion
  82.0 3.5 %all-to-all-start.1 = ((bf16[8,2,48,384]{3,2,1,0:T(8,128)(2,1)}), bf16[8,2,48,384]{3,2,1,0:T(8,128)(2,1)S(1)}, u32[]{:S(2)}, u32[]{:S(2)}) async-start(bf16[8,2,48,384]{3,2,1,0:T(8,128)(2,1)} %add_convert_fusion), calls=%async_computation.1 | async-start | bytes 1179648 | tf_op jit(solution)/shard_map/all_to_all | solution.py:423
  85.5 1.9 %collective-permute-start.5 = (bf16[64,768]{1,0:T(8,128)(2,1)S(1)}, bf16[64,768]{1,0:T(8,128)(2,1)S(1)}, u32[]{:S(2)}, u32[]{:S(2)}) collective-permute-start(bf16[64,768]{1,0:T(8,128)(2,1)S(1)} %copy-done.5), channel_id=1, source_target_pairs={{504,0},{505,1},{506,2},{507,3},{508,4},{509,5},{510,6},{511,7},{0... | collective-permute-start | bytes 294920 | tf_op jit(solution)/shard_map/ppermute | solution.py:433
  87.5 6.7 %collective-permute-done.5.column = bf16[64,768]{1,0:T(8,128)(2,1)S(1)} collective-permute-done((bf16[64,768]{1,0:T(8,128)(2,1)S(1)}, bf16[64,768]{1,0:T(8,128)(2,1)S(1)}, u32[]{:S(2)}, u32[]{:S(2)}) %collective-permute-start.5) | collective-permute-done | bytes 98336 | tf_op jit(solution)/shard_map/ppermute | solution.py:433
  94.2 1.3 all-to-all-done.1.parts
  95.4 0.8 sum_copies.3
  96.2 3.5 %all-to-all-start.2 = ((bf16[4,2,48,384]{3,2,1,0:T(8,128)(2,1)}), bf16[4,2,48,384]{3,2,1,0:T(8,128)(2,1)S(1)}, u32[]{:S(2)}, u32[]{:S(2)}) async-start(bf16[4,2,48,384]{3,2,1,0:T(8,128)(2,1)} %sum_copies.3), calls=%async_computation.2 | async-start | bytes 589824 | tf_op jit(solution)/shard_map/all_to_all | solution.py:423
  99.7 2.1 %collective-permute-start.6 = (bf16[64,768]{1,0:T(8,128)(2,1)S(1)}, bf16[64,768]{1,0:T(8,128)(2,1)S(1)}, u32[]{:S(2)}, u32[]{:S(2)}) collective-permute-start(bf16[64,768]{1,0:T(8,128)(2,1)S(1)} %pad_maximum_fusion), channel_id=1, source_target_pairs={{7,0},{0,1},{1,2},{2,3},{3,4},{4,5},{5,6},{6,7},{15,8},{8,9},{9,10... | collective-permute-start | bytes 294920 | tf_op jit(solution)/shard_map/ppermute | solution.py:433
  101.9 6.9 %collective-permute-done.6.row = bf16[64,768]{1,0:T(8,128)(2,1)S(1)} collective-permute-done((bf16[64,768]{1,0:T(8,128)(2,1)S(1)}, bf16[64,768]{1,0:T(8,128)(2,1)S(1)}, u32[]{:S(2)}, u32[]{:S(2)}) %collective-permute-start.6) | collective-permute-done | bytes 98336 | tf_op jit(solution)/shard_map/ppermute | solution.py:433
  108.8 0.9 sum_copies.4
  109.7 6.1 %all-to-all-start.3 = ((bf16[8,2,48,384]{3,2,1,0:T(8,128)(2,1)}), bf16[8,2,48,384]{3,2,1,0:T(8,128)(2,1)S(1)}, u32[]{:S(2)}, u32[]{:S(2)}) async-start(bf16[8,2,48,384]{3,2,1,0:T(8,128)(2,1)} %sum_copies.4), calls=%async_computation.3 | async-start | bytes 1179648 | tf_op jit(solution)/shard_map/all_to_all | solution.py:423
  115.8 5.5 %plain_back.1 = bf16[128,768]{1,0:T(8,128)(2,1)} custom-call(s32[1]{0:T(128)} %bitcast.core_ref.refs_0_, bf16[128,768]{1,0:T(8,128)(2,1)} %bitcast.12, bf16[32,768]{1,0:T(8,128)(2,1)} %get-tuple-element.61.own_far, f32[64,768]{1,0:T(8,128)} %get-tuple-element.37.bias_p_far.bias_far, bf16[8,384,384]{2,1,0:T(8,128)(2,1)} %copy-done, ...), custom_call_target="tpu_custom_call" | custom-call | flops 4000000000 | bytes 4000000 | tf_op jit(solution)/shard_map/plain_back/pallas_call | solution.py:556
  121.3 8.9 %all-to-all-done.3.parts = bf16[8,2,48,384]{3,2,1,0:T(8,128)(2,1)S(1)} async-done(((bf16[8,2,48,384]{3,2,1,0:T(8,128)(2,1)}), bf16[8,2,48,384]{3,2,1,0:T(8,128)(2,1)S(1)}, u32[]{:S(2)}, u32[]{:S(2)}) %all-to-all-start.3) | async-done | bytes 589856 | tf_op jit(solution)/shard_map/all_to_all | solution.py:423
  130.2 0.1 sum_copies.5
  130.3 7.0 %all_gather.3.parts = bf16[2,2,48,384]{3,2,1,0:T(8,128)(2,1)S(1)} all-gather(bf16[1,2,48,384]{3,2,1,0:T(8,128)(2,1)S(1)} %sum_copies.5), channel_id=1, replica_groups={{0,8},{16,24},{32,40},{48,56},{64,72},{80,88},{96,104},{112,120},{128,1..., dimensions={0}, use_global_device_ids=true | all-gather | bytes 221184 | tf_op jit(solution)/shard_map/all_gather | solution.py:579
  137.3 0.7 finish.1
  (17 shorter events, 0.1 us)
Async XLA Ops:
  3.3 6.0 %copy-start.2 = (f32[12,225]{1,0:T(8,128)S(1)}, f32[12,225]{1,0:T(8,128)}, u32[]{:S(2)}) copy-start(f32[12,225]{1,0:T(8,128)} %table_p.1) | copy-start | bytes 32404
  3.3 6.0 %copy-start.3 = (f32[12,225]{1,0:T(8,128)S(1)}, f32[12,225]{1,0:T(8,128)}, u32[]{:S(2)}) copy-start(f32[12,225]{1,0:T(8,128)} %table_s.1) | copy-start | bytes 32404
  3.3 31.2 %all-to-all-start = ((bf16[8,384,384]{2,1,0:T(8,128)(2,1)}), bf16[8,384,384]{2,1,0:T(8,128)(2,1)S(1)}, u32[]{:S(2)}, u32[]{:S(2)}) async-start(bf16[8,384,384]{2,1,0:T(8,128)(2,1)} %prepare.1), calls=%async_computation | async-start | bytes 4718592 | tf_op jit(solution)/shard_map/all_to_all | solution.py:423
  34.5 35.5 %copy-start = (bf16[8,384,384]{2,1,0:T(8,128)(2,1)}, bf16[8,384,384]{2,1,0:T(8,128)(2,1)S(1)}, u32[]{:S(2)}) copy-start(bf16[8,384,384]{2,1,0:T(8,128)(2,1)S(1)} %all-to-all-done.w_mine_ref.refs_5_.mine_far) | copy-start | bytes 7077892
  34.5 11.5 %collective-permute-start = (bf16[8,384,384]{2,1,0:T(8,128)(2,1)S(1)}, bf16[8,384,384]{2,1,0:T(8,128)(2,1)S(1)}, u32[]{:S(2)}, u32[]{:S(2)}) collective-permute-start(bf16[8,384,384]{2,1,0:T(8,128)(2,1)S(1)} %all-to-all-done.w_mine_ref.refs_5_.mine_far), channel_id=1, source_target_pairs={{0,8},{8,0},{16,24},{24,16},{32,40},{40,32},{48,56},{56,48},{64,72... | collective-permute-start | bytes 7077896 | tf_op jit(solution)/shard_map/ppermute | solution.py:437
  46.0 24.0 %copy-start.1 = (bf16[8,384,384]{2,1,0:T(8,128)(2,1)}, bf16[8,384,384]{2,1,0:T(8,128)(2,1)S(1)}, u32[]{:S(2)}) copy-start(bf16[8,384,384]{2,1,0:T(8,128)(2,1)S(1)} %collective-permute-done.w_other_ref.refs_6_.other_far) | copy-start | bytes 7077892
  47.9 20.2 %collective-permute-start.1 = (bf16[32,1920]{1,0:T(8,128)(2,1)S(1)}, bf16[32,1920]{1,0:T(8,128)(2,1)S(1)}, u32[]{:S(2)}, u32[]{:S(2)}) collective-permute-start(bf16[32,1920]{1,0:T(8,128)(2,1)S(1)} %get-tuple-element.46), channel_id=1, source_target_pairs={{8,0},{9,1},{10,2},{11,3},{12,4},{13,5},{14,6},{15,7},{16,8},{17,9... | collective-permute-start | bytes 368648 | tf_op jit(solution)/shard_map/ppermute | solution.py:433
  50.2 17.9 %collective-permute-start.2 = (bf16[32,1920]{1,0:T(8,128)(2,1)S(1)}, bf16[32,1920]{1,0:T(8,128)(2,1)S(1)}, u32[]{:S(2)}, u32[]{:S(2)}) collective-permute-start(bf16[32,1920]{1,0:T(8,128)(2,1)S(1)} %get-tuple-element.47), channel_id=1, source_target_pairs={{1,0},{2,1},{3,2},{4,3},{5,4},{6,5},{7,6},{0,7},{9,8},{10,9},{11,1... | collective-permute-start | bytes 368648 | tf_op jit(solution)/shard_map/ppermute | solution.py:433
  53.3 16.7 %collective-permute-start.3 = (bf16[32,1920]{1,0:T(8,128)(2,1)S(1)}, bf16[32,1920]{1,0:T(8,128)(2,1)S(1)}, u32[]{:S(2)}, u32[]{:S(2)}) collective-permute-start(bf16[32,1920]{1,0:T(8,128)(2,1)S(1)} %get-tuple-element.48), channel_id=1, source_target_pairs={{9,0},{10,1},{11,2},{12,3},{13,4},{14,5},{15,6},{8,7},{17,8},{18,9... | collective-permute-start | bytes 368648 | tf_op jit(solution)/shard_map/ppermute | solution.py:433
  74.8 10.7 %copy-start.5 = (bf16[64,768]{1,0:T(8,128)(2,1)S(1)}, bf16[64,768]{1,0:T(8,128)(2,1)}, u32[]{:S(2)}) copy-start(bf16[64,768]{1,0:T(8,128)(2,1)} %get-tuple-element.55) | copy-start | bytes 294916
  74.8 24.9 %copy-start.4 = (bf16[32,768]{1,0:T(8,128)(2,1)S(1)}, bf16[32,768]{1,0:T(8,128)(2,1)}, u32[]{:S(2)}) copy-start(bf16[32,768]{1,0:T(8,128)(2,1)} %get-tuple-element.58) | copy-start | bytes 147460
  74.8 6.2 %collective-permute-start.4 = (bf16[8,2,48,384]{3,2,1,0:T(8,128)(2,1)S(1)}, bf16[8,2,48,384]{3,2,1,0:T(8,128)(2,1)S(1)}, u32[]{:S(2)}, u32[]{:S(2)}) collective-permute-start(bf16[8,2,48,384]{3,2,1,0:T(8,128)(2,1)S(1)} %get-tuple-element.51), channel_id=1, source_target_pairs={{0,8},{8,0},{16,24},{24,16},{32,40},{40,32},{48,56},{56,48},{64,72... | collective-permute-start | bytes 1769480 | tf_op jit(solution)/shard_map/ppermute | solution.py:437
  82.0 13.5 %all-to-all-start.1 = ((bf16[8,2,48,384]{3,2,1,0:T(8,128)(2,1)}), bf16[8,2,48,384]{3,2,1,0:T(8,128)(2,1)S(1)}, u32[]{:S(2)}, u32[]{:S(2)}) async-start(bf16[8,2,48,384]{3,2,1,0:T(8,128)(2,1)} %add_convert_fusion), calls=%async_computation.1 | async-start | bytes 1179648 | tf_op jit(solution)/shard_map/all_to_all | solution.py:423
  85.5 8.6 %collective-permute-start.5 = (bf16[64,768]{1,0:T(8,128)(2,1)S(1)}, bf16[64,768]{1,0:T(8,128)(2,1)S(1)}, u32[]{:S(2)}, u32[]{:S(2)}) collective-permute-start(bf16[64,768]{1,0:T(8,128)(2,1)S(1)} %copy-done.5), channel_id=1, source_target_pairs={{504,0},{505,1},{506,2},{507,3},{508,4},{509,5},{510,6},{511,7},{0... | collective-permute-start | bytes 294920 | tf_op jit(solution)/shard_map/ppermute | solution.py:433
  96.2 12.6 %all-to-all-start.2 = ((bf16[4,2,48,384]{3,2,1,0:T(8,128)(2,1)}), bf16[4,2,48,384]{3,2,1,0:T(8,128)(2,1)S(1)}, u32[]{:S(2)}, u32[]{:S(2)}) async-start(bf16[4,2,48,384]{3,2,1,0:T(8,128)(2,1)} %sum_copies.3), calls=%async_computation.2 | async-start | bytes 589824 | tf_op jit(solution)/shard_map/all_to_all | solution.py:423
  99.7 9.1 %collective-permute-start.6 = (bf16[64,768]{1,0:T(8,128)(2,1)S(1)}, bf16[64,768]{1,0:T(8,128)(2,1)S(1)}, u32[]{:S(2)}, u32[]{:S(2)}) collective-permute-start(bf16[64,768]{1,0:T(8,128)(2,1)S(1)} %pad_maximum_fusion), channel_id=1, source_target_pairs={{7,0},{0,1},{1,2},{2,3},{3,4},{4,5},{5,6},{6,7},{15,8},{8,9},{9,10... | collective-permute-start | bytes 294920 | tf_op jit(solution)/shard_map/ppermute | solution.py:433
  109.7 20.5 %all-to-all-start.3 = ((bf16[8,2,48,384]{3,2,1,0:T(8,128)(2,1)}), bf16[8,2,48,384]{3,2,1,0:T(8,128)(2,1)S(1)}, u32[]{:S(2)}, u32[]{:S(2)}) async-start(bf16[8,2,48,384]{3,2,1,0:T(8,128)(2,1)} %sum_copies.4), calls=%async_computation.3 | async-start | bytes 1179648 | tf_op jit(solution)/shard_map/all_to_all | solution.py:423

commit v11 on v9

--- a/solution.py
+++ b/solution.py
@@ -185,10 +185,9 @@
     bias_far,
     w_mine_ref,
     w_other_ref,
-    out_o,
-    out_r,
-    out_b,
-    out_d,
+    out_own,
+    out_top,
+    out_column,
     tok,
     cot,
     bias_p,
@@ -221,8 +220,13 @@
     loads[2].wait()
     for whole, first in ((block_out, 0), (mixed, D), (cot[...], D + WIDE)):
         packets[:, first : first + whole.shape[1]] = dot(pick, whole).astype(BF16)
-    outs = (out_d, out_b, out_r, out_o)
-    wait_all(copy_all([(packets.at[i * 32 : (i + 1) * 32], out) for i, out in enumerate(outs)], sems, 3))
+    stores = [
+        (packets.at[0:32], out_column.at[0:32]),
+        (packets.at[64:96], out_column.at[32:64]),
+        (packets.at[32:64], out_top),
+        (packets.at[96:128], out_own),
+    ]
+    wait_all(copy_all(stores, sems, 3))
 
 
 def main_kernel(
@@ -232,7 +236,6 @@
     bias_far,
     right,
     below,
-    diag,
     w_mine_ref,
     w_other_ref,
     to_own,
@@ -252,8 +255,8 @@
     mine, other = sides(core_ref)
     loads = copy_all([(own_far, staged.at[0:32]), (bias_far, bias_s)], sems)
     mask[...] = head_mask()
-    for i, part in ((1, right), (2, below), (3, diag)):
-        staged[i * 32 : (i + 1) * 32] = part[...]
+    staged[32:64] = right[32:64]
+    staged[64:128] = below[...]
     wait_all(loads)
     pick = quadrant_pick(True)
     grads[...] = dot(pick, staged[:, D + WIDE :]).astype(BF16)
@@ -478,11 +481,12 @@
     second_mine = swap(second_share, "freq")
     first_other = other_core(first_mine)
     packet = pltpu.HBM((32, 2 * D + WIDE), BF16)
-    own, to_left, to_above, to_diag = pl.pallas_call(
+    wide = pltpu.HBM((64, 2 * D + WIDE), BF16)
+    own, to_above, to_left = pl.pallas_call(
         plain_forward,
-        out_shape=(packet,) * 4,
+        out_shape=(packet, packet, wide),
         in_specs=[SMEM] + [HBM] * 3 + [VMEM] * 2,
-        out_specs=[HBM] * 4,
+        out_specs=[HBM] * 3,
         scratch_shapes=[
             pltpu.VMEM((128, D), BF16),
             pltpu.VMEM((128, D), BF16),
@@ -498,11 +502,8 @@
         name="plain_forward",
     )(core, far(tok), far(cot), far(bias_p), first_mine, first_other)
     right = from_offset(to_left, 1, 0)
-    below = from_offset(to_above, 0, 1)
-    diag = from_offset(to_diag, 1, 1)
-    second_mine, right, below, diag = lax.optimization_barrier(
-        (second_mine, right, below, diag)
-    )
+    second_mine, right = lax.optimization_barrier((second_mine, right))
+    below = from_offset(jnp.concatenate([to_above, right[0:32]], axis=0), 0, 1)
     second_other = other_core(second_mine)
     piece = pltpu.HBM((32, D), BF16)
     column = pltpu.HBM((64, D), BF16)
@@ -510,7 +511,7 @@
     g_own, to_right, to_below, keep, send = pl.pallas_call(
         lambda *refs: main_kernel(grad_scale, *refs),
         out_shape=(piece, column, piece, local, local),
-        in_specs=[SMEM] + [HBM] * 2 + [VMEM] * 5,
+        in_specs=[SMEM] + [HBM] * 2 + [VMEM] * 4,
         out_specs=[HBM] * 3 + [VMEM] * 2,
         scratch_shapes=[
             pltpu.VMEM((SPOTS, LANES), F32),
@@ -525,7 +526,7 @@
         compiler_params=params(),
         cost_estimate=cost(1_000_000, 1_000_000),
         name="main",
-    )(core, far(own), far(bias_s), right, below, diag, second_mine, second_other)
+    )(core, far(own), far(bias_s), right, below, second_mine, second_other)
 
     part = (keep.astype(F32) + other_core(send).astype(F32)).astype(BF16)
     part, to_right, to_below = lax.optimization_barrier((part, to_right, to_below))

time: 138 us -> 143 us (1.036)
  waiting for transfers between devices: 39.6 us -> 49.5 us
  starting transfers between devices: 64.7 us -> 55.8 us
  blocking collectives: 6.49 us -> 9.15 us
    ppermute x5 -> x4, starting transfers between devices: 25.5 us -> 11.1 us  [from_offset(): return lax.ppermute(value, ('tm', 'freq'), pairs)]
    ppermute x5 -> x4, waiting for transfers between devices: 16.6 us -> 25.6 us  [from_offset(): return lax.ppermute(value, ('tm', 'freq'), pairs)]
    all_to_all x5, waiting for transfers between devices: 18.9 us -> 22.3 us  [swap(): return lax.all_to_all(value, axis, 0, 0, axis_index_groups=groups)]
    all_to_all x5, starting transfers between devices: 24.1 us -> 27.5 us  [swap(): return lax.all_to_all(value, axis, 0, 0, axis_index_groups=groups)]
    all_gather x1, blocking collectives: 6.49 us -> 9.15 us  [shards(): part = lax.all_gather(part, 'tm', axis_index_groups=tm_groups('core'))]
    ppermute x3, waiting for transfers between devices: 4.06 us -> 1.61 us  [other_core(): lax.ppermute(value, 'tm', [(i, i ^ 1) for i in range(lax.axis_size('tm'))])]
    ppermute x3, starting transfers between devices: 15 us -> 17.1 us  [other_core(): lax.ppermute(value, 'tm', [(i, i ^ 1) for i in range(lax.axis_size('tm'))])]
  transfers between devices with their start and end apart: 13 -> 12, of which waited for: 8 -> 9; matrix products, arithmetic and copies ran while one was open for 0% -> 1% of each run, Pallas kernels for 10% -> 10%
where the time goes in v11:
time: 143 us; the launch traced here: 142 us
  starting transfers between devices  55.8 us (39%)
  waiting for transfers between devices  49.5 us (35%)
  Pallas kernels  24.5 us (17%)
  blocking collectives  9.15 us (6%)
  other arithmetic  1.98 us (1%)
    all_to_all x5, starting transfers between devices, swap(): return lax.all_to_all(value, axis, 0, 0, axis_index_groups=groups)  27.5 us
    ppermute x4, waiting for transfers between devices, from_offset(): return lax.ppermute(value, ('tm', 'freq'), pairs)  25.6 us
    all_to_all x5, waiting for transfers between devices, swap(): return lax.all_to_all(value, axis, 0, 0, axis_index_groups=groups)  22.3 us
    ppermute x3, starting transfers between devices, other_core(): lax.ppermute(value, 'tm', [(i, i ^ 1) for i in range(lax.axis_size('tm'))])  17.1 us
    ppermute x4, starting transfers between devices, from_offset(): return lax.ppermute(value, ('tm', 'freq'), pairs)  11.1 us
    all_gather x1, blocking collectives, shards(): part = lax.all_gather(part, 'tm', axis_index_groups=tm_groups('core'))  9.15 us
    pallas_call x1, Pallas kernels, shards(): pl.pallas_call(lambda *refs: main_kernel(grad_scale, *refs), out_shape=(p...  5.73 us
    pallas_call x1, Pallas kernels, shards(): pl.pallas_call(plain_back, out_shape=jax.ShapeDtypeStruct((128, D), BF16)...  5.54 us
  transfers between devices with their start and end apart: 12, of which 9 were waited for; matrix products, arithmetic and copies ran while one was open for 1% of the time, Pallas kernels for 10%

profile of v11, /device:TPU:1, one launch (start us, length us, event | category | flops | bytes accessed | tf_op | source)
XLA Modules:
  0.0 141.8 jit_solution(2528543838749804035)
XLA Ops:
  0.6 2.1 %prepare.2 = bf16[8,192,384]{2,1,0:T(8,128)(2,1)} custom-call(s32[1]{0:T(128)} %bitcast.core_ref.refs_0_, bf16[144,768]{1,0:T(8,128)(2,1)} %bitcast.8, bf16[48,768]{1,0:T(8,128)(2,1)} %proj.2), custom_call_target="tpu_custom_call" | custom-call | tf_op jit(solution)/shard_map/prepare/pallas_call | solution.py:446
  2.8 5.9 %all-to-all-start = ((bf16[8,192,384]{2,1,0:T(8,128)(2,1)}), bf16[8,192,384]{2,1,0:T(8,128)(2,1)S(1)}, u32[]{:S(2)}, u32[]{:S(2)}) async-start(bf16[8,192,384]{2,1,0:T(8,128)(2,1)} %prepare.2), calls=%async_computation | async-start | bytes 2359296 | tf_op jit(solution)/shard_map/all_to_all | solution.py:406
  8.7 2.1 %prepare.3 = bf16[8,192,384]{2,1,0:T(8,128)(2,1)} custom-call(s32[1]{0:T(128)} %bitcast.core_ref.refs_0_, bf16[144,768]{1,0:T(8,128)(2,1)} %bitcast.9, bf16[48,768]{1,0:T(8,128)(2,1)} %proj.3), custom_call_target="tpu_custom_call" | custom-call | tf_op jit(solution)/shard_map/prepare/pallas_call | solution.py:446
  10.9 2.0 %biases.1 = (f32[64,768]{1,0:T(8,128)}, f32[64,768]{1,0:T(8,128)}) custom-call(s32[2]{0:T(128)S(1)} %add_convert_fusion.1.edge_ref, f32[12,225]{1,0:T(8,128)S(1)} %copy-done.1, f32[12,225]{1,0:T(8,128)S(1)} %copy-done.2), custom_call_target="tpu_custom_call" | custom-call | tf_op jit(solution)/shard_map/biases/pallas_call | solution.py:462
  12.9 8.5 %all-to-all-done.w_mine_ref.mine_far = bf16[8,192,384]{2,1,0:T(8,128)(2,1)S(1)} async-done(((bf16[8,192,384]{2,1,0:T(8,128)(2,1)}), bf16[8,192,384]{2,1,0:T(8,128)(2,1)S(1)}, u32[]{:S(2)}, u32[]{:S(2)}) %all-to-all-start) | async-done | bytes 1179680 | tf_op jit(solution)/shard_map/all_to_all | solution.py:406
  21.4 7.3 %collective-permute-start = (bf16[8,192,384]{2,1,0:T(8,128)(2,1)S(1)}, bf16[8,192,384]{2,1,0:T(8,128)(2,1)S(1)}, u32[]{:S(2)}, u32[]{:S(2)}) collective-permute-start(bf16[8,192,384]{2,1,0:T(8,128)(2,1)S(1)} %all-to-all-done.w_mine_ref.mine_far), channel_id=1, source_target_pairs={{0,8},{8,0},{16,24},{24,16},{32,40},{40,32},{48,56},{56,48},{64,72... | collective-permute-start | bytes 3538952 | tf_op jit(solution)/shard_map/ppermute | solution.py:420
  28.7 3.6 %all-to-all-start.1 = ((bf16[8,192,384]{2,1,0:T(8,128)(2,1)}), bf16[8,192,384]{2,1,0:T(8,128)(2,1)S(1)}, u32[]{:S(2)}, u32[]{:S(2)}) async-start(bf16[8,192,384]{2,1,0:T(8,128)(2,1)} %prepare.3), calls=%async_computation.1 | async-start | bytes 2359296 | tf_op jit(solution)/shard_map/all_to_all | solution.py:406
  32.3 4.5 %plain_forward.1 = (bf16[32,1920]{1,0:T(8,128)(2,1)}, bf16[32,1920]{1,0:T(8,128)(2,1)}, bf16[64,1920]{1,0:T(8,128)(2,1)}) custom-call(s32[1]{0:T(128)} %bitcast.core_ref.refs_0_, bf16[128,768]{1,0:T(8,128)(2,1)} %bitcast.11, bf16[128,768]{1,0:T(8,128)(2,1)} %bitcast.10, f32[64,768]{1,0:T(8,128)} %get-tuple-element.33.bias_far, ...), custom_call_target="tpu_custom_call" | custom-call | flops 20000000000 | bytes 1000000 | tf_op jit(solution)/shard_map/plain_forward/pallas_call | solution.py:485
  36.9 1.9 %collective-permute-start.1 = (bf16[64,1920]{1,0:T(8,128)(2,1)}, bf16[64,1920]{1,0:T(8,128)(2,1)S(1)}, u32[]{:S(2)}, u32[]{:S(2)}) collective-permute-start(bf16[64,1920]{1,0:T(8,128)(2,1)} %get-tuple-element.38), channel_id=1, source_target_pairs={{8,0},{9,1},{10,2},{11,3},{12,4},{13,5},{14,6},{15,7},{16,8},{17,9... | collective-permute-start | bytes 737288 | tf_op jit(solution)/shard_map/ppermute | solution.py:416
  38.8 7.0 %collective-permute-done.1.refs_3_ = bf16[64,1920]{1,0:T(8,128)(2,1)S(1)} collective-permute-done((bf16[64,1920]{1,0:T(8,128)(2,1)}, bf16[64,1920]{1,0:T(8,128)(2,1)S(1)}, u32[]{:S(2)}, u32[]{:S(2)}) %collective-permute-start.1) | collective-permute-done | bytes 245792 | tf_op jit(solution)/shard_map/ppermute | solution.py:416
  45.8 6.3 %all-to-all-done.1.refs_5_ = bf16[8,192,384]{2,1,0:T(8,128)(2,1)S(1)} async-done(((bf16[8,192,384]{2,1,0:T(8,128)(2,1)}), bf16[8,192,384]{2,1,0:T(8,128)(2,1)S(1)}, u32[]{:S(2)}, u32[]{:S(2)}) %all-to-all-start.1) | async-done | bytes 1179680 | tf_op jit(solution)/shard_map/all_to_all | solution.py:406
  52.2 7.1 %collective-permute-start.3 = (bf16[8,192,384]{2,1,0:T(8,128)(2,1)S(1)}, bf16[8,192,384]{2,1,0:T(8,128)(2,1)S(1)}, u32[]{:S(2)}, u32[]{:S(2)}) collective-permute-start(bf16[8,192,384]{2,1,0:T(8,128)(2,1)S(1)} %all-to-all-done.1.refs_5_), channel_id=1, source_target_pairs={{0,8},{8,0},{16,24},{24,16},{32,40},{40,32},{48,56},{56,48},{64,72... | collective-permute-start | bytes 3538952 | tf_op jit(solution)/shard_map/ppermute | solution.py:420
  59.3 0.9 pad_maximum_fusion
  60.2 2.8 %collective-permute-start.2 = (bf16[64,1920]{1,0:T(8,128)(2,1)S(1)}, bf16[64,1920]{1,0:T(8,128)(2,1)S(1)}, u32[]{:S(2)}, u32[]{:S(2)}) collective-permute-start(bf16[64,1920]{1,0:T(8,128)(2,1)S(1)} %pad_maximum_fusion), channel_id=1, source_target_pairs={{1,0},{2,1},{3,2},{4,3},{5,4},{6,5},{7,6},{0,7},{9,8},{10,9},{11,1... | collective-permute-start | bytes 737288 | tf_op jit(solution)/shard_map/ppermute | solution.py:416
  63.0 6.6 %collective-permute-done.2.refs_4_ = bf16[64,1920]{1,0:T(8,128)(2,1)S(1)} collective-permute-done((bf16[64,1920]{1,0:T(8,128)(2,1)S(1)}, bf16[64,1920]{1,0:T(8,128)(2,1)S(1)}, u32[]{:S(2)}, u32[]{:S(2)}) %collective-permute-start.2) | collective-permute-done | bytes 245792 | tf_op jit(solution)/shard_map/ppermute | solution.py:416
  69.7 5.7 %main.1 = (bf16[32,768]{1,0:T(8,128)(2,1)}, bf16[64,768]{1,0:T(8,128)(2,1)}, bf16[32,768]{1,0:T(8,128)(2,1)}, bf16[8,2,48,384]{3,2,1,0:T(8,128)(2,1)S(1)}, bf16[8,2,48,384]{3,2,1,0:T(8,128)(2,1)S(1)}) custom-call(s32[1]{0:T(128)} %bitcast.core_ref.refs_0_, bf16[32,1920]{1,0:T(8,128)(2,1)} %get-tuple-element.35.refs_1_, f32[64,768]{1,0:T(8,128)} %get-tuple-element.36.refs_2_, ...), custom_call_target="tpu_custom_call" | custom-call | flops 1000000 | bytes 1000000 | tf_op jit(solution)/shard_map/main/pallas_call | solution.py:511
  75.4 2.7 %collective-permute-start.4 = (bf16[8,2,48,384]{3,2,1,0:T(8,128)(2,1)S(1)}, bf16[8,2,48,384]{3,2,1,0:T(8,128)(2,1)S(1)}, u32[]{:S(2)}, u32[]{:S(2)}) collective-permute-start(bf16[8,2,48,384]{3,2,1,0:T(8,128)(2,1)S(1)} %get-tuple-element.43), channel_id=1, source_target_pairs={{0,8},{8,0},{16,24},{24,16},{32,40},{40,32},{48,56},{56,48},{64,72... | collective-permute-start | bytes 1769480 | tf_op jit(solution)/shard_map/ppermute | solution.py:420
  78.1 1.6 %collective-permute-done.4 = bf16[8,2,48,384]{3,2,1,0:T(8,128)(2,1)S(1)} collective-permute-done((bf16[8,2,48,384]{3,2,1,0:T(8,128)(2,1)S(1)}, bf16[8,2,48,384]{3,2,1,0:T(8,128)(2,1)S(1)}, u32[]{:S(2)}, u32[]{:S(2)}) %collective-permute-start.4) | collective-permute-done | bytes 589856 | tf_op jit(solution)/shard_map/ppermute | solution.py:420
  79.7 1.0 add_convert_fusion
  80.7 4.6 %all-to-all-start.2 = ((bf16[8,2,48,384]{3,2,1,0:T(8,128)(2,1)}), bf16[8,2,48,384]{3,2,1,0:T(8,128)(2,1)S(1)}, u32[]{:S(2)}, u32[]{:S(2)}) async-start(bf16[8,2,48,384]{3,2,1,0:T(8,128)(2,1)} %add_convert_fusion), calls=%async_computation.2 | async-start | bytes 1179648 | tf_op jit(solution)/shard_map/all_to_all | solution.py:406
  85.3 3.8 %collective-permute-start.5 = (bf16[64,768]{1,0:T(8,128)(2,1)S(1)}, bf16[64,768]{1,0:T(8,128)(2,1)S(1)}, u32[]{:S(2)}, u32[]{:S(2)}) collective-permute-start(bf16[64,768]{1,0:T(8,128)(2,1)S(1)} %copy-done.5), channel_id=1, source_target_pairs={{504,0},{505,1},{506,2},{507,3},{508,4},{509,5},{510,6},{511,7},{0... | collective-permute-start | bytes 294920 | tf_op jit(solution)/shard_map/ppermute | solution.py:416
  89.1 5.3 %collective-permute-done.5.column = bf16[64,768]{1,0:T(8,128)(2,1)S(1)} collective-permute-done((bf16[64,768]{1,0:T(8,128)(2,1)S(1)}, bf16[64,768]{1,0:T(8,128)(2,1)S(1)}, u32[]{:S(2)}, u32[]{:S(2)}) %collective-permute-start.5) | collective-permute-done | bytes 98336 | tf_op jit(solution)/shard_map/ppermute | solution.py:416
  94.5 0.8 all-to-all-done.2.parts
  95.3 0.8 sum_copies.3
  96.1 3.5 %all-to-all-start.3 = ((bf16[4,2,48,384]{3,2,1,0:T(8,128)(2,1)}), bf16[4,2,48,384]{3,2,1,0:T(8,128)(2,1)S(1)}, u32[]{:S(2)}, u32[]{:S(2)}) async-start(bf16[4,2,48,384]{3,2,1,0:T(8,128)(2,1)} %sum_copies.3), calls=%async_computation.3 | async-start | bytes 589824 | tf_op jit(solution)/shard_map/all_to_all | solution.py:406
  99.6 2.6 %collective-permute-start.6 = (bf16[64,768]{1,0:T(8,128)(2,1)S(1)}, bf16[64,768]{1,0:T(8,128)(2,1)S(1)}, u32[]{:S(2)}, u32[]{:S(2)}) collective-permute-start(bf16[64,768]{1,0:T(8,128)(2,1)S(1)} %pad_maximum_fusion.1), channel_id=1, source_target_pairs={{7,0},{0,1},{1,2},{2,3},{3,4},{4,5},{5,6},{6,7},{15,8},{8,9},{9,10... | collective-permute-start | bytes 294920 | tf_op jit(solution)/shard_map/ppermute | solution.py:416
  102.1 6.6 %collective-permute-done.6.row = bf16[64,768]{1,0:T(8,128)(2,1)S(1)} collective-permute-done((bf16[64,768]{1,0:T(8,128)(2,1)S(1)}, bf16[64,768]{1,0:T(8,128)(2,1)S(1)}, u32[]{:S(2)}, u32[]{:S(2)}) %collective-permute-start.6) | collective-permute-done | bytes 98336 | tf_op jit(solution)/shard_map/ppermute | solution.py:416
  108.7 0.9 sum_copies.4
  109.6 10.0 %all-to-all-start.4 = ((bf16[8,2,48,384]{3,2,1,0:T(8,128)(2,1)}), bf16[8,2,48,384]{3,2,1,0:T(8,128)(2,1)S(1)}, u32[]{:S(2)}, u32[]{:S(2)}) async-start(bf16[8,2,48,384]{3,2,1,0:T(8,128)(2,1)} %sum_copies.4), calls=%async_computation.4 | async-start | bytes 1179648 | tf_op jit(solution)/shard_map/all_to_all | solution.py:406
  119.6 5.5 %plain_back.1 = bf16[128,768]{1,0:T(8,128)(2,1)} custom-call(s32[1]{0:T(128)} %bitcast.core_ref.refs_0_, bf16[128,768]{1,0:T(8,128)(2,1)} %bitcast.12, bf16[32,768]{1,0:T(8,128)(2,1)} %get-tuple-element.53.own_far, f32[64,768]{1,0:T(8,128)} %get-tuple-element.33.bias_far, bf16[8,192,384]{2,1,0:T(8,128)(2,1)} %copy-done, bf16[8,192,384]{2,1,0:T(8,128)(2,1)} %copy-done.3, ...), custom_call_target="tpu_custom_call" | custom-call | flops 4000000000 | bytes 4000000 | tf_op jit(solution)/shard_map/plain_back/pallas_call | solution.py:540
  125.2 6.7 %all-to-all-done.4.parts = bf16[8,2,48,384]{3,2,1,0:T(8,128)(2,1)S(1)} async-done(((bf16[8,2,48,384]{3,2,1,0:T(8,128)(2,1)}), bf16[8,2,48,384]{3,2,1,0:T(8,128)(2,1)S(1)}, u32[]{:S(2)}, u32[]{:S(2)}) %all-to-all-start.4) | async-done | bytes 589856 | tf_op jit(solution)/shard_map/all_to_all | solution.py:406
  132.0 9.2 %all_gather.3.parts = bf16[2,2,48,384]{3,2,1,0:T(8,128)(2,1)S(1)} all-gather(bf16[1,2,48,384]{3,2,1,0:T(8,128)(2,1)S(1)} %sum_copies.5), channel_id=1, replica_groups={{0,8},{16,24},{32,40},{48,56},{64,72},{80,88},{96,104},{112,120},{128,1..., dimensions={0}, use_global_device_ids=true | all-gather | bytes 221184 | tf_op jit(solution)/shard_map/all_gather | solution.py:563
  (21 shorter events, 0.9 us)
Async XLA Ops:
  2.8 18.6 %all-to-all-start = ((bf16[8,192,384]{2,1,0:T(8,128)(2,1)}), bf16[8,192,384]{2,1,0:T(8,128)(2,1)S(1)}, u32[]{:S(2)}, u32[]{:S(2)}) async-start(bf16[8,192,384]{2,1,0:T(8,128)(2,1)} %prepare.2), calls=%async_computation | async-start | bytes 2359296 | tf_op jit(solution)/shard_map/all_to_all | solution.py:406
  8.7 2.2 %copy-start.1 = (f32[12,225]{1,0:T(8,128)S(1)}, f32[12,225]{1,0:T(8,128)}, u32[]{:S(2)}) copy-start(f32[12,225]{1,0:T(8,128)} %table_p.1) | copy-start | bytes 32404
  8.7 2.2 %copy-start.2 = (f32[12,225]{1,0:T(8,128)S(1)}, f32[12,225]{1,0:T(8,128)}, u32[]{:S(2)}) copy-start(f32[12,225]{1,0:T(8,128)} %table_s.1) | copy-start | bytes 32404
  21.4 11.0 %copy-start = (bf16[8,192,384]{2,1,0:T(8,128)(2,1)}, bf16[8,192,384]{2,1,0:T(8,128)(2,1)S(1)}, u32[]{:S(2)}) copy-start(bf16[8,192,384]{2,1,0:T(8,128)(2,1)S(1)} %all-to-all-done.w_mine_ref.mine_far) | copy-start | bytes 3538948
  21.4 10.9 %collective-permute-start = (bf16[8,192,384]{2,1,0:T(8,128)(2,1)S(1)}, bf16[8,192,384]{2,1,0:T(8,128)(2,1)S(1)}, u32[]{:S(2)}, u32[]{:S(2)}) collective-permute-start(bf16[8,192,384]{2,1,0:T(8,128)(2,1)S(1)} %all-to-all-done.w_mine_ref.mine_far), channel_id=1, source_target_pairs={{0,8},{8,0},{16,24},{24,16},{32,40},{40,32},{48,56},{56,48},{64,72... | collective-permute-start | bytes 3538952 | tf_op jit(solution)/shard_map/ppermute | solution.py:420
  28.7 23.5 %all-to-all-start.1 = ((bf16[8,192,384]{2,1,0:T(8,128)(2,1)}), bf16[8,192,384]{2,1,0:T(8,128)(2,1)S(1)}, u32[]{:S(2)}, u32[]{:S(2)}) async-start(bf16[8,192,384]{2,1,0:T(8,128)(2,1)} %prepare.3), calls=%async_computation.1 | async-start | bytes 2359296 | tf_op jit(solution)/shard_map/all_to_all | solution.py:406
  32.3 4.6 %copy-start.3 = (bf16[8,192,384]{2,1,0:T(8,128)(2,1)}, bf16[8,192,384]{2,1,0:T(8,128)(2,1)S(1)}, u32[]{:S(2)}) copy-start(bf16[8,192,384]{2,1,0:T(8,128)(2,1)S(1)} %collective-permute-done.w_other_ref.other_far) | copy-start | bytes 3538948
  36.9 9.0 %collective-permute-start.1 = (bf16[64,1920]{1,0:T(8,128)(2,1)}, bf16[64,1920]{1,0:T(8,128)(2,1)S(1)}, u32[]{:S(2)}, u32[]{:S(2)}) collective-permute-start(bf16[64,1920]{1,0:T(8,128)(2,1)} %get-tuple-element.38), channel_id=1, source_target_pairs={{8,0},{9,1},{10,2},{11,3},{12,4},{13,5},{14,6},{15,7},{16,8},{17,9... | collective-permute-start | bytes 737288 | tf_op jit(solution)/shard_map/ppermute | solution.py:416
  52.2 17.5 %collective-permute-start.3 = (bf16[8,192,384]{2,1,0:T(8,128)(2,1)S(1)}, bf16[8,192,384]{2,1,0:T(8,128)(2,1)S(1)}, u32[]{:S(2)}, u32[]{:S(2)}) collective-permute-start(bf16[8,192,384]{2,1,0:T(8,128)(2,1)S(1)} %all-to-all-done.1.refs_5_), channel_id=1, source_target_pairs={{0,8},{8,0},{16,24},{24,16},{32,40},{40,32},{48,56},{56,48},{64,72... | collective-permute-start | bytes 3538952 | tf_op jit(solution)/shard_map/ppermute | solution.py:420
  60.2 9.5 %collective-permute-start.2 = (bf16[64,1920]{1,0:T(8,128)(2,1)S(1)}, bf16[64,1920]{1,0:T(8,128)(2,1)S(1)}, u32[]{:S(2)}, u32[]{:S(2)}) collective-permute-start(bf16[64,1920]{1,0:T(8,128)(2,1)S(1)} %pad_maximum_fusion), channel_id=1, source_target_pairs={{1,0},{2,1},{3,2},{4,3},{5,4},{6,5},{7,6},{0,7},{9,8},{10,9},{11,1... | collective-permute-start | bytes 737288 | tf_op jit(solution)/shard_map/ppermute | solution.py:416
  75.4 4.3 %collective-permute-start.4 = (bf16[8,2,48,384]{3,2,1,0:T(8,128)(2,1)S(1)}, bf16[8,2,48,384]{3,2,1,0:T(8,128)(2,1)S(1)}, u32[]{:S(2)}, u32[]{:S(2)}) collective-permute-start(bf16[8,2,48,384]{3,2,1,0:T(8,128)(2,1)S(1)} %get-tuple-element.43), channel_id=1, source_target_pairs={{0,8},{8,0},{16,24},{24,16},{32,40},{40,32},{48,56},{56,48},{64,72... | collective-permute-start | bytes 1769480 | tf_op jit(solution)/shard_map/ppermute | solution.py:420
  79.7 5.6 %copy-start.5 = (bf16[64,768]{1,0:T(8,128)(2,1)S(1)}, bf16[64,768]{1,0:T(8,128)(2,1)}, u32[]{:S(2)}) copy-start(bf16[64,768]{1,0:T(8,128)(2,1)} %get-tuple-element.47) | copy-start | bytes 294916
  80.7 18.8 %copy-start.4 = (bf16[32,768]{1,0:T(8,128)(2,1)S(1)}, bf16[32,768]{1,0:T(8,128)(2,1)}, u32[]{:S(2)}) copy-start(bf16[32,768]{1,0:T(8,128)(2,1)} %get-tuple-element.50) | copy-start | bytes 147460
  80.7 14.5 %all-to-all-start.2 = ((bf16[8,2,48,384]{3,2,1,0:T(8,128)(2,1)}), bf16[8,2,48,384]{3,2,1,0:T(8,128)(2,1)S(1)}, u32[]{:S(2)}, u32[]{:S(2)}) async-start(bf16[8,2,48,384]{3,2,1,0:T(8,128)(2,1)} %add_convert_fusion), calls=%async_computation.2 | async-start | bytes 1179648 | tf_op jit(solution)/shard_map/all_to_all | solution.py:406
  85.3 9.1 %collective-permute-start.5 = (bf16[64,768]{1,0:T(8,128)(2,1)S(1)}, bf16[64,768]{1,0:T(8,128)(2,1)S(1)}, u32[]{:S(2)}, u32[]{:S(2)}) collective-permute-start(bf16[64,768]{1,0:T(8,128)(2,1)S(1)} %copy-done.5), channel_id=1, source_target_pairs={{504,0},{505,1},{506,2},{507,3},{508,4},{509,5},{510,6},{511,7},{0... | collective-permute-start | bytes 294920 | tf_op jit(solution)/shard_map/ppermute | solution.py:416
  96.1 12.7 %all-to-all-start.3 = ((bf16[4,2,48,384]{3,2,1,0:T(8,128)(2,1)}), bf16[4,2,48,384]{3,2,1,0:T(8,128)(2,1)S(1)}, u32[]{:S(2)}, u32[]{:S(2)}) async-start(bf16[4,2,48,384]{3,2,1,0:T(8,128)(2,1)} %sum_copies.3), calls=%async_computation.3 | async-start | bytes 589824 | tf_op jit(solution)/shard_map/all_to_all | solution.py:406
  99.6 9.2 %collective-permute-start.6 = (bf16[64,768]{1,0:T(8,128)(2,1)S(1)}, bf16[64,768]{1,0:T(8,128)(2,1)S(1)}, u32[]{:S(2)}, u32[]{:S(2)}) collective-permute-start(bf16[64,768]{1,0:T(8,128)(2,1)S(1)} %pad_maximum_fusion.1), channel_id=1, source_target_pairs={{7,0},{0,1},{1,2},{2,3},{3,4},{4,5},{5,6},{6,7},{15,8},{8,9},{9,10... | collective-permute-start | bytes 294920 | tf_op jit(solution)/shard_map/ppermute | solution.py:416
  109.6 22.3 %all-to-all-start.4 = ((bf16[8,2,48,384]{3,2,1,0:T(8,128)(2,1)}), bf16[8,2,48,384]{3,2,1,0:T(8,128)(2,1)S(1)}, u32[]{:S(2)}, u32[]{:S(2)}) async-start(bf16[8,2,48,384]{3,2,1,0:T(8,128)(2,1)} %sum_copies.4), calls=%async_computation.4 | async-start | bytes 1179648 | tf_op jit(solution)/shard_map/all_to_all | solution.py:406

commit v12 on v9

--- a/solution.py
+++ b/solution.py
@@ -107,13 +107,6 @@
 def wait_all(moves):
     for move in moves:
         move.wait()
-
-
-def prepare(core_ref, qkv, proj, out, block, sems):
-    start = pl.multiple_of(core_ref[0] * HALF, 128)
-    block[0:SHARE] = qkv[:, pl.ds(start, HALF)]
-    block[SHARE : SHARE + ROWS] = proj[:, pl.ds(start, HALF)]
-    wait_all(copy_all([(block, out.at[i]) for i in range(8)], sems))
 
 
 def biases(edge_ref, table_p, table_s, to_p, to_s, out_p, out_s, tables, wide, sems):
@@ -440,18 +433,9 @@
     cot = cotangent.reshape(128, D)
 
     def share(qkv, proj):
-        return pl.pallas_call(
-            prepare,
-            out_shape=pltpu.HBM((8, SHARE + ROWS, HALF), BF16),
-            in_specs=[SMEM, VMEM, VMEM],
-            out_specs=HBM,
-            scratch_shapes=[
-                pltpu.VMEM((SHARE + ROWS, HALF), BF16),
-                pltpu.SemaphoreType.DMA((8,)),
-            ],
-            compiler_params=params(60),
-            name="prepare",
-        )(core, qkv.T, proj)
+        rows = jnp.concatenate([qkv.T, proj], axis=0)
+        half = lax.dynamic_slice_in_dim(rows, core[0] * HALF, HALF, axis=1)
+        return jnp.broadcast_to(half[None], (8, SHARE + ROWS, HALF))
 
     first_mine = swap(share(qkv_plain, proj_plain), "freq")
     second_share = share(qkv_shift, proj_shift)

time: 138 us -> 139 us (level)
  Pallas kernels: 24.5 us -> 20.3 us
  local copies, waits for them, and re-layouts: 0.03 us -> 2.4 us
  waiting for transfers between devices: 39.6 us -> 41.6 us
    pallas_call x2 -> x0, Pallas kernels: 4.23 us -> none  [share(): pl.pallas_call(prepare, out_shape=pltpu.HBM((8, SHARE + ROWS, HALF), BF16...]
    broadcast_in_dim x0 -> x2, local copies, waits for them, and re-layouts: none -> 2.36 us  [share(): return jnp.broadcast_to(half[None], (8, SHARE + ROWS, HALF))]
    all_to_all x5, waiting for transfers between devices: 18.9 us -> 21 us  [swap(): return lax.all_to_all(value, axis, 0, 0, axis_index_groups=groups)]
  transfers between devices with their start and end apart: 13 -> 13, of which waited for: 8 -> 8; matrix products, arithmetic and copies ran while one was open for 0% -> 0% of each run, Pallas kernels for 10% -> 9%
where the time goes in v12:
time: 139 us
  starting transfers between devices  64.8 us (47%)
  waiting for transfers between devices  41.6 us (30%)
  Pallas kernels  20.3 us (15%)
  blocking collectives  6.49 us (5%)
  local copies, waits for them, and re-layouts  2.4 us (2%)
  other arithmetic  2 us (1%)
    ppermute x5, starting transfers between devices, from_offset(): return lax.ppermute(value, ('tm', 'freq'), pairs)  25.5 us
    all_to_all x5, starting transfers between devices, swap(): return lax.all_to_all(value, axis, 0, 0, axis_index_groups=groups)  24.3 us
    all_to_all x5, waiting for transfers between devices, swap(): return lax.all_to_all(value, axis, 0, 0, axis_index_groups=groups)  21 us
    ppermute x5, waiting for transfers between devices, from_offset(): return lax.ppermute(value, ('tm', 'freq'), pairs)  16.6 us
    ppermute x3, starting transfers between devices, other_core(): lax.ppermute(value, 'tm', [(i, i ^ 1) for i in range(lax.axis_size('tm'))])  15 us
    all_gather x1, blocking collectives, shards(): part = lax.all_gather(part, 'tm', axis_index_groups=tm_groups('core'))  6.49 us
    pallas_call x1, Pallas kernels, shards(): pl.pallas_call(lambda *refs: main_kernel(grad_scale, *refs), out_shape=(p...  5.73 us
    pallas_call x1, Pallas kernels, shards(): pl.pallas_call(plain_back, out_shape=jax.ShapeDtypeStruct((128, D), BF16)...  5.55 us
  transfers between devices with their start and end apart: 13, of which 8 were waited for; matrix products, arithmetic and copies ran while one was open for 0% of the time, Pallas kernels for 9%

profile of v12, /device:TPU:1, one launch (start us, length us, event | category | flops | bytes accessed | tf_op | source)
XLA Modules:
  0.0 138.5 jit_solution(15816448710476478934)
XLA Ops:
  0.6 0.9 fusion.1
  1.6 1.1 broadcast_in_dim.4
  2.7 6.0 %all-to-all-start = ((bf16[8,192,384]{2,1,0:T(8,128)(2,1)}), bf16[8,192,384]{2,1,0:T(8,128)(2,1)S(1)}, u32[]{:S(2)}, u32[]{:S(2)}) async-start(bf16[8,192,384]{2,1,0:T(8,128)(2,1)} %broadcast_in_dim.4), calls=%async_computation | async-start | bytes 2359296 | tf_op jit(solution)/shard_map/all_to_all | solution.py:396
  8.8 2.0 %biases.1 = (f32[64,768]{1,0:T(8,128)}, f32[64,768]{1,0:T(8,128)}) custom-call(s32[2]{0:T(128)S(1)} %add_convert_fusion.1.edge_ref, f32[12,225]{1,0:T(8,128)S(1)} %copy-done.1, f32[12,225]{1,0:T(8,128)S(1)} %copy-done.2), custom_call_target="tpu_custom_call" | custom-call | tf_op jit(solution)/shard_map/biases/pallas_call | solution.py:443
  10.8 10.6 %all-to-all-done.w_mine_ref.mine_far = bf16[8,192,384]{2,1,0:T(8,128)(2,1)S(1)} async-done(((bf16[8,192,384]{2,1,0:T(8,128)(2,1)}), bf16[8,192,384]{2,1,0:T(8,128)(2,1)S(1)}, u32[]{:S(2)}, u32[]{:S(2)}) %all-to-all-start) | async-done | bytes 1179680 | tf_op jit(solution)/shard_map/all_to_all | solution.py:396
  21.4 1.2 broadcast_in_dim.5
  22.7 7.3 %collective-permute-start = (bf16[8,192,384]{2,1,0:T(8,128)(2,1)S(1)}, bf16[8,192,384]{2,1,0:T(8,128)(2,1)S(1)}, u32[]{:S(2)}, u32[]{:S(2)}) collective-permute-start(bf16[8,192,384]{2,1,0:T(8,128)(2,1)S(1)} %all-to-all-done.w_mine_ref.mine_far), channel_id=1, source_target_pairs={{0,8},{8,0},{16,24},{24,16},{32,40},{40,32},{48,56},{56,48},{64,72... | collective-permute-start | bytes 3538952 | tf_op jit(solution)/shard_map/ppermute | solution.py:410
  30.0 3.6 %all-to-all-start.1 = ((bf16[8,192,384]{2,1,0:T(8,128)(2,1)}), bf16[8,192,384]{2,1,0:T(8,128)(2,1)S(1)}, u32[]{:S(2)}, u32[]{:S(2)}) async-start(bf16[8,192,384]{2,1,0:T(8,128)(2,1)} %broadcast_in_dim.5), calls=%async_computation.1 | async-start | bytes 2359296 | tf_op jit(solution)/shard_map/all_to_all | solution.py:396
  33.6 4.6 %plain_forward.1 = (bf16[32,1920]{1,0:T(8,128)(2,1)}, bf16[32,1920]{1,0:T(8,128)(2,1)}, bf16[32,1920]{1,0:T(8,128)(2,1)}, bf16[32,1920]{1,0:T(8,128)(2,1)}) custom-call(s32[1]{0:T(128)} %bitcast.core_ref.refs_0_, bf16[128,768]{1,0:T(8,128)(2,1)} %bitcast.11, bf16[128,768]{1,0:T(8,128)(2,1)} %bitcast.10, f32[64,768]{1,0:T(8,128)} %get-tuple-element.36.bias_far, ...), custom_call_target="tpu_custom_call" | custom-call | flops 20000000000 | bytes 1000000 | tf_op jit(solution)/shard_map/plain_forward/pallas_call | solution.py:465
  38.2 1.9 %collective-permute-start.1 = (bf16[32,1920]{1,0:T(8,128)(2,1)}, bf16[32,1920]{1,0:T(8,128)(2,1)S(1)}, u32[]{:S(2)}, u32[]{:S(2)}) collective-permute-start(bf16[32,1920]{1,0:T(8,128)(2,1)} %get-tuple-element.41), channel_id=1, source_target_pairs={{8,0},{9,1},{10,2},{11,3},{12,4},{13,5},{14,6},{15,7},{16,8},{17,9... | collective-permute-start | bytes 368648 | tf_op jit(solution)/shard_map/ppermute | solution.py:406
  40.1 5.7 %collective-permute-start.2 = (bf16[32,1920]{1,0:T(8,128)(2,1)}, bf16[32,1920]{1,0:T(8,128)(2,1)S(1)}, u32[]{:S(2)}, u32[]{:S(2)}) collective-permute-start(bf16[32,1920]{1,0:T(8,128)(2,1)} %get-tuple-element.42), channel_id=1, source_target_pairs={{1,0},{2,1},{3,2},{4,3},{5,4},{6,5},{7,6},{0,7},{9,8},{10,9},{11,1... | collective-permute-start | bytes 368648 | tf_op jit(solution)/shard_map/ppermute | solution.py:406
  45.8 14.0 %collective-permute-start.3 = (bf16[32,1920]{1,0:T(8,128)(2,1)}, bf16[32,1920]{1,0:T(8,128)(2,1)S(1)}, u32[]{:S(2)}, u32[]{:S(2)}) collective-permute-start(bf16[32,1920]{1,0:T(8,128)(2,1)} %get-tuple-element.43), channel_id=1, source_target_pairs={{9,0},{10,1},{11,2},{12,3},{13,4},{14,5},{15,6},{8,7},{17,8},{18,9... | collective-permute-start | bytes 368648 | tf_op jit(solution)/shard_map/ppermute | solution.py:406
  59.8 2.1 %collective-permute-done.3.refs_5_ = bf16[32,1920]{1,0:T(8,128)(2,1)S(1)} collective-permute-done((bf16[32,1920]{1,0:T(8,128)(2,1)}, bf16[32,1920]{1,0:T(8,128)(2,1)S(1)}, u32[]{:S(2)}, u32[]{:S(2)}) %collective-permute-start.3) | collective-permute-done | bytes 122912 | tf_op jit(solution)/shard_map/ppermute | solution.py:406
  62.0 5.4 %collective-permute-start.4 = (bf16[8,192,384]{2,1,0:T(8,128)(2,1)S(1)}, bf16[8,192,384]{2,1,0:T(8,128)(2,1)S(1)}, u32[]{:S(2)}, u32[]{:S(2)}) collective-permute-start(bf16[8,192,384]{2,1,0:T(8,128)(2,1)S(1)} %all-to-all-done.1.refs_6_), channel_id=1, source_target_pairs={{0,8},{8,0},{16,24},{24,16},{32,40},{40,32},{48,56},{56,48},{64,72... | collective-permute-start | bytes 3538952 | tf_op jit(solution)/shard_map/ppermute | solution.py:410
  67.3 2.5 %collective-permute-done.4.refs_7_ = bf16[8,192,384]{2,1,0:T(8,128)(2,1)S(1)} collective-permute-done((bf16[8,192,384]{2,1,0:T(8,128)(2,1)S(1)}, bf16[8,192,384]{2,1,0:T(8,128)(2,1)S(1)}, u32[]{:S(2)}, u32[]{:S(2)}) %collective-permute-start.4) | collective-permute-done | bytes 1179680 | tf_op jit(solution)/shard_map/ppermute | solution.py:410
  69.8 5.7 %main.1 = (bf16[32,768]{1,0:T(8,128)(2,1)}, bf16[64,768]{1,0:T(8,128)(2,1)}, bf16[32,768]{1,0:T(8,128)(2,1)}, bf16[8,2,48,384]{3,2,1,0:T(8,128)(2,1)S(1)}, bf16[8,2,48,384]{3,2,1,0:T(8,128)(2,1)S(1)}) custom-call(s32[1]{0:T(128)} %bitcast.core_ref.refs_0_, bf16[32,1920]{1,0:T(8,128)(2,1)} %get-tuple-element.38.refs_1_, f32[64,768]{1,0:T(8,128)} %get-tuple-element.39.refs_2_, ...), custom_call_target="tpu_custom_call" | custom-call | flops 1000000 | bytes 1000000 | tf_op jit(solution)/shard_map/main/pallas_call | solution.py:494
  75.5 2.3 %collective-permute-start.5 = (bf16[8,2,48,384]{3,2,1,0:T(8,128)(2,1)S(1)}, bf16[8,2,48,384]{3,2,1,0:T(8,128)(2,1)S(1)}, u32[]{:S(2)}, u32[]{:S(2)}) collective-permute-start(bf16[8,2,48,384]{3,2,1,0:T(8,128)(2,1)S(1)} %get-tuple-element.49), channel_id=1, source_target_pairs={{0,8},{8,0},{16,24},{24,16},{32,40},{40,32},{48,56},{56,48},{64,72... | collective-permute-start | bytes 1769480 | tf_op jit(solution)/shard_map/ppermute | solution.py:410
  77.8 1.6 %collective-permute-done.5 = bf16[8,2,48,384]{3,2,1,0:T(8,128)(2,1)S(1)} collective-permute-done((bf16[8,2,48,384]{3,2,1,0:T(8,128)(2,1)S(1)}, bf16[8,2,48,384]{3,2,1,0:T(8,128)(2,1)S(1)}, u32[]{:S(2)}, u32[]{:S(2)}) %collective-permute-start.5) | collective-permute-done | bytes 589856 | tf_op jit(solution)/shard_map/ppermute | solution.py:410
  79.4 1.0 add_convert_fusion
  80.4 3.7 %all-to-all-start.2 = ((bf16[8,2,48,384]{3,2,1,0:T(8,128)(2,1)}), bf16[8,2,48,384]{3,2,1,0:T(8,128)(2,1)S(1)}, u32[]{:S(2)}, u32[]{:S(2)}) async-start(bf16[8,2,48,384]{3,2,1,0:T(8,128)(2,1)} %add_convert_fusion), calls=%async_computation.2 | async-start | bytes 1179648 | tf_op jit(solution)/shard_map/all_to_all | solution.py:396
  84.1 1.9 %collective-permute-start.6 = (bf16[64,768]{1,0:T(8,128)(2,1)S(1)}, bf16[64,768]{1,0:T(8,128)(2,1)S(1)}, u32[]{:S(2)}, u32[]{:S(2)}) collective-permute-start(bf16[64,768]{1,0:T(8,128)(2,1)S(1)} %copy-done.7), channel_id=1, source_target_pairs={{504,0},{505,1},{506,2},{507,3},{508,4},{509,5},{510,6},{511,7},{0... | collective-permute-start | bytes 294920 | tf_op jit(solution)/shard_map/ppermute | solution.py:406
  86.0 7.2 %collective-permute-done.6.column = bf16[64,768]{1,0:T(8,128)(2,1)S(1)} collective-permute-done((bf16[64,768]{1,0:T(8,128)(2,1)S(1)}, bf16[64,768]{1,0:T(8,128)(2,1)S(1)}, u32[]{:S(2)}, u32[]{:S(2)}) %collective-permute-start.6) | collective-permute-done | bytes 98336 | tf_op jit(solution)/shard_map/ppermute | solution.py:406
  93.2 1.0 all-to-all-done.2.parts
  94.2 0.8 sum_copies.3
  95.0 3.5 %all-to-all-start.3 = ((bf16[4,2,48,384]{3,2,1,0:T(8,128)(2,1)}), bf16[4,2,48,384]{3,2,1,0:T(8,128)(2,1)S(1)}, u32[]{:S(2)}, u32[]{:S(2)}) async-start(bf16[4,2,48,384]{3,2,1,0:T(8,128)(2,1)} %sum_copies.3), calls=%async_computation.3 | async-start | bytes 589824 | tf_op jit(solution)/shard_map/all_to_all | solution.py:396
  98.5 2.0 %collective-permute-start.7 = (bf16[64,768]{1,0:T(8,128)(2,1)S(1)}, bf16[64,768]{1,0:T(8,128)(2,1)S(1)}, u32[]{:S(2)}, u32[]{:S(2)}) collective-permute-start(bf16[64,768]{1,0:T(8,128)(2,1)S(1)} %pad_maximum_fusion), channel_id=1, source_target_pairs={{7,0},{0,1},{1,2},{2,3},{3,4},{4,5},{5,6},{6,7},{15,8},{8,9},{9,10... | collective-permute-start | bytes 294920 | tf_op jit(solution)/shard_map/ppermute | solution.py:406
  100.6 7.2 %collective-permute-done.7.row = bf16[64,768]{1,0:T(8,128)(2,1)S(1)} collective-permute-done((bf16[64,768]{1,0:T(8,128)(2,1)S(1)}, bf16[64,768]{1,0:T(8,128)(2,1)S(1)}, u32[]{:S(2)}, u32[]{:S(2)}) %collective-permute-start.7) | collective-permute-done | bytes 98336 | tf_op jit(solution)/shard_map/ppermute | solution.py:406
  107.8 0.9 sum_copies.4
  108.7 7.6 %all-to-all-start.4 = ((bf16[8,2,48,384]{3,2,1,0:T(8,128)(2,1)}), bf16[8,2,48,384]{3,2,1,0:T(8,128)(2,1)S(1)}, u32[]{:S(2)}, u32[]{:S(2)}) async-start(bf16[8,2,48,384]{3,2,1,0:T(8,128)(2,1)} %sum_copies.4), calls=%async_computation.4 | async-start | bytes 1179648 | tf_op jit(solution)/shard_map/all_to_all | solution.py:396
  116.3 5.5 %plain_back.1 = bf16[128,768]{1,0:T(8,128)(2,1)} custom-call(s32[1]{0:T(128)} %bitcast.core_ref.refs_0_, bf16[128,768]{1,0:T(8,128)(2,1)} %bitcast.12, bf16[32,768]{1,0:T(8,128)(2,1)} %get-tuple-element.59.own_far, f32[64,768]{1,0:T(8,128)} %get-tuple-element.36.bias_far, bf16[8,192,384]{2,1,0:T(8,128)(2,1)} %copy-done, bf16[8,192,384]{2,1,0:T(8,128)(2,1)} %copy-done.3, ...), custom_call_target="tpu_custom_call" | custom-call | flops 4000000000 | bytes 4000000 | tf_op jit(solution)/shard_map/plain_back/pallas_call | solution.py:523
  121.8 9.4 %all-to-all-done.4.parts = bf16[8,2,48,384]{3,2,1,0:T(8,128)(2,1)S(1)} async-done(((bf16[8,2,48,384]{3,2,1,0:T(8,128)(2,1)}), bf16[8,2,48,384]{3,2,1,0:T(8,128)(2,1)S(1)}, u32[]{:S(2)}, u32[]{:S(2)}) %all-to-all-start.4) | async-done | bytes 589856 | tf_op jit(solution)/shard_map/all_to_all | solution.py:396
  131.3 6.5 %all_gather.3.parts = bf16[2,2,48,384]{3,2,1,0:T(8,128)(2,1)S(1)} all-gather(bf16[1,2,48,384]{3,2,1,0:T(8,128)(2,1)S(1)} %sum_copies.5), channel_id=1, replica_groups={{0,8},{16,24},{32,40},{48,56},{64,72},{80,88},{96,104},{112,120},{128,1..., dimensions={0}, use_global_device_ids=true | all-gather | bytes 221184 | tf_op jit(solution)/shard_map/all_gather | solution.py:546
  (27 shorter events, 1.0 us)
Async XLA Ops:
  2.7 6.1 %copy-start.1 = (f32[12,225]{1,0:T(8,128)S(1)}, f32[12,225]{1,0:T(8,128)}, u32[]{:S(2)}) copy-start(f32[12,225]{1,0:T(8,128)} %table_p.1) | copy-start | bytes 32404
  2.7 6.1 %copy-start.2 = (f32[12,225]{1,0:T(8,128)S(1)}, f32[12,225]{1,0:T(8,128)}, u32[]{:S(2)}) copy-start(f32[12,225]{1,0:T(8,128)} %table_s.1) | copy-start | bytes 32404
  2.7 8.1 %copy-start.4 = (bf16[768,144]{0,1:T(8,128)(2,1)S(1)}, bf16[768,144]{0,1:T(8,128)(2,1)}, u32[]{:S(2)}) copy-start(bf16[768,144]{0,1:T(8,128)(2,1)} %param.11) | copy-start | bytes 663556
  2.7 8.1 %copy-start.5 = (bf16[48,768]{1,0:T(8,128)(2,1)S(1)}, bf16[48,768]{1,0:T(8,128)(2,1)}, u32[]{:S(2)}) copy-start(bf16[48,768]{1,0:T(8,128)(2,1)} %param.13) | copy-start | bytes 221188
  2.7 18.7 %all-to-all-start = ((bf16[8,192,384]{2,1,0:T(8,128)(2,1)}), bf16[8,192,384]{2,1,0:T(8,128)(2,1)S(1)}, u32[]{:S(2)}, u32[]{:S(2)}) async-start(bf16[8,192,384]{2,1,0:T(8,128)(2,1)} %broadcast_in_dim.4), calls=%async_computation | async-start | bytes 2359296 | tf_op jit(solution)/shard_map/all_to_all | solution.py:396
  21.4 12.2 %copy-start = (bf16[8,192,384]{2,1,0:T(8,128)(2,1)}, bf16[8,192,384]{2,1,0:T(8,128)(2,1)S(1)}, u32[]{:S(2)}) copy-start(bf16[8,192,384]{2,1,0:T(8,128)(2,1)S(1)} %all-to-all-done.w_mine_ref.mine_far) | copy-start | bytes 3538948
  22.7 10.9 %collective-permute-start = (bf16[8,192,384]{2,1,0:T(8,128)(2,1)S(1)}, bf16[8,192,384]{2,1,0:T(8,128)(2,1)S(1)}, u32[]{:S(2)}, u32[]{:S(2)}) collective-permute-start(bf16[8,192,384]{2,1,0:T(8,128)(2,1)S(1)} %all-to-all-done.w_mine_ref.mine_far), channel_id=1, source_target_pairs={{0,8},{8,0},{16,24},{24,16},{32,40},{40,32},{48,56},{56,48},{64,72... | collective-permute-start | bytes 3538952 | tf_op jit(solution)/shard_map/ppermute | solution.py:410
  30.0 31.9 %all-to-all-start.1 = ((bf16[8,192,384]{2,1,0:T(8,128)(2,1)}), bf16[8,192,384]{2,1,0:T(8,128)(2,1)S(1)}, u32[]{:S(2)}, u32[]{:S(2)}) async-start(bf16[8,192,384]{2,1,0:T(8,128)(2,1)} %broadcast_in_dim.5), calls=%async_computation.1 | async-start | bytes 2359296 | tf_op jit(solution)/shard_map/all_to_all | solution.py:396
  33.6 4.6 %copy-start.3 = (bf16[8,192,384]{2,1,0:T(8,128)(2,1)}, bf16[8,192,384]{2,1,0:T(8,128)(2,1)S(1)}, u32[]{:S(2)}) copy-start(bf16[8,192,384]{2,1,0:T(8,128)(2,1)S(1)} %collective-permute-done.w_other_ref.other_far) | copy-start | bytes 3538948
  38.2 21.6 %collective-permute-start.1 = (bf16[32,1920]{1,0:T(8,128)(2,1)}, bf16[32,1920]{1,0:T(8,128)(2,1)S(1)}, u32[]{:S(2)}, u32[]{:S(2)}) collective-permute-start(bf16[32,1920]{1,0:T(8,128)(2,1)} %get-tuple-element.41), channel_id=1, source_target_pairs={{8,0},{9,1},{10,2},{11,3},{12,4},{13,5},{14,6},{15,7},{16,8},{17,9... | collective-permute-start | bytes 368648 | tf_op jit(solution)/shard_map/ppermute | solution.py:406
  40.1 19.7 %collective-permute-start.2 = (bf16[32,1920]{1,0:T(8,128)(2,1)}, bf16[32,1920]{1,0:T(8,128)(2,1)S(1)}, u32[]{:S(2)}, u32[]{:S(2)}) collective-permute-start(bf16[32,1920]{1,0:T(8,128)(2,1)} %get-tuple-element.42), channel_id=1, source_target_pairs={{1,0},{2,1},{3,2},{4,3},{5,4},{6,5},{7,6},{0,7},{9,8},{10,9},{11,1... | collective-permute-start | bytes 368648 | tf_op jit(solution)/shard_map/ppermute | solution.py:406
  45.8 16.1 %collective-permute-start.3 = (bf16[32,1920]{1,0:T(8,128)(2,1)}, bf16[32,1920]{1,0:T(8,128)(2,1)S(1)}, u32[]{:S(2)}, u32[]{:S(2)}) collective-permute-start(bf16[32,1920]{1,0:T(8,128)(2,1)} %get-tuple-element.43), channel_id=1, source_target_pairs={{9,0},{10,1},{11,2},{12,3},{13,4},{14,5},{15,6},{8,7},{17,8},{18,9... | collective-permute-start | bytes 368648 | tf_op jit(solution)/shard_map/ppermute | solution.py:406
  62.0 7.8 %collective-permute-start.4 = (bf16[8,192,384]{2,1,0:T(8,128)(2,1)S(1)}, bf16[8,192,384]{2,1,0:T(8,128)(2,1)S(1)}, u32[]{:S(2)}, u32[]{:S(2)}) collective-permute-start(bf16[8,192,384]{2,1,0:T(8,128)(2,1)S(1)} %all-to-all-done.1.refs_6_), channel_id=1, source_target_pairs={{0,8},{8,0},{16,24},{24,16},{32,40},{40,32},{48,56},{56,48},{64,72... | collective-permute-start | bytes 3538952 | tf_op jit(solution)/shard_map/ppermute | solution.py:410
  75.5 3.9 %collective-permute-start.5 = (bf16[8,2,48,384]{3,2,1,0:T(8,128)(2,1)S(1)}, bf16[8,2,48,384]{3,2,1,0:T(8,128)(2,1)S(1)}, u32[]{:S(2)}, u32[]{:S(2)}) collective-permute-start(bf16[8,2,48,384]{3,2,1,0:T(8,128)(2,1)S(1)} %get-tuple-element.49), channel_id=1, source_target_pairs={{0,8},{8,0},{16,24},{24,16},{32,40},{40,32},{48,56},{56,48},{64,72... | collective-permute-start | bytes 1769480 | tf_op jit(solution)/shard_map/ppermute | solution.py:410
  79.4 4.7 %copy-start.7 = (bf16[64,768]{1,0:T(8,128)(2,1)S(1)}, bf16[64,768]{1,0:T(8,128)(2,1)}, u32[]{:S(2)}) copy-start(bf16[64,768]{1,0:T(8,128)(2,1)} %get-tuple-element.53) | copy-start | bytes 294916
  80.4 18.1 %copy-start.6 = (bf16[32,768]{1,0:T(8,128)(2,1)S(1)}, bf16[32,768]{1,0:T(8,128)(2,1)}, u32[]{:S(2)}) copy-start(bf16[32,768]{1,0:T(8,128)(2,1)} %get-tuple-element.56) | copy-start | bytes 147460
  80.4 13.9 %all-to-all-start.2 = ((bf16[8,2,48,384]{3,2,1,0:T(8,128)(2,1)}), bf16[8,2,48,384]{3,2,1,0:T(8,128)(2,1)S(1)}, u32[]{:S(2)}, u32[]{:S(2)}) async-start(bf16[8,2,48,384]{3,2,1,0:T(8,128)(2,1)} %add_convert_fusion), calls=%async_computation.2 | async-start | bytes 1179648 | tf_op jit(solution)/shard_map/all_to_all | solution.py:396
  84.1 9.1 %collective-permute-start.6 = (bf16[64,768]{1,0:T(8,128)(2,1)S(1)}, bf16[64,768]{1,0:T(8,128)(2,1)S(1)}, u32[]{:S(2)}, u32[]{:S(2)}) collective-permute-start(bf16[64,768]{1,0:T(8,128)(2,1)S(1)} %copy-done.7), channel_id=1, source_target_pairs={{504,0},{505,1},{506,2},{507,3},{508,4},{509,5},{510,6},{511,7},{0... | collective-permute-start | bytes 294920 | tf_op jit(solution)/shard_map/ppermute | solution.py:406
  95.0 12.8 %all-to-all-start.3 = ((bf16[4,2,48,384]{3,2,1,0:T(8,128)(2,1)}), bf16[4,2,48,384]{3,2,1,0:T(8,128)(2,1)S(1)}, u32[]{:S(2)}, u32[]{:S(2)}) async-start(bf16[4,2,48,384]{3,2,1,0:T(8,128)(2,1)} %sum_copies.3), calls=%async_computation.3 | async-start | bytes 589824 | tf_op jit(solution)/shard_map/all_to_all | solution.py:396
  98.5 9.3 %collective-permute-start.7 = (bf16[64,768]{1,0:T(8,128)(2,1)S(1)}, bf16[64,768]{1,0:T(8,128)(2,1)S(1)}, u32[]{:S(2)}, u32[]{:S(2)}) collective-permute-start(bf16[64,768]{1,0:T(8,128)(2,1)S(1)} %pad_maximum_fusion), channel_id=1, source_target_pairs={{7,0},{0,1},{1,2},{2,3},{3,4},{4,5},{5,6},{6,7},{15,8},{8,9},{9,10... | collective-permute-start | bytes 294920 | tf_op jit(solution)/shard_map/ppermute | solution.py:406
  108.7 22.5 %all-to-all-start.4 = ((bf16[8,2,48,384]{3,2,1,0:T(8,128)(2,1)}), bf16[8,2,48,384]{3,2,1,0:T(8,128)(2,1)S(1)}, u32[]{:S(2)}, u32[]{:S(2)}) async-start(bf16[8,2,48,384]{3,2,1,0:T(8,128)(2,1)} %sum_copies.4), calls=%async_computation.4 | async-start | bytes 1179648 | tf_op jit(solution)/shard_map/all_to_all | solution.py:396

commit v13 on v9

--- a/solution.py
+++ b/solution.py
@@ -116,7 +116,32 @@
     wait_all(copy_all([(block, out.at[i]) for i in range(8)], sems))
 
 
-def biases(edge_ref, table_p, table_s, to_p, to_s, out_p, out_s, tables, wide, sems):
+def biases(
+    edge_ref,
+    table_p,
+    table_s,
+    cot,
+    to_p,
+    to_s,
+    to_diag,
+    to_above,
+    to_left,
+    to_own,
+    out_p,
+    out_s,
+    tables,
+    wide,
+    quads,
+    sems,
+):
+    quads[...] = dot(quadrant_pick(), cot[...]).astype(BF16)
+    stores = copy_all(
+        [
+            (quads.at[i * 32 : (i + 1) * 32], out)
+            for i, out in enumerate((to_diag, to_above, to_left, to_own))
+        ],
+        sems,
+    )
     tables[...] = jnp.zeros_like(tables)
     tables[0:HEADS, 0:REL] = table_p[...]
     tables[HEADS : 2 * HEADS, 0:REL] = table_s[...]
@@ -144,7 +169,7 @@
     cross = at ^ key_at
     barred = (cross & 32) * edge_ref[0] + (cross & 4) * edge_ref[1]
     out_s[...] = jnp.where(barred != 0, NEG, out_s[...])
-    wait_all(copy_all([(out_p, to_p), (out_s, to_s)], sems))
+    wait_all(stores + copy_all([(out_p, to_p), (out_s, to_s)], sems, 4))
 
 
 def project(rows_ref, w_mine, w_other, mine, other):
@@ -181,7 +206,6 @@
 def plain_forward(
     core_ref,
     tok_far,
-    cot_far,
     bias_far,
     w_mine_ref,
     w_other_ref,
@@ -190,7 +214,6 @@
     out_b,
     out_d,
     tok,
-    cot,
     bias_p,
     packets,
     rows,
@@ -199,7 +222,7 @@
     sems,
 ):
     mine, other = sides(core_ref)
-    loads = copy_all([(tok_far, tok), (bias_far, bias_p), (cot_far, cot)], sems)
+    loads = copy_all([(tok_far, tok), (bias_far, bias_p)], sems)
     mask[...] = head_mask()
     loads[0].wait()
     inputs = tok[...].astype(F32)
@@ -218,11 +241,10 @@
     sums[:, pl.ds(other, HALF)] = dot(mixed, proj_of(w_other_ref))
     block_out = (inputs + sums[...]).astype(BF16)
     pick = quadrant_pick()
-    loads[2].wait()
-    for whole, first in ((block_out, 0), (mixed, D), (cot[...], D + WIDE)):
+    for whole, first in ((block_out, 0), (mixed, D)):
         packets[:, first : first + whole.shape[1]] = dot(pick, whole).astype(BF16)
     outs = (out_d, out_b, out_r, out_o)
-    wait_all(copy_all([(packets.at[i * 32 : (i + 1) * 32], out) for i, out in enumerate(outs)], sems, 3))
+    wait_all(copy_all([(packets.at[i * 32 : (i + 1) * 32], out) for i, out in enumerate(outs)], sems, 2))
 
 
 def main_kernel(
@@ -230,6 +252,10 @@
     core_ref,
     own_far,
     bias_far,
+    cot_own,
+    cot_right,
+    cot_below,
+    cot_diag,
     right,
     below,
     diag,
@@ -243,6 +269,7 @@
     bias_s,
     quads,
     staged,
+    staged_cot,
     rows_small,
     grads,
     sums,
@@ -251,15 +278,18 @@
 ):
     mine, other = sides(core_ref)
     loads = copy_all([(own_far, staged.at[0:32]), (bias_far, bias_s)], sems)
+    cots = (cot_own, cot_right, cot_below, cot_diag)
+    loads += copy_all([(c, staged_cot.at[i * 32 : (i + 1) * 32]) for i, c in enumerate(cots)], sems, 2)
     mask[...] = head_mask()
     for i, part in ((1, right), (2, below), (3, diag)):
         staged[i * 32 : (i + 1) * 32] = part[...]
-    wait_all(loads)
+    loads[0].wait()
     pick = quadrant_pick(True)
-    grads[...] = dot(pick, staged[:, D + WIDE :]).astype(BF16)
     block_out = dot(pick, staged[:, 0:D])
     mixed_plain = dot(pick, staged[:, D : D + WIDE]).astype(BF16)
     normed, rstd = normalize(block_out)
+    wait_all(loads[1:])
+    grads[...] = dot(pick, staged_cot[...]).astype(BF16)
     rows_small[...] = normed.astype(BF16)
     w_mine, w_other = qkv_of(w_mine_ref), qkv_of(w_other_ref)
     packed = project(rows_small, w_mine, w_other, mine, other).astype(BF16)
@@ -289,7 +319,7 @@
             (quads.at[64:96], to_below),
         ],
         sems,
-        2,
+        6,
     )
     rows_small[...] = grad
     for out, start in ((out_send, other), (out_keep, mine)):
@@ -456,47 +486,51 @@
     first_mine = swap(share(qkv_plain, proj_plain), "freq")
     second_share = share(qkv_shift, proj_shift)
     table = pltpu.HBM((SPOTS, LANES), F32)
-    bias_p, bias_s = pl.pallas_call(
+    piece = pltpu.HBM((32, D), BF16)
+    bias_p, bias_s, cot_diag, cot_above, cot_left, cot_own = pl.pallas_call(
         biases,
-        out_shape=(table, table),
-        in_specs=[SMEM, VMEM, VMEM],
-        out_specs=[HBM] * 2,
+        out_shape=(table, table) + (piece,) * 4,
+        in_specs=[SMEM] + [VMEM] * 3,
+        out_specs=[HBM] * 6,
         scratch_shapes=[
             pltpu.VMEM((SPOTS, LANES), F32),
             pltpu.VMEM((SPOTS, LANES), F32),
             pltpu.VMEM((32, 256), F32),
             pltpu.VMEM((2 * HEADS * WIN, 128), F32),
-            pltpu.SemaphoreType.DMA((2,)),
+            pltpu.VMEM((128, D), BF16),
+            pltpu.SemaphoreType.DMA((6,)),
         ],
         compiler_params=params(),
         name="biases",
-    )(edge, table_plain, table_shift)
-
-    first_mine, second_share, bias_p, bias_s = lax.optimization_barrier(
-        (first_mine, second_share, bias_p, bias_s)
+    )(edge, table_plain, table_shift, cot)
+    cot_right = from_offset(cot_left, 1, 0)
+    cot_below = from_offset(cot_above, 0, 1)
+    cot_diag = from_offset(cot_diag, 1, 1)
+
+    first_mine, second_share, bias_p, bias_s, cot_right, cot_below, cot_diag = lax.optimization_barrier(
+        (first_mine, second_share, bias_p, bias_s, cot_right, cot_below, cot_diag)
     )
     second_mine = swap(second_share, "freq")
     first_other = other_core(first_mine)
-    packet = pltpu.HBM((32, 2 * D + WIDE), BF16)
+    packet = pltpu.HBM((32, D + WIDE), BF16)
     own, to_left, to_above, to_diag = pl.pallas_call(
         plain_forward,
         out_shape=(packet,) * 4,
-        in_specs=[SMEM] + [HBM] * 3 + [VMEM] * 2,
+        in_specs=[SMEM] + [HBM] * 2 + [VMEM] * 2,
         out_specs=[HBM] * 4,
         scratch_shapes=[
             pltpu.VMEM((128, D), BF16),
-            pltpu.VMEM((128, D), BF16),
             pltpu.VMEM((SPOTS, LANES), F32),
-            pltpu.VMEM((128, 2 * D + WIDE), BF16),
+            pltpu.VMEM((128, D + WIDE), BF16),
             pltpu.VMEM((128, D), BF16),
             pltpu.VMEM((128, D), F32),
             pltpu.VMEM((LANES, WIDE), BF16),
-            pltpu.SemaphoreType.DMA((7,)),
+            pltpu.SemaphoreType.DMA((6,)),
         ],
         compiler_params=params(),
         cost_estimate=cost(20_000_000_000, 1_000_000),
         name="plain_forward",
-    )(core, far(tok), far(cot), far(bias_p), first_mine, first_other)
+    )(core, far(tok), far(bias_p), first_mine, first_other)
     right = from_offset(to_left, 1, 0)
     below = from_offset(to_above, 0, 1)
     diag = from_offset(to_diag, 1, 1)
@@ -504,28 +538,31 @@
         (second_mine, right, below, diag)
     )
     second_other = other_core(second_mine)
-    piece = pltpu.HBM((32, D), BF16)
     column = pltpu.HBM((64, D), BF16)
     local = jax.ShapeDtypeStruct((8, 2, ROWS, HALF), BF16)
     g_own, to_right, to_below, keep, send = pl.pallas_call(
         lambda *refs: main_kernel(grad_scale, *refs),
         out_shape=(piece, column, piece, local, local),
-        in_specs=[SMEM] + [HBM] * 2 + [VMEM] * 5,
+        in_specs=[SMEM] + [HBM] * 6 + [VMEM] * 5,
         out_specs=[HBM] * 3 + [VMEM] * 2,
         scratch_shapes=[
             pltpu.VMEM((SPOTS, LANES), F32),
             pltpu.VMEM((128, D), BF16),
-            pltpu.VMEM((128, 2 * D + WIDE), BF16),
+            pltpu.VMEM((128, D + WIDE), BF16),
+            pltpu.VMEM((128, D), BF16),
             pltpu.VMEM((128, D), BF16),
             pltpu.VMEM((128, D), BF16),
             pltpu.VMEM((128, D), F32),
             pltpu.VMEM((LANES, WIDE), BF16),
-            pltpu.SemaphoreType.DMA((6,)),
+            pltpu.SemaphoreType.DMA((10,)),
         ],
         compiler_params=params(),
         cost_estimate=cost(1_000_000, 1_000_000),
         name="main",
-    )(core, far(own), far(bias_s), right, below, diag, second_mine, second_other)
+    )(
+        core, far(own), far(bias_s), far(cot_own), far(cot_right), far(cot_below), far(cot_diag),
+        right, below, diag, second_mine, second_other,
+    )
 
     part = (keep.astype(F32) + other_core(send).astype(F32)).astype(BF16)
     part, to_right, to_below = lax.optimization_barrier((part, to_right, to_below))

time: 138 us -> 139 us (level)
  starting transfers between devices: 64.7 us -> 73.6 us
  waiting for transfers between devices: 39.6 us -> 31.9 us
    ppermute x5 -> x8, starting transfers between devices: 25.5 us -> 41.4 us  [from_offset(): return lax.ppermute(value, ('tm', 'freq'), pairs)]
    all_to_all x5, waiting for transfers between devices: 18.9 us -> 11.7 us  [swap(): return lax.all_to_all(value, axis, 0, 0, axis_index_groups=groups)]
    ppermute x3, starting transfers between devices: 15 us -> 8.85 us  [other_core(): lax.ppermute(value, 'tm', [(i, i ^ 1) for i in range(lax.axis_size('tm'))])]
    ppermute x5 -> x8, waiting for transfers between devices: 16.6 us -> 16.2 us  [from_offset(): return lax.ppermute(value, ('tm', 'freq'), pairs)]
  transfers between devices with their start and end apart: 13 -> 16, of which waited for: 8 -> 7; matrix products, arithmetic and copies ran while one was open for 0% -> 0% of each run, Pallas kernels for 10% -> 10%
where the time goes in v13:
time: 139 us
  starting transfers between devices  73.6 us (53%)
  waiting for transfers between devices  31.9 us (23%)
  Pallas kernels  24.7 us (18%)
  blocking collectives  5.16 us (4%)
    ppermute x8, starting transfers between devices, from_offset(): return lax.ppermute(value, ('tm', 'freq'), pairs)  41.4 us
    all_to_all x5, starting transfers between devices, swap(): return lax.all_to_all(value, axis, 0, 0, axis_index_groups=groups)  23.3 us
    ppermute x8, waiting for transfers between devices, from_offset(): return lax.ppermute(value, ('tm', 'freq'), pairs)  16.2 us
    all_to_all x5, waiting for transfers between devices, swap(): return lax.all_to_all(value, axis, 0, 0, axis_index_groups=groups)  11.7 us
    ppermute x3, starting transfers between devices, other_core(): lax.ppermute(value, 'tm', [(i, i ^ 1) for i in range(lax.axis_size('tm'))])  8.85 us
    pallas_call x1, Pallas kernels, shards(): pl.pallas_call(lambda *refs: main_kernel(grad_scale, *refs), out_shape=(p...  5.97 us
    pallas_call x1, Pallas kernels, shards(): pl.pallas_call(plain_back, out_shape=jax.ShapeDtypeStruct((128, D), BF16)...  5.55 us
    all_gather x1, blocking collectives, shards(): part = lax.all_gather(part, 'tm', axis_index_groups=tm_groups('core'))  5.16 us
  transfers between devices with their start and end apart: 16, of which 7 were waited for; matrix products, arithmetic and copies ran while one was open for 0% of the time, Pallas kernels for 10%

profile of v13, /device:TPU:1, one launch (start us, length us, event | category | flops | bytes accessed | tf_op | source)
XLA Modules:
  0.0 138.5 jit_solution(16679488498705200415)
XLA Ops:
  0.6 2.1 %prepare.2 = bf16[8,192,384]{2,1,0:T(8,128)(2,1)} custom-call(s32[1]{0:T(128)} %bitcast.core_ref.refs_0_, bf16[144,768]{1,0:T(8,128)(2,1)} %bitcast.9, bf16[48,768]{1,0:T(8,128)(2,1)} %proj.2), custom_call_target="tpu_custom_call" | custom-call | tf_op jit(solution)/shard_map/prepare/pallas_call | solution.py:473
  2.8 6.0 %all-to-all-start = ((bf16[8,192,384]{2,1,0:T(8,128)(2,1)}), bf16[8,192,384]{2,1,0:T(8,128)(2,1)S(1)}, u32[]{:S(2)}, u32[]{:S(2)}) async-start(bf16[8,192,384]{2,1,0:T(8,128)(2,1)} %prepare.2), calls=%async_computation | async-start | bytes 2359296 | tf_op jit(solution)/shard_map/all_to_all | solution.py:433
  8.9 2.1 %biases.1 = (f32[64,768]{1,0:T(8,128)}, f32[64,768]{1,0:T(8,128)}, bf16[32,768]{1,0:T(8,128)(2,1)}, bf16[32,768]{1,0:T(8,128)(2,1)}, bf16[32,768]{1,0:T(8,128)(2,1)}, /*index=5*/bf16[32,768]{1,0:T(8,128)(2,1)}) custom-call(s32[2]{0:T(128)S(1)} %add_convert_fusion.1.edge_ref, f32[12,225]{1,0:T(8,128)S(1)} %copy-done.2, f32[12,225]{1,0:T(8,128)S(1)} %copy-done.3, ...), custom_call_target="tpu_custom_call" | custom-call | tf_op jit(solution)/shard_map/biases/pallas_call | solution.py:490
  11.0 6.5 %collective-permute-start = (bf16[32,768]{1,0:T(8,128)(2,1)}, bf16[32,768]{1,0:T(8,128)(2,1)S(1)}, u32[]{:S(2)}, u32[]{:S(2)}) collective-permute-start(bf16[32,768]{1,0:T(8,128)(2,1)} %get-tuple-element.43), channel_id=1, source_target_pairs={{8,0},{9,1},{10,2},{11,3},{12,4},{13,5},{14,6},{15,7},{16,8},{17,9... | collective-permute-start | bytes 147464 | tf_op jit(solution)/shard_map/ppermute | solution.py:443
  17.5 5.7 %collective-permute-start.1 = (bf16[32,768]{1,0:T(8,128)(2,1)}, bf16[32,768]{1,0:T(8,128)(2,1)S(1)}, u32[]{:S(2)}, u32[]{:S(2)}) collective-permute-start(bf16[32,768]{1,0:T(8,128)(2,1)} %get-tuple-element.44), channel_id=1, source_target_pairs={{1,0},{2,1},{3,2},{4,3},{5,4},{6,5},{7,6},{0,7},{9,8},{10,9},{11,1... | collective-permute-start | bytes 147464 | tf_op jit(solution)/shard_map/ppermute | solution.py:443
  23.2 9.5 %collective-permute-start.2 = (bf16[32,768]{1,0:T(8,128)(2,1)}, bf16[32,768]{1,0:T(8,128)(2,1)}, u32[]{:S(2)}, u32[]{:S(2)}) collective-permute-start(bf16[32,768]{1,0:T(8,128)(2,1)} %get-tuple-element.45), channel_id=1, source_target_pairs={{9,0},{10,1},{11,2},{12,3},{13,4},{14,5},{15,6},{8,7},{17,8},{18,9... | collective-permute-start | bytes 147464 | tf_op jit(solution)/shard_map/ppermute | solution.py:443
  32.7 2.1 %prepare.3 = bf16[8,192,384]{2,1,0:T(8,128)(2,1)} custom-call(s32[1]{0:T(128)} %bitcast.core_ref.refs_0_, bf16[144,768]{1,0:T(8,128)(2,1)} %bitcast.10, bf16[48,768]{1,0:T(8,128)(2,1)} %proj.3), custom_call_target="tpu_custom_call" | custom-call | tf_op jit(solution)/shard_map/prepare/pallas_call | solution.py:473
  36.0 2.2 %collective-permute-start.3 = (bf16[8,192,384]{2,1,0:T(8,128)(2,1)S(1)}, bf16[8,192,384]{2,1,0:T(8,128)(2,1)S(1)}, u32[]{:S(2)}, u32[]{:S(2)}) collective-permute-start(bf16[8,192,384]{2,1,0:T(8,128)(2,1)S(1)} %all-to-all-done.w_mine_ref.mine_far), channel_id=1, source_target_pairs={{0,8},{8,0},{16,24},{24,16},{32,40},{40,32},{48,56},{56,48},{64,72... | collective-permute-start | bytes 3538952 | tf_op jit(solution)/shard_map/ppermute | solution.py:447
  38.2 3.7 %all-to-all-start.1 = ((bf16[8,192,384]{2,1,0:T(8,128)(2,1)}), bf16[8,192,384]{2,1,0:T(8,128)(2,1)S(1)}, u32[]{:S(2)}, u32[]{:S(2)}) async-start(bf16[8,192,384]{2,1,0:T(8,128)(2,1)} %prepare.3), calls=%async_computation.1 | async-start | bytes 2359296 | tf_op jit(solution)/shard_map/all_to_all | solution.py:433
  41.9 4.4 %plain_forward.1 = (bf16[32,1152]{1,0:T(8,128)(2,1)}, bf16[32,1152]{1,0:T(8,128)(2,1)}, bf16[32,1152]{1,0:T(8,128)(2,1)}, bf16[32,1152]{1,0:T(8,128)(2,1)}) custom-call(s32[1]{0:T(128)} %bitcast.core_ref.refs_0_, bf16[128,768]{1,0:T(8,128)(2,1)} %bitcast.11, f32[64,768]{1,0:T(8,128)} %get-tuple-element.46.bias_far, ...), custom_call_target="tpu_custom_call" | custom-call | flops 20000000000 | bytes 1000000 | tf_op jit(solution)/shard_map/plain_forward/pallas_call | solution.py:516
  46.3 2.2 %collective-permute-start.4 = (bf16[32,1152]{1,0:T(8,128)(2,1)}, bf16[32,1152]{1,0:T(8,128)(2,1)S(1)}, u32[]{:S(2)}, u32[]{:S(2)}) collective-permute-start(bf16[32,1152]{1,0:T(8,128)(2,1)} %get-tuple-element.55), channel_id=1, source_target_pairs={{8,0},{9,1},{10,2},{11,3},{12,4},{13,5},{14,6},{15,7},{16,8},{17,9... | collective-permute-start | bytes 221192 | tf_op jit(solution)/shard_map/ppermute | solution.py:443
  48.5 5.8 %collective-permute-start.5 = (bf16[32,1152]{1,0:T(8,128)(2,1)}, bf16[32,1152]{1,0:T(8,128)(2,1)S(1)}, u32[]{:S(2)}, u32[]{:S(2)}) collective-permute-start(bf16[32,1152]{1,0:T(8,128)(2,1)} %get-tuple-element.56), channel_id=1, source_target_pairs={{1,0},{2,1},{3,2},{4,3},{5,4},{6,5},{7,6},{0,7},{9,8},{10,9},{11,1... | collective-permute-start | bytes 221192 | tf_op jit(solution)/shard_map/ppermute | solution.py:443
  54.3 7.7 %collective-permute-start.6 = (bf16[32,1152]{1,0:T(8,128)(2,1)}, bf16[32,1152]{1,0:T(8,128)(2,1)S(1)}, u32[]{:S(2)}, u32[]{:S(2)}) collective-permute-start(bf16[32,1152]{1,0:T(8,128)(2,1)} %get-tuple-element.57), channel_id=1, source_target_pairs={{9,0},{10,1},{11,2},{12,3},{13,4},{14,5},{15,6},{8,7},{17,8},{18,9... | collective-permute-start | bytes 221192 | tf_op jit(solution)/shard_map/ppermute | solution.py:443
  62.0 1.7 %collective-permute-done.6.refs_9_ = bf16[32,1152]{1,0:T(8,128)(2,1)S(1)} collective-permute-done((bf16[32,1152]{1,0:T(8,128)(2,1)}, bf16[32,1152]{1,0:T(8,128)(2,1)S(1)}, u32[]{:S(2)}, u32[]{:S(2)}) %collective-permute-start.6) | collective-permute-done | bytes 73760 | tf_op jit(solution)/shard_map/ppermute | solution.py:443
  63.7 4.4 %collective-permute-start.7 = (bf16[8,192,384]{2,1,0:T(8,128)(2,1)S(1)}, bf16[8,192,384]{2,1,0:T(8,128)(2,1)S(1)}, u32[]{:S(2)}, u32[]{:S(2)}) collective-permute-start(bf16[8,192,384]{2,1,0:T(8,128)(2,1)S(1)} %all-to-all-done.1.refs_10_), channel_id=1, source_target_pairs={{0,8},{8,0},{16,24},{24,16},{32,40},{40,32},{48,56},{56,48},{64,72... | collective-permute-start | bytes 3538952 | tf_op jit(solution)/shard_map/ppermute | solution.py:447
  68.1 2.5 %collective-permute-done.7.refs_11_ = bf16[8,192,384]{2,1,0:T(8,128)(2,1)S(1)} collective-permute-done((bf16[8,192,384]{2,1,0:T(8,128)(2,1)S(1)}, bf16[8,192,384]{2,1,0:T(8,128)(2,1)S(1)}, u32[]{:S(2)}, u32[]{:S(2)}) %collective-permute-start.7) | collective-permute-done | bytes 1179680 | tf_op jit(solution)/shard_map/ppermute | solution.py:447
  70.6 6.0 %main.1 = (bf16[32,768]{1,0:T(8,128)(2,1)}, bf16[64,768]{1,0:T(8,128)(2,1)}, bf16[32,768]{1,0:T(8,128)(2,1)}, bf16[8,2,48,384]{3,2,1,0:T(8,128)(2,1)S(1)}, bf16[8,2,48,384]{3,2,1,0:T(8,128)(2,1)S(1)}) custom-call(s32[1]{0:T(128)} %bitcast.core_ref.refs_0_, bf16[32,1152]{1,0:T(8,128)(2,1)} %get-tuple-element.48.refs_1_, f32[64,768]{1,0:T(8,128)} %get-tuple-element.49.refs_2_, ...), custom_call_target="tpu_custom_call" | custom-call | flops 1000000 | bytes 1000000 | tf_op jit(solution)/shard_map/main/pallas_call | solution.py:543
  76.6 2.3 %collective-permute-start.8 = (bf16[8,2,48,384]{3,2,1,0:T(8,128)(2,1)S(1)}, bf16[8,2,48,384]{3,2,1,0:T(8,128)(2,1)S(1)}, u32[]{:S(2)}, u32[]{:S(2)}) collective-permute-start(bf16[8,2,48,384]{3,2,1,0:T(8,128)(2,1)S(1)} %get-tuple-element.63), channel_id=1, source_target_pairs={{0,8},{8,0},{16,24},{24,16},{32,40},{40,32},{48,56},{56,48},{64,72... | collective-permute-start | bytes 1769480 | tf_op jit(solution)/shard_map/ppermute | solution.py:447
  78.8 1.6 %collective-permute-done.8 = bf16[8,2,48,384]{3,2,1,0:T(8,128)(2,1)S(1)} collective-permute-done((bf16[8,2,48,384]{3,2,1,0:T(8,128)(2,1)S(1)}, bf16[8,2,48,384]{3,2,1,0:T(8,128)(2,1)S(1)}, u32[]{:S(2)}, u32[]{:S(2)}) %collective-permute-start.8) | collective-permute-done | bytes 589856 | tf_op jit(solution)/shard_map/ppermute | solution.py:447
  80.5 1.0 add_convert_fusion
  81.4 3.7 %all-to-all-start.2 = ((bf16[8,2,48,384]{3,2,1,0:T(8,128)(2,1)}), bf16[8,2,48,384]{3,2,1,0:T(8,128)(2,1)S(1)}, u32[]{:S(2)}, u32[]{:S(2)}) async-start(bf16[8,2,48,384]{3,2,1,0:T(8,128)(2,1)} %add_convert_fusion), calls=%async_computation.2 | async-start | bytes 1179648 | tf_op jit(solution)/shard_map/all_to_all | solution.py:433
  85.1 1.9 %collective-permute-start.9 = (bf16[64,768]{1,0:T(8,128)(2,1)S(1)}, bf16[64,768]{1,0:T(8,128)(2,1)S(1)}, u32[]{:S(2)}, u32[]{:S(2)}) collective-permute-start(bf16[64,768]{1,0:T(8,128)(2,1)S(1)} %copy-done.8), channel_id=1, source_target_pairs={{504,0},{505,1},{506,2},{507,3},{508,4},{509,5},{510,6},{511,7},{0... | collective-permute-start | bytes 294920 | tf_op jit(solution)/shard_map/ppermute | solution.py:443
  87.0 7.2 %collective-permute-done.9.column = bf16[64,768]{1,0:T(8,128)(2,1)S(1)} collective-permute-done((bf16[64,768]{1,0:T(8,128)(2,1)S(1)}, bf16[64,768]{1,0:T(8,128)(2,1)S(1)}, u32[]{:S(2)}, u32[]{:S(2)}) %collective-permute-start.9) | collective-permute-done | bytes 98336 | tf_op jit(solution)/shard_map/ppermute | solution.py:443
  94.2 1.0 all-to-all-done.2.parts
  96.0 3.5 %all-to-all-start.3 = ((bf16[4,2,48,384]{3,2,1,0:T(8,128)(2,1)}), bf16[4,2,48,384]{3,2,1,0:T(8,128)(2,1)S(1)}, u32[]{:S(2)}, u32[]{:S(2)}) async-start(bf16[4,2,48,384]{3,2,1,0:T(8,128)(2,1)} %sum_copies.3), calls=%async_computation.3 | async-start | bytes 589824 | tf_op jit(solution)/shard_map/all_to_all | solution.py:433
  99.5 2.1 %collective-permute-start.10 = (bf16[64,768]{1,0:T(8,128)(2,1)S(1)}, bf16[64,768]{1,0:T(8,128)(2,1)S(1)}, u32[]{:S(2)}, u32[]{:S(2)}) collective-permute-start(bf16[64,768]{1,0:T(8,128)(2,1)S(1)} %pad_maximum_fusion), channel_id=1, source_target_pairs={{7,0},{0,1},{1,2},{2,3},{3,4},{4,5},{5,6},{6,7},{15,8},{8,9},{9,10... | collective-permute-start | bytes 294920 | tf_op jit(solution)/shard_map/ppermute | solution.py:443
  101.6 7.3 %collective-permute-done.10.row = bf16[64,768]{1,0:T(8,128)(2,1)S(1)} collective-permute-done((bf16[64,768]{1,0:T(8,128)(2,1)S(1)}, bf16[64,768]{1,0:T(8,128)(2,1)S(1)}, u32[]{:S(2)}, u32[]{:S(2)}) %collective-permute-start.10) | collective-permute-done | bytes 98336 | tf_op jit(solution)/shard_map/ppermute | solution.py:443
  108.9 0.9 sum_copies.4
  109.8 6.5 %all-to-all-start.4 = ((bf16[8,2,48,384]{3,2,1,0:T(8,128)(2,1)}), bf16[8,2,48,384]{3,2,1,0:T(8,128)(2,1)S(1)}, u32[]{:S(2)}, u32[]{:S(2)}) async-start(bf16[8,2,48,384]{3,2,1,0:T(8,128)(2,1)} %sum_copies.4), calls=%async_computation.4 | async-start | bytes 1179648 | tf_op jit(solution)/shard_map/all_to_all | solution.py:433
  116.3 5.5 %plain_back.1 = bf16[128,768]{1,0:T(8,128)(2,1)} custom-call(s32[1]{0:T(128)} %bitcast.core_ref.refs_0_, bf16[128,768]{1,0:T(8,128)(2,1)} %bitcast.12, bf16[32,768]{1,0:T(8,128)(2,1)} %get-tuple-element.73.own_far, f32[64,768]{1,0:T(8,128)} %get-tuple-element.46.bias_far, bf16[8,192,384]{2,1,0:T(8,128)(2,1)} %copy-done, bf16[8,192,384]{2,1,0:T(8,128)(2,1)} %copy-done.4, ...), custom_call_target="tpu_custom_call" | custom-call | flops 4000000000 | bytes 4000000 | tf_op jit(solution)/shard_map/plain_back/pallas_call | solution.py:576
  121.9 10.7 %all-to-all-done.4.parts = bf16[8,2,48,384]{3,2,1,0:T(8,128)(2,1)S(1)} async-done(((bf16[8,2,48,384]{3,2,1,0:T(8,128)(2,1)}), bf16[8,2,48,384]{3,2,1,0:T(8,128)(2,1)S(1)}, u32[]{:S(2)}, u32[]{:S(2)}) %all-to-all-start.4) | async-done | bytes 589856 | tf_op jit(solution)/shard_map/all_to_all | solution.py:433
  132.7 5.2 %all_gather.3.parts = bf16[2,2,48,384]{3,2,1,0:T(8,128)(2,1)S(1)} all-gather(bf16[1,2,48,384]{3,2,1,0:T(8,128)(2,1)S(1)} %sum_copies.5), channel_id=1, replica_groups={{0,8},{16,24},{32,40},{48,56},{64,72},{80,88},{96,104},{112,120},{128,1..., dimensions={0}, use_global_device_ids=true | all-gather | bytes 221184 | tf_op jit(solution)/shard_map/all_gather | solution.py:599
  (33 shorter events, 3.0 us)
Async XLA Ops:
  2.8 6.1 %copy-start.1 = (bf16[2,8,8,768]{3,2,1,0:T(8,128)(2,1)S(1)}, bf16[2,8,8,768]{3,2,1,0:T(8,128)(2,1)}, u32[]{:S(2)}) copy-start(bf16[2,8,8,768]{3,2,1,0:T(8,128)(2,1)} %param.9) | copy-start | bytes 589828
  2.8 6.1 %copy-start.2 = (f32[12,225]{1,0:T(8,128)S(1)}, f32[12,225]{1,0:T(8,128)}, u32[]{:S(2)}) copy-start(f32[12,225]{1,0:T(8,128)} %table_p.1) | copy-start | bytes 32404
  2.8 6.1 %copy-start.3 = (f32[12,225]{1,0:T(8,128)S(1)}, f32[12,225]{1,0:T(8,128)}, u32[]{:S(2)}) copy-start(f32[12,225]{1,0:T(8,128)} %table_s.1) | copy-start | bytes 32404
  2.8 33.2 %all-to-all-start = ((bf16[8,192,384]{2,1,0:T(8,128)(2,1)}), bf16[8,192,384]{2,1,0:T(8,128)(2,1)S(1)}, u32[]{:S(2)}, u32[]{:S(2)}) async-start(bf16[8,192,384]{2,1,0:T(8,128)(2,1)} %prepare.2), calls=%async_computation | async-start | bytes 2359296 | tf_op jit(solution)/shard_map/all_to_all | solution.py:433
  11.0 23.8 %collective-permute-start = (bf16[32,768]{1,0:T(8,128)(2,1)}, bf16[32,768]{1,0:T(8,128)(2,1)S(1)}, u32[]{:S(2)}, u32[]{:S(2)}) collective-permute-start(bf16[32,768]{1,0:T(8,128)(2,1)} %get-tuple-element.43), channel_id=1, source_target_pairs={{8,0},{9,1},{10,2},{11,3},{12,4},{13,5},{14,6},{15,7},{16,8},{17,9... | collective-permute-start | bytes 147464 | tf_op jit(solution)/shard_map/ppermute | solution.py:443
  17.5 17.3 %collective-permute-start.1 = (bf16[32,768]{1,0:T(8,128)(2,1)}, bf16[32,768]{1,0:T(8,128)(2,1)S(1)}, u32[]{:S(2)}, u32[]{:S(2)}) collective-permute-start(bf16[32,768]{1,0:T(8,128)(2,1)} %get-tuple-element.44), channel_id=1, source_target_pairs={{1,0},{2,1},{3,2},{4,3},{5,4},{6,5},{7,6},{0,7},{9,8},{10,9},{11,1... | collective-permute-start | bytes 147464 | tf_op jit(solution)/shard_map/ppermute | solution.py:443
  23.2 12.9 %collective-permute-start.2 = (bf16[32,768]{1,0:T(8,128)(2,1)}, bf16[32,768]{1,0:T(8,128)(2,1)}, u32[]{:S(2)}, u32[]{:S(2)}) collective-permute-start(bf16[32,768]{1,0:T(8,128)(2,1)} %get-tuple-element.45), channel_id=1, source_target_pairs={{9,0},{10,1},{11,2},{12,3},{13,4},{14,5},{15,6},{8,7},{17,8},{18,9... | collective-permute-start | bytes 147464 | tf_op jit(solution)/shard_map/ppermute | solution.py:443
  34.8 0.6 copy-start.6
  35.4 0.6 copy-start.7
  36.0 5.9 %copy-start = (bf16[8,192,384]{2,1,0:T(8,128)(2,1)}, bf16[8,192,384]{2,1,0:T(8,128)(2,1)S(1)}, u32[]{:S(2)}) copy-start(bf16[8,192,384]{2,1,0:T(8,128)(2,1)S(1)} %all-to-all-done.w_mine_ref.mine_far) | copy-start | bytes 3538948
  36.0 5.9 %collective-permute-start.3 = (bf16[8,192,384]{2,1,0:T(8,128)(2,1)S(1)}, bf16[8,192,384]{2,1,0:T(8,128)(2,1)S(1)}, u32[]{:S(2)}, u32[]{:S(2)}) collective-permute-start(bf16[8,192,384]{2,1,0:T(8,128)(2,1)S(1)} %all-to-all-done.w_mine_ref.mine_far), channel_id=1, source_target_pairs={{0,8},{8,0},{16,24},{24,16},{32,40},{40,32},{48,56},{56,48},{64,72... | collective-permute-start | bytes 3538952 | tf_op jit(solution)/shard_map/ppermute | solution.py:447
  38.2 25.5 %all-to-all-start.1 = ((bf16[8,192,384]{2,1,0:T(8,128)(2,1)}), bf16[8,192,384]{2,1,0:T(8,128)(2,1)S(1)}, u32[]{:S(2)}, u32[]{:S(2)}) async-start(bf16[8,192,384]{2,1,0:T(8,128)(2,1)} %prepare.3), calls=%async_computation.1 | async-start | bytes 2359296 | tf_op jit(solution)/shard_map/all_to_all | solution.py:433
  41.9 4.4 %copy-start.4 = (bf16[8,192,384]{2,1,0:T(8,128)(2,1)}, bf16[8,192,384]{2,1,0:T(8,128)(2,1)S(1)}, u32[]{:S(2)}) copy-start(bf16[8,192,384]{2,1,0:T(8,128)(2,1)S(1)} %collective-permute-done.3.w_other_ref.other_far) | copy-start | bytes 3538948
  46.3 15.7 %collective-permute-start.4 = (bf16[32,1152]{1,0:T(8,128)(2,1)}, bf16[32,1152]{1,0:T(8,128)(2,1)S(1)}, u32[]{:S(2)}, u32[]{:S(2)}) collective-permute-start(bf16[32,1152]{1,0:T(8,128)(2,1)} %get-tuple-element.55), channel_id=1, source_target_pairs={{8,0},{9,1},{10,2},{11,3},{12,4},{13,5},{14,6},{15,7},{16,8},{17,9... | collective-permute-start | bytes 221192 | tf_op jit(solution)/shard_map/ppermute | solution.py:443
  48.5 13.5 %collective-permute-start.5 = (bf16[32,1152]{1,0:T(8,128)(2,1)}, bf16[32,1152]{1,0:T(8,128)(2,1)S(1)}, u32[]{:S(2)}, u32[]{:S(2)}) collective-permute-start(bf16[32,1152]{1,0:T(8,128)(2,1)} %get-tuple-element.56), channel_id=1, source_target_pairs={{1,0},{2,1},{3,2},{4,3},{5,4},{6,5},{7,6},{0,7},{9,8},{10,9},{11,1... | collective-permute-start | bytes 221192 | tf_op jit(solution)/shard_map/ppermute | solution.py:443
  54.3 9.4 %collective-permute-start.6 = (bf16[32,1152]{1,0:T(8,128)(2,1)}, bf16[32,1152]{1,0:T(8,128)(2,1)S(1)}, u32[]{:S(2)}, u32[]{:S(2)}) collective-permute-start(bf16[32,1152]{1,0:T(8,128)(2,1)} %get-tuple-element.57), channel_id=1, source_target_pairs={{9,0},{10,1},{11,2},{12,3},{13,4},{14,5},{15,6},{8,7},{17,8},{18,9... | collective-permute-start | bytes 221192 | tf_op jit(solution)/shard_map/ppermute | solution.py:443
  63.7 6.9 %collective-permute-start.7 = (bf16[8,192,384]{2,1,0:T(8,128)(2,1)S(1)}, bf16[8,192,384]{2,1,0:T(8,128)(2,1)S(1)}, u32[]{:S(2)}, u32[]{:S(2)}) collective-permute-start(bf16[8,192,384]{2,1,0:T(8,128)(2,1)S(1)} %all-to-all-done.1.refs_10_), channel_id=1, source_target_pairs={{0,8},{8,0},{16,24},{24,16},{32,40},{40,32},{48,56},{56,48},{64,72... | collective-permute-start | bytes 3538952 | tf_op jit(solution)/shard_map/ppermute | solution.py:447
  76.6 3.9 %collective-permute-start.8 = (bf16[8,2,48,384]{3,2,1,0:T(8,128)(2,1)S(1)}, bf16[8,2,48,384]{3,2,1,0:T(8,128)(2,1)S(1)}, u32[]{:S(2)}, u32[]{:S(2)}) collective-permute-start(bf16[8,2,48,384]{3,2,1,0:T(8,128)(2,1)S(1)} %get-tuple-element.63), channel_id=1, source_target_pairs={{0,8},{8,0},{16,24},{24,16},{32,40},{40,32},{48,56},{56,48},{64,72... | collective-permute-start | bytes 1769480 | tf_op jit(solution)/shard_map/ppermute | solution.py:447
  80.5 4.6 %copy-start.8 = (bf16[64,768]{1,0:T(8,128)(2,1)S(1)}, bf16[64,768]{1,0:T(8,128)(2,1)}, u32[]{:S(2)}) copy-start(bf16[64,768]{1,0:T(8,128)(2,1)} %get-tuple-element.67) | copy-start | bytes 294916
  81.4 18.1 %copy-start.5 = (bf16[32,768]{1,0:T(8,128)(2,1)S(1)}, bf16[32,768]{1,0:T(8,128)(2,1)}, u32[]{:S(2)}) copy-start(bf16[32,768]{1,0:T(8,128)(2,1)} %get-tuple-element.70) | copy-start | bytes 147460
  81.4 13.8 %all-to-all-start.2 = ((bf16[8,2,48,384]{3,2,1,0:T(8,128)(2,1)}), bf16[8,2,48,384]{3,2,1,0:T(8,128)(2,1)S(1)}, u32[]{:S(2)}, u32[]{:S(2)}) async-start(bf16[8,2,48,384]{3,2,1,0:T(8,128)(2,1)} %add_convert_fusion), calls=%async_computation.2 | async-start | bytes 1179648 | tf_op jit(solution)/shard_map/all_to_all | solution.py:433
  85.1 9.1 %collective-permute-start.9 = (bf16[64,768]{1,0:T(8,128)(2,1)S(1)}, bf16[64,768]{1,0:T(8,128)(2,1)S(1)}, u32[]{:S(2)}, u32[]{:S(2)}) collective-permute-start(bf16[64,768]{1,0:T(8,128)(2,1)S(1)} %copy-done.8), channel_id=1, source_target_pairs={{504,0},{505,1},{506,2},{507,3},{508,4},{509,5},{510,6},{511,7},{0... | collective-permute-start | bytes 294920 | tf_op jit(solution)/shard_map/ppermute | solution.py:443
  96.0 12.9 %all-to-all-start.3 = ((bf16[4,2,48,384]{3,2,1,0:T(8,128)(2,1)}), bf16[4,2,48,384]{3,2,1,0:T(8,128)(2,1)S(1)}, u32[]{:S(2)}, u32[]{:S(2)}) async-start(bf16[4,2,48,384]{3,2,1,0:T(8,128)(2,1)} %sum_copies.3), calls=%async_computation.3 | async-start | bytes 589824 | tf_op jit(solution)/shard_map/all_to_all | solution.py:433
  99.5 9.4 %collective-permute-start.10 = (bf16[64,768]{1,0:T(8,128)(2,1)S(1)}, bf16[64,768]{1,0:T(8,128)(2,1)S(1)}, u32[]{:S(2)}, u32[]{:S(2)}) collective-permute-start(bf16[64,768]{1,0:T(8,128)(2,1)S(1)} %pad_maximum_fusion), channel_id=1, source_target_pairs={{7,0},{0,1},{1,2},{2,3},{3,4},{4,5},{5,6},{6,7},{15,8},{8,9},{9,10... | collective-permute-start | bytes 294920 | tf_op jit(solution)/shard_map/ppermute | solution.py:443
  109.8 22.8 %all-to-all-start.4 = ((bf16[8,2,48,384]{3,2,1,0:T(8,128)(2,1)}), bf16[8,2,48,384]{3,2,1,0:T(8,128)(2,1)S(1)}, u32[]{:S(2)}, u32[]{:S(2)}) async-start(bf16[8,2,48,384]{3,2,1,0:T(8,128)(2,1)} %sum_copies.4), calls=%async_computation.4 | async-start | bytes 1179648 | tf_op jit(solution)/shard_map/all_to_all | solution.py:433

commit v14 on v9

--- a/solution.py
+++ b/solution.py
@@ -236,8 +236,9 @@
     w_mine_ref,
     w_other_ref,
     to_own,
-    to_column,
+    to_right,
     to_below,
+    to_diag,
     out_keep,
     out_send,
     bias_s,
@@ -284,9 +285,9 @@
     stores = copy_all(
         [
             (quads.at[0:32], to_own),
-            (quads.at[32:64], to_column.at[0:32]),
-            (quads.at[96:128], to_column.at[32:64]),
+            (quads.at[32:64], to_right),
             (quads.at[64:96], to_below),
+            (quads.at[96:128], to_diag),
         ],
         sems,
         2,
@@ -319,8 +320,9 @@
     bias_far,
     mine_far,
     other_far,
-    column,
-    row,
+    g_left,
+    g_above,
+    g_diag,
     out,
     tok,
     bias_p,
@@ -345,9 +347,8 @@
         sems,
     )
     mask[...] = head_mask()
-    staged[0:32] = row[32:64]
-    staged[32:64] = row[0:32]
-    staged[64:96] = column[0:32]
+    for i, part in enumerate((g_diag, g_above, g_left)):
+        staged[i * 32 : (i + 1) * 32] = part[...]
     loads[0].wait()
     normed, rstd = normalize(tok[...].astype(F32))
     rows[...] = normed.astype(BF16)
@@ -505,13 +506,12 @@
     )
     second_other = other_core(second_mine)
     piece = pltpu.HBM((32, D), BF16)
-    column = pltpu.HBM((64, D), BF16)
     local = jax.ShapeDtypeStruct((8, 2, ROWS, HALF), BF16)
-    g_own, to_right, to_below, keep, send = pl.pallas_call(
+    g_own, to_right, to_below, to_diag, keep, send = pl.pallas_call(
         lambda *refs: main_kernel(grad_scale, *refs),
-        out_shape=(piece, column, piece, local, local),
+        out_shape=(piece,) * 4 + (local, local),
         in_specs=[SMEM] + [HBM] * 2 + [VMEM] * 5,
-        out_specs=[HBM] * 3 + [VMEM] * 2,
+        out_specs=[HBM] * 4 + [VMEM] * 2,
         scratch_shapes=[
             pltpu.VMEM((SPOTS, LANES), F32),
             pltpu.VMEM((128, D), BF16),
@@ -528,18 +528,20 @@
     )(core, far(own), far(bias_s), right, below, diag, second_mine, second_other)
 
     part = (keep.astype(F32) + other_core(send).astype(F32)).astype(BF16)
-    part, to_right, to_below = lax.optimization_barrier((part, to_right, to_below))
+    part, to_right, to_below, to_diag = lax.optimization_barrier(
+        (part, to_right, to_below, to_diag)
+    )
     part = swap(part, "freq")
-    column = from_offset(to_right, -1, 0)
-    part, column, to_below = lax.optimization_barrier((part, column, to_below))
+    left = from_offset(to_right, -1, 0)
+    above = from_offset(to_below, 0, -1)
+    corner = from_offset(to_diag, -1, -1)
+    part, left, above, corner = lax.optimization_barrier((part, left, above, corner))
     part = swap(summed(part, 4), "tm", tm_groups("y_hi"))
-    row = from_offset(jnp.concatenate([to_below, column[32:64]], axis=0), 0, -1)
-    part, row = lax.optimization_barrier((part, row))
     part = swap(summed(part, 8), "tm", tm_groups("z"))
     grad_tokens = pl.pallas_call(
         plain_back,
         out_shape=jax.ShapeDtypeStruct((128, D), BF16),
-        in_specs=[SMEM] + [HBM] * 5 + [VMEM] * 2,
+        in_specs=[SMEM] + [HBM] * 5 + [VMEM] * 3,
         out_specs=VMEM,
         scratch_shapes=[
             pltpu.VMEM((128, D), BF16),
@@ -556,7 +558,7 @@
         compiler_params=params(),
         cost_estimate=cost(4_000_000_000, 4_000_000),
         name="plain_back",
-    )(core, far(tok), far(g_own), far(bias_p), far(first_mine), far(first_other), column, row)
+    )(core, far(tok), far(g_own), far(bias_p), far(first_mine), far(first_other), left, above, corner)
     part, grad_tokens = lax.optimization_barrier((part, grad_tokens))
     part = summed(part, 1)[0]
     part = lax.all_gather(part, "tm", axis_index_groups=tm_groups("core"))

time: 138 us -> 141 us (1.022)
  blocking collectives: 6.49 us -> 14.8 us
  waiting for transfers between devices: 39.6 us -> 32.4 us
  starting transfers between devices: 64.7 us -> 67.3 us
    all_to_all x0 -> x1, blocking collectives: none -> 11.2 us  [swap(): return lax.all_to_all(value, axis, 0, 0, axis_index_groups=groups)]
    ppermute x5 -> x6, waiting for transfers between devices: 16.6 us -> 7.64 us  [from_offset(): return lax.ppermute(value, ('tm', 'freq'), pairs)]
    ppermute x5 -> x6, starting transfers between devices: 25.5 us -> 29 us  [from_offset(): return lax.ppermute(value, ('tm', 'freq'), pairs)]
    all_gather x1, blocking collectives: 6.49 us -> 3.65 us  [shards(): part = lax.all_gather(part, 'tm', axis_index_groups=tm_groups('core'))]
    all_to_all x5 -> x4, waiting for transfers between devices: 18.9 us -> 20.7 us  [swap(): return lax.all_to_all(value, axis, 0, 0, axis_index_groups=groups)]
    all_to_all x5 -> x4, starting transfers between devices: 24.1 us -> 23.2 us  [swap(): return lax.all_to_all(value, axis, 0, 0, axis_index_groups=groups)]
where the time goes in v14:
time: 141 us; the launch traced here: 140 us
  starting transfers between devices  67.3 us (48%)
  waiting for transfers between devices  32.4 us (23%)
  Pallas kernels  23.8 us (17%)
  blocking collectives  14.8 us (10%)
    ppermute x6, starting transfers between devices, from_offset(): return lax.ppermute(value, ('tm', 'freq'), pairs)  29 us
    all_to_all x4, starting transfers between devices, swap(): return lax.all_to_all(value, axis, 0, 0, axis_index_groups=groups)  23.2 us
    all_to_all x4, waiting for transfers between devices, swap(): return lax.all_to_all(value, axis, 0, 0, axis_index_groups=groups)  20.7 us
    ppermute x3, starting transfers between devices, other_core(): lax.ppermute(value, 'tm', [(i, i ^ 1) for i in range(lax.axis_size('tm'))])  15 us
    all_to_all x1, blocking collectives, swap(): return lax.all_to_all(value, axis, 0, 0, axis_index_groups=groups)  11.2 us
    ppermute x6, waiting for transfers between devices, from_offset(): return lax.ppermute(value, ('tm', 'freq'), pairs)  7.64 us
    pallas_call x1, Pallas kernels, shards(): pl.pallas_call(lambda *refs: main_kernel(grad_scale, *refs), out_shape=(p...  5.77 us
    pallas_call x1, Pallas kernels, shards(): pl.pallas_call(plain_back, out_shape=jax.ShapeDtypeStruct((128, D), BF16)...  5.55 us
  transfers between devices with their start and end apart: 13, of which 8 were waited for; matrix products, arithmetic and copies ran while one was open for 0% of the time, Pallas kernels for 10%

profile of v14, /device:TPU:1, one launch (start us, length us, event | category | flops | bytes accessed | tf_op | source)
XLA Modules:
  0.0 140.3 jit_solution(12630852024937433916)
XLA Ops:
  0.6 2.1 %prepare.2 = bf16[8,192,384]{2,1,0:T(8,128)(2,1)} custom-call(s32[1]{0:T(128)} %bitcast.core_ref.refs_0_, bf16[144,768]{1,0:T(8,128)(2,1)} %bitcast.8, bf16[48,768]{1,0:T(8,128)(2,1)} %proj.2), custom_call_target="tpu_custom_call" | custom-call | tf_op jit(solution)/shard_map/prepare/pallas_call | solution.py:444
  2.8 5.9 %all-to-all-start = ((bf16[8,192,384]{2,1,0:T(8,128)(2,1)}), bf16[8,192,384]{2,1,0:T(8,128)(2,1)S(1)}, u32[]{:S(2)}, u32[]{:S(2)}) async-start(bf16[8,192,384]{2,1,0:T(8,128)(2,1)} %prepare.2), calls=%async_computation | async-start | bytes 2359296 | tf_op jit(solution)/shard_map/all_to_all | solution.py:404
  8.7 2.1 %prepare.3 = bf16[8,192,384]{2,1,0:T(8,128)(2,1)} custom-call(s32[1]{0:T(128)} %bitcast.core_ref.refs_0_, bf16[144,768]{1,0:T(8,128)(2,1)} %bitcast.9, bf16[48,768]{1,0:T(8,128)(2,1)} %proj.3), custom_call_target="tpu_custom_call" | custom-call | tf_op jit(solution)/shard_map/prepare/pallas_call | solution.py:444
  10.9 2.0 %biases.1 = (f32[64,768]{1,0:T(8,128)}, f32[64,768]{1,0:T(8,128)}) custom-call(s32[2]{0:T(128)S(1)} %add_convert_fusion.1.edge_ref, f32[12,225]{1,0:T(8,128)S(1)} %copy-done.1, f32[12,225]{1,0:T(8,128)S(1)} %copy-done.2), custom_call_target="tpu_custom_call" | custom-call | tf_op jit(solution)/shard_map/biases/pallas_call | solution.py:460
  12.9 8.5 %all-to-all-done.w_mine_ref.mine_far = bf16[8,192,384]{2,1,0:T(8,128)(2,1)S(1)} async-done(((bf16[8,192,384]{2,1,0:T(8,128)(2,1)}), bf16[8,192,384]{2,1,0:T(8,128)(2,1)S(1)}, u32[]{:S(2)}, u32[]{:S(2)}) %all-to-all-start) | async-done | bytes 1179680 | tf_op jit(solution)/shard_map/all_to_all | solution.py:404
  21.4 7.3 %collective-permute-start = (bf16[8,192,384]{2,1,0:T(8,128)(2,1)S(1)}, bf16[8,192,384]{2,1,0:T(8,128)(2,1)S(1)}, u32[]{:S(2)}, u32[]{:S(2)}) collective-permute-start(bf16[8,192,384]{2,1,0:T(8,128)(2,1)S(1)} %all-to-all-done.w_mine_ref.mine_far), channel_id=1, source_target_pairs={{0,8},{8,0},{16,24},{24,16},{32,40},{40,32},{48,56},{56,48},{64,72... | collective-permute-start | bytes 3538952 | tf_op jit(solution)/shard_map/ppermute | solution.py:418
  28.7 3.6 %all-to-all-start.1 = ((bf16[8,192,384]{2,1,0:T(8,128)(2,1)}), bf16[8,192,384]{2,1,0:T(8,128)(2,1)S(1)}, u32[]{:S(2)}, u32[]{:S(2)}) async-start(bf16[8,192,384]{2,1,0:T(8,128)(2,1)} %prepare.3), calls=%async_computation.1 | async-start | bytes 2359296 | tf_op jit(solution)/shard_map/all_to_all | solution.py:404
  32.3 4.5 %plain_forward.1 = (bf16[32,1920]{1,0:T(8,128)(2,1)}, bf16[32,1920]{1,0:T(8,128)(2,1)}, bf16[32,1920]{1,0:T(8,128)(2,1)}, bf16[32,1920]{1,0:T(8,128)(2,1)}) custom-call(s32[1]{0:T(128)} %bitcast.core_ref.refs_0_, bf16[128,768]{1,0:T(8,128)(2,1)} %bitcast.11, bf16[128,768]{1,0:T(8,128)(2,1)} %bitcast.10, f32[64,768]{1,0:T(8,128)} %get-tuple-element.37.bias_far, ...), custom_call_target="tpu_custom_call" | custom-call | flops 20000000000 | bytes 1000000 | tf_op jit(solution)/shard_map/plain_forward/pallas_call | solution.py:482
  36.9 1.9 %collective-permute-start.1 = (bf16[32,1920]{1,0:T(8,128)(2,1)}, bf16[32,1920]{1,0:T(8,128)(2,1)S(1)}, u32[]{:S(2)}, u32[]{:S(2)}) collective-permute-start(bf16[32,1920]{1,0:T(8,128)(2,1)} %get-tuple-element.42), channel_id=1, source_target_pairs={{8,0},{9,1},{10,2},{11,3},{12,4},{13,5},{14,6},{15,7},{16,8},{17,9... | collective-permute-start | bytes 368648 | tf_op jit(solution)/shard_map/ppermute | solution.py:414
  38.8 5.7 %collective-permute-start.2 = (bf16[32,1920]{1,0:T(8,128)(2,1)}, bf16[32,1920]{1,0:T(8,128)(2,1)S(1)}, u32[]{:S(2)}, u32[]{:S(2)}) collective-permute-start(bf16[32,1920]{1,0:T(8,128)(2,1)} %get-tuple-element.43), channel_id=1, source_target_pairs={{1,0},{2,1},{3,2},{4,3},{5,4},{6,5},{7,6},{0,7},{9,8},{10,9},{11,1... | collective-permute-start | bytes 368648 | tf_op jit(solution)/shard_map/ppermute | solution.py:414
  44.5 14.0 %collective-permute-start.3 = (bf16[32,1920]{1,0:T(8,128)(2,1)}, bf16[32,1920]{1,0:T(8,128)(2,1)S(1)}, u32[]{:S(2)}, u32[]{:S(2)}) collective-permute-start(bf16[32,1920]{1,0:T(8,128)(2,1)} %get-tuple-element.44), channel_id=1, source_target_pairs={{9,0},{10,1},{11,2},{12,3},{13,4},{14,5},{15,6},{8,7},{17,8},{18,9... | collective-permute-start | bytes 368648 | tf_op jit(solution)/shard_map/ppermute | solution.py:414
  58.5 2.1 %collective-permute-done.3.refs_5_ = bf16[32,1920]{1,0:T(8,128)(2,1)S(1)} collective-permute-done((bf16[32,1920]{1,0:T(8,128)(2,1)}, bf16[32,1920]{1,0:T(8,128)(2,1)S(1)}, u32[]{:S(2)}, u32[]{:S(2)}) %collective-permute-start.3) | collective-permute-done | bytes 122912 | tf_op jit(solution)/shard_map/ppermute | solution.py:414
  60.6 5.4 %collective-permute-start.4 = (bf16[8,192,384]{2,1,0:T(8,128)(2,1)S(1)}, bf16[8,192,384]{2,1,0:T(8,128)(2,1)S(1)}, u32[]{:S(2)}, u32[]{:S(2)}) collective-permute-start(bf16[8,192,384]{2,1,0:T(8,128)(2,1)S(1)} %all-to-all-done.1.refs_6_), channel_id=1, source_target_pairs={{0,8},{8,0},{16,24},{24,16},{32,40},{40,32},{48,56},{56,48},{64,72... | collective-permute-start | bytes 3538952 | tf_op jit(solution)/shard_map/ppermute | solution.py:418
  66.0 2.5 %collective-permute-done.4.refs_7_ = bf16[8,192,384]{2,1,0:T(8,128)(2,1)S(1)} collective-permute-done((bf16[8,192,384]{2,1,0:T(8,128)(2,1)S(1)}, bf16[8,192,384]{2,1,0:T(8,128)(2,1)S(1)}, u32[]{:S(2)}, u32[]{:S(2)}) %collective-permute-start.4) | collective-permute-done | bytes 1179680 | tf_op jit(solution)/shard_map/ppermute | solution.py:418
  68.5 5.8 %main.1 = (bf16[32,768]{1,0:T(8,128)(2,1)}, bf16[32,768]{1,0:T(8,128)(2,1)}, bf16[32,768]{1,0:T(8,128)(2,1)}, bf16[32,768]{1,0:T(8,128)(2,1)}, bf16[8,2,48,384]{...) custom-call(s32[1]{0:T(128)} %bitcast.core_ref.refs_0_, bf16[32,1920]{1,0:T(8,128)(2,1)} %get-tuple-element.39.refs_1_, ...), custom_call_target="tpu_custom_call" | custom-call | flops 1000000 | bytes 1000000 | tf_op jit(solution)/shard_map/main/pallas_call | solution.py:510
  74.3 2.3 %collective-permute-start.5 = (bf16[8,2,48,384]{3,2,1,0:T(8,128)(2,1)S(1)}, bf16[8,2,48,384]{3,2,1,0:T(8,128)(2,1)S(1)}, u32[]{:S(2)}, u32[]{:S(2)}) collective-permute-start(bf16[8,2,48,384]{3,2,1,0:T(8,128)(2,1)S(1)} %get-tuple-element.50), channel_id=1, source_target_pairs={{0,8},{8,0},{16,24},{24,16},{32,40},{40,32},{48,56},{56,48},{64,72... | collective-permute-start | bytes 1769480 | tf_op jit(solution)/shard_map/ppermute | solution.py:418
  76.5 1.6 %collective-permute-done.5 = bf16[8,2,48,384]{3,2,1,0:T(8,128)(2,1)S(1)} collective-permute-done((bf16[8,2,48,384]{3,2,1,0:T(8,128)(2,1)S(1)}, bf16[8,2,48,384]{3,2,1,0:T(8,128)(2,1)S(1)}, u32[]{:S(2)}, u32[]{:S(2)}) %collective-permute-start.5) | collective-permute-done | bytes 589856 | tf_op jit(solution)/shard_map/ppermute | solution.py:418
  78.2 1.0 add_convert_fusion
  79.1 3.5 %all-to-all-start.2 = ((bf16[8,2,48,384]{3,2,1,0:T(8,128)(2,1)}), bf16[8,2,48,384]{3,2,1,0:T(8,128)(2,1)S(1)}, u32[]{:S(2)}, u32[]{:S(2)}) async-start(bf16[8,2,48,384]{3,2,1,0:T(8,128)(2,1)} %add_convert_fusion), calls=%async_computation.2 | async-start | bytes 1179648 | tf_op jit(solution)/shard_map/all_to_all | solution.py:404
  82.7 1.9 %collective-permute-start.6 = (bf16[32,768]{1,0:T(8,128)(2,1)S(1)}, bf16[32,768]{1,0:T(8,128)(2,1)S(1)}, u32[]{:S(2)}, u32[]{:S(2)}) collective-permute-start(bf16[32,768]{1,0:T(8,128)(2,1)S(1)} %copy-done.6), channel_id=1, source_target_pairs={{504,0},{505,1},{506,2},{507,3},{508,4},{509,5},{510,6},{511,7},{0... | collective-permute-start | bytes 147464 | tf_op jit(solution)/shard_map/ppermute | solution.py:414
  84.6 3.2 %collective-permute-start.7 = (bf16[32,768]{1,0:T(8,128)(2,1)S(1)}, bf16[32,768]{1,0:T(8,128)(2,1)S(1)}, u32[]{:S(2)}, u32[]{:S(2)}) collective-permute-start(bf16[32,768]{1,0:T(8,128)(2,1)S(1)} %copy-done.5), channel_id=1, source_target_pairs={{7,0},{0,1},{1,2},{2,3},{3,4},{4,5},{5,6},{6,7},{15,8},{8,9},{9,10... | collective-permute-start | bytes 147464 | tf_op jit(solution)/shard_map/ppermute | solution.py:414
  87.9 2.3 %collective-permute-start.8 = (bf16[32,768]{1,0:T(8,128)(2,1)S(1)}, bf16[32,768]{1,0:T(8,128)(2,1)S(1)}, u32[]{:S(2)}, u32[]{:S(2)}) collective-permute-start(bf16[32,768]{1,0:T(8,128)(2,1)S(1)} %copy-done.4), channel_id=1, source_target_pairs={{511,0},{504,1},{505,2},{506,3},{507,4},{508,5},{509,6},{510,7},{7... | collective-permute-start | bytes 147464 | tf_op jit(solution)/shard_map/ppermute | solution.py:414
  90.2 0.5 collective-permute-done.6.g_left
  90.8 3.5 %collective-permute-done.7.g_above = bf16[32,768]{1,0:T(8,128)(2,1)S(1)} collective-permute-done((bf16[32,768]{1,0:T(8,128)(2,1)S(1)}, bf16[32,768]{1,0:T(8,128)(2,1)S(1)}, u32[]{:S(2)}, u32[]{:S(2)}) %collective-permute-start.7) | collective-permute-done | bytes 49184 | tf_op jit(solution)/shard_map/ppermute | solution.py:414
  94.2 1.5 %collective-permute-done.8.g_diag = bf16[32,768]{1,0:T(8,128)(2,1)S(1)} collective-permute-done((bf16[32,768]{1,0:T(8,128)(2,1)S(1)}, bf16[32,768]{1,0:T(8,128)(2,1)S(1)}, u32[]{:S(2)}, u32[]{:S(2)}) %collective-permute-start.8) | collective-permute-done | bytes 49184 | tf_op jit(solution)/shard_map/ppermute | solution.py:414
  95.8 11.2 %all_to_all.25.parts = bf16[4,2,48,384]{3,2,1,0:T(8,128)(2,1)S(1)} all-to-all(bf16[4,2,48,384]{3,2,1,0:T(8,128)(2,1)S(1)} %sum_copies.3), channel_id=1, replica_groups={{0,16,32,48},{8,24,40,56},{64,80,96,112},{72,88,104,120},{128,144,160,1..., dimensions={0} | all-to-all | bytes 589824 | tf_op jit(solution)/shard_map/all_to_all | solution.py:404
  107.0 0.9 sum_copies.4
  107.9 10.2 %all-to-all-start.4 = ((bf16[8,2,48,384]{3,2,1,0:T(8,128)(2,1)}), bf16[8,2,48,384]{3,2,1,0:T(8,128)(2,1)S(1)}, u32[]{:S(2)}, u32[]{:S(2)}) async-start(bf16[8,2,48,384]{3,2,1,0:T(8,128)(2,1)} %sum_copies.4), calls=%async_computation.4 | async-start | bytes 1179648 | tf_op jit(solution)/shard_map/all_to_all | solution.py:404
  118.1 5.5 %plain_back.1 = bf16[128,768]{1,0:T(8,128)(2,1)} custom-call(s32[1]{0:T(128)} %bitcast.core_ref.refs_0_, bf16[128,768]{1,0:T(8,128)(2,1)} %bitcast.12, bf16[32,768]{1,0:T(8,128)(2,1)} %get-tuple-element.59.own_far, f32[64,768]{1,0:T(8,128)} %get-tuple-element.37.bias_far, bf16[8,192,384]{2,1,0:T(8,128)(2,1)} %copy-done, bf16[8,192,384]{2,1,0:T(8,128)(2,1)} %copy-done.3, ...), custom_call_target="tpu_custom_call" | custom-call | flops 4000000000 | bytes 4000000 | tf_op jit(solution)/shard_map/plain_back/pallas_call | solution.py:541
  123.7 12.2 %all-to-all-done.4.parts = bf16[8,2,48,384]{3,2,1,0:T(8,128)(2,1)S(1)} async-done(((bf16[8,2,48,384]{3,2,1,0:T(8,128)(2,1)}), bf16[8,2,48,384]{3,2,1,0:T(8,128)(2,1)S(1)}, u32[]{:S(2)}, u32[]{:S(2)}) %all-to-all-start.4) | async-done | bytes 589856 | tf_op jit(solution)/shard_map/all_to_all | solution.py:404
  136.0 3.6 %all_gather.3.parts = bf16[2,2,48,384]{3,2,1,0:T(8,128)(2,1)S(1)} all-gather(bf16[1,2,48,384]{3,2,1,0:T(8,128)(2,1)S(1)} %sum_copies.5), channel_id=1, replica_groups={{0,8},{16,24},{32,40},{48,56},{64,72},{80,88},{96,104},{112,120},{128,1..., dimensions={0}, use_global_device_ids=true | all-gather | bytes 221184 | tf_op jit(solution)/shard_map/all_gather | solution.py:564
  139.6 0.7 finish.1
  (22 shorter events, 0.3 us)
Async XLA Ops:
  2.8 18.6 %all-to-all-start = ((bf16[8,192,384]{2,1,0:T(8,128)(2,1)}), bf16[8,192,384]{2,1,0:T(8,128)(2,1)S(1)}, u32[]{:S(2)}, u32[]{:S(2)}) async-start(bf16[8,192,384]{2,1,0:T(8,128)(2,1)} %prepare.2), calls=%async_computation | async-start | bytes 2359296 | tf_op jit(solution)/shard_map/all_to_all | solution.py:404
  8.7 2.2 %copy-start.1 = (f32[12,225]{1,0:T(8,128)S(1)}, f32[12,225]{1,0:T(8,128)}, u32[]{:S(2)}) copy-start(f32[12,225]{1,0:T(8,128)} %table_p.1) | copy-start | bytes 32404
  8.7 2.2 %copy-start.2 = (f32[12,225]{1,0:T(8,128)S(1)}, f32[12,225]{1,0:T(8,128)}, u32[]{:S(2)}) copy-start(f32[12,225]{1,0:T(8,128)} %table_s.1) | copy-start | bytes 32404
  21.4 11.0 %copy-start = (bf16[8,192,384]{2,1,0:T(8,128)(2,1)}, bf16[8,192,384]{2,1,0:T(8,128)(2,1)S(1)}, u32[]{:S(2)}) copy-start(bf16[8,192,384]{2,1,0:T(8,128)(2,1)S(1)} %all-to-all-done.w_mine_ref.mine_far) | copy-start | bytes 3538948
  21.4 10.9 %collective-permute-start = (bf16[8,192,384]{2,1,0:T(8,128)(2,1)S(1)}, bf16[8,192,384]{2,1,0:T(8,128)(2,1)S(1)}, u32[]{:S(2)}, u32[]{:S(2)}) collective-permute-start(bf16[8,192,384]{2,1,0:T(8,128)(2,1)S(1)} %all-to-all-done.w_mine_ref.mine_far), channel_id=1, source_target_pairs={{0,8},{8,0},{16,24},{24,16},{32,40},{40,32},{48,56},{56,48},{64,72... | collective-permute-start | bytes 3538952 | tf_op jit(solution)/shard_map/ppermute | solution.py:418
  28.7 31.9 %all-to-all-start.1 = ((bf16[8,192,384]{2,1,0:T(8,128)(2,1)}), bf16[8,192,384]{2,1,0:T(8,128)(2,1)S(1)}, u32[]{:S(2)}, u32[]{:S(2)}) async-start(bf16[8,192,384]{2,1,0:T(8,128)(2,1)} %prepare.3), calls=%async_computation.1 | async-start | bytes 2359296 | tf_op jit(solution)/shard_map/all_to_all | solution.py:404
  32.3 4.6 %copy-start.3 = (bf16[8,192,384]{2,1,0:T(8,128)(2,1)}, bf16[8,192,384]{2,1,0:T(8,128)(2,1)S(1)}, u32[]{:S(2)}) copy-start(bf16[8,192,384]{2,1,0:T(8,128)(2,1)S(1)} %collective-permute-done.w_other_ref.other_far) | copy-start | bytes 3538948
  36.9 21.6 %collective-permute-start.1 = (bf16[32,1920]{1,0:T(8,128)(2,1)}, bf16[32,1920]{1,0:T(8,128)(2,1)S(1)}, u32[]{:S(2)}, u32[]{:S(2)}) collective-permute-start(bf16[32,1920]{1,0:T(8,128)(2,1)} %get-tuple-element.42), channel_id=1, source_target_pairs={{8,0},{9,1},{10,2},{11,3},{12,4},{13,5},{14,6},{15,7},{16,8},{17,9... | collective-permute-start | bytes 368648 | tf_op jit(solution)/shard_map/ppermute | solution.py:414
  38.8 19.7 %collective-permute-start.2 = (bf16[32,1920]{1,0:T(8,128)(2,1)}, bf16[32,1920]{1,0:T(8,128)(2,1)S(1)}, u32[]{:S(2)}, u32[]{:S(2)}) collective-permute-start(bf16[32,1920]{1,0:T(8,128)(2,1)} %get-tuple-element.43), channel_id=1, source_target_pairs={{1,0},{2,1},{3,2},{4,3},{5,4},{6,5},{7,6},{0,7},{9,8},{10,9},{11,1... | collective-permute-start | bytes 368648 | tf_op jit(solution)/shard_map/ppermute | solution.py:414
  44.5 16.1 %collective-permute-start.3 = (bf16[32,1920]{1,0:T(8,128)(2,1)}, bf16[32,1920]{1,0:T(8,128)(2,1)S(1)}, u32[]{:S(2)}, u32[]{:S(2)}) collective-permute-start(bf16[32,1920]{1,0:T(8,128)(2,1)} %get-tuple-element.44), channel_id=1, source_target_pairs={{9,0},{10,1},{11,2},{12,3},{13,4},{14,5},{15,6},{8,7},{17,8},{18,9... | collective-permute-start | bytes 368648 | tf_op jit(solution)/shard_map/ppermute | solution.py:414
  60.6 7.8 %collective-permute-start.4 = (bf16[8,192,384]{2,1,0:T(8,128)(2,1)S(1)}, bf16[8,192,384]{2,1,0:T(8,128)(2,1)S(1)}, u32[]{:S(2)}, u32[]{:S(2)}) collective-permute-start(bf16[8,192,384]{2,1,0:T(8,128)(2,1)S(1)} %all-to-all-done.1.refs_6_), channel_id=1, source_target_pairs={{0,8},{8,0},{16,24},{24,16},{32,40},{40,32},{48,56},{56,48},{64,72... | collective-permute-start | bytes 3538952 | tf_op jit(solution)/shard_map/ppermute | solution.py:418
  74.3 3.9 %collective-permute-start.5 = (bf16[8,2,48,384]{3,2,1,0:T(8,128)(2,1)S(1)}, bf16[8,2,48,384]{3,2,1,0:T(8,128)(2,1)S(1)}, u32[]{:S(2)}, u32[]{:S(2)}) collective-permute-start(bf16[8,2,48,384]{3,2,1,0:T(8,128)(2,1)S(1)} %get-tuple-element.50), channel_id=1, source_target_pairs={{0,8},{8,0},{16,24},{24,16},{32,40},{40,32},{48,56},{56,48},{64,72... | collective-permute-start | bytes 1769480 | tf_op jit(solution)/shard_map/ppermute | solution.py:418
  78.2 4.5 %copy-start.6 = (bf16[32,768]{1,0:T(8,128)(2,1)S(1)}, bf16[32,768]{1,0:T(8,128)(2,1)}, u32[]{:S(2)}) copy-start(bf16[32,768]{1,0:T(8,128)(2,1)} %get-tuple-element.55) | copy-start | bytes 147460
  78.2 6.5 %copy-start.5 = (bf16[32,768]{1,0:T(8,128)(2,1)S(1)}, bf16[32,768]{1,0:T(8,128)(2,1)}, u32[]{:S(2)}) copy-start(bf16[32,768]{1,0:T(8,128)(2,1)} %get-tuple-element.56) | copy-start | bytes 147460
  78.2 9.7 %copy-start.4 = (bf16[32,768]{1,0:T(8,128)(2,1)S(1)}, bf16[32,768]{1,0:T(8,128)(2,1)}, u32[]{:S(2)}) copy-start(bf16[32,768]{1,0:T(8,128)(2,1)} %get-tuple-element.57) | copy-start | bytes 147460
  79.1 16.6 %all-to-all-start.2 = ((bf16[8,2,48,384]{3,2,1,0:T(8,128)(2,1)}), bf16[8,2,48,384]{3,2,1,0:T(8,128)(2,1)S(1)}, u32[]{:S(2)}, u32[]{:S(2)}) async-start(bf16[8,2,48,384]{3,2,1,0:T(8,128)(2,1)} %add_convert_fusion), calls=%async_computation.2 | async-start | bytes 1179648 | tf_op jit(solution)/shard_map/all_to_all | solution.py:404
  82.7 8.1 %collective-permute-start.6 = (bf16[32,768]{1,0:T(8,128)(2,1)S(1)}, bf16[32,768]{1,0:T(8,128)(2,1)S(1)}, u32[]{:S(2)}, u32[]{:S(2)}) collective-permute-start(bf16[32,768]{1,0:T(8,128)(2,1)S(1)} %copy-done.6), channel_id=1, source_target_pairs={{504,0},{505,1},{506,2},{507,3},{508,4},{509,5},{510,6},{511,7},{0... | collective-permute-start | bytes 147464 | tf_op jit(solution)/shard_map/ppermute | solution.py:414
  84.6 9.6 %collective-permute-start.7 = (bf16[32,768]{1,0:T(8,128)(2,1)S(1)}, bf16[32,768]{1,0:T(8,128)(2,1)S(1)}, u32[]{:S(2)}, u32[]{:S(2)}) collective-permute-start(bf16[32,768]{1,0:T(8,128)(2,1)S(1)} %copy-done.5), channel_id=1, source_target_pairs={{7,0},{0,1},{1,2},{2,3},{3,4},{4,5},{5,6},{6,7},{15,8},{8,9},{9,10... | collective-permute-start | bytes 147464 | tf_op jit(solution)/shard_map/ppermute | solution.py:414
  87.9 7.8 %collective-permute-start.8 = (bf16[32,768]{1,0:T(8,128)(2,1)S(1)}, bf16[32,768]{1,0:T(8,128)(2,1)S(1)}, u32[]{:S(2)}, u32[]{:S(2)}) collective-permute-start(bf16[32,768]{1,0:T(8,128)(2,1)S(1)} %copy-done.4), channel_id=1, source_target_pairs={{511,0},{504,1},{505,2},{506,3},{507,4},{508,5},{509,6},{510,7},{7... | collective-permute-start | bytes 147464 | tf_op jit(solution)/shard_map/ppermute | solution.py:414
  107.9 28.0 %all-to-all-start.4 = ((bf16[8,2,48,384]{3,2,1,0:T(8,128)(2,1)}), bf16[8,2,48,384]{3,2,1,0:T(8,128)(2,1)S(1)}, u32[]{:S(2)}, u32[]{:S(2)}) async-start(bf16[8,2,48,384]{3,2,1,0:T(8,128)(2,1)} %sum_copies.4), calls=%async_computation.4 | async-start | bytes 1179648 | tf_op jit(solution)/shard_map/all_to_all | solution.py:404

commit v15 on v9

--- a/solution.py
+++ b/solution.py
@@ -225,8 +225,7 @@
     wait_all(copy_all([(packets.at[i * 32 : (i + 1) * 32], out) for i, out in enumerate(outs)], sems, 3))
 
 
-def main_kernel(
-    grad_scale,
+def main_begin(
     core_ref,
     own_far,
     bias_far,
@@ -234,36 +233,68 @@
     below,
     diag,
     w_mine_ref,
+    out_grads,
+    out_normed,
+    out_rows,
+    out_rstd,
+    out_mixed,
+    out_packed,
+    out_d_mixed,
+    out_bias,
+    staged,
+    sems,
+):
+    mine, _ = sides(core_ref)
+    loads = copy_all([(own_far, staged.at[0:32]), (bias_far, out_bias)], sems)
+    for i, part in ((1, right), (2, below), (3, diag)):
+        staged[i * 32 : (i + 1) * 32] = part[...]
+    pick = quadrant_pick(True)
+    loads[0].wait()
+    out_grads[...] = dot(pick, staged[:, D + WIDE :]).astype(BF16)
+    block_out = dot(pick, staged[:, 0:D])
+    out_mixed[...] = dot(pick, staged[:, D : D + WIDE]).astype(BF16)
+    normed, rstd = normalize(block_out)
+    out_normed[...] = normed
+    out_rstd[...] = jnp.broadcast_to(rstd, (128, 128))
+    out_rows[...] = normed.astype(BF16)
+    out_packed[...] = dot(out_rows[:, pl.ds(mine, HALF)], qkv_of(w_mine_ref), NT)
+    out_d_mixed[...] = dot(out_grads[:, pl.ds(mine, HALF)], proj_of(w_mine_ref), NT)
+    loads[1].wait()
+
+
+def main_kernel(
+    grad_scale,
+    core_ref,
+    grads,
+    normed_ref,
+    rows,
+    rstd_ref,
+    mixed_ref,
+    packed_ref,
+    d_mixed_ref,
+    bias_s,
+    w_mine_ref,
     w_other_ref,
     to_own,
     to_column,
     to_below,
     out_keep,
     out_send,
-    bias_s,
     quads,
-    staged,
     rows_small,
-    grads,
     sums,
     mask,
     sems,
 ):
     mine, other = sides(core_ref)
-    loads = copy_all([(own_far, staged.at[0:32]), (bias_far, bias_s)], sems)
     mask[...] = head_mask()
-    for i, part in ((1, right), (2, below), (3, diag)):
-        staged[i * 32 : (i + 1) * 32] = part[...]
-    wait_all(loads)
-    pick = quadrant_pick(True)
-    grads[...] = dot(pick, staged[:, D + WIDE :]).astype(BF16)
-    block_out = dot(pick, staged[:, 0:D])
-    mixed_plain = dot(pick, staged[:, D : D + WIDE]).astype(BF16)
-    normed, rstd = normalize(block_out)
-    rows_small[...] = normed.astype(BF16)
+    normed, rstd = normed_ref[...], rstd_ref[:, 0:1]
+    mixed_plain = mixed_ref[...]
     w_mine, w_other = qkv_of(w_mine_ref), qkv_of(w_other_ref)
-    packed = project(rows_small, w_mine, w_other, mine, other).astype(BF16)
-    d_mixed = project(grads, proj_of(w_mine_ref), proj_of(w_other_ref), mine, other).astype(BF16)
+    packed = packed_ref[...] + dot(rows[:, pl.ds(other, HALF)], w_other, NT)
+    packed = packed.astype(BF16)
+    d_mixed = d_mixed_ref[...] + dot(grads[:, pl.ds(other, HALF)], proj_of(w_other_ref), NT)
+    d_mixed = d_mixed.astype(BF16)
     mixed, d_packed = [], []
     for s in range(2):
         part = packed[s * SPOTS : (s + 1) * SPOTS]
@@ -289,7 +320,6 @@
             (quads.at[64:96], to_below),
         ],
         sems,
-        2,
     )
     rows_small[...] = grad
     for out, start in ((out_send, other), (out_keep, mine)):
@@ -507,25 +537,47 @@
     piece = pltpu.HBM((32, D), BF16)
     column = pltpu.HBM((64, D), BF16)
     local = jax.ShapeDtypeStruct((8, 2, ROWS, HALF), BF16)
+    def near(shape, dtype):
+        return jax.ShapeDtypeStruct(shape, dtype)
+
+    begun = pl.pallas_call(
+        main_begin,
+        out_shape=(
+            near((128, D), BF16),
+            near((128, D), F32),
+            near((128, D), BF16),
+            near((128, 128), F32),
+            near((128, WIDE), BF16),
+            near((128, 3 * WIDE), F32),
+            near((128, WIDE), F32),
+            near((SPOTS, LANES), F32),
+        ),
+        in_specs=[SMEM] + [HBM] * 2 + [VMEM] * 4,
+        out_specs=[VMEM] * 8,
+        scratch_shapes=[
+            pltpu.VMEM((128, 2 * D + WIDE), BF16),
+            pltpu.SemaphoreType.DMA((2,)),
+        ],
+        compiler_params=params(),
+        cost_estimate=cost(5_000_000_000, 1_000_000),
+        name="main_begin",
+    )(core, far(own), far(bias_s), right, below, diag, second_mine)
     g_own, to_right, to_below, keep, send = pl.pallas_call(
         lambda *refs: main_kernel(grad_scale, *refs),
         out_shape=(piece, column, piece, local, local),
-        in_specs=[SMEM] + [HBM] * 2 + [VMEM] * 5,
+        in_specs=[SMEM] + [VMEM] * 10,
         out_specs=[HBM] * 3 + [VMEM] * 2,
         scratch_shapes=[
-            pltpu.VMEM((SPOTS, LANES), F32),
-            pltpu.VMEM((128, D), BF16),
-            pltpu.VMEM((128, 2 * D + WIDE), BF16),
             pltpu.VMEM((128, D), BF16),
             pltpu.VMEM((128, D), BF16),
             pltpu.VMEM((128, D), F32),
             pltpu.VMEM((LANES, WIDE), BF16),
-            pltpu.SemaphoreType.DMA((6,)),
+            pltpu.SemaphoreType.DMA((4,)),
         ],
         compiler_params=params(),
         cost_estimate=cost(1_000_000, 1_000_000),
         name="main",
-    )(core, far(own), far(bias_s), right, below, diag, second_mine, second_other)
+    )(core, *begun, second_mine, second_other)
 
     part = (keep.astype(F32) + other_core(send).astype(F32)).astype(BF16)
     part, to_right, to_below = lax.optimization_barrier((part, to_right, to_below))

time: 138 us -> 136 us (0.986)
  waiting for transfers between devices: 39.6 us -> 37.7 us
    ppermute x3, waiting for transfers between devices: 4.06 us -> 2.18 us  [other_core(): lax.ppermute(value, 'tm', [(i, i ^ 1) for i in range(lax.axis_size('tm'))])]
    pallas_call x0 -> x1, Pallas kernels: none -> 1.87 us  [shards(): pl.pallas_call(main_begin, out_shape=(near((128, D), BF16), near((128, D)...]
    pallas_call x1, Pallas kernels: 5.74 us -> 4.04 us  [shards(): pl.pallas_call(lambda *refs: main_kernel(grad_scale, *refs), out_shape=(p...]
  transfers between devices with their start and end apart: 13 -> 13, of which waited for: 8 -> 8; matrix products, arithmetic and copies ran while one was open for 0% -> 0% of each run, Pallas kernels for 10% -> 12%
where the time goes in v15:
time: 136 us
  starting transfers between devices  64.7 us (48%)
  waiting for transfers between devices  37.7 us (28%)
  Pallas kernels  24.7 us (18%)
  blocking collectives  6.45 us (5%)
    ppermute x5, starting transfers between devices, from_offset(): return lax.ppermute(value, ('tm', 'freq'), pairs)  25.5 us
    all_to_all x5, starting transfers between devices, swap(): return lax.all_to_all(value, axis, 0, 0, axis_index_groups=groups)  24.2 us
    all_to_all x5, waiting for transfers between devices, swap(): return lax.all_to_all(value, axis, 0, 0, axis_index_groups=groups)  19 us
    ppermute x5, waiting for transfers between devices, from_offset(): return lax.ppermute(value, ('tm', 'freq'), pairs)  16.6 us
    ppermute x3, starting transfers between devices, other_core(): lax.ppermute(value, 'tm', [(i, i ^ 1) for i in range(lax.axis_size('tm'))])  15 us
    all_gather x1, blocking collectives, shards(): part = lax.all_gather(part, 'tm', axis_index_groups=tm_groups('core'))  6.45 us
    pallas_call x1, Pallas kernels, shards(): pl.pallas_call(plain_back, out_shape=jax.ShapeDtypeStruct((128, D), BF16)...  5.54 us
    pallas_call x1, Pallas kernels, shards(): pl.pallas_call(plain_forward, out_shape=(packet,) * 4, in_specs=[SMEM] +...  4.55 us
  transfers between devices with their start and end apart: 13, of which 8 were waited for; matrix products, arithmetic and copies ran while one was open for 0% of the time, Pallas kernels for 12%

profile of v15, /device:TPU:1, one launch (start us, length us, event | category | flops | bytes accessed | tf_op | source)
XLA Modules:
  0.0 135.6 jit_solution(15327366601735866772)
XLA Ops:
  0.6 2.1 %prepare.2 = bf16[8,192,384]{2,1,0:T(8,128)(2,1)} custom-call(s32[1]{0:T(128)} %bitcast.core_ref.refs_0_, bf16[144,768]{1,0:T(8,128)(2,1)} %bitcast.8, bf16[48,768]{1,0:T(8,128)(2,1)} %proj.2), custom_call_target="tpu_custom_call" | custom-call | tf_op jit(solution)/shard_map/prepare/pallas_call | solution.py:473
  2.8 5.9 %all-to-all-start = ((bf16[8,192,384]{2,1,0:T(8,128)(2,1)}), bf16[8,192,384]{2,1,0:T(8,128)(2,1)S(1)}, u32[]{:S(2)}, u32[]{:S(2)}) async-start(bf16[8,192,384]{2,1,0:T(8,128)(2,1)} %prepare.2), calls=%async_computation | async-start | bytes 2359296 | tf_op jit(solution)/shard_map/all_to_all | solution.py:433
  8.7 2.1 %prepare.3 = bf16[8,192,384]{2,1,0:T(8,128)(2,1)} custom-call(s32[1]{0:T(128)} %bitcast.core_ref.refs_0_, bf16[144,768]{1,0:T(8,128)(2,1)} %bitcast.9, bf16[48,768]{1,0:T(8,128)(2,1)} %proj.3), custom_call_target="tpu_custom_call" | custom-call | tf_op jit(solution)/shard_map/prepare/pallas_call | solution.py:473
  10.9 2.0 %biases.1 = (f32[64,768]{1,0:T(8,128)}, f32[64,768]{1,0:T(8,128)}) custom-call(s32[2]{0:T(128)S(1)} %add_convert_fusion.1.edge_ref, f32[12,225]{1,0:T(8,128)S(1)} %copy-done.1, f32[12,225]{1,0:T(8,128)S(1)} %copy-done.2), custom_call_target="tpu_custom_call" | custom-call | tf_op jit(solution)/shard_map/biases/pallas_call | solution.py:489
  12.8 8.5 %all-to-all-done.w_mine_ref.mine_far = bf16[8,192,384]{2,1,0:T(8,128)(2,1)S(1)} async-done(((bf16[8,192,384]{2,1,0:T(8,128)(2,1)}), bf16[8,192,384]{2,1,0:T(8,128)(2,1)S(1)}, u32[]{:S(2)}, u32[]{:S(2)}) %all-to-all-start) | async-done | bytes 1179680 | tf_op jit(solution)/shard_map/all_to_all | solution.py:433
  21.4 7.3 %collective-permute-start = (bf16[8,192,384]{2,1,0:T(8,128)(2,1)S(1)}, bf16[8,192,384]{2,1,0:T(8,128)(2,1)S(1)}, u32[]{:S(2)}, u32[]{:S(2)}) collective-permute-start(bf16[8,192,384]{2,1,0:T(8,128)(2,1)S(1)} %all-to-all-done.w_mine_ref.mine_far), channel_id=1, source_target_pairs={{0,8},{8,0},{16,24},{24,16},{32,40},{40,32},{48,56},{56,48},{64,72... | collective-permute-start | bytes 3538952 | tf_op jit(solution)/shard_map/ppermute | solution.py:447
  28.7 3.6 %all-to-all-start.1 = ((bf16[8,192,384]{2,1,0:T(8,128)(2,1)}), bf16[8,192,384]{2,1,0:T(8,128)(2,1)S(1)}, u32[]{:S(2)}, u32[]{:S(2)}) async-start(bf16[8,192,384]{2,1,0:T(8,128)(2,1)} %prepare.3), calls=%async_computation.1 | async-start | bytes 2359296 | tf_op jit(solution)/shard_map/all_to_all | solution.py:433
  32.3 4.6 %plain_forward.1 = (bf16[32,1920]{1,0:T(8,128)(2,1)}, bf16[32,1920]{1,0:T(8,128)(2,1)}, bf16[32,1920]{1,0:T(8,128)(2,1)}, bf16[32,1920]{1,0:T(8,128)(2,1)}) custom-call(s32[1]{0:T(128)} %bitcast.core_ref.refs_0_, bf16[128,768]{1,0:T(8,128)(2,1)} %bitcast.11, bf16[128,768]{1,0:T(8,128)(2,1)} %bitcast.10, f32[64,768]{1,0:T(8,128)} %get-tuple-element.44.bias_far, ...), custom_call_target="tpu_custom_call" | custom-call | flops 20000000000 | bytes 1000000 | tf_op jit(solution)/shard_map/plain_forward/pallas_call | solution.py:511
  36.9 1.9 %collective-permute-start.1 = (bf16[32,1920]{1,0:T(8,128)(2,1)}, bf16[32,1920]{1,0:T(8,128)(2,1)S(1)}, u32[]{:S(2)}, u32[]{:S(2)}) collective-permute-start(bf16[32,1920]{1,0:T(8,128)(2,1)} %get-tuple-element.49), channel_id=1, source_target_pairs={{8,0},{9,1},{10,2},{11,3},{12,4},{13,5},{14,6},{15,7},{16,8},{17,9... | collective-permute-start | bytes 368648 | tf_op jit(solution)/shard_map/ppermute | solution.py:443
  38.8 5.7 %collective-permute-start.2 = (bf16[32,1920]{1,0:T(8,128)(2,1)}, bf16[32,1920]{1,0:T(8,128)(2,1)S(1)}, u32[]{:S(2)}, u32[]{:S(2)}) collective-permute-start(bf16[32,1920]{1,0:T(8,128)(2,1)} %get-tuple-element.50), channel_id=1, source_target_pairs={{1,0},{2,1},{3,2},{4,3},{5,4},{6,5},{7,6},{0,7},{9,8},{10,9},{11,1... | collective-permute-start | bytes 368648 | tf_op jit(solution)/shard_map/ppermute | solution.py:443
  44.5 14.0 %collective-permute-start.3 = (bf16[32,1920]{1,0:T(8,128)(2,1)}, bf16[32,1920]{1,0:T(8,128)(2,1)S(1)}, u32[]{:S(2)}, u32[]{:S(2)}) collective-permute-start(bf16[32,1920]{1,0:T(8,128)(2,1)} %get-tuple-element.51), channel_id=1, source_target_pairs={{9,0},{10,1},{11,2},{12,3},{13,4},{14,5},{15,6},{8,7},{17,8},{18,9... | collective-permute-start | bytes 368648 | tf_op jit(solution)/shard_map/ppermute | solution.py:443
  58.5 2.1 %collective-permute-done.3.diag = bf16[32,1920]{1,0:T(8,128)(2,1)S(1)} collective-permute-done((bf16[32,1920]{1,0:T(8,128)(2,1)}, bf16[32,1920]{1,0:T(8,128)(2,1)S(1)}, u32[]{:S(2)}, u32[]{:S(2)}) %collective-permute-start.3) | collective-permute-done | bytes 122912 | tf_op jit(solution)/shard_map/ppermute | solution.py:443
  60.6 5.4 %collective-permute-start.4 = (bf16[8,192,384]{2,1,0:T(8,128)(2,1)S(1)}, bf16[8,192,384]{2,1,0:T(8,128)(2,1)S(1)}, u32[]{:S(2)}, u32[]{:S(2)}) collective-permute-start(bf16[8,192,384]{2,1,0:T(8,128)(2,1)S(1)} %all-to-all-done.1.w_mine_ref.refs_9_), channel_id=1, source_target_pairs={{0,8},{8,0},{16,24},{24,16},{32,40},{40,32},{48,56},{56,48},{64,72... | collective-permute-start | bytes 3538952 | tf_op jit(solution)/shard_map/ppermute | solution.py:447
  66.0 1.9 %main_begin.1 = (bf16[128,768]{1,0:T(8,128)(2,1)S(1)}, f32[128,768]{1,0:T(8,128)S(1)}, bf16[128,768]{1,0:T(8,128)(2,1)S(1)}, f32[128,128]{1,0:T(8,128)S(1)}, bf1...) custom-call(s32[1]{0:T(128)} %bitcast.core_ref.refs_0_, ...), custom_call_target="tpu_custom_call" | custom-call | flops 5000000000 | bytes 1000000 | tf_op jit(solution)/shard_map/main_begin/pallas_call | solution.py:543
  68.5 4.0 %main.1 = (bf16[32,768]{1,0:T(8,128)(2,1)}, bf16[64,768]{1,0:T(8,128)(2,1)}, bf16[32,768]{1,0:T(8,128)(2,1)}, bf16[8,2,48,384]{3,2,1,0:T(8,128)(2,1)S(1)}, bf16[8,2,48,384]{3,2,1,0:T(8,128)(2,1)S(1)}) custom-call(s32[1]{0:T(128)} %bitcast.core_ref.refs_0_, bf16[128,768]{1,0:T(8,128)(2,1)S(1)} %get-tuple-element.56.refs_1_, ...), custom_call_target="tpu_custom_call" | custom-call | flops 1000000 | bytes 1000000 | tf_op jit(solution)/shard_map/main/pallas_call | solution.py:565
  72.5 2.3 %collective-permute-start.5 = (bf16[8,2,48,384]{3,2,1,0:T(8,128)(2,1)S(1)}, bf16[8,2,48,384]{3,2,1,0:T(8,128)(2,1)S(1)}, u32[]{:S(2)}, u32[]{:S(2)}) collective-permute-start(bf16[8,2,48,384]{3,2,1,0:T(8,128)(2,1)S(1)} %get-tuple-element.65), channel_id=1, source_target_pairs={{0,8},{8,0},{16,24},{24,16},{32,40},{40,32},{48,56},{56,48},{64,72... | collective-permute-start | bytes 1769480 | tf_op jit(solution)/shard_map/ppermute | solution.py:447
  74.8 1.6 %collective-permute-done.5 = bf16[8,2,48,384]{3,2,1,0:T(8,128)(2,1)S(1)} collective-permute-done((bf16[8,2,48,384]{3,2,1,0:T(8,128)(2,1)S(1)}, bf16[8,2,48,384]{3,2,1,0:T(8,128)(2,1)S(1)}, u32[]{:S(2)}, u32[]{:S(2)}) %collective-permute-start.5) | collective-permute-done | bytes 589856 | tf_op jit(solution)/shard_map/ppermute | solution.py:447
  76.4 1.0 add_convert_fusion
  77.4 3.7 %all-to-all-start.2 = ((bf16[8,2,48,384]{3,2,1,0:T(8,128)(2,1)}), bf16[8,2,48,384]{3,2,1,0:T(8,128)(2,1)S(1)}, u32[]{:S(2)}, u32[]{:S(2)}) async-start(bf16[8,2,48,384]{3,2,1,0:T(8,128)(2,1)} %add_convert_fusion), calls=%async_computation.2 | async-start | bytes 1179648 | tf_op jit(solution)/shard_map/all_to_all | solution.py:433
  81.1 1.9 %collective-permute-start.6 = (bf16[64,768]{1,0:T(8,128)(2,1)S(1)}, bf16[64,768]{1,0:T(8,128)(2,1)S(1)}, u32[]{:S(2)}, u32[]{:S(2)}) collective-permute-start(bf16[64,768]{1,0:T(8,128)(2,1)S(1)} %copy-done.5), channel_id=1, source_target_pairs={{504,0},{505,1},{506,2},{507,3},{508,4},{509,5},{510,6},{511,7},{0... | collective-permute-start | bytes 294920 | tf_op jit(solution)/shard_map/ppermute | solution.py:443
  83.0 7.2 %collective-permute-done.6.column = bf16[64,768]{1,0:T(8,128)(2,1)S(1)} collective-permute-done((bf16[64,768]{1,0:T(8,128)(2,1)S(1)}, bf16[64,768]{1,0:T(8,128)(2,1)S(1)}, u32[]{:S(2)}, u32[]{:S(2)}) %collective-permute-start.6) | collective-permute-done | bytes 98336 | tf_op jit(solution)/shard_map/ppermute | solution.py:443
  90.2 1.0 all-to-all-done.2.parts
  91.3 0.8 sum_copies.3
  92.1 3.5 %all-to-all-start.3 = ((bf16[4,2,48,384]{3,2,1,0:T(8,128)(2,1)}), bf16[4,2,48,384]{3,2,1,0:T(8,128)(2,1)S(1)}, u32[]{:S(2)}, u32[]{:S(2)}) async-start(bf16[4,2,48,384]{3,2,1,0:T(8,128)(2,1)} %sum_copies.3), calls=%async_computation.3 | async-start | bytes 589824 | tf_op jit(solution)/shard_map/all_to_all | solution.py:433
  95.6 2.0 %collective-permute-start.7 = (bf16[64,768]{1,0:T(8,128)(2,1)S(1)}, bf16[64,768]{1,0:T(8,128)(2,1)S(1)}, u32[]{:S(2)}, u32[]{:S(2)}) collective-permute-start(bf16[64,768]{1,0:T(8,128)(2,1)S(1)} %pad_maximum_fusion), channel_id=1, source_target_pairs={{7,0},{0,1},{1,2},{2,3},{3,4},{4,5},{5,6},{6,7},{15,8},{8,9},{9,10... | collective-permute-start | bytes 294920 | tf_op jit(solution)/shard_map/ppermute | solution.py:443
  97.6 7.2 %collective-permute-done.7.row = bf16[64,768]{1,0:T(8,128)(2,1)S(1)} collective-permute-done((bf16[64,768]{1,0:T(8,128)(2,1)S(1)}, bf16[64,768]{1,0:T(8,128)(2,1)S(1)}, u32[]{:S(2)}, u32[]{:S(2)}) %collective-permute-start.7) | collective-permute-done | bytes 98336 | tf_op jit(solution)/shard_map/ppermute | solution.py:443
  104.9 0.9 sum_copies.4
  105.7 7.6 %all-to-all-start.4 = ((bf16[8,2,48,384]{3,2,1,0:T(8,128)(2,1)}), bf16[8,2,48,384]{3,2,1,0:T(8,128)(2,1)S(1)}, u32[]{:S(2)}, u32[]{:S(2)}) async-start(bf16[8,2,48,384]{3,2,1,0:T(8,128)(2,1)} %sum_copies.4), calls=%async_computation.4 | async-start | bytes 1179648 | tf_op jit(solution)/shard_map/all_to_all | solution.py:433
  113.4 5.5 %plain_back.1 = bf16[128,768]{1,0:T(8,128)(2,1)} custom-call(s32[1]{0:T(128)} %bitcast.core_ref.refs_0_, bf16[128,768]{1,0:T(8,128)(2,1)} %bitcast.12, bf16[32,768]{1,0:T(8,128)(2,1)} %get-tuple-element.75.own_far, f32[64,768]{1,0:T(8,128)} %get-tuple-element.44.bias_far, bf16[8,192,384]{2,1,0:T(8,128)(2,1)} %copy-done, bf16[8,192,384]{2,1,0:T(8,128)(2,1)} %copy-done.3, ...), custom_call_target="tpu_custom_call" | custom-call | flops 4000000000 | bytes 4000000 | tf_op jit(solution)/shard_map/plain_back/pallas_call | solution.py:591
  118.9 9.4 %all-to-all-done.4.parts = bf16[8,2,48,384]{3,2,1,0:T(8,128)(2,1)S(1)} async-done(((bf16[8,2,48,384]{3,2,1,0:T(8,128)(2,1)}), bf16[8,2,48,384]{3,2,1,0:T(8,128)(2,1)S(1)}, u32[]{:S(2)}, u32[]{:S(2)}) %all-to-all-start.4) | async-done | bytes 589856 | tf_op jit(solution)/shard_map/all_to_all | solution.py:433
  128.4 6.4 %all_gather.3.parts = bf16[2,2,48,384]{3,2,1,0:T(8,128)(2,1)S(1)} all-gather(bf16[1,2,48,384]{3,2,1,0:T(8,128)(2,1)S(1)} %sum_copies.5), channel_id=1, replica_groups={{0,8},{16,24},{32,40},{48,56},{64,72},{80,88},{96,104},{112,120},{128,1..., dimensions={0}, use_global_device_ids=true | all-gather | bytes 221184 | tf_op jit(solution)/shard_map/all_gather | solution.py:614
  134.9 0.7 finish.1
  (22 shorter events, 0.8 us)
Async XLA Ops:
  2.8 18.6 %all-to-all-start = ((bf16[8,192,384]{2,1,0:T(8,128)(2,1)}), bf16[8,192,384]{2,1,0:T(8,128)(2,1)S(1)}, u32[]{:S(2)}, u32[]{:S(2)}) async-start(bf16[8,192,384]{2,1,0:T(8,128)(2,1)} %prepare.2), calls=%async_computation | async-start | bytes 2359296 | tf_op jit(solution)/shard_map/all_to_all | solution.py:433
  8.7 2.2 %copy-start.1 = (f32[12,225]{1,0:T(8,128)S(1)}, f32[12,225]{1,0:T(8,128)}, u32[]{:S(2)}) copy-start(f32[12,225]{1,0:T(8,128)} %table_p.1) | copy-start | bytes 32404
  8.7 2.2 %copy-start.2 = (f32[12,225]{1,0:T(8,128)S(1)}, f32[12,225]{1,0:T(8,128)}, u32[]{:S(2)}) copy-start(f32[12,225]{1,0:T(8,128)} %table_s.1) | copy-start | bytes 32404
  21.4 11.0 %copy-start = (bf16[8,192,384]{2,1,0:T(8,128)(2,1)}, bf16[8,192,384]{2,1,0:T(8,128)(2,1)S(1)}, u32[]{:S(2)}) copy-start(bf16[8,192,384]{2,1,0:T(8,128)(2,1)S(1)} %all-to-all-done.w_mine_ref.mine_far) | copy-start | bytes 3538948
  21.4 10.9 %collective-permute-start = (bf16[8,192,384]{2,1,0:T(8,128)(2,1)S(1)}, bf16[8,192,384]{2,1,0:T(8,128)(2,1)S(1)}, u32[]{:S(2)}, u32[]{:S(2)}) collective-permute-start(bf16[8,192,384]{2,1,0:T(8,128)(2,1)S(1)} %all-to-all-done.w_mine_ref.mine_far), channel_id=1, source_target_pairs={{0,8},{8,0},{16,24},{24,16},{32,40},{40,32},{48,56},{56,48},{64,72... | collective-permute-start | bytes 3538952 | tf_op jit(solution)/shard_map/ppermute | solution.py:447
  28.7 31.9 %all-to-all-start.1 = ((bf16[8,192,384]{2,1,0:T(8,128)(2,1)}), bf16[8,192,384]{2,1,0:T(8,128)(2,1)S(1)}, u32[]{:S(2)}, u32[]{:S(2)}) async-start(bf16[8,192,384]{2,1,0:T(8,128)(2,1)} %prepare.3), calls=%async_computation.1 | async-start | bytes 2359296 | tf_op jit(solution)/shard_map/all_to_all | solution.py:433
  32.3 4.6 %copy-start.3 = (bf16[8,192,384]{2,1,0:T(8,128)(2,1)}, bf16[8,192,384]{2,1,0:T(8,128)(2,1)S(1)}, u32[]{:S(2)}) copy-start(bf16[8,192,384]{2,1,0:T(8,128)(2,1)S(1)} %collective-permute-done.w_other_ref.other_far) | copy-start | bytes 3538948
  36.9 21.6 %collective-permute-start.1 = (bf16[32,1920]{1,0:T(8,128)(2,1)}, bf16[32,1920]{1,0:T(8,128)(2,1)S(1)}, u32[]{:S(2)}, u32[]{:S(2)}) collective-permute-start(bf16[32,1920]{1,0:T(8,128)(2,1)} %get-tuple-element.49), channel_id=1, source_target_pairs={{8,0},{9,1},{10,2},{11,3},{12,4},{13,5},{14,6},{15,7},{16,8},{17,9... | collective-permute-start | bytes 368648 | tf_op jit(solution)/shard_map/ppermute | solution.py:443
  38.8 19.7 %collective-permute-start.2 = (bf16[32,1920]{1,0:T(8,128)(2,1)}, bf16[32,1920]{1,0:T(8,128)(2,1)S(1)}, u32[]{:S(2)}, u32[]{:S(2)}) collective-permute-start(bf16[32,1920]{1,0:T(8,128)(2,1)} %get-tuple-element.50), channel_id=1, source_target_pairs={{1,0},{2,1},{3,2},{4,3},{5,4},{6,5},{7,6},{0,7},{9,8},{10,9},{11,1... | collective-permute-start | bytes 368648 | tf_op jit(solution)/shard_map/ppermute | solution.py:443
  44.5 16.1 %collective-permute-start.3 = (bf16[32,1920]{1,0:T(8,128)(2,1)}, bf16[32,1920]{1,0:T(8,128)(2,1)S(1)}, u32[]{:S(2)}, u32[]{:S(2)}) collective-permute-start(bf16[32,1920]{1,0:T(8,128)(2,1)} %get-tuple-element.51), channel_id=1, source_target_pairs={{9,0},{10,1},{11,2},{12,3},{13,4},{14,5},{15,6},{8,7},{17,8},{18,9... | collective-permute-start | bytes 368648 | tf_op jit(solution)/shard_map/ppermute | solution.py:443
  60.6 7.8 %collective-permute-start.4 = (bf16[8,192,384]{2,1,0:T(8,128)(2,1)S(1)}, bf16[8,192,384]{2,1,0:T(8,128)(2,1)S(1)}, u32[]{:S(2)}, u32[]{:S(2)}) collective-permute-start(bf16[8,192,384]{2,1,0:T(8,128)(2,1)S(1)} %all-to-all-done.1.w_mine_ref.refs_9_), channel_id=1, source_target_pairs={{0,8},{8,0},{16,24},{24,16},{32,40},{40,32},{48,56},{56,48},{64,72... | collective-permute-start | bytes 3538952 | tf_op jit(solution)/shard_map/ppermute | solution.py:447
  72.5 3.9 %collective-permute-start.5 = (bf16[8,2,48,384]{3,2,1,0:T(8,128)(2,1)S(1)}, bf16[8,2,48,384]{3,2,1,0:T(8,128)(2,1)S(1)}, u32[]{:S(2)}, u32[]{:S(2)}) collective-permute-start(bf16[8,2,48,384]{3,2,1,0:T(8,128)(2,1)S(1)} %get-tuple-element.65), channel_id=1, source_target_pairs={{0,8},{8,0},{16,24},{24,16},{32,40},{40,32},{48,56},{56,48},{64,72... | collective-permute-start | bytes 1769480 | tf_op jit(solution)/shard_map/ppermute | solution.py:447
  76.4 4.7 %copy-start.5 = (bf16[64,768]{1,0:T(8,128)(2,1)S(1)}, bf16[64,768]{1,0:T(8,128)(2,1)}, u32[]{:S(2)}) copy-start(bf16[64,768]{1,0:T(8,128)(2,1)} %get-tuple-element.69) | copy-start | bytes 294916
  77.4 18.1 %copy-start.4 = (bf16[32,768]{1,0:T(8,128)(2,1)S(1)}, bf16[32,768]{1,0:T(8,128)(2,1)}, u32[]{:S(2)}) copy-start(bf16[32,768]{1,0:T(8,128)(2,1)} %get-tuple-element.72) | copy-start | bytes 147460
  77.4 13.9 %all-to-all-start.2 = ((bf16[8,2,48,384]{3,2,1,0:T(8,128)(2,1)}), bf16[8,2,48,384]{3,2,1,0:T(8,128)(2,1)S(1)}, u32[]{:S(2)}, u32[]{:S(2)}) async-start(bf16[8,2,48,384]{3,2,1,0:T(8,128)(2,1)} %add_convert_fusion), calls=%async_computation.2 | async-start | bytes 1179648 | tf_op jit(solution)/shard_map/all_to_all | solution.py:433
  81.1 9.1 %collective-permute-start.6 = (bf16[64,768]{1,0:T(8,128)(2,1)S(1)}, bf16[64,768]{1,0:T(8,128)(2,1)S(1)}, u32[]{:S(2)}, u32[]{:S(2)}) collective-permute-start(bf16[64,768]{1,0:T(8,128)(2,1)S(1)} %copy-done.5), channel_id=1, source_target_pairs={{504,0},{505,1},{506,2},{507,3},{508,4},{509,5},{510,6},{511,7},{0... | collective-permute-start | bytes 294920 | tf_op jit(solution)/shard_map/ppermute | solution.py:443
  92.1 12.8 %all-to-all-start.3 = ((bf16[4,2,48,384]{3,2,1,0:T(8,128)(2,1)}), bf16[4,2,48,384]{3,2,1,0:T(8,128)(2,1)S(1)}, u32[]{:S(2)}, u32[]{:S(2)}) async-start(bf16[4,2,48,384]{3,2,1,0:T(8,128)(2,1)} %sum_copies.3), calls=%async_computation.3 | async-start | bytes 589824 | tf_op jit(solution)/shard_map/all_to_all | solution.py:433
  95.6 9.3 %collective-permute-start.7 = (bf16[64,768]{1,0:T(8,128)(2,1)S(1)}, bf16[64,768]{1,0:T(8,128)(2,1)S(1)}, u32[]{:S(2)}, u32[]{:S(2)}) collective-permute-start(bf16[64,768]{1,0:T(8,128)(2,1)S(1)} %pad_maximum_fusion), channel_id=1, source_target_pairs={{7,0},{0,1},{1,2},{2,3},{3,4},{4,5},{5,6},{6,7},{15,8},{8,9},{9,10... | collective-permute-start | bytes 294920 | tf_op jit(solution)/shard_map/ppermute | solution.py:443
  105.7 22.6 %all-to-all-start.4 = ((bf16[8,2,48,384]{3,2,1,0:T(8,128)(2,1)}), bf16[8,2,48,384]{3,2,1,0:T(8,128)(2,1)S(1)}, u32[]{:S(2)}, u32[]{:S(2)}) async-start(bf16[8,2,48,384]{3,2,1,0:T(8,128)(2,1)} %sum_copies.4), calls=%async_computation.4 | async-start | bytes 1179648 | tf_op jit(solution)/shard_map/all_to_all | solution.py:433

commit v16 on v15

--- a/solution.py
+++ b/solution.py
@@ -116,7 +116,27 @@
     wait_all(copy_all([(block, out.at[i]) for i in range(8)], sems))
 
 
-def biases(edge_ref, table_p, table_s, to_p, to_s, out_p, out_s, tables, wide, sems):
+def biases(
+    edge_ref,
+    table_p,
+    table_s,
+    tok,
+    cot,
+    to_p,
+    to_s,
+    to_rows,
+    to_cot,
+    out_p,
+    out_s,
+    tables,
+    wide,
+    rows,
+    quads,
+    sems,
+):
+    rows[...] = normalize(tok[...].astype(F32))[0].astype(BF16)
+    quads[...] = dot(quadrant_pick(), cot[...]).astype(BF16)
+    stores = copy_all([(rows, to_rows), (quads, to_cot)], sems)
     tables[...] = jnp.zeros_like(tables)
     tables[0:HEADS, 0:REL] = table_p[...]
     tables[HEADS : 2 * HEADS, 0:REL] = table_s[...]
@@ -144,7 +164,7 @@
     cross = at ^ key_at
     barred = (cross & 32) * edge_ref[0] + (cross & 4) * edge_ref[1]
     out_s[...] = jnp.where(barred != 0, NEG, out_s[...])
-    wait_all(copy_all([(out_p, to_p), (out_s, to_s)], sems))
+    wait_all(stores + copy_all([(out_p, to_p), (out_s, to_s)], sems, 2))
 
 
 def project(rows_ref, w_mine, w_other, mine, other):
@@ -183,6 +203,7 @@
     tok_far,
     cot_far,
     bias_far,
+    rows_far,
     w_mine_ref,
     w_other_ref,
     out_o,
@@ -190,7 +211,6 @@
     out_b,
     out_d,
     tok,
-    cot,
     bias_p,
     packets,
     rows,
@@ -199,11 +219,17 @@
     sems,
 ):
     mine, other = sides(core_ref)
-    loads = copy_all([(tok_far, tok), (bias_far, bias_p), (cot_far, cot)], sems)
+    loads = copy_all(
+        [
+            (rows_far, rows),
+            (bias_far, bias_p),
+            (tok_far, tok),
+            (cot_far, packets.at[:, D + WIDE :]),
+        ],
+        sems,
+    )
     mask[...] = head_mask()
     loads[0].wait()
-    inputs = tok[...].astype(F32)
-    rows[...] = normalize(inputs)[0].astype(BF16)
     w_mine, w_other = qkv_of(w_mine_ref), qkv_of(w_other_ref)
     packed = project(rows, w_mine, w_other, mine, other).astype(BF16)
     loads[1].wait()
@@ -216,13 +242,13 @@
     mixed = jnp.concatenate(mixed, axis=0)
     sums[:, pl.ds(mine, HALF)] = dot(mixed, proj_of(w_mine_ref))
     sums[:, pl.ds(other, HALF)] = dot(mixed, proj_of(w_other_ref))
-    block_out = (inputs + sums[...]).astype(BF16)
+    wait_all(loads[2:])
+    block_out = (tok[...].astype(F32) + sums[...]).astype(BF16)
     pick = quadrant_pick()
-    loads[2].wait()
-    for whole, first in ((block_out, 0), (mixed, D), (cot[...], D + WIDE)):
+    for whole, first in ((block_out, 0), (mixed, D)):
         packets[:, first : first + whole.shape[1]] = dot(pick, whole).astype(BF16)
     outs = (out_d, out_b, out_r, out_o)
-    wait_all(copy_all([(packets.at[i * 32 : (i + 1) * 32], out) for i, out in enumerate(outs)], sems, 3))
+    wait_all(copy_all([(packets.at[i * 32 : (i + 1) * 32], out) for i, out in enumerate(outs)], sems, 4))
 
 
 def main_begin(
@@ -486,21 +512,24 @@
     first_mine = swap(share(qkv_plain, proj_plain), "freq")
     second_share = share(qkv_shift, proj_shift)
     table = pltpu.HBM((SPOTS, LANES), F32)
-    bias_p, bias_s = pl.pallas_call(
+    tile = pltpu.HBM((128, D), BF16)
+    bias_p, bias_s, rows, cot_quads = pl.pallas_call(
         biases,
-        out_shape=(table, table),
-        in_specs=[SMEM, VMEM, VMEM],
-        out_specs=[HBM] * 2,
+        out_shape=(table, table, tile, tile),
+        in_specs=[SMEM] + [VMEM] * 4,
+        out_specs=[HBM] * 4,
         scratch_shapes=[
             pltpu.VMEM((SPOTS, LANES), F32),
             pltpu.VMEM((SPOTS, LANES), F32),
             pltpu.VMEM((32, 256), F32),
             pltpu.VMEM((2 * HEADS * WIN, 128), F32),
-            pltpu.SemaphoreType.DMA((2,)),
+            pltpu.VMEM((128, D), BF16),
+            pltpu.VMEM((128, D), BF16),
+            pltpu.SemaphoreType.DMA((4,)),
         ],
         compiler_params=params(),
         name="biases",
-    )(edge, table_plain, table_shift)
+    )(edge, table_plain, table_shift, tok, cot)
 
     first_mine, second_share, bias_p, bias_s = lax.optimization_barrier(
         (first_mine, second_share, bias_p, bias_s)
@@ -511,22 +540,21 @@
     own, to_left, to_above, to_diag = pl.pallas_call(
         plain_forward,
         out_shape=(packet,) * 4,
-        in_specs=[SMEM] + [HBM] * 3 + [VMEM] * 2,
+        in_specs=[SMEM] + [HBM] * 4 + [VMEM] * 2,
         out_specs=[HBM] * 4,
         scratch_shapes=[
             pltpu.VMEM((128, D), BF16),
-            pltpu.VMEM((128, D), BF16),
             pltpu.VMEM((SPOTS, LANES), F32),
             pltpu.VMEM((128, 2 * D + WIDE), BF16),
             pltpu.VMEM((128, D), BF16),
             pltpu.VMEM((128, D), F32),
             pltpu.VMEM((LANES, WIDE), BF16),
-            pltpu.SemaphoreType.DMA((7,)),
+            pltpu.SemaphoreType.DMA((8,)),
         ],
         compiler_params=params(),
         cost_estimate=cost(20_000_000_000, 1_000_000),
         name="plain_forward",
-    )(core, far(tok), far(cot), far(bias_p), first_mine, first_other)
+    )(core, far(tok), far(cot_quads), far(bias_p), far(rows), first_mine, first_other)
     right = from_offset(to_left, 1, 0)
     below = from_offset(to_above, 0, 1)
     diag = from_offset(to_diag, 1, 1)

time: 136 us -> 136 us (level)
  no operation moved by 1% of the time
where the time goes in v16:
time: 136 us; the launch traced here: 135 us
  starting transfers between devices  64.7 us (48%)
  waiting for transfers between devices  37.1 us (27%)
  Pallas kernels  24.7 us (18%)
  blocking collectives  6.87 us (5%)
    ppermute x5, starting transfers between devices, from_offset(): return lax.ppermute(value, ('tm', 'freq'), pairs)  25.5 us
    all_to_all x5, starting transfers between devices, swap(): return lax.all_to_all(value, axis, 0, 0, axis_index_groups=groups)  24.1 us
    all_to_all x5, waiting for transfers between devices, swap(): return lax.all_to_all(value, axis, 0, 0, axis_index_groups=groups)  18.3 us
    ppermute x5, waiting for transfers between devices, from_offset(): return lax.ppermute(value, ('tm', 'freq'), pairs)  16.6 us
    ppermute x3, starting transfers between devices, other_core(): lax.ppermute(value, 'tm', [(i, i ^ 1) for i in range(lax.axis_size('tm'))])  15 us
    all_gather x1, blocking collectives, shards(): part = lax.all_gather(part, 'tm', axis_index_groups=tm_groups('core'))  6.87 us
    pallas_call x1, Pallas kernels, shards(): pl.pallas_call(plain_back, out_shape=jax.ShapeDtypeStruct((128, D), BF16)...  5.54 us
    pallas_call x1, Pallas kernels, shards(): pl.pallas_call(plain_forward, out_shape=(packet,) * 4, in_specs=[SMEM] +...  4.32 us
  transfers between devices with their start and end apart: 13, of which 8 were waited for; matrix products, arithmetic and copies ran while one was open for 0% of the time, Pallas kernels for 12%

profile of v16, /device:TPU:1, one launch (start us, length us, event | category | flops | bytes accessed | tf_op | source)
XLA Modules:
  0.0 135.3 jit_solution(13229511052349822308)
XLA Ops:
  0.6 2.1 %prepare.2 = bf16[8,192,384]{2,1,0:T(8,128)(2,1)} custom-call(s32[1]{0:T(128)} %bitcast.core_ref.refs_0_, bf16[144,768]{1,0:T(8,128)(2,1)} %bitcast.12, bf16[48,768]{1,0:T(8,128)(2,1)} %proj.2), custom_call_target="tpu_custom_call" | custom-call | tf_op jit(solution)/shard_map/prepare/pallas_call | solution.py:499
  2.8 5.9 %all-to-all-start = ((bf16[8,192,384]{2,1,0:T(8,128)(2,1)}), bf16[8,192,384]{2,1,0:T(8,128)(2,1)S(1)}, u32[]{:S(2)}, u32[]{:S(2)}) async-start(bf16[8,192,384]{2,1,0:T(8,128)(2,1)} %prepare.2), calls=%async_computation | async-start | bytes 2359296 | tf_op jit(solution)/shard_map/all_to_all | solution.py:459
  8.7 2.2 %prepare.3 = bf16[8,192,384]{2,1,0:T(8,128)(2,1)} custom-call(s32[1]{0:T(128)} %bitcast.core_ref.refs_0_, bf16[144,768]{1,0:T(8,128)(2,1)} %bitcast.13, bf16[48,768]{1,0:T(8,128)(2,1)} %proj.3), custom_call_target="tpu_custom_call" | custom-call | tf_op jit(solution)/shard_map/prepare/pallas_call | solution.py:499
  10.9 2.1 %biases.1 = (f32[64,768]{1,0:T(8,128)}, f32[64,768]{1,0:T(8,128)}, bf16[128,768]{1,0:T(8,128)(2,1)}, bf16[128,768]{1,0:T(8,128)(2,1)}) custom-call(s32[2]{0:T(128)S(1)} %add_convert_fusion.1.edge_ref, f32[12,225]{1,0:T(8,128)S(1)} %copy-done.3, f32[12,225]{1,0:T(8,128)S(1)} %copy-done.4, bf16[128,768]{1,0:T(8,128)(2,1)S(1)} %bitcast.11, ...), custom_call_target="tpu_custom_call" | custom-call | tf_op jit(solution)/shard_map/biases/pallas_call | solution.py:516
  13.0 8.3 %all-to-all-done.w_mine_ref.mine_far = bf16[8,192,384]{2,1,0:T(8,128)(2,1)S(1)} async-done(((bf16[8,192,384]{2,1,0:T(8,128)(2,1)}), bf16[8,192,384]{2,1,0:T(8,128)(2,1)S(1)}, u32[]{:S(2)}, u32[]{:S(2)}) %all-to-all-start) | async-done | bytes 1179680 | tf_op jit(solution)/shard_map/all_to_all | solution.py:459
  21.3 7.3 %collective-permute-start = (bf16[8,192,384]{2,1,0:T(8,128)(2,1)S(1)}, bf16[8,192,384]{2,1,0:T(8,128)(2,1)S(1)}, u32[]{:S(2)}, u32[]{:S(2)}) collective-permute-start(bf16[8,192,384]{2,1,0:T(8,128)(2,1)S(1)} %all-to-all-done.w_mine_ref.mine_far), channel_id=1, source_target_pairs={{0,8},{8,0},{16,24},{24,16},{32,40},{40,32},{48,56},{56,48},{64,72... | collective-permute-start | bytes 3538952 | tf_op jit(solution)/shard_map/ppermute | solution.py:473
  28.7 3.6 %all-to-all-start.1 = ((bf16[8,192,384]{2,1,0:T(8,128)(2,1)}), bf16[8,192,384]{2,1,0:T(8,128)(2,1)S(1)}, u32[]{:S(2)}, u32[]{:S(2)}) async-start(bf16[8,192,384]{2,1,0:T(8,128)(2,1)} %prepare.3), calls=%async_computation.1 | async-start | bytes 2359296 | tf_op jit(solution)/shard_map/all_to_all | solution.py:459
  32.3 4.3 %plain_forward.1 = (bf16[32,1920]{1,0:T(8,128)(2,1)}, bf16[32,1920]{1,0:T(8,128)(2,1)}, bf16[32,1920]{1,0:T(8,128)(2,1)}, bf16[32,1920]{1,0:T(8,128)(2,1)}) custom-call(s32[1]{0:T(128)} %bitcast.core_ref.refs_0_, bf16[128,768]{1,0:T(8,128)(2,1)} %bitcast.9, bf16[128,768]{1,0:T(8,128)(2,1)} %get-tuple-element.44.cot_far, ...), custom_call_target="tpu_custom_call" | custom-call | flops 20000000000 | bytes 1000000 | tf_op jit(solution)/shard_map/plain_forward/pallas_call | solution.py:540
  36.6 1.9 %collective-permute-start.1 = (bf16[32,1920]{1,0:T(8,128)(2,1)}, bf16[32,1920]{1,0:T(8,128)(2,1)S(1)}, u32[]{:S(2)}, u32[]{:S(2)}) collective-permute-start(bf16[32,1920]{1,0:T(8,128)(2,1)} %get-tuple-element.53), channel_id=1, source_target_pairs={{8,0},{9,1},{10,2},{11,3},{12,4},{13,5},{14,6},{15,7},{16,8},{17,9... | collective-permute-start | bytes 368648 | tf_op jit(solution)/shard_map/ppermute | solution.py:469
  38.6 5.7 %collective-permute-start.2 = (bf16[32,1920]{1,0:T(8,128)(2,1)}, bf16[32,1920]{1,0:T(8,128)(2,1)S(1)}, u32[]{:S(2)}, u32[]{:S(2)}) collective-permute-start(bf16[32,1920]{1,0:T(8,128)(2,1)} %get-tuple-element.54), channel_id=1, source_target_pairs={{1,0},{2,1},{3,2},{4,3},{5,4},{6,5},{7,6},{0,7},{9,8},{10,9},{11,1... | collective-permute-start | bytes 368648 | tf_op jit(solution)/shard_map/ppermute | solution.py:469
  44.3 14.0 %collective-permute-start.3 = (bf16[32,1920]{1,0:T(8,128)(2,1)}, bf16[32,1920]{1,0:T(8,128)(2,1)S(1)}, u32[]{:S(2)}, u32[]{:S(2)}) collective-permute-start(bf16[32,1920]{1,0:T(8,128)(2,1)} %get-tuple-element.55), channel_id=1, source_target_pairs={{9,0},{10,1},{11,2},{12,3},{13,4},{14,5},{15,6},{8,7},{17,8},{18,9... | collective-permute-start | bytes 368648 | tf_op jit(solution)/shard_map/ppermute | solution.py:469
  58.2 2.1 %collective-permute-done.3.diag = bf16[32,1920]{1,0:T(8,128)(2,1)S(1)} collective-permute-done((bf16[32,1920]{1,0:T(8,128)(2,1)}, bf16[32,1920]{1,0:T(8,128)(2,1)S(1)}, u32[]{:S(2)}, u32[]{:S(2)}) %collective-permute-start.3) | collective-permute-done | bytes 122912 | tf_op jit(solution)/shard_map/ppermute | solution.py:469
  60.4 5.4 %collective-permute-start.4 = (bf16[8,192,384]{2,1,0:T(8,128)(2,1)S(1)}, bf16[8,192,384]{2,1,0:T(8,128)(2,1)S(1)}, u32[]{:S(2)}, u32[]{:S(2)}) collective-permute-start(bf16[8,192,384]{2,1,0:T(8,128)(2,1)S(1)} %all-to-all-done.1.w_mine_ref.refs_9_), channel_id=1, source_target_pairs={{0,8},{8,0},{16,24},{24,16},{32,40},{40,32},{48,56},{56,48},{64,72... | collective-permute-start | bytes 3538952 | tf_op jit(solution)/shard_map/ppermute | solution.py:473
  65.8 1.9 %main_begin.1 = (bf16[128,768]{1,0:T(8,128)(2,1)S(1)}, f32[128,768]{1,0:T(8,128)S(1)}, bf16[128,768]{1,0:T(8,128)(2,1)S(1)}, f32[128,128]{1,0:T(8,128)S(1)}, bf1...) custom-call(s32[1]{0:T(128)} %bitcast.core_ref.refs_0_, ...), custom_call_target="tpu_custom_call" | custom-call | flops 5000000000 | bytes 1000000 | tf_op jit(solution)/shard_map/main_begin/pallas_call | solution.py:571
  68.2 4.0 %main.1 = (bf16[32,768]{1,0:T(8,128)(2,1)}, bf16[64,768]{1,0:T(8,128)(2,1)}, bf16[32,768]{1,0:T(8,128)(2,1)}, bf16[8,2,48,384]{3,2,1,0:T(8,128)(2,1)S(1)}, bf16[8,2,48,384]{3,2,1,0:T(8,128)(2,1)S(1)}) custom-call(s32[1]{0:T(128)} %bitcast.core_ref.refs_0_, bf16[128,768]{1,0:T(8,128)(2,1)S(1)} %get-tuple-element.60.refs_1_, ...), custom_call_target="tpu_custom_call" | custom-call | flops 1000000 | bytes 1000000 | tf_op jit(solution)/shard_map/main/pallas_call | solution.py:593
  72.3 2.3 %collective-permute-start.5 = (bf16[8,2,48,384]{3,2,1,0:T(8,128)(2,1)S(1)}, bf16[8,2,48,384]{3,2,1,0:T(8,128)(2,1)S(1)}, u32[]{:S(2)}, u32[]{:S(2)}) collective-permute-start(bf16[8,2,48,384]{3,2,1,0:T(8,128)(2,1)S(1)} %get-tuple-element.69), channel_id=1, source_target_pairs={{0,8},{8,0},{16,24},{24,16},{32,40},{40,32},{48,56},{56,48},{64,72... | collective-permute-start | bytes 1769480 | tf_op jit(solution)/shard_map/ppermute | solution.py:473
  74.6 1.6 %collective-permute-done.5 = bf16[8,2,48,384]{3,2,1,0:T(8,128)(2,1)S(1)} collective-permute-done((bf16[8,2,48,384]{3,2,1,0:T(8,128)(2,1)S(1)}, bf16[8,2,48,384]{3,2,1,0:T(8,128)(2,1)S(1)}, u32[]{:S(2)}, u32[]{:S(2)}) %collective-permute-start.5) | collective-permute-done | bytes 589856 | tf_op jit(solution)/shard_map/ppermute | solution.py:473
  76.2 1.0 add_convert_fusion
  77.1 3.7 %all-to-all-start.2 = ((bf16[8,2,48,384]{3,2,1,0:T(8,128)(2,1)}), bf16[8,2,48,384]{3,2,1,0:T(8,128)(2,1)S(1)}, u32[]{:S(2)}, u32[]{:S(2)}) async-start(bf16[8,2,48,384]{3,2,1,0:T(8,128)(2,1)} %add_convert_fusion), calls=%async_computation.2 | async-start | bytes 1179648 | tf_op jit(solution)/shard_map/all_to_all | solution.py:459
  80.8 1.9 %collective-permute-start.6 = (bf16[64,768]{1,0:T(8,128)(2,1)S(1)}, bf16[64,768]{1,0:T(8,128)(2,1)S(1)}, u32[]{:S(2)}, u32[]{:S(2)}) collective-permute-start(bf16[64,768]{1,0:T(8,128)(2,1)S(1)} %copy-done.7), channel_id=1, source_target_pairs={{504,0},{505,1},{506,2},{507,3},{508,4},{509,5},{510,6},{511,7},{0... | collective-permute-start | bytes 294920 | tf_op jit(solution)/shard_map/ppermute | solution.py:469
  82.8 7.2 %collective-permute-done.6.column = bf16[64,768]{1,0:T(8,128)(2,1)S(1)} collective-permute-done((bf16[64,768]{1,0:T(8,128)(2,1)S(1)}, bf16[64,768]{1,0:T(8,128)(2,1)S(1)}, u32[]{:S(2)}, u32[]{:S(2)}) %collective-permute-start.6) | collective-permute-done | bytes 98336 | tf_op jit(solution)/shard_map/ppermute | solution.py:469
  90.0 1.0 all-to-all-done.2.parts
  91.0 0.8 sum_copies.3
  91.8 3.5 %all-to-all-start.3 = ((bf16[4,2,48,384]{3,2,1,0:T(8,128)(2,1)}), bf16[4,2,48,384]{3,2,1,0:T(8,128)(2,1)S(1)}, u32[]{:S(2)}, u32[]{:S(2)}) async-start(bf16[4,2,48,384]{3,2,1,0:T(8,128)(2,1)} %sum_copies.3), calls=%async_computation.3 | async-start | bytes 589824 | tf_op jit(solution)/shard_map/all_to_all | solution.py:459
  95.3 2.0 %collective-permute-start.7 = (bf16[64,768]{1,0:T(8,128)(2,1)S(1)}, bf16[64,768]{1,0:T(8,128)(2,1)S(1)}, u32[]{:S(2)}, u32[]{:S(2)}) collective-permute-start(bf16[64,768]{1,0:T(8,128)(2,1)S(1)} %pad_maximum_fusion), channel_id=1, source_target_pairs={{7,0},{0,1},{1,2},{2,3},{3,4},{4,5},{5,6},{6,7},{15,8},{8,9},{9,10... | collective-permute-start | bytes 294920 | tf_op jit(solution)/shard_map/ppermute | solution.py:469
  97.4 7.2 %collective-permute-done.7.row = bf16[64,768]{1,0:T(8,128)(2,1)S(1)} collective-permute-done((bf16[64,768]{1,0:T(8,128)(2,1)S(1)}, bf16[64,768]{1,0:T(8,128)(2,1)S(1)}, u32[]{:S(2)}, u32[]{:S(2)}) %collective-permute-start.7) | collective-permute-done | bytes 98336 | tf_op jit(solution)/shard_map/ppermute | solution.py:469
  104.6 0.9 sum_copies.4
  105.5 7.6 %all-to-all-start.4 = ((bf16[8,2,48,384]{3,2,1,0:T(8,128)(2,1)}), bf16[8,2,48,384]{3,2,1,0:T(8,128)(2,1)S(1)}, u32[]{:S(2)}, u32[]{:S(2)}) async-start(bf16[8,2,48,384]{3,2,1,0:T(8,128)(2,1)} %sum_copies.4), calls=%async_computation.4 | async-start | bytes 1179648 | tf_op jit(solution)/shard_map/all_to_all | solution.py:459
  113.1 5.5 %plain_back.1 = bf16[128,768]{1,0:T(8,128)(2,1)} custom-call(s32[1]{0:T(128)} %bitcast.core_ref.refs_0_, bf16[128,768]{1,0:T(8,128)(2,1)} %bitcast.10, bf16[32,768]{1,0:T(8,128)(2,1)} %get-tuple-element.79.own_far, f32[64,768]{1,0:T(8,128)} %get-tuple-element.47.bias_far, bf16[8,192,384]{2,1,0:T(8,128)(2,1)} %copy-done, bf16[8,192,384]{2,1,0:T(8,128)(2,1)} %copy-done.5, ...), custom_call_target="tpu_custom_call" | custom-call | flops 4000000000 | bytes 4000000 | tf_op jit(solution)/shard_map/plain_back/pallas_call | solution.py:619
  118.6 9.0 %all-to-all-done.4.parts = bf16[8,2,48,384]{3,2,1,0:T(8,128)(2,1)S(1)} async-done(((bf16[8,2,48,384]{3,2,1,0:T(8,128)(2,1)}), bf16[8,2,48,384]{3,2,1,0:T(8,128)(2,1)S(1)}, u32[]{:S(2)}, u32[]{:S(2)}) %all-to-all-start.4) | async-done | bytes 589856 | tf_op jit(solution)/shard_map/all_to_all | solution.py:459
  127.7 6.9 %all_gather.3.parts = bf16[2,2,48,384]{3,2,1,0:T(8,128)(2,1)S(1)} all-gather(bf16[1,2,48,384]{3,2,1,0:T(8,128)(2,1)S(1)} %sum_copies.5), channel_id=1, replica_groups={{0,8},{16,24},{32,40},{48,56},{64,72},{80,88},{96,104},{112,120},{128,1..., dimensions={0}, use_global_device_ids=true | all-gather | bytes 221184 | tf_op jit(solution)/shard_map/all_gather | solution.py:642
  134.6 0.7 finish.1
  (26 shorter events, 0.8 us)
Async XLA Ops:
  2.8 18.6 %all-to-all-start = ((bf16[8,192,384]{2,1,0:T(8,128)(2,1)}), bf16[8,192,384]{2,1,0:T(8,128)(2,1)S(1)}, u32[]{:S(2)}, u32[]{:S(2)}) async-start(bf16[8,192,384]{2,1,0:T(8,128)(2,1)} %prepare.2), calls=%async_computation | async-start | bytes 2359296 | tf_op jit(solution)/shard_map/all_to_all | solution.py:459
  8.6 2.3 %copy-start.1 = (bf16[2,8,8,768]{3,2,1,0:T(8,128)(2,1)S(1)}, bf16[2,8,8,768]{3,2,1,0:T(8,128)(2,1)}, u32[]{:S(2)}) copy-start(bf16[2,8,8,768]{3,2,1,0:T(8,128)(2,1)} %param.9) | copy-start | bytes 589828
  8.6 2.3 %copy-start.2 = (bf16[2,8,8,768]{3,2,1,0:T(8,128)(2,1)S(1)}, bf16[2,8,8,768]{3,2,1,0:T(8,128)(2,1)}, u32[]{:S(2)}) copy-start(bf16[2,8,8,768]{3,2,1,0:T(8,128)(2,1)} %param.8) | copy-start | bytes 589828
  8.6 2.3 %copy-start.3 = (f32[12,225]{1,0:T(8,128)S(1)}, f32[12,225]{1,0:T(8,128)}, u32[]{:S(2)}) copy-start(f32[12,225]{1,0:T(8,128)} %table_p.1) | copy-start | bytes 32404
  8.7 2.3 %copy-start.4 = (f32[12,225]{1,0:T(8,128)S(1)}, f32[12,225]{1,0:T(8,128)}, u32[]{:S(2)}) copy-start(f32[12,225]{1,0:T(8,128)} %table_s.1) | copy-start | bytes 32404
  21.3 11.0 %copy-start = (bf16[8,192,384]{2,1,0:T(8,128)(2,1)}, bf16[8,192,384]{2,1,0:T(8,128)(2,1)S(1)}, u32[]{:S(2)}) copy-start(bf16[8,192,384]{2,1,0:T(8,128)(2,1)S(1)} %all-to-all-done.w_mine_ref.mine_far) | copy-start | bytes 3538948
  21.3 10.9 %collective-permute-start = (bf16[8,192,384]{2,1,0:T(8,128)(2,1)S(1)}, bf16[8,192,384]{2,1,0:T(8,128)(2,1)S(1)}, u32[]{:S(2)}, u32[]{:S(2)}) collective-permute-start(bf16[8,192,384]{2,1,0:T(8,128)(2,1)S(1)} %all-to-all-done.w_mine_ref.mine_far), channel_id=1, source_target_pairs={{0,8},{8,0},{16,24},{24,16},{32,40},{40,32},{48,56},{56,48},{64,72... | collective-permute-start | bytes 3538952 | tf_op jit(solution)/shard_map/ppermute | solution.py:473
  28.7 31.7 %all-to-all-start.1 = ((bf16[8,192,384]{2,1,0:T(8,128)(2,1)}), bf16[8,192,384]{2,1,0:T(8,128)(2,1)S(1)}, u32[]{:S(2)}, u32[]{:S(2)}) async-start(bf16[8,192,384]{2,1,0:T(8,128)(2,1)} %prepare.3), calls=%async_computation.1 | async-start | bytes 2359296 | tf_op jit(solution)/shard_map/all_to_all | solution.py:459
  32.3 4.4 %copy-start.5 = (bf16[8,192,384]{2,1,0:T(8,128)(2,1)}, bf16[8,192,384]{2,1,0:T(8,128)(2,1)S(1)}, u32[]{:S(2)}) copy-start(bf16[8,192,384]{2,1,0:T(8,128)(2,1)S(1)} %collective-permute-done.w_other_ref.other_far) | copy-start | bytes 3538948
  36.6 21.6 %collective-permute-start.1 = (bf16[32,1920]{1,0:T(8,128)(2,1)}, bf16[32,1920]{1,0:T(8,128)(2,1)S(1)}, u32[]{:S(2)}, u32[]{:S(2)}) collective-permute-start(bf16[32,1920]{1,0:T(8,128)(2,1)} %get-tuple-element.53), channel_id=1, source_target_pairs={{8,0},{9,1},{10,2},{11,3},{12,4},{13,5},{14,6},{15,7},{16,8},{17,9... | collective-permute-start | bytes 368648 | tf_op jit(solution)/shard_map/ppermute | solution.py:469
  38.6 19.7 %collective-permute-start.2 = (bf16[32,1920]{1,0:T(8,128)(2,1)}, bf16[32,1920]{1,0:T(8,128)(2,1)S(1)}, u32[]{:S(2)}, u32[]{:S(2)}) collective-permute-start(bf16[32,1920]{1,0:T(8,128)(2,1)} %get-tuple-element.54), channel_id=1, source_target_pairs={{1,0},{2,1},{3,2},{4,3},{5,4},{6,5},{7,6},{0,7},{9,8},{10,9},{11,1... | collective-permute-start | bytes 368648 | tf_op jit(solution)/shard_map/ppermute | solution.py:469
  44.3 16.1 %collective-permute-start.3 = (bf16[32,1920]{1,0:T(8,128)(2,1)}, bf16[32,1920]{1,0:T(8,128)(2,1)S(1)}, u32[]{:S(2)}, u32[]{:S(2)}) collective-permute-start(bf16[32,1920]{1,0:T(8,128)(2,1)} %get-tuple-element.55), channel_id=1, source_target_pairs={{9,0},{10,1},{11,2},{12,3},{13,4},{14,5},{15,6},{8,7},{17,8},{18,9... | collective-permute-start | bytes 368648 | tf_op jit(solution)/shard_map/ppermute | solution.py:469
  60.4 7.8 %collective-permute-start.4 = (bf16[8,192,384]{2,1,0:T(8,128)(2,1)S(1)}, bf16[8,192,384]{2,1,0:T(8,128)(2,1)S(1)}, u32[]{:S(2)}, u32[]{:S(2)}) collective-permute-start(bf16[8,192,384]{2,1,0:T(8,128)(2,1)S(1)} %all-to-all-done.1.w_mine_ref.refs_9_), channel_id=1, source_target_pairs={{0,8},{8,0},{16,24},{24,16},{32,40},{40,32},{48,56},{56,48},{64,72... | collective-permute-start | bytes 3538952 | tf_op jit(solution)/shard_map/ppermute | solution.py:473
  72.3 3.9 %collective-permute-start.5 = (bf16[8,2,48,384]{3,2,1,0:T(8,128)(2,1)S(1)}, bf16[8,2,48,384]{3,2,1,0:T(8,128)(2,1)S(1)}, u32[]{:S(2)}, u32[]{:S(2)}) collective-permute-start(bf16[8,2,48,384]{3,2,1,0:T(8,128)(2,1)S(1)} %get-tuple-element.69), channel_id=1, source_target_pairs={{0,8},{8,0},{16,24},{24,16},{32,40},{40,32},{48,56},{56,48},{64,72... | collective-permute-start | bytes 1769480 | tf_op jit(solution)/shard_map/ppermute | solution.py:473
  76.2 4.6 %copy-start.7 = (bf16[64,768]{1,0:T(8,128)(2,1)S(1)}, bf16[64,768]{1,0:T(8,128)(2,1)}, u32[]{:S(2)}) copy-start(bf16[64,768]{1,0:T(8,128)(2,1)} %get-tuple-element.73) | copy-start | bytes 294916
  77.1 18.2 %copy-start.6 = (bf16[32,768]{1,0:T(8,128)(2,1)S(1)}, bf16[32,768]{1,0:T(8,128)(2,1)}, u32[]{:S(2)}) copy-start(bf16[32,768]{1,0:T(8,128)(2,1)} %get-tuple-element.76) | copy-start | bytes 147460
  77.1 13.9 %all-to-all-start.2 = ((bf16[8,2,48,384]{3,2,1,0:T(8,128)(2,1)}), bf16[8,2,48,384]{3,2,1,0:T(8,128)(2,1)S(1)}, u32[]{:S(2)}, u32[]{:S(2)}) async-start(bf16[8,2,48,384]{3,2,1,0:T(8,128)(2,1)} %add_convert_fusion), calls=%async_computation.2 | async-start | bytes 1179648 | tf_op jit(solution)/shard_map/all_to_all | solution.py:459
  80.8 9.1 %collective-permute-start.6 = (bf16[64,768]{1,0:T(8,128)(2,1)S(1)}, bf16[64,768]{1,0:T(8,128)(2,1)S(1)}, u32[]{:S(2)}, u32[]{:S(2)}) collective-permute-start(bf16[64,768]{1,0:T(8,128)(2,1)S(1)} %copy-done.7), channel_id=1, source_target_pairs={{504,0},{505,1},{506,2},{507,3},{508,4},{509,5},{510,6},{511,7},{0... | collective-permute-start | bytes 294920 | tf_op jit(solution)/shard_map/ppermute | solution.py:469
  91.8 12.8 %all-to-all-start.3 = ((bf16[4,2,48,384]{3,2,1,0:T(8,128)(2,1)}), bf16[4,2,48,384]{3,2,1,0:T(8,128)(2,1)S(1)}, u32[]{:S(2)}, u32[]{:S(2)}) async-start(bf16[4,2,48,384]{3,2,1,0:T(8,128)(2,1)} %sum_copies.3), calls=%async_computation.3 | async-start | bytes 589824 | tf_op jit(solution)/shard_map/all_to_all | solution.py:459
  95.3 9.3 %collective-permute-start.7 = (bf16[64,768]{1,0:T(8,128)(2,1)S(1)}, bf16[64,768]{1,0:T(8,128)(2,1)S(1)}, u32[]{:S(2)}, u32[]{:S(2)}) collective-permute-start(bf16[64,768]{1,0:T(8,128)(2,1)S(1)} %pad_maximum_fusion), channel_id=1, source_target_pairs={{7,0},{0,1},{1,2},{2,3},{3,4},{4,5},{5,6},{6,7},{15,8},{8,9},{9,10... | collective-permute-start | bytes 294920 | tf_op jit(solution)/shard_map/ppermute | solution.py:469
  105.5 22.1 %all-to-all-start.4 = ((bf16[8,2,48,384]{3,2,1,0:T(8,128)(2,1)}), bf16[8,2,48,384]{3,2,1,0:T(8,128)(2,1)S(1)}, u32[]{:S(2)}, u32[]{:S(2)}) async-start(bf16[8,2,48,384]{3,2,1,0:T(8,128)(2,1)} %sum_copies.4), calls=%async_computation.4 | async-start | bytes 1179648 | tf_op jit(solution)/shard_map/all_to_all | solution.py:459

commit v17 on v16

--- a/solution.py
+++ b/solution.py
@@ -267,6 +267,7 @@
     out_packed,
     out_d_mixed,
     out_bias,
+    out_mask,
     staged,
     sems,
 ):
@@ -275,6 +276,7 @@
     for i, part in ((1, right), (2, below), (3, diag)):
         staged[i * 32 : (i + 1) * 32] = part[...]
     pick = quadrant_pick(True)
+    out_mask[...] = head_mask()
     loads[0].wait()
     out_grads[...] = dot(pick, staged[:, D + WIDE :]).astype(BF16)
     block_out = dot(pick, staged[:, 0:D])
@@ -299,6 +301,7 @@
     packed_ref,
     d_mixed_ref,
     bias_s,
+    mask,
     w_mine_ref,
     w_other_ref,
     to_own,
@@ -309,11 +312,9 @@
     quads,
     rows_small,
     sums,
-    mask,
     sems,
 ):
     mine, other = sides(core_ref)
-    mask[...] = head_mask()
     normed, rstd = normed_ref[...], rstd_ref[:, 0:1]
     mixed_plain = mixed_ref[...]
     w_mine, w_other = qkv_of(w_mine_ref), qkv_of(w_other_ref)
@@ -579,9 +580,10 @@
             near((128, 3 * WIDE), F32),
             near((128, WIDE), F32),
             near((SPOTS, LANES), F32),
+            near((LANES, WIDE), BF16),
         ),
         in_specs=[SMEM] + [HBM] * 2 + [VMEM] * 4,
-        out_specs=[VMEM] * 8,
+        out_specs=[VMEM] * 9,
         scratch_shapes=[
             pltpu.VMEM((128, 2 * D + WIDE), BF16),
             pltpu.SemaphoreType.DMA((2,)),
@@ -593,13 +595,12 @@
     g_own, to_right, to_below, keep, send = pl.pallas_call(
         lambda *refs: main_kernel(grad_scale, *refs),
         out_shape=(piece, column, piece, local, local),
-        in_specs=[SMEM] + [VMEM] * 10,
+        in_specs=[SMEM] + [VMEM] * 11,
         out_specs=[HBM] * 3 + [VMEM] * 2,
         scratch_shapes=[
             pltpu.VMEM((128, D), BF16),
             pltpu.VMEM((128, D), BF16),
             pltpu.VMEM((128, D), F32),
-            pltpu.VMEM((LANES, WIDE), BF16),
             pltpu.SemaphoreType.DMA((4,)),
         ],
         compiler_params=params(),

time: 136 us -> 136 us (level)
  no operation moved by 1% of the time
where the time goes in v17:
time: 136 us; the launch traced here: 135 us
  starting transfers between devices  64.7 us (48%)
  waiting for transfers between devices  37.1 us (27%)
  Pallas kernels  24.6 us (18%)
  blocking collectives  6.88 us (5%)
    ppermute x5, starting transfers between devices, from_offset(): return lax.ppermute(value, ('tm', 'freq'), pairs)  25.5 us
    all_to_all x5, starting transfers between devices, swap(): return lax.all_to_all(value, axis, 0, 0, axis_index_groups=groups)  24.1 us
    all_to_all x5, waiting for transfers between devices, swap(): return lax.all_to_all(value, axis, 0, 0, axis_index_groups=groups)  18.3 us
    ppermute x5, waiting for transfers between devices, from_offset(): return lax.ppermute(value, ('tm', 'freq'), pairs)  16.6 us
    ppermute x3, starting transfers between devices, other_core(): lax.ppermute(value, 'tm', [(i, i ^ 1) for i in range(lax.axis_size('tm'))])  15 us
    all_gather x1, blocking collectives, shards(): part = lax.all_gather(part, 'tm', axis_index_groups=tm_groups('core'))  6.88 us
    pallas_call x1, Pallas kernels, shards(): pl.pallas_call(plain_back, out_shape=jax.ShapeDtypeStruct((128, D), BF16)...  5.55 us
    pallas_call x1, Pallas kernels, shards(): pl.pallas_call(plain_forward, out_shape=(packet,) * 4, in_specs=[SMEM] +...  4.32 us
  transfers between devices with their start and end apart: 13, of which 8 were waited for; matrix products, arithmetic and copies ran while one was open for 0% of the time, Pallas kernels for 12%

profile of v17, /device:TPU:1, one launch (start us, length us, event | category | flops | bytes accessed | tf_op | source)
XLA Modules:
  0.0 135.2 jit_solution(18381298276977501772)
XLA Ops:
  0.6 2.1 %prepare.2 = bf16[8,192,384]{2,1,0:T(8,128)(2,1)} custom-call(s32[1]{0:T(128)} %bitcast.core_ref.refs_0_, bf16[144,768]{1,0:T(8,128)(2,1)} %bitcast.12, bf16[48,768]{1,0:T(8,128)(2,1)} %proj.2), custom_call_target="tpu_custom_call" | custom-call | tf_op jit(solution)/shard_map/prepare/pallas_call | solution.py:500
  2.8 5.9 %all-to-all-start = ((bf16[8,192,384]{2,1,0:T(8,128)(2,1)}), bf16[8,192,384]{2,1,0:T(8,128)(2,1)S(1)}, u32[]{:S(2)}, u32[]{:S(2)}) async-start(bf16[8,192,384]{2,1,0:T(8,128)(2,1)} %prepare.2), calls=%async_computation | async-start | bytes 2359296 | tf_op jit(solution)/shard_map/all_to_all | solution.py:460
  8.7 2.2 %prepare.3 = bf16[8,192,384]{2,1,0:T(8,128)(2,1)} custom-call(s32[1]{0:T(128)} %bitcast.core_ref.refs_0_, bf16[144,768]{1,0:T(8,128)(2,1)} %bitcast.13, bf16[48,768]{1,0:T(8,128)(2,1)} %proj.3), custom_call_target="tpu_custom_call" | custom-call | tf_op jit(solution)/shard_map/prepare/pallas_call | solution.py:500
  10.9 2.1 %biases.1 = (f32[64,768]{1,0:T(8,128)}, f32[64,768]{1,0:T(8,128)}, bf16[128,768]{1,0:T(8,128)(2,1)}, bf16[128,768]{1,0:T(8,128)(2,1)}) custom-call(s32[2]{0:T(128)S(1)} %add_convert_fusion.1.edge_ref, f32[12,225]{1,0:T(8,128)S(1)} %copy-done.3, f32[12,225]{1,0:T(8,128)S(1)} %copy-done.4, bf16[128,768]{1,0:T(8,128)(2,1)S(1)} %bitcast.11, ...), custom_call_target="tpu_custom_call" | custom-call | tf_op jit(solution)/shard_map/biases/pallas_call | solution.py:517
  13.0 8.3 %all-to-all-done.w_mine_ref.mine_far = bf16[8,192,384]{2,1,0:T(8,128)(2,1)S(1)} async-done(((bf16[8,192,384]{2,1,0:T(8,128)(2,1)}), bf16[8,192,384]{2,1,0:T(8,128)(2,1)S(1)}, u32[]{:S(2)}, u32[]{:S(2)}) %all-to-all-start) | async-done | bytes 1179680 | tf_op jit(solution)/shard_map/all_to_all | solution.py:460
  21.3 7.3 %collective-permute-start = (bf16[8,192,384]{2,1,0:T(8,128)(2,1)S(1)}, bf16[8,192,384]{2,1,0:T(8,128)(2,1)S(1)}, u32[]{:S(2)}, u32[]{:S(2)}) collective-permute-start(bf16[8,192,384]{2,1,0:T(8,128)(2,1)S(1)} %all-to-all-done.w_mine_ref.mine_far), channel_id=1, source_target_pairs={{0,8},{8,0},{16,24},{24,16},{32,40},{40,32},{48,56},{56,48},{64,72... | collective-permute-start | bytes 3538952 | tf_op jit(solution)/shard_map/ppermute | solution.py:474
  28.7 3.6 %all-to-all-start.1 = ((bf16[8,192,384]{2,1,0:T(8,128)(2,1)}), bf16[8,192,384]{2,1,0:T(8,128)(2,1)S(1)}, u32[]{:S(2)}, u32[]{:S(2)}) async-start(bf16[8,192,384]{2,1,0:T(8,128)(2,1)} %prepare.3), calls=%async_computation.1 | async-start | bytes 2359296 | tf_op jit(solution)/shard_map/all_to_all | solution.py:460
  32.3 4.3 %plain_forward.1 = (bf16[32,1920]{1,0:T(8,128)(2,1)}, bf16[32,1920]{1,0:T(8,128)(2,1)}, bf16[32,1920]{1,0:T(8,128)(2,1)}, bf16[32,1920]{1,0:T(8,128)(2,1)}) custom-call(s32[1]{0:T(128)} %bitcast.core_ref.refs_0_, bf16[128,768]{1,0:T(8,128)(2,1)} %bitcast.9, bf16[128,768]{1,0:T(8,128)(2,1)} %get-tuple-element.45.cot_far, ...), custom_call_target="tpu_custom_call" | custom-call | flops 20000000000 | bytes 1000000 | tf_op jit(solution)/shard_map/plain_forward/pallas_call | solution.py:541
  36.6 1.9 %collective-permute-start.1 = (bf16[32,1920]{1,0:T(8,128)(2,1)}, bf16[32,1920]{1,0:T(8,128)(2,1)S(1)}, u32[]{:S(2)}, u32[]{:S(2)}) collective-permute-start(bf16[32,1920]{1,0:T(8,128)(2,1)} %get-tuple-element.54), channel_id=1, source_target_pairs={{8,0},{9,1},{10,2},{11,3},{12,4},{13,5},{14,6},{15,7},{16,8},{17,9... | collective-permute-start | bytes 368648 | tf_op jit(solution)/shard_map/ppermute | solution.py:470
  38.6 5.7 %collective-permute-start.2 = (bf16[32,1920]{1,0:T(8,128)(2,1)}, bf16[32,1920]{1,0:T(8,128)(2,1)S(1)}, u32[]{:S(2)}, u32[]{:S(2)}) collective-permute-start(bf16[32,1920]{1,0:T(8,128)(2,1)} %get-tuple-element.55), channel_id=1, source_target_pairs={{1,0},{2,1},{3,2},{4,3},{5,4},{6,5},{7,6},{0,7},{9,8},{10,9},{11,1... | collective-permute-start | bytes 368648 | tf_op jit(solution)/shard_map/ppermute | solution.py:470
  44.3 14.0 %collective-permute-start.3 = (bf16[32,1920]{1,0:T(8,128)(2,1)}, bf16[32,1920]{1,0:T(8,128)(2,1)S(1)}, u32[]{:S(2)}, u32[]{:S(2)}) collective-permute-start(bf16[32,1920]{1,0:T(8,128)(2,1)} %get-tuple-element.56), channel_id=1, source_target_pairs={{9,0},{10,1},{11,2},{12,3},{13,4},{14,5},{15,6},{8,7},{17,8},{18,9... | collective-permute-start | bytes 368648 | tf_op jit(solution)/shard_map/ppermute | solution.py:470
  58.2 2.1 %collective-permute-done.3.diag = bf16[32,1920]{1,0:T(8,128)(2,1)S(1)} collective-permute-done((bf16[32,1920]{1,0:T(8,128)(2,1)}, bf16[32,1920]{1,0:T(8,128)(2,1)S(1)}, u32[]{:S(2)}, u32[]{:S(2)}) %collective-permute-start.3) | collective-permute-done | bytes 122912 | tf_op jit(solution)/shard_map/ppermute | solution.py:470
  60.4 5.4 %collective-permute-start.4 = (bf16[8,192,384]{2,1,0:T(8,128)(2,1)S(1)}, bf16[8,192,384]{2,1,0:T(8,128)(2,1)S(1)}, u32[]{:S(2)}, u32[]{:S(2)}) collective-permute-start(bf16[8,192,384]{2,1,0:T(8,128)(2,1)S(1)} %all-to-all-done.1.w_mine_ref.refs_10_), channel_id=1, source_target_pairs={{0,8},{8,0},{16,24},{24,16},{32,40},{40,32},{48,56},{56,48},{64,72... | collective-permute-start | bytes 3538952 | tf_op jit(solution)/shard_map/ppermute | solution.py:474
  65.8 1.9 %main_begin.1 = (bf16[128,768]{1,0:T(8,128)(2,1)S(1)}, f32[128,768]{1,0:T(8,128)S(1)}, bf16[128,768]{1,0:T(8,128)(2,1)S(1)}, f32[128,128]{1,0:T(8,128)S(1)}, bf1...) custom-call(s32[1]{0:T(128)} %bitcast.core_ref.refs_0_, ...), custom_call_target="tpu_custom_call" | custom-call | flops 5000000000 | bytes 1000000 | tf_op jit(solution)/shard_map/main_begin/pallas_call | solution.py:572
  68.2 4.0 %main.1 = (bf16[32,768]{1,0:T(8,128)(2,1)}, bf16[64,768]{1,0:T(8,128)(2,1)}, bf16[32,768]{1,0:T(8,128)(2,1)}, bf16[8,2,48,384]{3,2,1,0:T(8,128)(2,1)S(1)}, bf16[8,2,48,384]{3,2,1,0:T(8,128)(2,1)S(1)}) custom-call(s32[1]{0:T(128)} %bitcast.core_ref.refs_0_, bf16[128,768]{1,0:T(8,128)(2,1)S(1)} %get-tuple-element.61.refs_1_, ...), custom_call_target="tpu_custom_call" | custom-call | flops 1000000 | bytes 1000000 | tf_op jit(solution)/shard_map/main/pallas_call | solution.py:595
  72.2 2.3 %collective-permute-start.5 = (bf16[8,2,48,384]{3,2,1,0:T(8,128)(2,1)S(1)}, bf16[8,2,48,384]{3,2,1,0:T(8,128)(2,1)S(1)}, u32[]{:S(2)}, u32[]{:S(2)}) collective-permute-start(bf16[8,2,48,384]{3,2,1,0:T(8,128)(2,1)S(1)} %get-tuple-element.71), channel_id=1, source_target_pairs={{0,8},{8,0},{16,24},{24,16},{32,40},{40,32},{48,56},{56,48},{64,72... | collective-permute-start | bytes 1769480 | tf_op jit(solution)/shard_map/ppermute | solution.py:474
  74.6 1.6 %collective-permute-done.5 = bf16[8,2,48,384]{3,2,1,0:T(8,128)(2,1)S(1)} collective-permute-done((bf16[8,2,48,384]{3,2,1,0:T(8,128)(2,1)S(1)}, bf16[8,2,48,384]{3,2,1,0:T(8,128)(2,1)S(1)}, u32[]{:S(2)}, u32[]{:S(2)}) %collective-permute-start.5) | collective-permute-done | bytes 589856 | tf_op jit(solution)/shard_map/ppermute | solution.py:474
  76.2 1.0 add_convert_fusion
  77.1 3.7 %all-to-all-start.2 = ((bf16[8,2,48,384]{3,2,1,0:T(8,128)(2,1)}), bf16[8,2,48,384]{3,2,1,0:T(8,128)(2,1)S(1)}, u32[]{:S(2)}, u32[]{:S(2)}) async-start(bf16[8,2,48,384]{3,2,1,0:T(8,128)(2,1)} %add_convert_fusion), calls=%async_computation.2 | async-start | bytes 1179648 | tf_op jit(solution)/shard_map/all_to_all | solution.py:460
  80.8 1.9 %collective-permute-start.6 = (bf16[64,768]{1,0:T(8,128)(2,1)S(1)}, bf16[64,768]{1,0:T(8,128)(2,1)S(1)}, u32[]{:S(2)}, u32[]{:S(2)}) collective-permute-start(bf16[64,768]{1,0:T(8,128)(2,1)S(1)} %copy-done.7), channel_id=1, source_target_pairs={{504,0},{505,1},{506,2},{507,3},{508,4},{509,5},{510,6},{511,7},{0... | collective-permute-start | bytes 294920 | tf_op jit(solution)/shard_map/ppermute | solution.py:470
  82.8 7.2 %collective-permute-done.6.column = bf16[64,768]{1,0:T(8,128)(2,1)S(1)} collective-permute-done((bf16[64,768]{1,0:T(8,128)(2,1)S(1)}, bf16[64,768]{1,0:T(8,128)(2,1)S(1)}, u32[]{:S(2)}, u32[]{:S(2)}) %collective-permute-start.6) | collective-permute-done | bytes 98336 | tf_op jit(solution)/shard_map/ppermute | solution.py:470
  90.0 1.0 all-to-all-done.2.parts
  91.0 0.8 sum_copies.3
  91.8 3.5 %all-to-all-start.3 = ((bf16[4,2,48,384]{3,2,1,0:T(8,128)(2,1)}), bf16[4,2,48,384]{3,2,1,0:T(8,128)(2,1)S(1)}, u32[]{:S(2)}, u32[]{:S(2)}) async-start(bf16[4,2,48,384]{3,2,1,0:T(8,128)(2,1)} %sum_copies.3), calls=%async_computation.3 | async-start | bytes 589824 | tf_op jit(solution)/shard_map/all_to_all | solution.py:460
  95.3 2.0 %collective-permute-start.7 = (bf16[64,768]{1,0:T(8,128)(2,1)S(1)}, bf16[64,768]{1,0:T(8,128)(2,1)S(1)}, u32[]{:S(2)}, u32[]{:S(2)}) collective-permute-start(bf16[64,768]{1,0:T(8,128)(2,1)S(1)} %pad_maximum_fusion), channel_id=1, source_target_pairs={{7,0},{0,1},{1,2},{2,3},{3,4},{4,5},{5,6},{6,7},{15,8},{8,9},{9,10... | collective-permute-start | bytes 294920 | tf_op jit(solution)/shard_map/ppermute | solution.py:470
  97.4 7.2 %collective-permute-done.7.row = bf16[64,768]{1,0:T(8,128)(2,1)S(1)} collective-permute-done((bf16[64,768]{1,0:T(8,128)(2,1)S(1)}, bf16[64,768]{1,0:T(8,128)(2,1)S(1)}, u32[]{:S(2)}, u32[]{:S(2)}) %collective-permute-start.7) | collective-permute-done | bytes 98336 | tf_op jit(solution)/shard_map/ppermute | solution.py:470
  104.6 0.9 sum_copies.4
  105.5 7.5 %all-to-all-start.4 = ((bf16[8,2,48,384]{3,2,1,0:T(8,128)(2,1)}), bf16[8,2,48,384]{3,2,1,0:T(8,128)(2,1)S(1)}, u32[]{:S(2)}, u32[]{:S(2)}) async-start(bf16[8,2,48,384]{3,2,1,0:T(8,128)(2,1)} %sum_copies.4), calls=%async_computation.4 | async-start | bytes 1179648 | tf_op jit(solution)/shard_map/all_to_all | solution.py:460
  113.0 5.5 %plain_back.1 = bf16[128,768]{1,0:T(8,128)(2,1)} custom-call(s32[1]{0:T(128)} %bitcast.core_ref.refs_0_, bf16[128,768]{1,0:T(8,128)(2,1)} %bitcast.10, bf16[32,768]{1,0:T(8,128)(2,1)} %get-tuple-element.81.own_far, f32[64,768]{1,0:T(8,128)} %get-tuple-element.48.bias_far, bf16[8,192,384]{2,1,0:T(8,128)(2,1)} %copy-done, bf16[8,192,384]{2,1,0:T(8,128)(2,1)} %copy-done.5, ...), custom_call_target="tpu_custom_call" | custom-call | flops 4000000000 | bytes 4000000 | tf_op jit(solution)/shard_map/plain_back/pallas_call | solution.py:620
  118.6 9.0 %all-to-all-done.4.parts = bf16[8,2,48,384]{3,2,1,0:T(8,128)(2,1)S(1)} async-done(((bf16[8,2,48,384]{3,2,1,0:T(8,128)(2,1)}), bf16[8,2,48,384]{3,2,1,0:T(8,128)(2,1)S(1)}, u32[]{:S(2)}, u32[]{:S(2)}) %all-to-all-start.4) | async-done | bytes 589856 | tf_op jit(solution)/shard_map/all_to_all | solution.py:460
  127.6 6.9 %all_gather.3.parts = bf16[2,2,48,384]{3,2,1,0:T(8,128)(2,1)S(1)} all-gather(bf16[1,2,48,384]{3,2,1,0:T(8,128)(2,1)S(1)} %sum_copies.5), channel_id=1, replica_groups={{0,8},{16,24},{32,40},{48,56},{64,72},{80,88},{96,104},{112,120},{128,1..., dimensions={0}, use_global_device_ids=true | all-gather | bytes 221184 | tf_op jit(solution)/shard_map/all_gather | solution.py:643
  134.5 0.7 finish.1
  (26 shorter events, 0.8 us)
Async XLA Ops:
  2.8 18.6 %all-to-all-start = ((bf16[8,192,384]{2,1,0:T(8,128)(2,1)}), bf16[8,192,384]{2,1,0:T(8,128)(2,1)S(1)}, u32[]{:S(2)}, u32[]{:S(2)}) async-start(bf16[8,192,384]{2,1,0:T(8,128)(2,1)} %prepare.2), calls=%async_computation | async-start | bytes 2359296 | tf_op jit(solution)/shard_map/all_to_all | solution.py:460
  8.6 2.3 %copy-start.1 = (bf16[2,8,8,768]{3,2,1,0:T(8,128)(2,1)S(1)}, bf16[2,8,8,768]{3,2,1,0:T(8,128)(2,1)}, u32[]{:S(2)}) copy-start(bf16[2,8,8,768]{3,2,1,0:T(8,128)(2,1)} %param.9) | copy-start | bytes 589828
  8.6 2.3 %copy-start.2 = (bf16[2,8,8,768]{3,2,1,0:T(8,128)(2,1)S(1)}, bf16[2,8,8,768]{3,2,1,0:T(8,128)(2,1)}, u32[]{:S(2)}) copy-start(bf16[2,8,8,768]{3,2,1,0:T(8,128)(2,1)} %param.8) | copy-start | bytes 589828
  8.6 2.3 %copy-start.3 = (f32[12,225]{1,0:T(8,128)S(1)}, f32[12,225]{1,0:T(8,128)}, u32[]{:S(2)}) copy-start(f32[12,225]{1,0:T(8,128)} %table_p.1) | copy-start | bytes 32404
  8.7 2.3 %copy-start.4 = (f32[12,225]{1,0:T(8,128)S(1)}, f32[12,225]{1,0:T(8,128)}, u32[]{:S(2)}) copy-start(f32[12,225]{1,0:T(8,128)} %table_s.1) | copy-start | bytes 32404
  21.3 11.0 %copy-start = (bf16[8,192,384]{2,1,0:T(8,128)(2,1)}, bf16[8,192,384]{2,1,0:T(8,128)(2,1)S(1)}, u32[]{:S(2)}) copy-start(bf16[8,192,384]{2,1,0:T(8,128)(2,1)S(1)} %all-to-all-done.w_mine_ref.mine_far) | copy-start | bytes 3538948
  21.3 10.9 %collective-permute-start = (bf16[8,192,384]{2,1,0:T(8,128)(2,1)S(1)}, bf16[8,192,384]{2,1,0:T(8,128)(2,1)S(1)}, u32[]{:S(2)}, u32[]{:S(2)}) collective-permute-start(bf16[8,192,384]{2,1,0:T(8,128)(2,1)S(1)} %all-to-all-done.w_mine_ref.mine_far), channel_id=1, source_target_pairs={{0,8},{8,0},{16,24},{24,16},{32,40},{40,32},{48,56},{56,48},{64,72... | collective-permute-start | bytes 3538952 | tf_op jit(solution)/shard_map/ppermute | solution.py:474
  28.7 31.7 %all-to-all-start.1 = ((bf16[8,192,384]{2,1,0:T(8,128)(2,1)}), bf16[8,192,384]{2,1,0:T(8,128)(2,1)S(1)}, u32[]{:S(2)}, u32[]{:S(2)}) async-start(bf16[8,192,384]{2,1,0:T(8,128)(2,1)} %prepare.3), calls=%async_computation.1 | async-start | bytes 2359296 | tf_op jit(solution)/shard_map/all_to_all | solution.py:460
  32.3 4.4 %copy-start.5 = (bf16[8,192,384]{2,1,0:T(8,128)(2,1)}, bf16[8,192,384]{2,1,0:T(8,128)(2,1)S(1)}, u32[]{:S(2)}) copy-start(bf16[8,192,384]{2,1,0:T(8,128)(2,1)S(1)} %collective-permute-done.w_other_ref.other_far) | copy-start | bytes 3538948
  36.6 21.6 %collective-permute-start.1 = (bf16[32,1920]{1,0:T(8,128)(2,1)}, bf16[32,1920]{1,0:T(8,128)(2,1)S(1)}, u32[]{:S(2)}, u32[]{:S(2)}) collective-permute-start(bf16[32,1920]{1,0:T(8,128)(2,1)} %get-tuple-element.54), channel_id=1, source_target_pairs={{8,0},{9,1},{10,2},{11,3},{12,4},{13,5},{14,6},{15,7},{16,8},{17,9... | collective-permute-start | bytes 368648 | tf_op jit(solution)/shard_map/ppermute | solution.py:470
  38.6 19.7 %collective-permute-start.2 = (bf16[32,1920]{1,0:T(8,128)(2,1)}, bf16[32,1920]{1,0:T(8,128)(2,1)S(1)}, u32[]{:S(2)}, u32[]{:S(2)}) collective-permute-start(bf16[32,1920]{1,0:T(8,128)(2,1)} %get-tuple-element.55), channel_id=1, source_target_pairs={{1,0},{2,1},{3,2},{4,3},{5,4},{6,5},{7,6},{0,7},{9,8},{10,9},{11,1... | collective-permute-start | bytes 368648 | tf_op jit(solution)/shard_map/ppermute | solution.py:470
  44.3 16.1 %collective-permute-start.3 = (bf16[32,1920]{1,0:T(8,128)(2,1)}, bf16[32,1920]{1,0:T(8,128)(2,1)S(1)}, u32[]{:S(2)}, u32[]{:S(2)}) collective-permute-start(bf16[32,1920]{1,0:T(8,128)(2,1)} %get-tuple-element.56), channel_id=1, source_target_pairs={{9,0},{10,1},{11,2},{12,3},{13,4},{14,5},{15,6},{8,7},{17,8},{18,9... | collective-permute-start | bytes 368648 | tf_op jit(solution)/shard_map/ppermute | solution.py:470
  60.4 7.8 %collective-permute-start.4 = (bf16[8,192,384]{2,1,0:T(8,128)(2,1)S(1)}, bf16[8,192,384]{2,1,0:T(8,128)(2,1)S(1)}, u32[]{:S(2)}, u32[]{:S(2)}) collective-permute-start(bf16[8,192,384]{2,1,0:T(8,128)(2,1)S(1)} %all-to-all-done.1.w_mine_ref.refs_10_), channel_id=1, source_target_pairs={{0,8},{8,0},{16,24},{24,16},{32,40},{40,32},{48,56},{56,48},{64,72... | collective-permute-start | bytes 3538952 | tf_op jit(solution)/shard_map/ppermute | solution.py:474
  72.2 3.9 %collective-permute-start.5 = (bf16[8,2,48,384]{3,2,1,0:T(8,128)(2,1)S(1)}, bf16[8,2,48,384]{3,2,1,0:T(8,128)(2,1)S(1)}, u32[]{:S(2)}, u32[]{:S(2)}) collective-permute-start(bf16[8,2,48,384]{3,2,1,0:T(8,128)(2,1)S(1)} %get-tuple-element.71), channel_id=1, source_target_pairs={{0,8},{8,0},{16,24},{24,16},{32,40},{40,32},{48,56},{56,48},{64,72... | collective-permute-start | bytes 1769480 | tf_op jit(solution)/shard_map/ppermute | solution.py:474
  76.2 4.6 %copy-start.7 = (bf16[64,768]{1,0:T(8,128)(2,1)S(1)}, bf16[64,768]{1,0:T(8,128)(2,1)}, u32[]{:S(2)}) copy-start(bf16[64,768]{1,0:T(8,128)(2,1)} %get-tuple-element.75) | copy-start | bytes 294916
  77.1 18.2 %copy-start.6 = (bf16[32,768]{1,0:T(8,128)(2,1)S(1)}, bf16[32,768]{1,0:T(8,128)(2,1)}, u32[]{:S(2)}) copy-start(bf16[32,768]{1,0:T(8,128)(2,1)} %get-tuple-element.78) | copy-start | bytes 147460
  77.1 13.9 %all-to-all-start.2 = ((bf16[8,2,48,384]{3,2,1,0:T(8,128)(2,1)}), bf16[8,2,48,384]{3,2,1,0:T(8,128)(2,1)S(1)}, u32[]{:S(2)}, u32[]{:S(2)}) async-start(bf16[8,2,48,384]{3,2,1,0:T(8,128)(2,1)} %add_convert_fusion), calls=%async_computation.2 | async-start | bytes 1179648 | tf_op jit(solution)/shard_map/all_to_all | solution.py:460
  80.8 9.1 %collective-permute-start.6 = (bf16[64,768]{1,0:T(8,128)(2,1)S(1)}, bf16[64,768]{1,0:T(8,128)(2,1)S(1)}, u32[]{:S(2)}, u32[]{:S(2)}) collective-permute-start(bf16[64,768]{1,0:T(8,128)(2,1)S(1)} %copy-done.7), channel_id=1, source_target_pairs={{504,0},{505,1},{506,2},{507,3},{508,4},{509,5},{510,6},{511,7},{0... | collective-permute-start | bytes 294920 | tf_op jit(solution)/shard_map/ppermute | solution.py:470
  91.8 12.8 %all-to-all-start.3 = ((bf16[4,2,48,384]{3,2,1,0:T(8,128)(2,1)}), bf16[4,2,48,384]{3,2,1,0:T(8,128)(2,1)S(1)}, u32[]{:S(2)}, u32[]{:S(2)}) async-start(bf16[4,2,48,384]{3,2,1,0:T(8,128)(2,1)} %sum_copies.3), calls=%async_computation.3 | async-start | bytes 589824 | tf_op jit(solution)/shard_map/all_to_all | solution.py:460
  95.3 9.3 %collective-permute-start.7 = (bf16[64,768]{1,0:T(8,128)(2,1)S(1)}, bf16[64,768]{1,0:T(8,128)(2,1)S(1)}, u32[]{:S(2)}, u32[]{:S(2)}) collective-permute-start(bf16[64,768]{1,0:T(8,128)(2,1)S(1)} %pad_maximum_fusion), channel_id=1, source_target_pairs={{7,0},{0,1},{1,2},{2,3},{3,4},{4,5},{5,6},{6,7},{15,8},{8,9},{9,10... | collective-permute-start | bytes 294920 | tf_op jit(solution)/shard_map/ppermute | solution.py:470
  105.5 22.1 %all-to-all-start.4 = ((bf16[8,2,48,384]{3,2,1,0:T(8,128)(2,1)}), bf16[8,2,48,384]{3,2,1,0:T(8,128)(2,1)S(1)}, u32[]{:S(2)}, u32[]{:S(2)}) async-start(bf16[8,2,48,384]{3,2,1,0:T(8,128)(2,1)} %sum_copies.4), calls=%async_computation.4 | async-start | bytes 1179648 | tf_op jit(solution)/shard_map/all_to_all | solution.py:460
